TPU v7x, 32 devices: a whole 2x2x4 slice. The times are simulated.
32 devices in a mesh: groups: 2 (over y), dp: 4 (over z), tensor: 2 (over x), seq: 2 (over core).
Axes of the slice: x: 2, y: 2, z: 4, core: 2. Of those that a mesh axis runs over, the one named last changes fastest.
Arguments:
- inputs: bfloat16 [8192, 4096], P(('groups', 'dp', 'seq'), 'tensor'), parts along dimension 0, may hold values from -6 to 6
- cotangent: bfloat16 [8192, 4096], P(('groups', 'dp', 'seq'), 'tensor'), parts along dimension 0, may hold values from -6 to 6
- gate_pre: bfloat16 [8192, 11008], P(('groups', 'dp', 'seq'), 'tensor'), parts along dimension 0, may hold values from -8 to 8
- down_weight: bfloat16 [11008, 4096], P('tensor', 'dp'), may hold values from -0.0546875 to 0.0546875
- proj_in: bfloat16 [4096, 32], P('tensor'), may hold values from -0.09375 to 0.09375
- proj_out: bfloat16 [11008, 32], P('tensor'), may hold values from -0.0546875 to 0.0546875
- doc_lens: int32 [8, 16], P(('groups', 'dp')), parts along dimension 0, may hold values from 1 to 256, 1024 in all within a row
- queries: float32 [512, 1024], replicated, may hold values from -0.06 to 0.06
Outputs:
- doc_grads: float32 [128, 1024], P(('groups', 'dp')), parts along dimension 0
- fisher: float32 [2048, 1024], P(('groups', 'tensor', 'seq')), parts along dimension 0
- scores: float32 [512, 128], P(None, ('groups', 'dp')), parts along dimension 1
There are 2 independent parts, one for each index of `groups`. A program takes and returns all parts, laid end to end along the dimension named above; an argument that names none is the same for every part. Nothing has to cross between parts.
Inputs may be any that keep to these rules, and one draw needn't show every extreme that they name: `doc_lens`: each row sums to 1024 and its largest entry is exactly 256.
All inputs are finite; a program needn't handle non-finite values.
Results may differ from a plain program's by a relative error of at most 0.0041.
Values may be sent and summed in bfloat16 or wider, within the bound.
No kernel may reach another device: no remote copies, remote signals or barrier semaphores. Data moves between devices by JAX's collectives and lax.ppermute only.
A program may use at most 192 MiB of HBM per device.

v0:
```python
import jax
import jax.numpy as jnp
from jax import lax
from jax.sharding import PartitionSpec as P


def on_device(inputs, cotangent, gate_pre, down_weight, proj_in, proj_out, doc_lens, queries):
    rows = inputs.shape[0]
    full_cotangent = lax.all_gather(cotangent, "tensor", axis=1, tiled=True)
    hidden_grad = lax.dot_general(
        full_cotangent,
        lax.all_gather(down_weight, "dp", axis=1, tiled=True),
        (((1,), (1,)), ((), ())),
        preferred_element_type=jnp.float32,
    )
    up_grad = (hidden_grad * jax.nn.silu(gate_pre.astype(jnp.float32))).astype(jnp.bfloat16)
    left_part = jnp.dot(up_grad, proj_out, preferred_element_type=jnp.float32)
    right_part = jnp.dot(inputs, proj_in, preferred_element_type=jnp.float32)
    left, right = lax.psum((left_part, right_part), "tensor")
    docs = doc_lens.shape[1]
    rank = proj_in.shape[1]
    width = rank * rank
    ends = jnp.cumsum(doc_lens[0])
    position = lax.axis_index("seq") * rows + jnp.arange(rows, dtype=jnp.int32)
    document = jnp.sum((position[:, None] >= ends[None, :]).astype(jnp.int32), axis=1)
    onehot = (document[:, None] == jnp.arange(docs, dtype=jnp.int32)[None, :]).astype(jnp.float32)
    partial_grads = jnp.einsum(
        "tc,ti,tj->cij", onehot, left, right, precision=lax.Precision.HIGHEST
    ).reshape(docs, width)
    doc_grads = lax.psum(partial_grads, "seq")
    local_raw = jnp.dot(doc_grads.T, doc_grads, precision=lax.Precision.HIGHEST)
    raw = lax.psum(local_raw, "dp")
    mean_diag = jnp.trace(raw) / width
    fisher = raw / mean_diag
    damped = fisher + jnp.eye(width, dtype=jnp.float32)
    factor = jnp.linalg.cholesky(damped)
    solved = jax.scipy.linalg.cho_solve((factor, True), doc_grads.T)
    scores = jnp.dot(queries, solved, precision=lax.Precision.HIGHEST)
    pieces = lax.axis_size("tensor") * lax.axis_size("seq")
    share = width // pieces
    which = lax.axis_index("tensor") * lax.axis_size("seq") + lax.axis_index("seq")
    fisher_rows = lax.dynamic_slice_in_dim(fisher, which * share, share, 0)
    return (doc_grads, fisher_rows, scores)


def solution(mesh):
    return jax.shard_map(
        on_device,
        mesh=mesh,
        in_specs=(
            P(("groups", "dp", "seq"), "tensor"),
            P(("groups", "dp", "seq"), "tensor"),
            P(("groups", "dp", "seq"), "tensor"),
            P("tensor", "dp"),
            P("tensor", None),
            P("tensor", None),
            P(("groups", "dp"), None),
            P(),
        ),
        out_specs=(
            P(("groups", "dp"), None),
            P(("groups", "tensor", "seq"), None),
            P(None, ("groups", "dp")),
        ),
        check_vma=False,
    )
```

profile of v0, /device:TPU:0, one launch (start us, length us, event | category | flops | bytes accessed | tf_op | source)
XLA Modules:
  0.0 1431.7 jit_solution(7421819609732123211)
XLA Ops:
  10.5 58.6 %all-gather.3.cloned.1.call-done = bf16[512,4096]{1,0:T(8,128)(2,1)} async-done(((bf16[512,2048]{1,0:T(8,128)(2,1)}), bf16[512,4096]{1,0:T(8,128)(2,1)}) %all-gather.3.cloned.1.call-update) | async-done | bytes 4194320 | tf_op jit(solution)/shard_map/all_gather | solution.py:9
  69.0 752.4 %all-gather.5.cloned.1.call-done = bf16[5504,4096]{1,0:T(8,128)(2,1)} async-done(((bf16[5504,1024]{1,0:T(8,128)(2,1)}), bf16[5504,4096]{1,0:T(8,128)(2,1)}) %all-gather.5.cloned.1.call-update) | async-done | bytes 45088784 | tf_op jit(solution)/shard_map/all_gather | solution.py:12
  821.4 35.0 %fusion.105 = f32[512,32]{0,1:T(8,128)} fusion(bf16[5504,32]{0,1:T(8,128)(2,1)S(1)} %copy-done.7, bf16[512,5504]{1,0:T(8,128)(2,1)} %param.10, bf16[512,4096]{1,0:T(8,128)(2,1)} %all-gather.3.cloned.1.call-done, bf16[5504,4096]{1,0:T(8,128)(2,1)} %all-gather.5.cloned.1.call-done), kind=kOutput, calls=%fused_computation.235 | convolution fusion | flops 23285530624 | bytes 55336960 | tf_op jit(solution)/shard_map/dot_general | solution.py:17
  856.5 19.9 %all-reduce.10.cloned.1.call-done = (f32[512,32]{0,1:T(8,128)}, f32[512,32]{0,1:T(8,128)}) async-done(((f32[512,32]{0,1:T(8,128)}, f32[512,32]{0,1:T(8,128)}), (f32[512,32]{0,1:T(8,128)}, f32[512,32]{0,1:T(8,128)})) %all-reduce.10.cloned.1.call-update) | async-done | bytes 131088 | tf_op jit(solution)/shard_map/psum | solution.py:19
  879.2 17.8 %all-reduce.6.cloned.1.call-done = f32[16,1024]{1,0:T(8,128)} async-done(((f32[16,1024]{1,0:T(8,128)}), f32[16,1024]{1,0:T(8,128)}) %all-reduce.6.cloned.1.call-update) | async-done | bytes 65552 | tf_op jit(solution)/shard_map/psum | solution.py:30
  897.0 6.3 fusion.107
  903.3 156.3 %all-reduce.8.cloned.1.call-done = f32[1024,1024]{0,1:T(8,128)} async-done(((f32[1024,1024]{0,1:T(8,128)}), f32[1024,1024]{0,1:T(8,128)}) %all-reduce.8.cloned.1.call-update) | async-done | bytes 4194320 | tf_op jit(solution)/shard_map/psum | solution.py:32
  1063.2 6.9 convert_add_fusion
  1070.1 5.5 copy.55
  1075.6 4.5 fusion.5
  1082.1 11.7 cholesky.222
  1093.9 9.8 custom-call.66
  1107.0 11.7 cholesky.243
  1119.1 9.8 custom-call.67
  1134.4 11.7 cholesky.466
  1146.9 9.8 custom-call.68
  1158.0 3.5 convolution_subtract_fusion.2
  1161.5 11.7 cholesky.485
  1174.0 9.8 custom-call.69
  1184.9 3.1 convolution_subtract_fusion.3
  1188.1 11.9 cholesky.504
  1200.8 9.8 custom-call.70
  1211.7 3.2 convolution_subtract_fusion.4
  1214.9 11.7 cholesky.524
  1227.4 9.8 custom-call.71
  1241.2 11.7 cholesky.544
  1253.7 9.8 custom-call.72
  1266.6 11.7 cholesky.562
  1291.3 5.1 select_select_fusion
  1296.4 23.9 %while.1 = (s32[]{:T(128)}, f32[1024,1024]{0,1:T(8,128)}, s32[8,2]{0,1:T(2,128)S(1)}, f32[8,128,128]{2,1,0:T(8,128)S(1)}, s32[]{:T(128)}) while((s32[]{:T(128)}, f32[1024,1024]{0,1:T(8,128)}, s32[8,2]{0,1:T(2,128)S(1)}, f32[8,128,128]{2,1,0:T(8,128)S(1)}, s32[]{:T(128)}) %tuple.59), condition=%wide.while_cond, body=%wide.while_body.sunk | while | flops 2 | bytes 393329 | solution.py:37
  1320.3 78.6 %custom-call.73 = f32[8,128,128]{1,2,0:T(8,128)S(1)} custom-call(f32[8,128,128]{2,1,0:T(8,128)S(1)} %get-tuple-element.10), custom_call_target="InvertDiagBlocksLowerTriangular" | custom-call | tf_op jit(solution)/shard_map/jit(_cho_solve)/triangular_solve | solution.py:37
  1420.0 4.0 convolution_bitcast_fusion.1
  (186 shorter events, 87.8 us)
Async XLA Ops:
  7.2 1.9 copy-start
  7.2 61.9 %all-gather.3.cloned.1.call-start = ((), (), s32[]{:S(2)}) async-start(), calls=%async_computation | async-start | bytes 6291456 | tf_op jit(solution)/shard_map/all_gather | solution.py:9
  7.9 0.8 copy-start.6
  7.9 1.2 copy-start.5
  7.9 813.5 %copy-start.7 = (bf16[5504,32]{0,1:T(8,128)(2,1)S(1)}, bf16[5504,32]{0,1:T(8,128)(2,1)}, u32[]{:S(2)}) copy-start(bf16[5504,32]{0,1:T(8,128)(2,1)} %param.13) | copy-start | bytes 1056772
  7.9 813.5 %all-gather.5.cloned.1.call-start = ((), (), s32[]{:S(2)}) async-start(), calls=%async_computation.1 | async-start | bytes 56360960 | tf_op jit(solution)/shard_map/all_gather | solution.py:12
  8.7 867.7 %all-reduce.10.cloned.1.call-start = ((), (), s32[]{:S(2)}) async-start(), calls=%async_computation.4 | async-start | bytes 262144 | tf_op jit(solution)/shard_map/psum | solution.py:19
  856.5 40.5 %all-reduce.6.cloned.1.call-start = ((), (), s32[]{:S(2)}) async-start(), calls=%async_computation.2 | async-start | bytes 131072 | tf_op jit(solution)/shard_map/psum | solution.py:30
  879.1 180.5 %all-reduce.8.cloned.1.call-start = ((), (), s32[]{:S(2)}) async-start(), calls=%async_computation.3 | async-start | bytes 8388608 | tf_op jit(solution)/shard_map/psum | solution.py:32
  1080.1 2.0 copy-start.3
  1130.0 2.0 copy-start.2
  1291.3 107.6 %copy-start.4 = (f32[16,1024]{1,0:T(8,128)S(1)}, f32[16,1024]{1,0:T(8,128)}, u32[]{:S(2)}) copy-start(f32[16,1024]{1,0:T(8,128)} %all-reduce.6.cloned.1.call-done) | copy-start | bytes 196612
  1400.1 24.6 %copy-start.1 = (bf16[512,2048]{1,0:T(8,128)(2,1)S(1)}, bf16[512,2048]{1,0:T(8,128)(2,1)}, u32[]{:S(2)}) copy-start(bf16[512,2048]{1,0:T(8,128)(2,1)} %param.8) | copy-start | bytes 6291460
Sparse Core Ops, SparseCore 0:
  9.6 59.4 all-gather.2
  70.6 750.7 all-gather.4
  856.6 19.7 all-reduce.9
  879.2 17.7 all-reduce.5
  903.4 156.1 all-reduce.7
where the time goes:
time: 1440 us; the launch traced here: 1430 us
  waiting for transfers between devices  1010 us (70%)
  other arithmetic  266 us (18%)
  matrix products  95.6 us (7%)
  local copies, waits for them, and re-layouts  43.1 us (3%)
  between operations  20.5 us (1%)
    all_gather x1, waiting for transfers between devices, on_device(): lax.all_gather(down_weight, 'dp', axis=1, tiled=True)  752 us
    another operation x30, other arithmetic, on_device(): factor = jnp.linalg.cholesky(damped)  167 us
    psum x1, waiting for transfers between devices, on_device(): raw = lax.psum(local_raw, 'dp')  156 us
    another operation x3, other arithmetic, on_device(): solved = jax.scipy.linalg.cho_solve((factor, True), doc_grads.T)  83.7 us
    all_gather x1, waiting for transfers between devices, on_device(): full_cotangent = lax.all_gather(cotangent, 'tensor', axis=1, tiled=True)  58.6 us
    dot_general x1, matrix products, on_device(): left_part = jnp.dot(up_grad, proj_out, preferred_element_type=jnp.float32)  35 us
  transfers between devices with their start and end apart: 5, of which 5 were waited for; matrix products, arithmetic and copies ran while one was open for 0% of the time, Pallas kernels for 0%

commit v1 on v0

v1 whole, which is shorter than its diff:
```python
import jax
import jax.numpy as jnp
from jax import lax
from jax.sharding import PartitionSpec as P

HIGHEST = lax.Precision.HIGHEST
LANES = 128
CHUNKS = 4


def shifted(x, axes, sizes, shift):
    pairs = []
    if isinstance(axes, str):
        (n,) = sizes
        pairs = [(i, (i + shift[0]) % n) for i in range(n)]
    else:
        a, b = sizes
        for i in range(a):
            for j in range(b):
                pairs.append((i * b + j, ((i + shift[0]) % a) * b + (j + shift[1]) % b))
    return lax.ppermute(x, axes, pairs)


def gather_in_order(x, axis, dim):
    n = lax.axis_size(axis)
    me = lax.axis_index(axis)
    shape = list(x.shape)
    shape[dim] *= n
    out = jnp.zeros(shape, x.dtype)
    for r in range(n):
        piece = x if r == 0 else shifted(x, axis, (n,), (r,))
        out = lax.dynamic_update_slice_in_dim(out, piece, ((me - r) % n) * x.shape[dim], dim)
    return out


def sum_over(x, axis):
    n = lax.axis_size(axis)
    if n == 2:
        return x + shifted(x, axis, (2,), (1,))
    return jnp.sum(gather_in_order(x[None], axis, 0), axis=0)


def on_device(inputs, cotangent, gate_pre, down_weight, proj_in, proj_out, doc_lens, queries):
    n_groups, n_seq = lax.axis_size("groups"), lax.axis_size("seq")
    n_dp, n_tensor = lax.axis_size("dp"), lax.axis_size("tensor")
    group, half = lax.axis_index("groups"), lax.axis_index("seq")
    stage, side = lax.axis_index("dp"), lax.axis_index("tensor")
    rows = inputs.shape[0]
    units = gate_pre.shape[1]
    docs = doc_lens.shape[1]
    rank = proj_in.shape[1]
    width = rank * rank
    sharers = n_groups * n_seq
    part = min(units, -(-units // (sharers * LANES)) * LANES)
    pair = ("groups", "seq")
    sizes = (n_groups, n_seq)

    def first_unit(who):
        return jnp.minimum(who * part, units - part)

    mine = group * n_seq + half
    start = first_unit(mine)
    tiles = -(-part // LANES)
    bounds = sorted({min(part, -(-tiles * c // CHUNKS) * LANES) for c in range(CHUNKS + 1)})

    gathered = []
    token = None
    for low, high in zip(bounds[:-1], bounds[1:]):
        block = lax.dynamic_slice_in_dim(down_weight, start + low, high - low, 0)
        gathered.append(lax.all_gather(block, "dp", axis=1, tiled=True))

    order = [(dg, ds) for dg in range(n_groups) for ds in range(n_seq)]
    cots = []
    for dg in range(n_groups):
        own = cotangent if dg == 0 else shifted(cotangent, "groups", (n_groups,), (dg,))
        full = gather_in_order(own, "tensor", 1)
        for ds in range(n_seq):
            cots.append(full if ds == 0 else shifted(full, "seq", (n_seq,), (ds,)))
    gates = []
    for dg, ds in order:
        to = ((group + dg) % n_groups) * n_seq + (half + ds) % n_seq
        columns = lax.dynamic_slice_in_dim(gate_pre, first_unit(to), part, 1)
        gates.append(columns if dg == ds == 0 else shifted(columns, pair, sizes, (dg, ds)))

    right = sum_over(jnp.dot(inputs, proj_in, preferred_element_type=jnp.float32), "tensor")
    rights = [right if dg == ds == 0 else shifted(right, pair, sizes, (dg, ds)) for dg, ds in order]
    lens = [doc_lens if dg == 0 else shifted(doc_lens, "groups", (n_groups,), (dg,)) for dg in range(n_groups)]

    cot = jnp.concatenate(cots, axis=0)
    gate = jnp.concatenate(gates, axis=0)
    slope = jax.nn.silu(gate.astype(jnp.float32))
    numbers = start + jnp.arange(part, dtype=jnp.int32)
    out_factor = lax.dynamic_slice_in_dim(proj_out, start, part, 0)
    out_factor = jnp.where((numbers >= mine * part)[:, None], out_factor, 0).astype(proj_out.dtype)

    left = 0.0
    for weight, low, high in zip(gathered, bounds[:-1], bounds[1:]):
        hidden_grad = lax.dot_general(
            cot, weight, (((1,), (1,)), ((), ())), preferred_element_type=jnp.float32
        )
        up_grad = (hidden_grad * slope[:, low:high]).astype(jnp.bfloat16)
        left = left + jnp.dot(up_grad, out_factor[low:high], preferred_element_type=jnp.float32)

    parts = []
    for dg in range(n_groups):
        ends = jnp.cumsum(lens[dg][0])
        position = jnp.concatenate(
            [((half - ds) % n_seq) * rows + jnp.arange(rows, dtype=jnp.int32) for ds in range(n_seq)]
        )
        document = jnp.sum((position[:, None] >= ends[None, :]).astype(jnp.int32), axis=1)
        onehot = (document[:, None] == jnp.arange(docs, dtype=jnp.int32)[None, :]).astype(jnp.float32)
        span = slice(dg * n_seq * rows, (dg + 1) * n_seq * rows)
        right_block = jnp.concatenate(rights[dg * n_seq:(dg + 1) * n_seq], axis=0)
        grads = jnp.einsum(
            "tc,ti,tj->cij", onehot, left[span], right_block, precision=HIGHEST
        ).reshape(docs, width)
        parts.append(grads)
    grads = parts[0]
    if n_groups == 2:
        grads = grads + shifted(parts[1], "groups", (2,), (1,))
    else:
        for dg in range(1, n_groups):
            grads = grads + shifted(parts[dg], "groups", (n_groups,), (-dg,))
    doc_grads = sum_over(sum_over(grads, "tensor"), "seq")

    every = gather_in_order(doc_grads, "dp", 0)
    mean_diag = jnp.sum(every * every) / width
    pieces = n_tensor * n_seq
    share = width // pieces
    which = side * n_seq + half
    columns = lax.dynamic_slice_in_dim(every, which * share, share, 1)
    fisher_rows = lax.dot_general(
        columns, every, (((0,), (0,)), ((), ())), precision=HIGHEST, preferred_element_type=jnp.float32
    ) / mean_diag

    total = every.shape[0]
    gram = lax.dot_general(
        every, every, (((1,), (1,)), ((), ())), precision=HIGHEST, preferred_element_type=jnp.float32
    )
    damped = gram / mean_diag + jnp.eye(total, dtype=jnp.float32)
    factor = jnp.linalg.cholesky(damped)
    chosen = (jnp.arange(total)[:, None] == stage * docs + jnp.arange(docs)[None, :]).astype(jnp.float32)
    solved = jax.scipy.linalg.cho_solve((factor, True), chosen)
    products = lax.dot_general(
        queries, every, (((1,), (1,)), ((), ())), precision=HIGHEST, preferred_element_type=jnp.float32
    )
    scores = jnp.dot(products, solved, precision=HIGHEST)
    return (doc_grads, fisher_rows, scores)


def solution(mesh):
    return jax.shard_map(
        on_device,
        mesh=mesh,
        in_specs=(
            P(("groups", "dp", "seq"), "tensor"),
            P(("groups", "dp", "seq"), "tensor"),
            P(("groups", "dp", "seq"), "tensor"),
            P("tensor", "dp"),
            P("tensor", None),
            P("tensor", None),
            P(("groups", "dp"), None),
            P(),
        ),
        out_specs=(
            P(("groups", "dp"), None),
            P(("groups", "tensor", "seq"), None),
            P(None, ("groups", "dp")),
        ),
        check_vma=False,
    )
```

time: 1440 us -> 331 us (0.23)
  waiting for transfers between devices: 1010 us -> 138 us
  other arithmetic: 266 us -> 27.8 us
  starting transfers between devices: 0.2 us -> 20.5 us
  local copies, waits for them, and re-layouts: 43.1 us -> 28.6 us
    all_gather x2 -> x4, waiting for transfers between devices: 811 us -> 0.06 us  [on_device(): gathered.append(lax.all_gather(block, 'dp', axis=1, tiled=True))]
    psum x3 -> x0, waiting for transfers between devices: 194 us -> none  [the longest x1 156 us: on_device(): raw = lax.psum(local_raw, 'dp')]
    another operation x30 -> x3, other arithmetic: 167 us -> 6.52 us  [on_device(): factor = jnp.linalg.cholesky(damped)]
    ppermute x0 -> x19, waiting for transfers between devices: none -> 137 us  [shifted(): return lax.ppermute(x, axes, pairs)]
    another operation x6 -> x8, other arithmetic: 83.8 us -> 7.69 us  [the longest x2 5.55 us: on_device(): solved = jax.scipy.linalg.cho_solve((factor, True), chosen)]
    another operation x44 -> x2, matrix products: 47.1 us -> 0.37 us  [on_device(): solved = jax.scipy.linalg.cho_solve((factor, True), chosen)]
    dot_general x5 -> x11, matrix products: 48.5 us -> 94.3 us  [the longest x4 80.8 us: on_device(): jnp.dot(up_grad, out_factor[low:high], preferred_element_type=jnp.float32)]
    another operation x71 -> x4, local copies, waits for them, and re-layouts: 29.4 us -> 6.02 us
  transfers between devices with their start and end apart: 5 -> 23, of which waited for: 5 -> 10; matrix products, arithmetic and copies ran while one was open for 0% -> 40% of each run, Pallas kernels for 0% -> 0%
where the time goes in v1:
time: 331 us; the launch traced here: 324 us
  waiting for transfers between devices  138 us (42%)
  matrix products  94.7 us (29%)
  local copies, waits for them, and re-layouts  28.6 us (9%)
  other arithmetic  27.8 us (8%)
  starting transfers between devices  20.5 us (6%)
  between operations  15.1 us (5%)
    ppermute x19, waiting for transfers between devices, shifted(): return lax.ppermute(x, axes, pairs)  137 us
    dot_general x4, matrix products, on_device(): jnp.dot(up_grad, out_factor[low:high], preferred_element_type=jnp.float32)  80.8 us
    ppermute x19, starting transfers between devices, shifted(): return lax.ppermute(x, axes, pairs)  20.4 us
    dynamic_update_slice x7, local copies, waits for them, and re-layouts, gather_in_order(): lax.dynamic_update_slice_in_dim(out, piece, (me - r) % n * x.shape[dim],...  11.2 us
    mul x1, other arithmetic, on_device(): slope = jax.nn.silu(gate.astype(jnp.float32))  8.32 us
  transfers between devices with their start and end apart: 23, of which 10 were waited for; matrix products, arithmetic and copies ran while one was open for 40% of the time, Pallas kernels for 0%

profile of v1, /device:TPU:0, one launch (start us, length us, event | category | flops | bytes accessed | tf_op | source)
XLA Modules:
  0.0 324.4 jit_solution(11861486014978479076)
XLA Ops:
  7.3 3.5 %constant_dynamic-slice_fusion.1 = (bf16[384,1024]{1,0:T(8,128)(2,1)}, bf16[384,1024]{1,0:T(8,128)(2,1)}, bf16[384,1024]{1,0:T(8,128)(2,1)}) fusion(bf16[5504,1024]{1,0:T(8,128)(2,1)} %param.11, s32[]{:T(128)S(6)} %select_n.136, s32[]{:T(128)S(6)} %select_n.135, s32[]{:T(128)S(6)} %select_n.125), kind=kLoop, calls=%fused_computation.71 | loop fusion | bytes 4718604 | tf_op jit(solution)/shard_map/dynamic_slice | solution.py:69
  11.6 3.0 collective-permute-start.2
  16.2 44.3 %collective-permute-done.2 = bf16[512,2048]{1,0:T(8,128)(2,1)} collective-permute-done((bf16[512,2048]{1,0:T(8,128)(2,1)}, bf16[512,2048]{1,0:T(8,128)(2,1)}, u32[]{:S(2)}, u32[]{:S(2)}) %collective-permute-start.2) | collective-permute-done | bytes 2097184 | tf_op jit(solution)/shard_map/ppermute | solution.py:21
  60.6 1.7 collective-permute-start.3
  62.3 2.9 fusion.45
  65.5 2.6 broadcast.110.clone.1
  69.5 3.2 constant_dynamic-update-slice_fusion.6
  72.8 2.6 broadcast.110.clone
  75.4 3.3 %constant_dynamic-update-slice_fusion.5 = bf16[512,4096]{1,0:T(8,128)(2,1)} fusion(bf16[512,4096]{1,0:T(8,128)(2,1)} %broadcast.110.clone, bf16[512,2048]{1,0:T(8,128)(2,1)} %collective-permute-done.2, s32[]{:T(128)S(6)} %select_n.122), kind=kLoop, calls=%fused_computation.79 | loop fusion | bytes 4194308 | tf_op jit(solution)/shard_map/dynamic_update_slice | solution.py:32
  78.7 29.7 %collective-permute-done.3 = bf16[512,2048]{1,0:T(8,128)(2,1)} collective-permute-done((bf16[512,2048]{1,0:T(8,128)(2,1)}, bf16[512,2048]{1,0:T(8,128)(2,1)}, u32[]{:S(2)}, u32[]{:S(2)}) %collective-permute-start.3) | collective-permute-done | bytes 2097184 | tf_op jit(solution)/shard_map/ppermute | solution.py:21
  108.4 3.2 constant_dynamic-update-slice_fusion.4
  111.6 5.3 %constant_dynamic-slice_fusion.6 = (bf16[512,1408]{1,0:T(8,128)(2,1)S(1)}, bf16[512,1408]{1,0:T(8,128)(2,1)}, bf16[512,1408]{1,0:T(8,128)(2,1)}, bf16[512,1408]{1,0:T(8,128)(2,1)}) fusion(bf16[512,5504]{1,0:T(8,128)(2,1)S(1)} %bitcast.40, s32[]{:T(128)S(6)} %select_n.128, s32[]{:T(128)S(6)} %select_n.130, s32[]{:T(128)S(6)} %select_n.133, s32[]{:T(128)S(6)} %select_n.132), kind=kLoop, calls=%fused_computation.76 | loop fusion | bytes 11534352 | tf_op jit(solution)/shard_map/dynamic_slice | solution.py:82
  118.9 2.1 collective-permute-done.10
  122.4 2.0 constant_dynamic-slice_fusion
  125.9 1.6 dynamic-slice_select_fusion
  132.6 23.3 %collective-permute-done.6 = bf16[512,1408]{1,0:T(8,128)(2,1)} collective-permute-done((bf16[512,1408]{1,0:T(8,128)(2,1)}, bf16[512,1408]{1,0:T(8,128)(2,1)}, u32[]{:S(2)}, u32[]{:S(2)}) %collective-permute-start.6) | collective-permute-done | bytes 1441824 | tf_op jit(solution)/shard_map/ppermute | solution.py:21
  155.8 29.5 %collective-permute-done.7 = bf16[512,1408]{1,0:T(8,128)(2,1)} collective-permute-done((bf16[512,1408]{1,0:T(8,128)(2,1)}, bf16[512,1408]{1,0:T(8,128)(2,1)}, u32[]{:S(2)}, u32[]{:S(2)}) %collective-permute-start.7) | collective-permute-done | bytes 1441824 | tf_op jit(solution)/shard_map/ppermute | solution.py:21
  186.5 8.3 %convert_multiply_fusion = f32[2048,1408]{1,0:T(8,128)} fusion(bf16[512,1408]{1,0:T(8,128)(2,1)} %collective-permute-done.7, bf16[512,1408]{1,0:T(8,128)(2,1)} %collective-permute-done.6, bf16[512,1408]{1,0:T(8,128)(2,1)} %collective-permute-done.5, bf16[512,1408]{1,0:T(8,128)(2,1)S(1)} %get-tuple-element.10), kind=kLoop, calls=%fused_computation.1 | loop fusion | flops 34603008 | bytes 17301504 | tf_op jit(solution)/shard_map/jit(silu)/mul | solution.py:91
  194.8 20.4 %fusion.21 = f32[2048,32]{0,1:T(8,128)S(1)} fusion(f32[2048,1408]{1,0:T(8,128)} %convert_multiply_fusion, bf16[384,4096]{1,0:T(8,128)(2,1)} %all-gather.5.cloned.1.call-done, bf16[1408,32]{0,1:T(8,128)(2,1)} %dynamic-slice_select_fusion, bf16[512,4096]{1,0:T(8,128)(2,1)} %collective-permute-done.4, ...), kind=kOutput, calls=%fused_computation.29 | convolution fusion | flops 6561464320 | bytes 23355392 | tf_op jit(solution)/shard_map/dot_general | solution.py:102
  215.3 20.6 %convolution_add_fusion.2 = f32[2048,32]{0,1:T(8,128)S(1)} fusion(f32[2048,32]{0,1:T(8,128)S(1)} %fusion.21, f32[2048,1408]{1,0:T(8,128)} %convert_multiply_fusion, bf16[384,4096]{1,0:T(8,128)(2,1)} %all-gather.7.cloned.1.call-done, bf16[1408,32]{0,1:T(8,128)(2,1)S(1)} %copy-done.3, bf16[512,4096]{1,0:T(8,128)(2,1)} %collective-permute-done.4, ...), kind=kOutput, calls=%fused_computation.16 | convolution fusion | flops 6561529856 | bytes 23617536 | tf_op jit(solution)/shard_map/dot_general | solution.py:102
  235.9 20.5 %convolution_add_fusion.1 = f32[2048,32]{0,1:T(8,128)S(1)} fusion(f32[2048,32]{0,1:T(8,128)S(1)} %convolution_add_fusion.2, f32[2048,1408]{1,0:T(8,128)} %convert_multiply_fusion, bf16[384,4096]{1,0:T(8,128)(2,1)} %all-gather.9.cloned.1.call-done, bf16[1408,32]{0,1:T(8,128)(2,1)S(1)} %copy-done.3, bf16[512,4096]{1,0:T(8,128)(2,1)} %collective-permute-done.4, ...), kind=kOutput, calls=%fused_computation.15 | convolution fusion | flops 6561529856 | bytes 23617536 | tf_op jit(solution)/shard_map/dot_general | solution.py:102
  256.5 19.2 %convolution_add_fusion = f32[2048,32]{0,1:T(8,128)S(1)} fusion(f32[2048,32]{0,1:T(8,128)S(1)} %convolution_add_fusion.1, bf16[256,4096]{1,0:T(8,128)(2,1)} %all-gather.11.cloned.1.call-done, f32[2048,1408]{1,0:T(8,128)} %convert_multiply_fusion, bf16[1408,32]{0,1:T(8,128)(2,1)S(1)} %copy-done.3, bf16[512,4096]{1,0:T(8,128)(2,1)} %collective-permute-done.4, ...), kind=kOutput, calls=%fused_computation.14 | convolution fusion | flops 4396744704 | bytes 21512192 | tf_op jit(solution)/shard_map/dot_general | solution.py:102
  275.8 2.6 fusion.14
  280.2 2.6 fusion.11
  283.1 1.6 collective-permute-start.14
  284.7 2.7 collective-permute-done.14
  290.1 2.9 collective-permute-start.17
  295.5 2.3 collective-permute-done.17
  300.1 5.8 %cholesky.17 = f32[64,64]{1,0:T(8,128)S(1)} custom-call(f32[64,64]{1,0:T(8,128)S(1)} %fusion.35), custom_call_target="Cholesky" | custom-call | tf_op jit(solution)/shard_map/jit(cholesky)/cholesky | solution.py:141
  307.3 4.9 %custom-call.10 = f32[1,64,64]{1,2,0:T(8,128)S(1)} custom-call(f32[1,64,64]{2,1,0:T(8,128)S(1)} %fusion.29), custom_call_target="InvertDiagBlocksLowerTriangular" | custom-call | tf_op jit(solution)/shard_map/jit(_cho_solve)/triangular_solve | solution.py:143
  312.6 2.1 fusion.46
  314.7 2.0 convolution_divide_fusion
  (99 shorter events, 26.6 us)
Async XLA Ops:
  7.2 305.4 %copy-start = (f32[512,1024]{1,0:T(8,128)S(1)}, f32[512,1024]{1,0:T(8,128)}, u32[]{:S(2)}) copy-start(f32[512,1024]{1,0:T(8,128)} %param.15) | copy-start | bytes 6291460
  7.2 55.1 %copy-start.2 = (bf16[2048,32]{0,1:T(8,128)(2,1)S(1)}, bf16[2048,32]{0,1:T(8,128)(2,1)}, u32[]{:S(2)}) copy-start(bf16[2048,32]{0,1:T(8,128)(2,1)} %param.12) | copy-start | bytes 393220
  7.2 187.6 %all-gather.5.cloned.1.call-start = ((), (), s32[]{:S(2)}) async-start(), calls=%async_computation | async-start | bytes 3932160 | tf_op jit(solution)/shard_map/all_gather | solution.py:70
  10.8 204.5 %all-gather.7.cloned.1.call-start = ((), (), s32[]{:S(2)}) async-start(), calls=%async_computation.1 | async-start | bytes 3932160 | tf_op jit(solution)/shard_map/all_gather | solution.py:70
  11.5 224.4 %all-gather.9.cloned.1.call-start = ((), (), s32[]{:S(2)}) async-start(), calls=%async_computation.2 | async-start | bytes 3932160 | tf_op jit(solution)/shard_map/all_gather | solution.py:70
  11.6 49.0 %collective-permute-start.2 = (bf16[512,2048]{1,0:T(8,128)(2,1)}, bf16[512,2048]{1,0:T(8,128)(2,1)}, u32[]{:S(2)}, u32[]{:S(2)}) collective-permute-start(bf16[512,2048]{1,0:T(8,128)(2,1)} %param.9), channel_id=1, source_target_pairs={{0,16},{16,0},{1,17},{17,1},{2,18},{18,2},{3,19},{19,3},{4,20},{20... | collective-permute-start | bytes 6291464 | tf_op jit(solution)/shard_map/ppermute | solution.py:21
  14.6 241.8 %all-gather.11.cloned.1.call-start = ((), (), s32[]{:S(2)}) async-start(), calls=%async_computation.3 | async-start | bytes 2621440 | tf_op jit(solution)/shard_map/all_gather | solution.py:70
  14.7 54.9 %collective-permute-start = (bf16[512,2048]{1,0:T(8,128)(2,1)}, bf16[512,2048]{1,0:T(8,128)(2,1)}, u32[]{:S(2)}, u32[]{:S(2)}) collective-permute-start(bf16[512,2048]{1,0:T(8,128)(2,1)} %param.9), channel_id=1, source_target_pairs={{0,2},{2,0},{1,3},{3,1},{4,6},{6,4},{5,7},{7,5},{8,10},{10,8},{9,1... | collective-permute-start | bytes 6291464 | tf_op jit(solution)/shard_map/ppermute | solution.py:21
  60.6 47.8 %collective-permute-start.3 = (bf16[512,2048]{1,0:T(8,128)(2,1)}, bf16[512,2048]{1,0:T(8,128)(2,1)}, u32[]{:S(2)}, u32[]{:S(2)}) collective-permute-start(bf16[512,2048]{1,0:T(8,128)(2,1)} %collective-permute-done.2), channel_id=1, source_target_pairs={{0,2},{2,0},{1,3},{3,1},{4,6},{6,4},{5,7},{7,5},{8,10},{10,8},{9,1... | collective-permute-start | bytes 6291464 | tf_op jit(solution)/shard_map/ppermute | solution.py:21
  65.2 57.2 %collective-permute-start.8 = (f32[512,32]{0,1:T(8,128)}, f32[512,32]{0,1:T(8,128)}, u32[]{:S(2)}, u32[]{:S(2)}) collective-permute-start(f32[512,32]{0,1:T(8,128)} %fusion.45), channel_id=1, source_target_pairs={{0,2},{2,0},{1,3},{3,1},{4,6},{6,4},{5,7},{7,5},{8,10},{10,8},{9,1... | collective-permute-start | bytes 196616 | tf_op jit(solution)/shard_map/ppermute | solution.py:21
  72.8 122.0 %collective-permute-start.1 = (bf16[512,4096]{1,0:T(8,128)(2,1)}, bf16[512,4096]{1,0:T(8,128)(2,1)}, u32[]{:S(2)}, u32[]{:S(2)}) collective-permute-start(bf16[512,4096]{1,0:T(8,128)(2,1)} %constant_dynamic-update-slice_fusion.6), channel_id=1, source_target_pairs={{0,1},{1,0},{2,3},{3,2},{4,5},{5,4},{6,7},{7,6},{8,9},{9,8},{10,11... | collective-permute-start | bytes 12582920 | tf_op jit(solution)/shard_map/ppermute | solution.py:21
  72.8 38.8 %slice-start = ((s8[5636096]{0:T(1024)(128)(4,1)}), s8[4194304]{0:T(1024)(128)(4,1)S(1)}, s32[]{:S(2)}) async-start(s8[5636096]{0:T(1024)(128)(4,1)} %bitcast.39), calls=%async_computation.4 | async-start | bytes 8388608
  75.4 36.2 %slice-start.1 = ((s8[5636096]{0:T(1024)(128)(4,1)}), s8[1441792]{0:T(1024)(128)(4,1)S(1)}, s32[]{:S(2)}) async-start(s8[5636096]{0:T(1024)(128)(4,1)} %bitcast.39), calls=%async_computation.5 | async-start | bytes 2883584
  111.6 5.9 %copy-start.7 = (s32[1,16]{1,0:T(1,128)S(1)}, s32[1,16]{1,0:T(1,128)}, u32[]{:S(2)}) copy-start(s32[1,16]{1,0:T(1,128)} %param.14) | copy-start | bytes 196
  111.6 83.2 %collective-permute-start.4 = (bf16[512,4096]{1,0:T(8,128)(2,1)}, bf16[512,4096]{1,0:T(8,128)(2,1)}, u32[]{:S(2)}, u32[]{:S(2)}) collective-permute-start(bf16[512,4096]{1,0:T(8,128)(2,1)} %constant_dynamic-update-slice_fusion.4), channel_id=1, source_target_pairs={{0,1},{1,0},{2,3},{3,2},{4,5},{5,4},{6,7},{7,6},{8,9},{9,8},{10,11... | collective-permute-start | bytes 12582920 | tf_op jit(solution)/shard_map/ppermute | solution.py:21
  116.9 15.0 %collective-permute-start.5 = (bf16[512,1408]{1,0:T(8,128)(2,1)}, bf16[512,1408]{1,0:T(8,128)(2,1)}, u32[]{:S(2)}, u32[]{:S(2)}) collective-permute-start(bf16[512,1408]{1,0:T(8,128)(2,1)} %get-tuple-element.11), channel_id=1, source_target_pairs={{0,1},{1,0},{16,17},{17,16},{2,3},{3,2},{18,19},{19,18},{4,5},{5,4... | collective-permute-start | bytes 4325384 | tf_op jit(solution)/shard_map/ppermute | solution.py:21
  117.4 3.5 %collective-permute-start.10 = (s32[1,16]{1,0:T(1,128)S(1)}, s32[1,16]{1,0:T(1,128)S(1)}, u32[]{:S(2)}, u32[]{:S(2)}) collective-permute-start(s32[1,16]{1,0:T(1,128)S(1)} %copy-done.7), channel_id=1, source_target_pairs={{0,16},{16,0},{1,17},{17,1},{2,18},{18,2},{3,19},{19,3},{4,20},{20... | collective-permute-start | bytes 200 | tf_op jit(solution)/shard_map/ppermute | solution.py:21
  121.0 34.8 %collective-permute-start.6 = (bf16[512,1408]{1,0:T(8,128)(2,1)}, bf16[512,1408]{1,0:T(8,128)(2,1)}, u32[]{:S(2)}, u32[]{:S(2)}) collective-permute-start(bf16[512,1408]{1,0:T(8,128)(2,1)} %get-tuple-element.13), channel_id=1, source_target_pairs={{0,16},{1,17},{16,0},{17,1},{2,18},{3,19},{18,2},{19,3},{4,20},{5,... | collective-permute-start | bytes 4325384 | tf_op jit(solution)/shard_map/ppermute | solution.py:21
  122.4 62.9 %collective-permute-start.7 = (bf16[512,1408]{1,0:T(8,128)(2,1)}, bf16[512,1408]{1,0:T(8,128)(2,1)}, u32[]{:S(2)}, u32[]{:S(2)}) collective-permute-start(bf16[512,1408]{1,0:T(8,128)(2,1)} %get-tuple-element.12), channel_id=1, source_target_pairs={{0,17},{1,16},{16,1},{17,0},{2,19},{3,18},{18,3},{19,2},{4,21},{5,... | collective-permute-start | bytes 4325384 | tf_op jit(solution)/shard_map/ppermute | solution.py:21
  131.9 143.8 %collective-permute-start.11 = (f32[512,32]{0,1:T(8,128)}, f32[512,32]{0,1:T(8,128)}, u32[]{:S(2)}, u32[]{:S(2)}) collective-permute-start(f32[512,32]{0,1:T(8,128)} %add.257), channel_id=1, source_target_pairs={{0,16},{1,17},{16,0},{17,1},{2,18},{3,19},{18,2},{19,3},{4,20},{5,... | collective-permute-start | bytes 196616 | tf_op jit(solution)/shard_map/ppermute | solution.py:21
  155.8 119.9 %collective-permute-start.12 = (f32[512,32]{0,1:T(8,128)}, f32[512,32]{0,1:T(8,128)}, u32[]{:S(2)}, u32[]{:S(2)}) collective-permute-start(f32[512,32]{0,1:T(8,128)} %add.257), channel_id=1, source_target_pairs={{0,17},{1,16},{16,1},{17,0},{2,19},{3,18},{18,3},{19,2},{4,21},{5,... | collective-permute-start | bytes 196616 | tf_op jit(solution)/shard_map/ppermute | solution.py:21
  185.3 94.9 %collective-permute-start.9 = (f32[512,32]{0,1:T(8,128)}, f32[512,32]{0,1:T(8,128)}, u32[]{:S(2)}, u32[]{:S(2)}) collective-permute-start(f32[512,32]{0,1:T(8,128)} %add.257), channel_id=1, source_target_pairs={{0,1},{1,0},{16,17},{17,16},{2,3},{3,2},{18,19},{19,18},{4,5},{5,4... | collective-permute-start | bytes 196616 | tf_op jit(solution)/shard_map/ppermute | solution.py:21
  194.8 20.5 %copy-start.3 = (bf16[1408,32]{0,1:T(8,128)(2,1)S(1)}, bf16[1408,32]{0,1:T(8,128)(2,1)}, u32[]{:S(2)}) copy-start(bf16[1408,32]{0,1:T(8,128)(2,1)} %dynamic-slice_select_fusion) | copy-start | bytes 270340
  256.4 19.3 %copy-start.5 = (f32[1024,16]{0,1:T(8,128)S(1)}, f32[1024,16]{0,1:T(8,128)}, u32[]{:S(2)}) copy-start(f32[1024,16]{0,1:T(8,128)} %fusion.28) | copy-start | bytes 196612
  256.4 23.7 %copy-start.4 = (f32[1024,16]{0,1:T(8,128)S(1)}, f32[1024,16]{0,1:T(8,128)}, u32[]{:S(2)}) copy-start(f32[1024,16]{0,1:T(8,128)} %fusion.27) | copy-start | bytes 196612
  278.7 4.4 %collective-permute-start.13 = (f32[16,1024]{1,0:T(8,128)S(1)}, f32[16,1024]{1,0:T(8,128)S(1)}, u32[]{:S(2)}, u32[]{:S(2)}) collective-permute-start(f32[16,1024]{1,0:T(8,128)S(1)} %reshape.91), channel_id=1, source_target_pairs={{0,16},{16,0},{1,17},{17,1},{2,18},{18,2},{3,19},{19,3},{4,20},{20... | collective-permute-start | bytes 196616 | tf_op jit(solution)/shard_map/ppermute | solution.py:21
  283.1 4.3 %collective-permute-start.14 = (f32[16,1024]{1,0:T(8,128)S(1)}, f32[16,1024]{1,0:T(8,128)S(1)}, u32[]{:S(2)}, u32[]{:S(2)}) collective-permute-start(f32[16,1024]{1,0:T(8,128)S(1)} %add.258), channel_id=1, source_target_pairs={{0,2},{2,0},{1,3},{3,1},{4,6},{6,4},{5,7},{7,5},{8,10},{10,8},{9,1... | collective-permute-start | bytes 196616 | tf_op jit(solution)/shard_map/ppermute | solution.py:21
  287.4 1.3 collective-permute-start.15
  288.8 28.8 %copy-start.6 = (f32[16,1024]{1,0:T(8,128)}, f32[16,1024]{1,0:T(8,128)S(1)}, u32[]{:S(2)}) copy-start(f32[16,1024]{1,0:T(8,128)S(1)} %get-tuple-element.6) | copy-start | bytes 196612
  288.8 6.7 %collective-permute-start.16 = (f32[16,1024]{1,0:T(8,128)S(1)}, f32[16,1024]{1,0:T(8,128)S(1)}, u32[]{:S(2)}, u32[]{:S(2)}) collective-permute-start(f32[16,1024]{1,0:T(8,128)S(1)} %get-tuple-element.6), channel_id=1, source_target_pairs={{0,4},{4,8},{8,12},{12,0},{1,5},{5,9},{9,13},{13,1},{2,6},{6,10},{... | collective-permute-start | bytes 196616 | tf_op jit(solution)/shard_map/ppermute | solution.py:21
  290.1 7.6 %collective-permute-start.17 = (f32[16,1024]{1,0:T(8,128)S(1)}, f32[16,1024]{1,0:T(8,128)S(1)}, u32[]{:S(2)}, u32[]{:S(2)}) collective-permute-start(f32[16,1024]{1,0:T(8,128)S(1)} %get-tuple-element.6), channel_id=1, source_target_pairs={{0,8},{4,12},{8,0},{12,4},{1,9},{5,13},{9,1},{13,5},{2,10},{6,14},... | collective-permute-start | bytes 196616 | tf_op jit(solution)/shard_map/ppermute | solution.py:21
  293.0 5.3 %collective-permute-start.18 = (f32[16,1024]{1,0:T(8,128)S(1)}, f32[16,1024]{1,0:T(8,128)S(1)}, u32[]{:S(2)}, u32[]{:S(2)}) collective-permute-start(f32[16,1024]{1,0:T(8,128)S(1)} %get-tuple-element.6), channel_id=1, source_target_pairs={{0,12},{4,0},{8,4},{12,8},{1,13},{5,1},{9,5},{13,9},{2,14},{6,2},{... | collective-permute-start | bytes 196616 | tf_op jit(solution)/shard_map/ppermute | solution.py:21
  (2 other events, 6.0 us)
Sparse Core Ops, SparseCore 0:
  10.9 66.1 all-gather.4
  78.7 62.1 all-gather.6
  143.0 62.1 all-gather.8
  206.6 44.6 all-gather.10

commit v2 on v1

--- a/solution.py
+++ b/solution.py
@@ -1,36 +1,44 @@
+import functools
+
 import jax
 import jax.numpy as jnp
 from jax import lax
+from jax.experimental import pallas as pl
+from jax.experimental.pallas import tpu as pltpu
 from jax.sharding import PartitionSpec as P
 
 HIGHEST = lax.Precision.HIGHEST
-LANES = 128
-CHUNKS = 4
+CHUNK = 384
 
 
 def shifted(x, axes, sizes, shift):
-    pairs = []
     if isinstance(axes, str):
         (n,) = sizes
         pairs = [(i, (i + shift[0]) % n) for i in range(n)]
     else:
         a, b = sizes
-        for i in range(a):
-            for j in range(b):
-                pairs.append((i * b + j, ((i + shift[0]) % a) * b + (j + shift[1]) % b))
+        pairs = [
+            (i * b + j, ((i + shift[0]) % a) * b + (j + shift[1]) % b)
+            for i in range(a) for j in range(b)
+        ]
     return lax.ppermute(x, axes, pairs)
+
+
+def in_order(pieces, axis, dim):
+    n = len(pieces)
+    me = lax.axis_index(axis)
+    shape = list(pieces[0].shape)
+    size = shape[dim]
+    shape[dim] *= n
+    out = jnp.zeros(shape, pieces[0].dtype)
+    for r, piece in enumerate(pieces):
+        out = lax.dynamic_update_slice_in_dim(out, piece, ((me - r) % n) * size, dim)
+    return out
 
 
 def gather_in_order(x, axis, dim):
     n = lax.axis_size(axis)
-    me = lax.axis_index(axis)
-    shape = list(x.shape)
-    shape[dim] *= n
-    out = jnp.zeros(shape, x.dtype)
-    for r in range(n):
-        piece = x if r == 0 else shifted(x, axis, (n,), (r,))
-        out = lax.dynamic_update_slice_in_dim(out, piece, ((me - r) % n) * x.shape[dim], dim)
-    return out
+    return in_order([x if r == 0 else shifted(x, axis, (n,), (r,)) for r in range(n)], axis, dim)
 
 
 def sum_over(x, axis):
@@ -38,6 +46,63 @@
     if n == 2:
         return x + shifted(x, axis, (2,), (1,))
     return jnp.sum(gather_in_order(x[None], axis, 0), axis=0)
+
+
+def chunk_kernel(n, me_ref, cot_ref, gate_ref, factor_ref, before_ref, *rest):
+    slots, (after_ref, weight, sems) = rest[:n], rest[n:]
+    columns = slots[0].shape[1]
+
+    @pl.when(pl.program_id(0) == 0)
+    def _():
+        copies = []
+        for r in range(n):
+            at = pl.multiple_of(lax.rem(me_ref[0] + (n - r), n) * columns, columns)
+            copies.append(pltpu.make_async_copy(slots[r], weight.at[:, pl.ds(at, columns)], sems.at[r]))
+        for copy in copies:
+            copy.start()
+        for copy in copies:
+            copy.wait()
+
+    hidden = lax.dot_general(
+        cot_ref[...], weight[...], (((1,), (1,)), ((), ())), preferred_element_type=jnp.float32
+    )
+    gate = gate_ref[...].astype(jnp.float32)
+    up_grad = (hidden * (gate / (1.0 + jnp.exp(-gate)))).astype(jnp.bfloat16)
+    after_ref[...] = before_ref[...] + jnp.dot(
+        up_grad, factor_ref[...], preferred_element_type=jnp.float32
+    )
+
+
+def add_chunk(me, cot, gate, factor, before, slots, tile):
+    tokens, depth = cot.shape
+    height = gate.shape[1]
+    rank = factor.shape[1]
+    n = len(slots)
+    return pl.pallas_call(
+        functools.partial(chunk_kernel, n),
+        out_shape=jax.ShapeDtypeStruct((tokens, rank), jnp.float32),
+        grid_spec=pltpu.PrefetchScalarGridSpec(
+            num_scalar_prefetch=1,
+            grid=(tokens // tile,),
+            in_specs=[
+                pl.BlockSpec((tile, depth), lambda i, me: (i, 0)),
+                pl.BlockSpec((tile, height), lambda i, me: (i, 0)),
+                pl.BlockSpec((height, rank), lambda i, me: (0, 0)),
+                pl.BlockSpec((tile, rank), lambda i, me: (i, 0)),
+            ] + [pl.BlockSpec(memory_space=pl.ANY)] * n,
+            out_specs=pl.BlockSpec((tile, rank), lambda i, me: (i, 0)),
+            scratch_shapes=[
+                pltpu.VMEM((height, depth), jnp.bfloat16),
+                pltpu.SemaphoreType.DMA((n,)),
+            ],
+        ),
+        compiler_params=pltpu.CompilerParams(vmem_limit_bytes=40 * 1024 * 1024),
+        cost_estimate=pl.CostEstimate(
+            flops=2 * tokens * depth * height,
+            bytes_accessed=2 * (tokens * depth + height * depth + tokens * height),
+            transcendentals=tokens * height,
+        ),
+    )(me, cot, gate, factor, before, *slots)
 
 
 def on_device(inputs, cotangent, gate_pre, down_weight, proj_in, proj_out, doc_lens, queries):
@@ -50,36 +115,39 @@
     docs = doc_lens.shape[1]
     rank = proj_in.shape[1]
     width = rank * rank
-    sharers = n_groups * n_seq
-    part = min(units, -(-units // (sharers * LANES)) * LANES)
+    part = units // (n_groups * n_seq)
     pair = ("groups", "seq")
     sizes = (n_groups, n_seq)
-
-    def first_unit(who):
-        return jnp.minimum(who * part, units - part)
-
     mine = group * n_seq + half
-    start = first_unit(mine)
-    tiles = -(-part // LANES)
-    bounds = sorted({min(part, -(-tiles * c // CHUNKS) * LANES) for c in range(CHUNKS + 1)})
-
-    gathered = []
-    token = None
-    for low, high in zip(bounds[:-1], bounds[1:]):
-        block = lax.dynamic_slice_in_dim(down_weight, start + low, high - low, 0)
-        gathered.append(lax.all_gather(block, "dp", axis=1, tiled=True))
+
+    bounds = list(range(0, part, CHUNK)) + [part]
+    spans = list(zip(bounds[:-1], bounds[1:]))
+    chunks = [
+        [lax.dynamic_slice_in_dim(down_weight, mine * part + low, high - low, 0)] for low, high in spans
+    ]
+    sent = []
+    for first in range(0, len(chunks), 2):
+        for _ in range(n_dp - 1):
+            for slots in chunks[first:first + 2]:
+                block = slots[-1]
+                if len(sent) >= 2:
+                    block, sent[-2][-1] = lax.optimization_barrier((block, sent[-2][-1]))
+                slots.append(shifted(block, "dp", (n_dp,), (1,)))
+                sent.append(slots)
 
     order = [(dg, ds) for dg in range(n_groups) for ds in range(n_seq)]
     cots = []
     for dg in range(n_groups):
         own = cotangent if dg == 0 else shifted(cotangent, "groups", (n_groups,), (dg,))
-        full = gather_in_order(own, "tensor", 1)
+        pieces = [own if r == 0 else shifted(own, "tensor", (n_tensor,), (r,)) for r in range(n_tensor)]
         for ds in range(n_seq):
-            cots.append(full if ds == 0 else shifted(full, "seq", (n_seq,), (ds,)))
+            cots.append(in_order(
+                pieces if ds == 0 else [shifted(x, "seq", (n_seq,), (ds,)) for x in pieces], "tensor", 1
+            ))
     gates = []
     for dg, ds in order:
         to = ((group + dg) % n_groups) * n_seq + (half + ds) % n_seq
-        columns = lax.dynamic_slice_in_dim(gate_pre, first_unit(to), part, 1)
+        columns = lax.dynamic_slice_in_dim(gate_pre, to * part, part, 1)
         gates.append(columns if dg == ds == 0 else shifted(columns, pair, sizes, (dg, ds)))
 
     right = sum_over(jnp.dot(inputs, proj_in, preferred_element_type=jnp.float32), "tensor")
@@ -88,18 +156,12 @@
 
     cot = jnp.concatenate(cots, axis=0)
     gate = jnp.concatenate(gates, axis=0)
-    slope = jax.nn.silu(gate.astype(jnp.float32))
-    numbers = start + jnp.arange(part, dtype=jnp.int32)
-    out_factor = lax.dynamic_slice_in_dim(proj_out, start, part, 0)
-    out_factor = jnp.where((numbers >= mine * part)[:, None], out_factor, 0).astype(proj_out.dtype)
-
-    left = 0.0
-    for weight, low, high in zip(gathered, bounds[:-1], bounds[1:]):
-        hidden_grad = lax.dot_general(
-            cot, weight, (((1,), (1,)), ((), ())), preferred_element_type=jnp.float32
-        )
-        up_grad = (hidden_grad * slope[:, low:high]).astype(jnp.bfloat16)
-        left = left + jnp.dot(up_grad, out_factor[low:high], preferred_element_type=jnp.float32)
+    out_factor = lax.dynamic_slice_in_dim(proj_out, mine * part, part, 0)
+    me = jnp.reshape(stage, (1,)).astype(jnp.int32)
+
+    left = jnp.zeros((n_groups * n_seq * rows, rank), jnp.float32)
+    for slots, (low, high) in zip(chunks, spans):
+        left = add_chunk(me, cot, gate[:, low:high], out_factor[low:high], left, slots, rows)
 
     parts = []
     for dg in range(n_groups):
@@ -116,11 +178,8 @@
         ).reshape(docs, width)
         parts.append(grads)
     grads = parts[0]
-    if n_groups == 2:
-        grads = grads + shifted(parts[1], "groups", (2,), (1,))
-    else:
-        for dg in range(1, n_groups):
-            grads = grads + shifted(parts[dg], "groups", (n_groups,), (-dg,))
+    for dg in range(1, n_groups):
+        grads = grads + shifted(parts[dg], "groups", (n_groups,), (-dg,))
     doc_grads = sum_over(sum_over(grads, "tensor"), "seq")
 
     every = gather_in_order(doc_grads, "dp", 0)

time: 331 us -> 342 us (1.033); the launches traced: 324 us -> 340 us
  matrix products: 94.7 us -> 13.3 us
  Pallas kernels: 0 us -> 53.2 us
  local copies, waits for them, and re-layouts: 28.6 us -> 54.6 us
  between operations: 15.1 us -> 1.9 us
  waiting for transfers between devices: 138 us -> 150 us
  starting transfers between devices: 20.5 us -> 31.5 us
  other arithmetic: 27.8 us -> 35.8 us
    dot_general x4 -> x0, matrix products: 80.8 us -> none  [on_device(): jnp.dot(up_grad, out_factor[low:high], preferred_element_type=jnp.float32)]
    pallas_call x0 -> x4, Pallas kernels: none -> 53.2 us  [add_chunk(): pl.pallas_call(functools.partial(chunk_kernel, n), out_shape=jax.ShapeDty...]
    concatenate x0 -> x2, other arithmetic: none -> 18.3 us  [the longest x1 9.63 us: on_device(): cot = jnp.concatenate(cots, axis=0)]
    ppermute x19 -> x33, waiting for transfers between devices: 137 us -> 150 us  [shifted(): return lax.ppermute(x, axes, pairs)]
    unnamed x22 -> x35, local copies, waits for them, and re-layouts: 0.05 us -> 11.7 us
    ppermute x19 -> x33, starting transfers between devices: 20.4 us -> 31.5 us  [shifted(): return lax.ppermute(x, axes, pairs)]
    mul x1 -> x0, other arithmetic: 8.32 us -> none  [on_device(): slope = jax.nn.silu(gate.astype(jnp.float32))]
    ppermute x0 -> x3, local copies, waits for them, and re-layouts: none -> 7.64 us  [shifted(): return lax.ppermute(x, axes, pairs)]
  transfers between devices with their start and end apart: 23 -> 33, of which waited for: 10 -> 15; matrix products, arithmetic and copies ran while one was open for 40% -> 24% of each run, Pallas kernels for 0% -> 16%
where the time goes in v2:
time: 342 us; the launch traced here: 340 us
  waiting for transfers between devices  150 us (44%)
  local copies, waits for them, and re-layouts  54.6 us (16%)
  Pallas kernels  53.2 us (16%)
  other arithmetic  35.8 us (10%)
  starting transfers between devices  31.5 us (9%)
  matrix products  13.3 us (4%)
    ppermute x33, waiting for transfers between devices, shifted(): return lax.ppermute(x, axes, pairs)  150 us
    pallas_call x4, Pallas kernels, add_chunk(): pl.pallas_call(functools.partial(chunk_kernel, n), out_shape=jax.ShapeDty...  53.2 us
    ppermute x33, starting transfers between devices, shifted(): return lax.ppermute(x, axes, pairs)  31.5 us
    dynamic_update_slice x11, local copies, waits for them, and re-layouts, in_order(): out = lax.dynamic_update_slice_in_dim(out, piece, (me - r) % n * size, dim)  16.2 us
    unnamed x35, local copies, waits for them, and re-layouts  11.7 us
    concatenate x1, other arithmetic, on_device(): cot = jnp.concatenate(cots, axis=0)  9.63 us
    concatenate x1, other arithmetic, on_device(): gate = jnp.concatenate(gates, axis=0)  8.66 us
    dynamic_slice x1, local copies, waits for them, and re-layouts, on_device(): columns = lax.dynamic_slice_in_dim(gate_pre, to * part, part, 1)  8.06 us
  transfers between devices with their start and end apart: 33, of which 15 were waited for; matrix products, arithmetic and copies ran while one was open for 24% of the time, Pallas kernels for 16%

profile of v2, /device:TPU:0, one launch (start us, length us, event | category | flops | bytes accessed | tf_op | source)
XLA Modules:
  0.0 340.4 jit_solution(9138860694504274549)
XLA Ops:
  0.6 3.0 collective-permute-start.3
  3.7 8.1 %constant_dynamic-slice_fusion.11 = (bf16[512,1376]{1,0:T(8,128)(2,1)}, bf16[512,1376]{1,0:T(8,128)(2,1)}, bf16[512,1376]{1,0:T(8,128)(2,1)}, bf16[512,1376]{1,0:T(8,128)(2,1)S(1)}) fusion(bf16[512,5504]{1,0:T(8,128)(2,1)} %param.10, s32[]{:T(128)S(6)} %select_n.135, s32[]{:T(128)S(6)} %select_n.139, s32[]{:T(128)S(6)} %select_n.137, s32[]{:T(128)S(6)} %select_n.140), kind=kLoop, calls=%fused_computation.64 | loop fusion | bytes 11272208 | tf_op jit(solution)/shard_map/dynamic_slice | solution.py:150
  13.3 3.0 constant_dynamic-slice_fusion.4
  20.7 2.6 copy.59
  23.3 56.4 %collective-permute-done.24 = s32[1,16]{1,0:T(1,128)S(1)} collective-permute-done((s32[1,16]{1,0:T(1,128)S(1)}, s32[1,16]{1,0:T(1,128)S(1)}, u32[]{:S(2)}, u32[]{:S(2)}) %collective-permute-start.24) | collective-permute-done | bytes 96 | tf_op jit(solution)/shard_map/ppermute | solution.py:24
  85.9 2.8 collective-permute-done.22
  92.4 2.5 copy.58
  95.5 13.4 %collective-permute-done.11.rest_2_ = bf16[384,1024]{1,0:T(8,128)(2,1)} collective-permute-done((bf16[384,1024]{1,0:T(8,128)(2,1)}, bf16[384,1024]{1,0:T(8,128)(2,1)}, u32[]{:S(2)}, u32[]{:S(2)}) %collective-permute-start.11) | collective-permute-done | bytes 786464 | tf_op jit(solution)/shard_map/ppermute | solution.py:24
  109.0 3.2 collective-permute-done.8
  115.4 16.1 %collective-permute-done.14.rest_2_ = bf16[384,1024]{1,0:T(8,128)(2,1)} collective-permute-done((bf16[384,1024]{1,0:T(8,128)(2,1)}, bf16[384,1024]{1,0:T(8,128)(2,1)}, u32[]{:S(2)}, u32[]{:S(2)}) %collective-permute-start.14) | collective-permute-done | bytes 786464 | tf_op jit(solution)/shard_map/ppermute | solution.py:24
  131.5 13.0 %collective-permute-done.12.rest_3_ = bf16[384,1024]{1,0:T(8,128)(2,1)} collective-permute-done((bf16[384,1024]{1,0:T(8,128)(2,1)}, bf16[384,1024]{1,0:T(8,128)(2,1)}, u32[]{:S(2)}, u32[]{:S(2)}) %collective-permute-start.12) | collective-permute-done | bytes 786464 | tf_op jit(solution)/shard_map/ppermute | solution.py:24
  150.4 3.2 constant_dynamic-update-slice_fusion.11
  154.7 12.4 %collective-permute-done.15.rest_3_ = bf16[384,1024]{1,0:T(8,128)(2,1)} collective-permute-done((bf16[384,1024]{1,0:T(8,128)(2,1)}, bf16[384,1024]{1,0:T(8,128)(2,1)}, u32[]{:S(2)}, u32[]{:S(2)}) %collective-permute-start.15) | collective-permute-done | bytes 786464 | tf_op jit(solution)/shard_map/ppermute | solution.py:24
  169.3 2.5 copy.47
  171.8 2.6 copy.46
  174.4 2.5 copy.45
  184.4 8.7 %pad_maximum_fusion.1 = (bf16[2048,384]{1,0:T(8,128)(2,1)S(1)}, bf16[2048,384]{1,0:T(8,128)(2,1)S(1)}, bf16[2048,384]{1,0:T(8,128)(2,1)S(1)}) fusion(bf16[512,1376]{1,0:T(8,128)(2,1)S(1)} %copy-done.4, bf16[512,1376]{1,0:T(8,128)(2,1)S(1)} %copy-done.5, bf16[512,1376]{1,0:T(8,128)(2,1)S(1)} %copy-done.6, bf16[512,1376]{1,0:T(8,128)(2,1)S(1)} %copy-done.3), kind=kLoop, calls=%fused_computation.5 | loop fusion | flops 18874368 | bytes 10354688 | tf_op jit(solution)/shard_map/concatenate | solution.py:158
  201.2 3.3 constant_dynamic-update-slice_fusion.10
  204.4 20.5 %collective-permute-done.20.rest_2_ = bf16[224,1024]{1,0:T(8,128)(2,1)S(1)} collective-permute-done((bf16[224,1024]{1,0:T(8,128)(2,1)S(1)}, bf16[224,1024]{1,0:T(8,128)(2,1)S(1)}, u32[]{:S(2)}, u32[]{:S(2)}) %collective-permute-start.20) | collective-permute-done | bytes 458784 | tf_op jit(solution)/shard_map/ppermute | solution.py:24
  235.3 9.6 %pad_maximum_fusion.cot_ref = bf16[2048,4096]{1,0:T(8,128)(2,1)} fusion(bf16[512,4096]{1,0:T(8,128)(2,1)S(1)} %constant_dynamic-update-slice_fusion.4, bf16[512,4096]{1,0:T(8,128)(2,1)S(1)} %constant_dynamic-update-slice_fusion.6, bf16[512,4096]{1,0:T(8,128)(2,1)S(1)} %constant_dynamic-update-slice_fusion.8, ...), kind=kLoop, calls=%fused_computation | loop fusion | flops 67108864 | bytes 33554432 | tf_op jit(solution)/shard_map/concatenate | solution.py:157
  245.0 14.9 %shard_map.103.before_ref = f32[2048,32]{1,0:T(8,128)S(1)} custom-call(s32[1]{0:T(128)} %bitcast.me_ref, bf16[2048,4096]{1,0:T(8,128)(2,1)} %pad_maximum_fusion.cot_ref, bf16[2048,384]{1,0:T(8,128)(2,1)S(1)} %get-tuple-element.50.gate_ref, bf16[384,32]{1,0:T(8,128)(2,1)S(1)} %copy-done.2, f32[2048,32]{1,0:T(8,128)S(1)} %broadcast_in_dim.5.before_ref, ...), custom_call_target="tpu_custom_call" | custom-call | flops 6442450944 | bytes 21495808 | tf_op jit(solution)/shard_map/pallas_call | solution.py:81
  260.0 14.9 %shard_map.104.before_ref = f32[2048,32]{1,0:T(8,128)S(1)} custom-call(s32[1]{0:T(128)} %bitcast.me_ref, bf16[2048,4096]{1,0:T(8,128)(2,1)} %pad_maximum_fusion.cot_ref, bf16[2048,384]{1,0:T(8,128)(2,1)S(1)} %get-tuple-element.51.gate_ref, bf16[384,32]{1,0:T(8,128)(2,1)S(1)} %copy-done.1, f32[2048,32]{1,0:T(8,128)S(1)} %shard_map.103.before_ref, ...), custom_call_target="tpu_custom_call" | custom-call | flops 6442450944 | bytes 21495808 | tf_op jit(solution)/shard_map/pallas_call | solution.py:81
  274.9 14.2 %shard_map.105.before_ref = f32[2048,32]{1,0:T(8,128)S(1)} custom-call(s32[1]{0:T(128)} %bitcast.me_ref, bf16[2048,4096]{1,0:T(8,128)(2,1)} %pad_maximum_fusion.cot_ref, bf16[2048,384]{1,0:T(8,128)(2,1)S(1)} %get-tuple-element.52.gate_ref, bf16[384,32]{1,0:T(8,128)(2,1)S(1)} %copy.63.factor_ref, f32[2048,32]{1,0:T(8,128)S(1)} %shard_map.104.before_ref, ...), custom_call_target="tpu_custom_call" | custom-call | flops 6442450944 | bytes 21495808 | tf_op jit(solution)/shard_map/pallas_call | solution.py:81
  289.1 9.2 %shard_map.106 = f32[2048,32]{1,0:T(8,128)S(1)} custom-call(s32[1]{0:T(128)} %bitcast.me_ref, bf16[2048,4096]{1,0:T(8,128)(2,1)} %pad_maximum_fusion.cot_ref, bf16[2048,224]{1,0:T(8,128)(2,1)S(1)} %pad_maximum_fusion.6.gate_ref, bf16[224,32]{1,0:T(8,128)(2,1)S(1)} %copy.62.factor_ref, f32[2048,32]{1,0:T(8,128)S(1)} %shard_map.105.before_ref, ...), custom_call_target="tpu_custom_call" | custom-call | flops 3758096384 | bytes 19529728 | tf_op jit(solution)/shard_map/pallas_call | solution.py:81
  299.2 2.6 fusion.7
  302.8 2.6 fusion.4
  308.1 2.8 collective-permute-done.28
  312.6 2.8 collective-permute-start.31
  315.5 2.8 collective-permute-start.32
  318.5 2.7 collective-permute-done.31
  327.1 5.8 %cholesky.17 = f32[64,64]{1,0:T(8,128)S(1)} custom-call(f32[64,64]{1,0:T(8,128)S(1)} %fusion.27), custom_call_target="Cholesky" | custom-call | tf_op jit(solution)/shard_map/jit(cholesky)/cholesky | solution.py:200
  334.3 4.9 %custom-call.10 = f32[1,64,64]{1,2,0:T(8,128)S(1)} custom-call(f32[1,64,64]{2,1,0:T(8,128)S(1)} %fusion.21), custom_call_target="InvertDiagBlocksLowerTriangular" | custom-call | tf_op jit(solution)/shard_map/jit(_cho_solve)/triangular_solve | solution.py:202
  (141 shorter events, 68.5 us)
Async XLA Ops:
  0.6 94.3 %collective-permute-start.3 = (bf16[512,2048]{1,0:T(8,128)(2,1)}, bf16[512,2048]{1,0:T(8,128)(2,1)}, u32[]{:S(2)}, u32[]{:S(2)}) collective-permute-start(bf16[512,2048]{1,0:T(8,128)(2,1)} %param.9), channel_id=1, source_target_pairs={{0,16},{16,0},{1,17},{17,1},{2,18},{18,2},{3,19},{19,3},{4,20},{20... | collective-permute-start | bytes 6291464 | tf_op jit(solution)/shard_map/ppermute | solution.py:24
  13.3 81.6 %collective-permute-start.9 = (bf16[512,1376]{0,1:T(8,128)(2,1)}, bf16[512,1376]{0,1:T(8,128)(2,1)}, u32[]{:S(2)}, u32[]{:S(2)}) collective-permute-start(bf16[512,1376]{0,1:T(8,128)(2,1)} %copy.60), channel_id=1, source_target_pairs={{0,17},{1,16},{16,1},{17,0},{2,19},{3,18},{18,3},{19,2},{4,21},{5,... | collective-permute-start | bytes 4227080 | tf_op jit(solution)/shard_map/ppermute | solution.py:24
  16.3 67.5 %collective-permute-start.10 = (bf16[384,1024]{1,0:T(8,128)(2,1)}, bf16[384,1024]{1,0:T(8,128)(2,1)}, u32[]{:S(2)}, u32[]{:S(2)}) collective-permute-start(bf16[384,1024]{1,0:T(8,128)(2,1)} %get-tuple-element.49.rest_0_), channel_id=1, source_target_pairs={{0,4},{4,8},{8,12},{12,0},{1,5},{5,9},{9,13},{13,1},{2,6},{6,10},{... | collective-permute-start | bytes 2359304 | tf_op jit(solution)/shard_map/ppermute | solution.py:24
  17.9 73.0 %collective-permute-start.13 = (bf16[384,1024]{1,0:T(8,128)(2,1)}, bf16[384,1024]{1,0:T(8,128)(2,1)}, u32[]{:S(2)}, u32[]{:S(2)}) collective-permute-start(bf16[384,1024]{1,0:T(8,128)(2,1)} %get-tuple-element.47.rest_0_), channel_id=1, source_target_pairs={{0,4},{4,8},{8,12},{12,0},{1,5},{5,9},{9,13},{13,1},{2,6},{6,10},{... | collective-permute-start | bytes 2359304 | tf_op jit(solution)/shard_map/ppermute | solution.py:24
  19.5 60.2 %collective-permute-start.24 = (s32[1,16]{1,0:T(1,128)S(1)}, s32[1,16]{1,0:T(1,128)S(1)}, u32[]{:S(2)}, u32[]{:S(2)}) collective-permute-start(s32[1,16]{1,0:T(1,128)S(1)} %copy-done.13), channel_id=1, source_target_pairs={{0,16},{16,0},{1,17},{17,1},{2,18},{18,2},{3,19},{19,3},{4,20},{20... | collective-permute-start | bytes 200 | tf_op jit(solution)/shard_map/ppermute | solution.py:24
  79.7 32.5 %collective-permute-start.8 = (bf16[512,1376]{0,1:T(8,128)(2,1)}, bf16[512,1376]{0,1:T(8,128)(2,1)}, u32[]{:S(2)}, u32[]{:S(2)}) collective-permute-start(bf16[512,1376]{0,1:T(8,128)(2,1)} %copy.59), channel_id=1, source_target_pairs={{0,16},{1,17},{16,0},{17,1},{2,18},{3,19},{18,2},{19,3},{4,20},{5,... | collective-permute-start | bytes 4227080 | tf_op jit(solution)/shard_map/ppermute | solution.py:24
  84.4 4.3 %collective-permute-start.22 = (f32[512,32]{0,1:T(8,128)S(1)}, f32[512,32]{0,1:T(8,128)S(1)}, u32[]{:S(2)}, u32[]{:S(2)}) collective-permute-start(f32[512,32]{0,1:T(8,128)S(1)} %fusion.33), channel_id=1, source_target_pairs={{0,2},{2,0},{1,3},{3,1},{4,6},{6,4},{5,7},{7,5},{8,10},{10,8},{9,1... | collective-permute-start | bytes 196616 | tf_op jit(solution)/shard_map/ppermute | solution.py:24
  89.3 19.7 %collective-permute-start.11 = (bf16[384,1024]{1,0:T(8,128)(2,1)}, bf16[384,1024]{1,0:T(8,128)(2,1)}, u32[]{:S(2)}, u32[]{:S(2)}) collective-permute-start(bf16[384,1024]{1,0:T(8,128)(2,1)} %collective-permute-done.10.rest_1_), channel_id=1, source_target_pairs={{0,4},{4,8},{8,12},{12,0},{1,5},{5,9},{9,13},{13,1},{2,6},{6,10},{... | collective-permute-start | bytes 2359304 | tf_op jit(solution)/shard_map/ppermute | solution.py:24
  90.9 63.1 %collective-permute-start = (bf16[512,2048]{1,0:T(8,128)(2,1)}, bf16[512,2048]{1,0:T(8,128)(2,1)}, u32[]{:S(2)}, u32[]{:S(2)}) collective-permute-start(bf16[512,2048]{1,0:T(8,128)(2,1)} %param.9), channel_id=1, source_target_pairs={{0,2},{2,0},{1,3},{3,1},{4,6},{6,4},{5,7},{7,5},{8,10},{10,8},{9,1... | collective-permute-start | bytes 6291464 | tf_op jit(solution)/shard_map/ppermute | solution.py:24
  94.9 52.7 %collective-permute-start.7 = (bf16[512,1376]{0,1:T(8,128)(2,1)}, bf16[512,1376]{0,1:T(8,128)(2,1)}, u32[]{:S(2)}, u32[]{:S(2)}) collective-permute-start(bf16[512,1376]{0,1:T(8,128)(2,1)} %copy.58), channel_id=1, source_target_pairs={{0,1},{1,0},{16,17},{17,16},{2,3},{3,2},{18,19},{19,18},{4,5},{5,4... | collective-permute-start | bytes 4227080 | tf_op jit(solution)/shard_map/ppermute | solution.py:24
  94.9 86.5 %collective-permute-start.4 = (bf16[512,2048]{1,0:T(8,128)(2,1)}, bf16[512,2048]{1,0:T(8,128)(2,1)}, u32[]{:S(2)}, u32[]{:S(2)}) collective-permute-start(bf16[512,2048]{1,0:T(8,128)(2,1)} %collective-permute-done.3), channel_id=1, source_target_pairs={{0,2},{2,0},{1,3},{3,1},{4,6},{6,4},{5,7},{7,5},{8,10},{10,8},{9,1... | collective-permute-start | bytes 6291464 | tf_op jit(solution)/shard_map/ppermute | solution.py:24
  108.9 22.6 %collective-permute-start.14 = (bf16[384,1024]{1,0:T(8,128)(2,1)}, bf16[384,1024]{1,0:T(8,128)(2,1)}, u32[]{:S(2)}, u32[]{:S(2)}) collective-permute-start(bf16[384,1024]{1,0:T(8,128)(2,1)} %collective-permute-done.13.rest_1_), channel_id=1, source_target_pairs={{0,4},{4,8},{8,12},{12,0},{1,5},{5,9},{9,13},{13,1},{2,6},{6,10},{... | collective-permute-start | bytes 2359304 | tf_op jit(solution)/shard_map/ppermute | solution.py:24
  112.2 32.3 %collective-permute-start.12 = (bf16[384,1024]{1,0:T(8,128)(2,1)}, bf16[384,1024]{1,0:T(8,128)(2,1)}, u32[]{:S(2)}, u32[]{:S(2)}) collective-permute-start(bf16[384,1024]{1,0:T(8,128)(2,1)} %collective-permute-done.11.rest_2_), channel_id=1, source_target_pairs={{0,4},{4,8},{8,12},{12,0},{1,5},{5,9},{9,13},{13,1},{2,6},{6,10},{... | collective-permute-start | bytes 2359304 | tf_op jit(solution)/shard_map/ppermute | solution.py:24
  131.5 65.6 %collective-permute-start.1 = (bf16[512,2048]{1,0:T(8,128)(2,1)}, bf16[512,2048]{1,0:T(8,128)(2,1)}, u32[]{:S(2)}, u32[]{:S(2)}) collective-permute-start(bf16[512,2048]{1,0:T(8,128)(2,1)} %param.9), channel_id=1, source_target_pairs={{0,1},{1,0},{2,3},{3,2},{4,5},{5,4},{6,7},{7,6},{8,9},{9,8},{10,11... | collective-permute-start | bytes 6291464 | tf_op jit(solution)/shard_map/ppermute | solution.py:24
  144.5 22.6 %collective-permute-start.15 = (bf16[384,1024]{1,0:T(8,128)(2,1)}, bf16[384,1024]{1,0:T(8,128)(2,1)}, u32[]{:S(2)}, u32[]{:S(2)}) collective-permute-start(bf16[384,1024]{1,0:T(8,128)(2,1)} %collective-permute-done.14.rest_2_), channel_id=1, source_target_pairs={{0,4},{4,8},{8,12},{12,0},{1,5},{5,9},{9,13},{13,1},{2,6},{6,10},{... | collective-permute-start | bytes 2359304 | tf_op jit(solution)/shard_map/ppermute | solution.py:24
  147.7 31.5 %collective-permute-start.16 = (bf16[384,1024]{1,0:T(8,128)(2,1)S(1)}, bf16[384,1024]{1,0:T(8,128)(2,1)}, u32[]{:S(2)}, u32[]{:S(2)}) collective-permute-start(bf16[384,1024]{1,0:T(8,128)(2,1)S(1)} %get-tuple-element.33.rest_0_), channel_id=1, source_target_pairs={{0,4},{4,8},{8,12},{12,0},{1,5},{5,9},{9,13},{13,1},{2,6},{6,10},{... | collective-permute-start | bytes 2359304 | tf_op jit(solution)/shard_map/ppermute | solution.py:24
  154.0 73.5 %collective-permute-start.5 = (bf16[512,2048]{1,0:T(8,128)(2,1)}, bf16[512,2048]{1,0:T(8,128)(2,1)}, u32[]{:S(2)}, u32[]{:S(2)}) collective-permute-start(bf16[512,2048]{1,0:T(8,128)(2,1)} %collective-permute-done.3), channel_id=1, source_target_pairs={{0,1},{1,0},{2,3},{3,2},{4,5},{5,4},{6,7},{7,6},{8,9},{9,8},{10,11... | collective-permute-start | bytes 6291464 | tf_op jit(solution)/shard_map/ppermute | solution.py:24
  167.1 64.3 %collective-permute-start.2 = (bf16[512,2048]{1,0:T(8,128)(2,1)}, bf16[512,2048]{1,0:T(8,128)(2,1)}, u32[]{:S(2)}, u32[]{:S(2)}) collective-permute-start(bf16[512,2048]{1,0:T(8,128)(2,1)} %collective-permute-done), channel_id=1, source_target_pairs={{0,1},{1,0},{2,3},{3,2},{4,5},{5,4},{6,7},{7,6},{8,9},{9,8},{10,11... | collective-permute-start | bytes 6291464 | tf_op jit(solution)/shard_map/ppermute | solution.py:24
  179.2 13.9 %collective-permute-start.19 = (bf16[224,1024]{1,0:T(8,128)(2,1)S(1)}, bf16[224,1024]{1,0:T(8,128)(2,1)S(1)}, u32[]{:S(2)}, u32[]{:S(2)}) collective-permute-start(bf16[224,1024]{1,0:T(8,128)(2,1)S(1)} %constant_dynamic-slice_fusion.3.rest_0_), channel_id=1, source_target_pairs={{0,4},{4,8},{8,12},{12,0},{1,5},{5,9},{9,13},{13,1},{2,6},{6,10},{... | collective-permute-start | bytes 1376264 | tf_op jit(solution)/shard_map/ppermute | solution.py:24
  181.4 52.0 %collective-permute-start.6 = (bf16[512,2048]{1,0:T(8,128)(2,1)}, bf16[512,2048]{1,0:T(8,128)(2,1)S(1)}, u32[]{:S(2)}, u32[]{:S(2)}) collective-permute-start(bf16[512,2048]{1,0:T(8,128)(2,1)} %collective-permute-done.4), channel_id=1, source_target_pairs={{0,1},{1,0},{2,3},{3,2},{4,5},{5,4},{6,7},{7,6},{8,9},{9,8},{10,11... | collective-permute-start | bytes 6291464 | tf_op jit(solution)/shard_map/ppermute | solution.py:24
  193.1 31.9 %collective-permute-start.17 = (bf16[384,1024]{1,0:T(8,128)(2,1)}, bf16[384,1024]{1,0:T(8,128)(2,1)S(1)}, u32[]{:S(2)}, u32[]{:S(2)}) collective-permute-start(bf16[384,1024]{1,0:T(8,128)(2,1)} %collective-permute-done.16.rest_1_), channel_id=1, source_target_pairs={{0,4},{4,8},{8,12},{12,0},{1,5},{5,9},{9,13},{13,1},{2,6},{6,10},{... | collective-permute-start | bytes 2359304 | tf_op jit(solution)/shard_map/ppermute | solution.py:24
  197.1 27.8 %collective-permute-start.20 = (bf16[224,1024]{1,0:T(8,128)(2,1)S(1)}, bf16[224,1024]{1,0:T(8,128)(2,1)S(1)}, u32[]{:S(2)}, u32[]{:S(2)}) collective-permute-start(bf16[224,1024]{1,0:T(8,128)(2,1)S(1)} %collective-permute-done.19.rest_1_), channel_id=1, source_target_pairs={{0,4},{4,8},{8,12},{12,0},{1,5},{5,9},{9,13},{13,1},{2,6},{6,10},{... | collective-permute-start | bytes 1376264 | tf_op jit(solution)/shard_map/ppermute | solution.py:24
  224.9 77.8 %collective-permute-start.23 = (f32[512,32]{0,1:T(8,128)}, f32[512,32]{0,1:T(8,128)}, u32[]{:S(2)}, u32[]{:S(2)}) collective-permute-start(f32[512,32]{0,1:T(8,128)} %add.236), channel_id=1, source_target_pairs={{0,1},{1,0},{16,17},{17,16},{2,3},{3,2},{18,19},{19,18},{4,5},{5,4... | collective-permute-start | bytes 196616 | tf_op jit(solution)/shard_map/ppermute | solution.py:24
  225.0 73.6 %collective-permute-start.26 = (f32[512,32]{0,1:T(8,128)}, f32[512,32]{0,1:T(8,128)}, u32[]{:S(2)}, u32[]{:S(2)}) collective-permute-start(f32[512,32]{0,1:T(8,128)} %add.236), channel_id=1, source_target_pairs={{0,17},{1,16},{16,1},{17,0},{2,19},{3,18},{18,3},{19,2},{4,21},{5,... | collective-permute-start | bytes 196616 | tf_op jit(solution)/shard_map/ppermute | solution.py:24
  227.5 71.1 %collective-permute-start.25 = (f32[512,32]{0,1:T(8,128)}, f32[512,32]{0,1:T(8,128)}, u32[]{:S(2)}, u32[]{:S(2)}) collective-permute-start(f32[512,32]{0,1:T(8,128)} %add.236), channel_id=1, source_target_pairs={{0,16},{1,17},{16,0},{17,1},{2,18},{3,19},{18,2},{19,3},{4,20},{5,... | collective-permute-start | bytes 196616 | tf_op jit(solution)/shard_map/ppermute | solution.py:24
  231.4 57.6 %collective-permute-start.21 = (bf16[224,1024]{1,0:T(8,128)(2,1)S(1)}, bf16[224,1024]{1,0:T(8,128)(2,1)S(1)}, u32[]{:S(2)}, u32[]{:S(2)}) collective-permute-start(bf16[224,1024]{1,0:T(8,128)(2,1)S(1)} %collective-permute-done.20.rest_2_), channel_id=1, source_target_pairs={{0,4},{4,8},{8,12},{12,0},{1,5},{5,9},{9,13},{13,1},{2,6},{6,10},{... | collective-permute-start | bytes 1376264 | tf_op jit(solution)/shard_map/ppermute | solution.py:24
  233.4 41.5 %collective-permute-start.18 = (bf16[384,1024]{1,0:T(8,128)(2,1)S(1)}, bf16[384,1024]{1,0:T(8,128)(2,1)S(1)}, u32[]{:S(2)}, u32[]{:S(2)}) collective-permute-start(bf16[384,1024]{1,0:T(8,128)(2,1)S(1)} %collective-permute-done.17.rest_2_), channel_id=1, source_target_pairs={{0,4},{4,8},{8,12},{12,0},{1,5},{5,9},{9,13},{13,1},{2,6},{6,10},{... | collective-permute-start | bytes 2359304 | tf_op jit(solution)/shard_map/ppermute | solution.py:24
  302.2 4.3 %collective-permute-start.27 = (f32[16,1024]{1,0:T(8,128)S(1)}, f32[16,1024]{1,0:T(8,128)S(1)}, u32[]{:S(2)}, u32[]{:S(2)}) collective-permute-start(f32[16,1024]{1,0:T(8,128)S(1)} %reshape.90), channel_id=1, source_target_pairs={{0,16},{16,0},{1,17},{17,1},{2,18},{18,2},{3,19},{19,3},{4,20},{20... | collective-permute-start | bytes 196616 | tf_op jit(solution)/shard_map/ppermute | solution.py:24
  306.6 4.3 %collective-permute-start.28 = (f32[16,1024]{1,0:T(8,128)S(1)}, f32[16,1024]{1,0:T(8,128)S(1)}, u32[]{:S(2)}, u32[]{:S(2)}) collective-permute-start(f32[16,1024]{1,0:T(8,128)S(1)} %add.237), channel_id=1, source_target_pairs={{0,2},{2,0},{1,3},{3,1},{4,6},{6,4},{5,7},{7,5},{8,10},{10,8},{9,1... | collective-permute-start | bytes 196616 | tf_op jit(solution)/shard_map/ppermute | solution.py:24
  312.3 6.2 %collective-permute-start.30 = (f32[16,1024]{1,0:T(8,128)S(1)}, f32[16,1024]{1,0:T(8,128)S(1)}, u32[]{:S(2)}, u32[]{:S(2)}) collective-permute-start(f32[16,1024]{1,0:T(8,128)S(1)} %get-tuple-element.46), channel_id=1, source_target_pairs={{0,4},{4,8},{8,12},{12,0},{1,5},{5,9},{9,13},{13,1},{2,6},{6,10},{... | collective-permute-start | bytes 196616 | tf_op jit(solution)/shard_map/ppermute | solution.py:24
  312.6 8.5 %collective-permute-start.31 = (f32[16,1024]{1,0:T(8,128)S(1)}, f32[16,1024]{1,0:T(8,128)S(1)}, u32[]{:S(2)}, u32[]{:S(2)}) collective-permute-start(f32[16,1024]{1,0:T(8,128)S(1)} %get-tuple-element.46), channel_id=1, source_target_pairs={{0,8},{4,12},{8,0},{12,4},{1,9},{5,13},{9,1},{13,5},{2,10},{6,14},... | collective-permute-start | bytes 196616 | tf_op jit(solution)/shard_map/ppermute | solution.py:24
  315.5 5.7 %collective-permute-start.32 = (f32[16,1024]{1,0:T(8,128)S(1)}, f32[16,1024]{1,0:T(8,128)S(1)}, u32[]{:S(2)}, u32[]{:S(2)}) collective-permute-start(f32[16,1024]{1,0:T(8,128)S(1)} %get-tuple-element.46), channel_id=1, source_target_pairs={{0,12},{4,0},{8,4},{12,8},{1,13},{5,1},{9,5},{13,9},{2,14},{6,2},{... | collective-permute-start | bytes 196616 | tf_op jit(solution)/shard_map/ppermute | solution.py:24
  (15 other events, 450.0 us)

commit v3 on v2

--- a/solution.py
+++ b/solution.py
@@ -8,7 +8,7 @@
 from jax.sharding import PartitionSpec as P
 
 HIGHEST = lax.Precision.HIGHEST
-CHUNK = 384
+LAST = 256
 
 
 def shifted(x, axes, sizes, shift):
@@ -48,23 +48,9 @@
     return jnp.sum(gather_in_order(x[None], axis, 0), axis=0)
 
 
-def chunk_kernel(n, me_ref, cot_ref, gate_ref, factor_ref, before_ref, *rest):
-    slots, (after_ref, weight, sems) = rest[:n], rest[n:]
-    columns = slots[0].shape[1]
-
-    @pl.when(pl.program_id(0) == 0)
-    def _():
-        copies = []
-        for r in range(n):
-            at = pl.multiple_of(lax.rem(me_ref[0] + (n - r), n) * columns, columns)
-            copies.append(pltpu.make_async_copy(slots[r], weight.at[:, pl.ds(at, columns)], sems.at[r]))
-        for copy in copies:
-            copy.start()
-        for copy in copies:
-            copy.wait()
-
+def chunk_kernel(contract, cot_ref, gate_ref, factor_ref, before_ref, weight_ref, after_ref):
     hidden = lax.dot_general(
-        cot_ref[...], weight[...], (((1,), (1,)), ((), ())), preferred_element_type=jnp.float32
+        cot_ref[...], weight_ref[...], (((1,), (contract,)), ((), ())), preferred_element_type=jnp.float32
     )
     gate = gate_ref[...].astype(jnp.float32)
     up_grad = (hidden * (gate / (1.0 + jnp.exp(-gate)))).astype(jnp.bfloat16)
@@ -73,36 +59,29 @@
     )
 
 
-def add_chunk(me, cot, gate, factor, before, slots, tile):
+def add_chunk(cot, gate, factor, before, weight, contract, tile):
     tokens, depth = cot.shape
     height = gate.shape[1]
     rank = factor.shape[1]
-    n = len(slots)
     return pl.pallas_call(
-        functools.partial(chunk_kernel, n),
+        functools.partial(chunk_kernel, contract),
         out_shape=jax.ShapeDtypeStruct((tokens, rank), jnp.float32),
-        grid_spec=pltpu.PrefetchScalarGridSpec(
-            num_scalar_prefetch=1,
-            grid=(tokens // tile,),
-            in_specs=[
-                pl.BlockSpec((tile, depth), lambda i, me: (i, 0)),
-                pl.BlockSpec((tile, height), lambda i, me: (i, 0)),
-                pl.BlockSpec((height, rank), lambda i, me: (0, 0)),
-                pl.BlockSpec((tile, rank), lambda i, me: (i, 0)),
-            ] + [pl.BlockSpec(memory_space=pl.ANY)] * n,
-            out_specs=pl.BlockSpec((tile, rank), lambda i, me: (i, 0)),
-            scratch_shapes=[
-                pltpu.VMEM((height, depth), jnp.bfloat16),
-                pltpu.SemaphoreType.DMA((n,)),
-            ],
-        ),
-        compiler_params=pltpu.CompilerParams(vmem_limit_bytes=40 * 1024 * 1024),
+        grid=(tokens // tile,),
+        in_specs=[
+            pl.BlockSpec((tile, depth), lambda i: (i, 0)),
+            pl.BlockSpec((tile, height), lambda i: (i, 0)),
+            pl.BlockSpec((height, rank), lambda i: (0, 0)),
+            pl.BlockSpec((tile, rank), lambda i: (i, 0)),
+            pl.BlockSpec(weight.shape, lambda i: (0, 0)),
+        ],
+        out_specs=pl.BlockSpec((tile, rank), lambda i: (i, 0)),
+        compiler_params=pltpu.CompilerParams(vmem_limit_bytes=44 * 1024 * 1024),
         cost_estimate=pl.CostEstimate(
             flops=2 * tokens * depth * height,
             bytes_accessed=2 * (tokens * depth + height * depth + tokens * height),
             transcendentals=tokens * height,
         ),
-    )(me, cot, gate, factor, before, *slots)
+    )(cot, gate, factor, before, weight)
 
 
 def on_device(inputs, cotangent, gate_pre, down_weight, proj_in, proj_out, doc_lens, queries):
@@ -120,20 +99,12 @@
     sizes = (n_groups, n_seq)
     mine = group * n_seq + half
 
-    bounds = list(range(0, part, CHUNK)) + [part]
-    spans = list(zip(bounds[:-1], bounds[1:]))
-    chunks = [
-        [lax.dynamic_slice_in_dim(down_weight, mine * part + low, high - low, 0)] for low, high in spans
-    ]
-    sent = []
-    for first in range(0, len(chunks), 2):
-        for _ in range(n_dp - 1):
-            for slots in chunks[first:first + 2]:
-                block = slots[-1]
-                if len(sent) >= 2:
-                    block, sent[-2][-1] = lax.optimization_barrier((block, sent[-2][-1]))
-                slots.append(shifted(block, "dp", (n_dp,), (1,)))
-                sent.append(slots)
+    early = lax.all_gather(
+        lax.dynamic_slice_in_dim(down_weight, mine * part + LAST, part - LAST, 0), "dp", axis=1, tiled=True
+    )
+    piece = lax.dynamic_slice_in_dim(down_weight, mine * part, LAST, 0).T
+    piece, early = lax.optimization_barrier((piece, early))
+    late = lax.all_gather(piece, "dp", axis=0, tiled=True)
 
     order = [(dg, ds) for dg in range(n_groups) for ds in range(n_seq)]
     cots = []
@@ -150,18 +121,18 @@
         columns = lax.dynamic_slice_in_dim(gate_pre, to * part, part, 1)
         gates.append(columns if dg == ds == 0 else shifted(columns, pair, sizes, (dg, ds)))
 
-    right = sum_over(jnp.dot(inputs, proj_in, preferred_element_type=jnp.float32), "tensor")
+    cot = jnp.concatenate(cots, axis=0)
+    gate = jnp.concatenate(gates, axis=0)
+    right_part = jnp.dot(inputs, proj_in, preferred_element_type=jnp.float32)
+    right_part, doc_lens, cot, gate = lax.optimization_barrier((right_part, doc_lens, cot, gate))
+    right = sum_over(right_part, "tensor")
     rights = [right if dg == ds == 0 else shifted(right, pair, sizes, (dg, ds)) for dg, ds in order]
     lens = [doc_lens if dg == 0 else shifted(doc_lens, "groups", (n_groups,), (dg,)) for dg in range(n_groups)]
 
-    cot = jnp.concatenate(cots, axis=0)
-    gate = jnp.concatenate(gates, axis=0)
     out_factor = lax.dynamic_slice_in_dim(proj_out, mine * part, part, 0)
-    me = jnp.reshape(stage, (1,)).astype(jnp.int32)
-
     left = jnp.zeros((n_groups * n_seq * rows, rank), jnp.float32)
-    for slots, (low, high) in zip(chunks, spans):
-        left = add_chunk(me, cot, gate[:, low:high], out_factor[low:high], left, slots, rows)
+    left = add_chunk(cot, gate[:, LAST:], out_factor[LAST:], left, early, 1, rows)
+    left = add_chunk(cot, gate[:, :LAST], out_factor[:LAST], left, late, 0, rows)
 
     parts = []
     for dg in range(n_groups):

time: 342 us -> 300 us (0.88)
  waiting for transfers between devices: 150 us -> 105 us
  Pallas kernels: 53.2 us -> 38.2 us
  local copies, waits for them, and re-layouts: 54.6 us -> 69.6 us
  between operations: 1.9 us -> 15.1 us
  starting transfers between devices: 31.5 us -> 20.5 us
    ppermute x33 -> x21, waiting for transfers between devices: 150 us -> 89.5 us  [shifted(): return lax.ppermute(x, axes, pairs)]
    pallas_call x4 -> x2, Pallas kernels: 53.2 us -> 38.2 us  [add_chunk(): pl.pallas_call(functools.partial(chunk_kernel, contract), out_shape=jax.S...]
    all_gather x0 -> x2, waiting for transfers between devices: none -> 15 us  [the longest x1 15 us: on_device(): lax.all_gather(lax.dynamic_slice_in_dim(down_weight, mine * part + LAST,...]
    ppermute x33 -> x21, starting transfers between devices: 31.5 us -> 20.4 us  [shifted(): return lax.ppermute(x, axes, pairs)]
    slice x2 -> x4, local copies, waits for them, and re-layouts: 1.73 us -> 7.95 us  [the longest x1 4.87 us: on_device(): gate[:, LAST:]]
    another operation x6, local copies, waits for them, and re-layouts: 4.1 us -> 8.55 us
    concatenate x1, other arithmetic: 9.63 us -> 13.7 us  [on_device(): cot = jnp.concatenate(cots, axis=0)]
    unnamed x35 -> x26, local copies, waits for them, and re-layouts: 11.7 us -> 14.3 us
  transfers between devices with their start and end apart: 33 -> 23, of which waited for: 15 -> 11; matrix products, arithmetic and copies ran while one was open for 24% -> 31% of each run, Pallas kernels for 16% -> 13%
where the time goes in v3:
time: 300 us; the launch traced here: 298 us
  waiting for transfers between devices  105 us (35%)
  local copies, waits for them, and re-layouts  69.6 us (23%)
  Pallas kernels  38.2 us (13%)
  other arithmetic  36.3 us (12%)
  starting transfers between devices  20.5 us (7%)
  between operations  15.1 us (5%)
  matrix products  14.2 us (5%)
    ppermute x21, waiting for transfers between devices, shifted(): return lax.ppermute(x, axes, pairs)  89.5 us
    pallas_call x2, Pallas kernels, add_chunk(): pl.pallas_call(functools.partial(chunk_kernel, contract), out_shape=jax.S...  38.2 us
    ppermute x21, starting transfers between devices, shifted(): return lax.ppermute(x, axes, pairs)  20.4 us
    dynamic_update_slice x11, local copies, waits for them, and re-layouts, in_order(): out = lax.dynamic_update_slice_in_dim(out, piece, (me - r) % n * size, dim)  17.6 us
    all_gather x1, waiting for transfers between devices, on_device(): lax.all_gather(lax.dynamic_slice_in_dim(down_weight, mine * part + LAST,...  15 us
    unnamed x26, local copies, waits for them, and re-layouts  14.3 us
    concatenate x1, other arithmetic, on_device(): cot = jnp.concatenate(cots, axis=0)  13.7 us
    another operation x6, local copies, waits for them, and re-layouts  8.55 us
  transfers between devices with their start and end apart: 23, of which 11 were waited for; matrix products, arithmetic and copies ran while one was open for 31% of the time, Pallas kernels for 13%

profile of v3, /device:TPU:0, one launch (start us, length us, event | category | flops | bytes accessed | tf_op | source)
XLA Modules:
  0.0 298.5 jit_solution(1958684952295025163)
XLA Ops:
  7.2 3.4 %constant_dynamic-slice_fusion.1 = bf16[1120,1024]{1,0:T(8,128)(2,1)} fusion(bf16[5504,1024]{1,0:T(8,128)(2,1)} %param.11, s32[]{:T(128)S(6)} %select_n.136), kind=kLoop, calls=%fused_computation.49 | loop fusion | bytes 4587524 | tf_op jit(solution)/shard_map/dynamic_slice | solution.py:103
  10.7 3.0 %collective-permute-start.3 = (bf16[512,2048]{1,0:T(8,128)(2,1)}, bf16[512,2048]{1,0:T(8,128)(2,1)}, u32[]{:S(2)}, u32[]{:S(2)}) collective-permute-start(bf16[512,2048]{1,0:T(8,128)(2,1)} %param.9), channel_id=1, source_target_pairs={{0,16},{16,0},{1,17},{17,1},{2,18},{18,2},{3,19},{19,3},{4,20},{20... | collective-permute-start | bytes 6291464 | tf_op jit(solution)/shard_map/ppermute | solution.py:24
  13.7 8.1 %constant_dynamic-slice_fusion.7 = (bf16[512,1376]{1,0:T(8,128)(2,1)}, bf16[512,1376]{1,0:T(8,128)(2,1)}, bf16[512,1376]{1,0:T(8,128)(2,1)S(1)}, bf16[512,1376]{1,0:T(8,128)(2,1)}) fusion(bf16[512,5504]{1,0:T(8,128)(2,1)} %param.10, s32[]{:T(128)S(6)} %select_n.129, s32[]{:T(128)S(6)} %select_n.133, s32[]{:T(128)S(6)} %select_n.131, s32[]{:T(128)S(6)} %select_n.134), kind=kLoop, calls=%fused_computation.55 | loop fusion | bytes 11272208 | tf_op jit(solution)/shard_map/dynamic_slice | solution.py:121
  21.9 2.7 copy.64
  26.0 34.5 %collective-permute-done.3 = bf16[512,2048]{1,0:T(8,128)(2,1)} collective-permute-done((bf16[512,2048]{1,0:T(8,128)(2,1)}, bf16[512,2048]{1,0:T(8,128)(2,1)}, u32[]{:S(2)}, u32[]{:S(2)}) %collective-permute-start.3) | collective-permute-done | bytes 2097184 | tf_op jit(solution)/shard_map/ppermute | solution.py:24
  62.5 2.5 copy.63
  69.1 21.2 %collective-permute-done.9 = bf16[512,1376]{0,1:T(8,128)(2,1)} collective-permute-done((bf16[512,1376]{0,1:T(8,128)(2,1)}, bf16[512,1376]{0,1:T(8,128)(2,1)}, u32[]{:S(2)}, u32[]{:S(2)}) %collective-permute-start.9) | collective-permute-done | bytes 1409056 | tf_op jit(solution)/shard_map/ppermute | solution.py:24
  94.1 3.1 %fusion.33 = f32[512,32]{0,1:T(8,128)} fusion(bf16[512,2048]{1,0:T(8,128)(2,1)} %param.8, bf16[2048,32]{0,1:T(8,128)(2,1)} %param.12), kind=kOutput, calls=%fused_computation.72 | convolution fusion | flops 67108864 | bytes 2293760 | tf_op jit(solution)/shard_map/dot_general | solution.py:126
  97.2 22.8 %collective-permute-done.8 = bf16[512,1376]{0,1:T(8,128)(2,1)} collective-permute-done((bf16[512,1376]{0,1:T(8,128)(2,1)}, bf16[512,1376]{0,1:T(8,128)(2,1)}, u32[]{:S(2)}, u32[]{:S(2)}) %collective-permute-start.8) | collective-permute-done | bytes 1409056 | tf_op jit(solution)/shard_map/ppermute | solution.py:24
  120.1 2.6 broadcast.100.clone.3
  124.1 2.6 copy.50
  126.6 2.5 copy.49
  129.1 2.5 copy.48
  132.3 6.7 %pad_maximum_fusion.1 = bf16[2048,1376]{1,0:T(8,128)(2,1)} fusion(bf16[512,1376]{1,0:T(8,128)(2,1)} %copy.50, bf16[512,1376]{1,0:T(8,128)(2,1)} %copy.49, bf16[512,1376]{1,0:T(8,128)(2,1)} %copy.48, bf16[512,1376]{1,0:T(8,128)(2,1)} %get-tuple-element.19), kind=kLoop, calls=%fused_computation.1 | loop fusion | flops 22544384 | bytes 11272192 | tf_op jit(solution)/shard_map/concatenate | solution.py:125
  141.3 2.5 broadcast.100.clone.2
  143.8 3.1 %constant_dynamic-update-slice_fusion.9 = bf16[512,4096]{1,0:T(8,128)(2,1)} fusion(bf16[512,4096]{1,0:T(8,128)(2,1)} %broadcast.100.clone.2, bf16[512,2048]{1,0:T(8,128)(2,1)} %collective-permute-done.1, s32[]{:T(128)S(6)} %select_n.124), kind=kLoop, calls=%fused_computation.61 | loop fusion | bytes 4194308 | tf_op jit(solution)/shard_map/dynamic_update_slice | solution.py:35
  147.0 3.2 %constant_dynamic-update-slice_fusion.10 = bf16[512,4096]{1,0:T(8,128)(2,1)} fusion(bf16[512,4096]{1,0:T(8,128)(2,1)} %constant_dynamic-update-slice_fusion.11, bf16[512,2048]{1,0:T(8,128)(2,1)} %collective-permute-done, s32[]{:T(128)S(6)} %select_n.126), kind=kLoop, calls=%fused_computation.62 | loop fusion | bytes 4194308 | tf_op jit(solution)/shard_map/dynamic_update_slice | solution.py:35
  152.0 2.8 broadcast.100.clone
  154.9 3.1 %constant_dynamic-update-slice_fusion.5 = bf16[512,4096]{1,0:T(8,128)(2,1)} fusion(bf16[512,4096]{1,0:T(8,128)(2,1)} %broadcast.100.clone, bf16[512,2048]{1,0:T(8,128)(2,1)} %collective-permute-done.5, s32[]{:T(128)S(6)} %select_n.124), kind=kLoop, calls=%fused_computation.57 | loop fusion | bytes 4194308 | tf_op jit(solution)/shard_map/dynamic_update_slice | solution.py:35
  160.9 15.0 %all-gather.3.cloned.1.call-done.weight_ref = bf16[1120,4096]{1,0:T(8,128)(2,1)} async-done(((bf16[1120,1024]{1,0:T(8,128)(2,1)}), bf16[1120,4096]{1,0:T(8,128)(2,1)}) %all-gather.3.cloned.1.call-update) | async-done | bytes 9175056 | tf_op jit(solution)/shard_map/all_gather | solution.py:102
  176.0 13.7 %pad_maximum_fusion.cot_ref = bf16[2048,4096]{1,0:T(8,128)(2,1)} fusion(bf16[512,4096]{1,0:T(8,128)(2,1)} %constant_dynamic-update-slice_fusion.4, bf16[512,4096]{1,0:T(8,128)(2,1)} %copy-done.5, bf16[512,4096]{1,0:T(8,128)(2,1)} %constant_dynamic-update-slice_fusion.8, bf16[512,4096]{1,0:T(8,128)(2,1)} %constant_dynamic-update-slice_fusion.10), kind=kLoop, calls=%fused_computation | loop fusion | flops 67108864 | bytes 33554432 | tf_op jit(solution)/shard_map/concatenate | solution.py:124
  191.0 4.9 %slice.38.gate_ref = bf16[2048,1120]{1,0:T(8,128)(2,1)} slice(bf16[2048,1376]{1,0:T(8,128)(2,1)} %pad_maximum_fusion.1), slice={[0:2048], [256:1376]} | slice | bytes 9175040 | tf_op jit(solution)/shard_map/slice | solution.py:134
  205.9 2.3 copy-done.1
  208.3 29.2 %shard_map.103.before_ref = f32[2048,32]{1,0:T(8,128)S(1)} custom-call(bf16[2048,4096]{1,0:T(8,128)(2,1)} %pad_maximum_fusion.cot_ref, bf16[2048,1120]{1,0:T(8,128)(2,1)S(1)} %copy-done.1, bf16[1120,32]{1,0:T(8,128)(2,1)S(1)} %copy.67.factor_ref, f32[2048,32]{1,0:T(8,128)S(1)} %broadcast_in_dim.5.before_ref, ...), custom_call_target="tpu_custom_call" | custom-call | flops 18790481920 | bytes 30539776 | tf_op jit(solution)/shard_map/pallas_call | solution.py:66
  241.3 8.9 %shard_map.104 = f32[2048,32]{1,0:T(8,128)S(1)} custom-call(bf16[2048,4096]{1,0:T(8,128)(2,1)} %pad_maximum_fusion.cot_ref, bf16[2048,256]{1,0:T(8,128)(2,1)S(1)} %slice.36.gate_ref, bf16[256,32]{1,0:T(8,128)(2,1)S(1)} %copy.66.factor_ref, f32[2048,32]{1,0:T(8,128)S(1)} %copy-done.4, bf16[4096,256]{1,0:T(8,128)(2,1)S(1)} %copy-done.2), custom_call_target="tpu_custom_call" | custom-call | flops 4294967296 | bytes 19922944 | tf_op jit(solution)/shard_map/pallas_call | solution.py:66
  250.5 2.7 fusion.7
  254.3 2.6 fusion.4
  259.5 2.8 collective-permute-done.16
  264.9 2.7 collective-permute-start.20
  267.5 2.9 collective-permute-done.18
  278.4 5.8 %cholesky.17 = f32[64,64]{1,0:T(8,128)S(1)} custom-call(f32[64,64]{1,0:T(8,128)S(1)} %fusion.27), custom_call_target="Cholesky" | custom-call | tf_op jit(solution)/shard_map/jit(cholesky)/cholesky | solution.py:171
  285.5 4.9 %custom-call.10 = f32[1,64,64]{1,2,0:T(8,128)S(1)} custom-call(f32[1,64,64]{2,1,0:T(8,128)S(1)} %fusion.21), custom_call_target="InvertDiagBlocksLowerTriangular" | custom-call | tf_op jit(solution)/shard_map/jit(_cho_solve)/triangular_solve | solution.py:173
  (113 shorter events, 51.8 us)
Async XLA Ops:
  7.2 269.0 %copy-start = (f32[512,1024]{1,0:T(8,128)S(1)}, f32[512,1024]{1,0:T(8,128)}, u32[]{:S(2)}) copy-start(f32[512,1024]{1,0:T(8,128)} %param.15) | copy-start | bytes 6291460
  7.2 168.8 %all-gather.3.cloned.1.call-start = ((), (), s32[]{:S(2)}) async-start(), calls=%async_computation | async-start | bytes 11468800 | tf_op jit(solution)/shard_map/all_gather | solution.py:102
  10.6 227.8 %all-gather.5.cloned.1.call-start = ((), (), s32[]{:S(2)}) async-start(), calls=%async_computation.1 | async-start | bytes 2621440 | tf_op jit(solution)/shard_map/all_gather | solution.py:107
  10.7 49.8 %collective-permute-start.3 = (bf16[512,2048]{1,0:T(8,128)(2,1)}, bf16[512,2048]{1,0:T(8,128)(2,1)}, u32[]{:S(2)}, u32[]{:S(2)}) collective-permute-start(bf16[512,2048]{1,0:T(8,128)(2,1)} %param.9), channel_id=1, source_target_pairs={{0,16},{16,0},{1,17},{17,1},{2,18},{18,2},{3,19},{19,3},{4,20},{20... | collective-permute-start | bytes 6291464 | tf_op jit(solution)/shard_map/ppermute | solution.py:24
  24.6 65.7 %collective-permute-start.9 = (bf16[512,1376]{0,1:T(8,128)(2,1)}, bf16[512,1376]{0,1:T(8,128)(2,1)}, u32[]{:S(2)}, u32[]{:S(2)}) collective-permute-start(bf16[512,1376]{0,1:T(8,128)(2,1)} %copy.64), channel_id=1, source_target_pairs={{0,17},{1,16},{16,1},{17,0},{2,19},{3,18},{18,3},{19,2},{4,21},{5,... | collective-permute-start | bytes 4227080 | tf_op jit(solution)/shard_map/ppermute | solution.py:24
  24.6 107.1 %collective-permute-start = (bf16[512,2048]{1,0:T(8,128)(2,1)}, bf16[512,2048]{1,0:T(8,128)(2,1)}, u32[]{:S(2)}, u32[]{:S(2)}) collective-permute-start(bf16[512,2048]{1,0:T(8,128)(2,1)} %param.9), channel_id=1, source_target_pairs={{0,2},{2,0},{1,3},{3,1},{4,6},{6,4},{5,7},{7,5},{8,10},{10,8},{9,1... | collective-permute-start | bytes 6291464 | tf_op jit(solution)/shard_map/ppermute | solution.py:24
  60.5 71.7 %collective-permute-start.4 = (bf16[512,2048]{1,0:T(8,128)(2,1)}, bf16[512,2048]{1,0:T(8,128)(2,1)}, u32[]{:S(2)}, u32[]{:S(2)}) collective-permute-start(bf16[512,2048]{1,0:T(8,128)(2,1)} %collective-permute-done.3), channel_id=1, source_target_pairs={{0,2},{2,0},{1,3},{3,1},{4,6},{6,4},{5,7},{7,5},{8,10},{10,8},{9,1... | collective-permute-start | bytes 6291464 | tf_op jit(solution)/shard_map/ppermute | solution.py:24
  65.1 55.0 %collective-permute-start.8 = (bf16[512,1376]{0,1:T(8,128)(2,1)}, bf16[512,1376]{0,1:T(8,128)(2,1)}, u32[]{:S(2)}, u32[]{:S(2)}) collective-permute-start(bf16[512,1376]{0,1:T(8,128)(2,1)} %copy.63), channel_id=1, source_target_pairs={{0,16},{1,17},{16,0},{17,1},{2,18},{3,19},{18,2},{19,3},{4,20},{5,... | collective-permute-start | bytes 4227080 | tf_op jit(solution)/shard_map/ppermute | solution.py:24
  68.1 61.0 %collective-permute-start.7 = (bf16[512,1376]{0,1:T(8,128)(2,1)}, bf16[512,1376]{0,1:T(8,128)(2,1)}, u32[]{:S(2)}, u32[]{:S(2)}) collective-permute-start(bf16[512,1376]{0,1:T(8,128)(2,1)} %copy.62), channel_id=1, source_target_pairs={{0,1},{1,0},{16,17},{17,16},{2,3},{3,2},{18,19},{19,18},{4,5},{5,4... | collective-permute-start | bytes 4227080 | tf_op jit(solution)/shard_map/ppermute | solution.py:24
  90.3 51.1 %collective-permute-start.1 = (bf16[512,2048]{1,0:T(8,128)(2,1)}, bf16[512,2048]{1,0:T(8,128)(2,1)}, u32[]{:S(2)}, u32[]{:S(2)}) collective-permute-start(bf16[512,2048]{1,0:T(8,128)(2,1)} %param.9), channel_id=1, source_target_pairs={{0,1},{1,0},{2,3},{3,2},{4,5},{5,4},{6,7},{7,6},{8,9},{9,8},{10,11... | collective-permute-start | bytes 6291464 | tf_op jit(solution)/shard_map/ppermute | solution.py:24
  94.1 28.5 %copy-start.6 = (bf16[512,2048]{1,0:T(8,128)(2,1)S(1)}, bf16[512,2048]{1,0:T(8,128)(2,1)}, u32[]{:S(2)}) copy-start(bf16[512,2048]{1,0:T(8,128)(2,1)} %param.9) | copy-start | bytes 6291460
  120.1 32.0 %collective-permute-start.5 = (bf16[512,2048]{1,0:T(8,128)(2,1)}, bf16[512,2048]{1,0:T(8,128)(2,1)}, u32[]{:S(2)}, u32[]{:S(2)}) collective-permute-start(bf16[512,2048]{1,0:T(8,128)(2,1)} %collective-permute-done.3), channel_id=1, source_target_pairs={{0,1},{1,0},{2,3},{3,2},{4,5},{5,4},{6,7},{7,6},{8,9},{9,8},{10,11... | collective-permute-start | bytes 6291464 | tf_op jit(solution)/shard_map/ppermute | solution.py:24
  131.7 26.3 %collective-permute-start.2 = (bf16[512,2048]{1,0:T(8,128)(2,1)}, bf16[512,2048]{1,0:T(8,128)(2,1)S(1)}, u32[]{:S(2)}, u32[]{:S(2)}) collective-permute-start(bf16[512,2048]{1,0:T(8,128)(2,1)} %collective-permute-done), channel_id=1, source_target_pairs={{0,1},{1,0},{2,3},{3,2},{4,5},{5,4},{6,7},{7,6},{8,9},{9,8},{10,11... | collective-permute-start | bytes 6291464 | tf_op jit(solution)/shard_map/ppermute | solution.py:24
  132.2 27.3 %collective-permute-start.6 = (bf16[512,2048]{1,0:T(8,128)(2,1)}, bf16[512,2048]{1,0:T(8,128)(2,1)S(1)}, u32[]{:S(2)}, u32[]{:S(2)}) collective-permute-start(bf16[512,2048]{1,0:T(8,128)(2,1)} %collective-permute-done.4), channel_id=1, source_target_pairs={{0,1},{1,0},{2,3},{3,2},{4,5},{5,4},{6,7},{7,6},{8,9},{9,8},{10,11... | collective-permute-start | bytes 6291464 | tf_op jit(solution)/shard_map/ppermute | solution.py:24
  152.0 6.0 %copy-start.5 = (bf16[512,4096]{1,0:T(8,128)(2,1)}, bf16[512,4096]{1,0:T(8,128)(2,1)S(1)}, u32[]{:S(2)}) copy-start(bf16[512,4096]{1,0:T(8,128)(2,1)S(1)} %constant_dynamic-update-slice_fusion.6) | copy-start | bytes 12582916
  191.0 4.9 %copy-start.9 = (s32[1,16]{1,0:T(1,128)S(1)}, s32[1,16]{1,0:T(1,128)}, u32[]{:S(2)}) copy-start(s32[1,16]{1,0:T(1,128)} %param.14) | copy-start | bytes 196
  195.8 3.5 %collective-permute-start.12 = (s32[1,16]{1,0:T(1,128)S(1)}, s32[1,16]{1,0:T(1,128)S(1)}, u32[]{:S(2)}, u32[]{:S(2)}) collective-permute-start(s32[1,16]{1,0:T(1,128)S(1)} %copy-done.9), channel_id=1, source_target_pairs={{0,16},{16,0},{1,17},{17,1},{2,18},{18,2},{3,19},{19,3},{4,20},{20... | collective-permute-start | bytes 200 | tf_op jit(solution)/shard_map/ppermute | solution.py:24
  197.6 4.6 %collective-permute-start.10 = (f32[512,32]{0,1:T(8,128)}, f32[512,32]{0,1:T(8,128)}, u32[]{:S(2)}, u32[]{:S(2)}) collective-permute-start(f32[512,32]{0,1:T(8,128)} %fusion.33), channel_id=1, source_target_pairs={{0,2},{2,0},{1,3},{3,1},{4,6},{6,4},{5,7},{7,5},{8,10},{10,8},{9,1... | collective-permute-start | bytes 196616 | tf_op jit(solution)/shard_map/ppermute | solution.py:24
  203.7 50.6 %collective-permute-start.11 = (f32[512,32]{0,1:T(8,128)}, f32[512,32]{0,1:T(8,128)}, u32[]{:S(2)}, u32[]{:S(2)}) collective-permute-start(f32[512,32]{0,1:T(8,128)} %add.216), channel_id=1, source_target_pairs={{0,1},{1,0},{16,17},{17,16},{2,3},{3,2},{18,19},{19,18},{4,5},{5,4... | collective-permute-start | bytes 196616 | tf_op jit(solution)/shard_map/ppermute | solution.py:24
  203.7 46.8 %collective-permute-start.14 = (f32[512,32]{0,1:T(8,128)}, f32[512,32]{0,1:T(8,128)}, u32[]{:S(2)}, u32[]{:S(2)}) collective-permute-start(f32[512,32]{0,1:T(8,128)} %add.216), channel_id=1, source_target_pairs={{0,17},{1,16},{16,1},{17,0},{2,19},{3,18},{18,3},{19,2},{4,21},{5,... | collective-permute-start | bytes 196616 | tf_op jit(solution)/shard_map/ppermute | solution.py:24
  204.4 46.1 %collective-permute-start.13 = (f32[512,32]{0,1:T(8,128)}, f32[512,32]{0,1:T(8,128)}, u32[]{:S(2)}, u32[]{:S(2)}) collective-permute-start(f32[512,32]{0,1:T(8,128)} %add.216), channel_id=1, source_target_pairs={{0,16},{1,17},{16,0},{17,1},{2,18},{3,19},{18,2},{19,3},{4,20},{5,... | collective-permute-start | bytes 196616 | tf_op jit(solution)/shard_map/ppermute | solution.py:24
  205.9 2.4 copy-start.1
  238.5 1.6 copy-start.2
  240.1 1.2 copy-start.4
  250.2 4.0 %copy-start.7 = (f32[1024,16]{0,1:T(8,128)S(1)}, f32[1024,16]{0,1:T(8,128)}, u32[]{:S(2)}) copy-start(f32[1024,16]{0,1:T(8,128)} %fusion.19) | copy-start | bytes 196612
  253.6 4.3 %collective-permute-start.15 = (f32[16,1024]{1,0:T(8,128)S(1)}, f32[16,1024]{1,0:T(8,128)S(1)}, u32[]{:S(2)}, u32[]{:S(2)}) collective-permute-start(f32[16,1024]{1,0:T(8,128)S(1)} %reshape.86), channel_id=1, source_target_pairs={{0,16},{16,0},{1,17},{17,1},{2,18},{18,2},{3,19},{19,3},{4,20},{20... | collective-permute-start | bytes 196616 | tf_op jit(solution)/shard_map/ppermute | solution.py:24
  257.9 4.3 %collective-permute-start.16 = (f32[16,1024]{1,0:T(8,128)S(1)}, f32[16,1024]{1,0:T(8,128)S(1)}, u32[]{:S(2)}, u32[]{:S(2)}) collective-permute-start(f32[16,1024]{1,0:T(8,128)S(1)} %add.217), channel_id=1, source_target_pairs={{0,2},{2,0},{1,3},{3,1},{4,6},{6,4},{5,7},{7,5},{8,10},{10,8},{9,1... | collective-permute-start | bytes 196616 | tf_op jit(solution)/shard_map/ppermute | solution.py:24
  262.3 1.3 collective-permute-start.17
  263.6 28.0 %copy-start.8 = (f32[16,1024]{1,0:T(8,128)}, f32[16,1024]{1,0:T(8,128)S(1)}, u32[]{:S(2)}) copy-start(f32[16,1024]{1,0:T(8,128)S(1)} %get-tuple-element.18) | copy-start | bytes 196612
  263.7 6.8 %collective-permute-start.18 = (f32[16,1024]{1,0:T(8,128)S(1)}, f32[16,1024]{1,0:T(8,128)S(1)}, u32[]{:S(2)}, u32[]{:S(2)}) collective-permute-start(f32[16,1024]{1,0:T(8,128)S(1)} %get-tuple-element.18), channel_id=1, source_target_pairs={{0,4},{4,8},{8,12},{12,0},{1,5},{5,9},{9,13},{13,1},{2,6},{6,10},{... | collective-permute-start | bytes 196616 | tf_op jit(solution)/shard_map/ppermute | solution.py:24
  263.7 8.6 %collective-permute-start.19 = (f32[16,1024]{1,0:T(8,128)S(1)}, f32[16,1024]{1,0:T(8,128)S(1)}, u32[]{:S(2)}, u32[]{:S(2)}) collective-permute-start(f32[16,1024]{1,0:T(8,128)S(1)} %get-tuple-element.18), channel_id=1, source_target_pairs={{0,8},{4,12},{8,0},{12,4},{1,9},{5,13},{9,1},{13,5},{2,10},{6,14},... | collective-permute-start | bytes 196616 | tf_op jit(solution)/shard_map/ppermute | solution.py:24
  264.9 7.5 %collective-permute-start.20 = (f32[16,1024]{1,0:T(8,128)S(1)}, f32[16,1024]{1,0:T(8,128)S(1)}, u32[]{:S(2)}, u32[]{:S(2)}) collective-permute-start(f32[16,1024]{1,0:T(8,128)S(1)} %get-tuple-element.18), channel_id=1, source_target_pairs={{0,12},{4,0},{8,4},{12,8},{1,13},{5,1},{9,5},{13,9},{2,14},{6,2},{... | collective-permute-start | bytes 196616 | tf_op jit(solution)/shard_map/ppermute | solution.py:24
  (1 other events, 1.0 us)
Sparse Core Ops, SparseCore 0:
  10.8 165.1 all-gather.2
  177.5 44.1 all-gather.4

commit v4 on v3

--- a/solution.py
+++ b/solution.py
@@ -48,40 +48,71 @@
     return jnp.sum(gather_in_order(x[None], axis, 0), axis=0)
 
 
-def chunk_kernel(contract, cot_ref, gate_ref, factor_ref, before_ref, weight_ref, after_ref):
-    hidden = lax.dot_general(
-        cot_ref[...], weight_ref[...], (((1,), (contract,)), ((), ())), preferred_element_type=jnp.float32
-    )
-    gate = gate_ref[...].astype(jnp.float32)
-    up_grad = (hidden * (gate / (1.0 + jnp.exp(-gate)))).astype(jnp.bfloat16)
-    after_ref[...] = before_ref[...] + jnp.dot(
-        up_grad, factor_ref[...], preferred_element_type=jnp.float32
-    )
-
-
-def add_chunk(cot, gate, factor, before, weight, contract, tile):
-    tokens, depth = cot.shape
-    height = gate.shape[1]
-    rank = factor.shape[1]
+def chunk_kernel(n_blocks, n_tensor, contract, skip, side_ref, *refs):
+    refs = list(refs)
+    cots = [refs[b * n_tensor:(b + 1) * n_tensor] for b in range(n_blocks)]
+    gates = refs[n_blocks * n_tensor:n_blocks * (n_tensor + 1)]
+    factor_ref, before_ref, weight_ref, after_ref, cot_buf, gate_buf, sems = refs[n_blocks * (n_tensor + 1):]
+    rows, columns = cots[0][0].shape
+    gate_width = gate_buf.shape[2]
+
+    def copies(b):
+        slot = b % 2
+        out = []
+        for r in range(n_tensor):
+            at = pl.multiple_of(lax.rem(side_ref[0] + (n_tensor - r), n_tensor) * columns, columns)
+            out.append(pltpu.make_async_copy(
+                cots[b][r], cot_buf.at[slot, :, pl.ds(at, columns)], sems.at[slot, r]
+            ))
+        source = gates[b] if gate_width == gates[b].shape[1] else gates[b].at[:, pl.ds(0, gate_width)]
+        out.append(pltpu.make_async_copy(source, gate_buf.at[slot], sems.at[slot, n_tensor]))
+        return out
+
+    for copy in copies(0):
+        copy.start()
+    for b in range(n_blocks):
+        if b + 1 < n_blocks:
+            for copy in copies(b + 1):
+                copy.start()
+        for copy in copies(b):
+            copy.wait()
+        slot = b % 2
+        hidden = lax.dot_general(
+            cot_buf[slot], weight_ref[...], (((1,), (contract,)), ((), ())),
+            preferred_element_type=jnp.float32,
+        )
+        gate = gate_buf[slot, :, skip:].astype(jnp.float32)
+        up_grad = (hidden * (gate / (1.0 + jnp.exp(-gate)))).astype(jnp.bfloat16)
+        after_ref[pl.ds(b * rows, rows), :] = before_ref[pl.ds(b * rows, rows), :] + jnp.dot(
+            up_grad, factor_ref[...], preferred_element_type=jnp.float32
+        )
+
+
+def add_chunk(side, cots, gates, skip, factor, before, weight, contract, limit):
+    n_blocks, n_tensor = len(cots), len(cots[0])
+    rows, columns = cots[0][0].shape
+    height, rank = factor.shape
+    tokens, depth = n_blocks * rows, n_tensor * columns
+    width = gates[0].shape[1] if skip else height
+    in_vmem = pl.BlockSpec(memory_space=pltpu.VMEM)
     return pl.pallas_call(
-        functools.partial(chunk_kernel, contract),
+        functools.partial(chunk_kernel, n_blocks, n_tensor, contract, skip),
         out_shape=jax.ShapeDtypeStruct((tokens, rank), jnp.float32),
-        grid=(tokens // tile,),
-        in_specs=[
-            pl.BlockSpec((tile, depth), lambda i: (i, 0)),
-            pl.BlockSpec((tile, height), lambda i: (i, 0)),
-            pl.BlockSpec((height, rank), lambda i: (0, 0)),
-            pl.BlockSpec((tile, rank), lambda i: (i, 0)),
-            pl.BlockSpec(weight.shape, lambda i: (0, 0)),
+        in_specs=[pl.BlockSpec(memory_space=pltpu.SMEM)]
+        + [pl.BlockSpec(memory_space=pl.ANY)] * (n_blocks * (n_tensor + 1)) + [in_vmem] * 3,
+        out_specs=in_vmem,
+        scratch_shapes=[
+            pltpu.VMEM((2, rows, depth), jnp.bfloat16),
+            pltpu.VMEM((2, rows, width), jnp.bfloat16),
+            pltpu.SemaphoreType.DMA((2, n_tensor + 1)),
         ],
-        out_specs=pl.BlockSpec((tile, rank), lambda i: (i, 0)),
-        compiler_params=pltpu.CompilerParams(vmem_limit_bytes=44 * 1024 * 1024),
+        compiler_params=pltpu.CompilerParams(vmem_limit_bytes=limit * 1024 * 1024),
         cost_estimate=pl.CostEstimate(
             flops=2 * tokens * depth * height,
             bytes_accessed=2 * (tokens * depth + height * depth + tokens * height),
             transcendentals=tokens * height,
         ),
-    )(cot, gate, factor, before, weight)
+    )(side, *[piece for pieces in cots for piece in pieces], *gates, factor, before, weight)
 
 
 def on_device(inputs, cotangent, gate_pre, down_weight, proj_in, proj_out, doc_lens, queries):
@@ -112,27 +143,24 @@
         own = cotangent if dg == 0 else shifted(cotangent, "groups", (n_groups,), (dg,))
         pieces = [own if r == 0 else shifted(own, "tensor", (n_tensor,), (r,)) for r in range(n_tensor)]
         for ds in range(n_seq):
-            cots.append(in_order(
-                pieces if ds == 0 else [shifted(x, "seq", (n_seq,), (ds,)) for x in pieces], "tensor", 1
-            ))
+            cots.append(pieces if ds == 0 else [shifted(x, "seq", (n_seq,), (ds,)) for x in pieces])
     gates = []
     for dg, ds in order:
         to = ((group + dg) % n_groups) * n_seq + (half + ds) % n_seq
         columns = lax.dynamic_slice_in_dim(gate_pre, to * part, part, 1)
         gates.append(columns if dg == ds == 0 else shifted(columns, pair, sizes, (dg, ds)))
 
-    cot = jnp.concatenate(cots, axis=0)
-    gate = jnp.concatenate(gates, axis=0)
     right_part = jnp.dot(inputs, proj_in, preferred_element_type=jnp.float32)
-    right_part, doc_lens, cot, gate = lax.optimization_barrier((right_part, doc_lens, cot, gate))
+    right_part, doc_lens, cots, gates = lax.optimization_barrier((right_part, doc_lens, cots, gates))
     right = sum_over(right_part, "tensor")
     rights = [right if dg == ds == 0 else shifted(right, pair, sizes, (dg, ds)) for dg, ds in order]
     lens = [doc_lens if dg == 0 else shifted(doc_lens, "groups", (n_groups,), (dg,)) for dg in range(n_groups)]
 
     out_factor = lax.dynamic_slice_in_dim(proj_out, mine * part, part, 0)
     left = jnp.zeros((n_groups * n_seq * rows, rank), jnp.float32)
-    left = add_chunk(cot, gate[:, LAST:], out_factor[LAST:], left, early, 1, rows)
-    left = add_chunk(cot, gate[:, :LAST], out_factor[:LAST], left, late, 0, rows)
+    where = jnp.reshape(side, (1,)).astype(jnp.int32)
+    left = add_chunk(where, cots, gates, LAST, out_factor[LAST:], left, early, 1, 32)
+    left = add_chunk(where, cots, gates, 0, out_factor[:LAST], left, late, 0, 18)
 
     parts = []
     for dg in range(n_groups):

time: 300 us -> 321 us (1.070)
  waiting for transfers between devices: 105 us -> 146 us
  other arithmetic: 36.3 us -> 17.8 us
  local copies, waits for them, and re-layouts: 69.6 us -> 55.8 us
  Pallas kernels: 38.2 us -> 46.2 us
    all_gather x1, waiting for transfers between devices: 15 us -> 61.2 us  [on_device(): lax.all_gather(lax.dynamic_slice_in_dim(down_weight, mine * part + LAST,...]
    concatenate x2 -> x0, other arithmetic: 20.3 us -> none  [the longest x1 13.7 us: on_device(): cot = jnp.concatenate(cots, axis=0)]
    dynamic_update_slice x11 -> x3, local copies, waits for them, and re-layouts: 17.6 us -> 0.03 us  [in_order(): out = lax.dynamic_update_slice_in_dim(out, piece, (me - r) % n * size, dim)]
    unnamed x26 -> x40, local copies, waits for them, and re-layouts: 14.3 us -> 29.9 us
    pallas_call x2, Pallas kernels: 38.2 us -> 46.2 us  [add_chunk(): pl.pallas_call(functools.partial(chunk_kernel, n_blocks, n_tensor, contra...]
    optimization_barrier x0 -> x3, local copies, waits for them, and re-layouts: none -> 7.64 us  [on_device(): lax.optimization_barrier((right_part, doc_lens, cots, gates))]
    ppermute x3 -> x0, local copies, waits for them, and re-layouts: 7.63 us -> none  [shifted(): return lax.ppermute(x, axes, pairs)]
    another operation x6 -> x2, local copies, waits for them, and re-layouts: 8.55 us -> 1.5 us
  transfers between devices with their start and end apart: 23 -> 23, of which waited for: 11 -> 8; matrix products, arithmetic and copies ran while one was open for 31% -> 15% of each run, Pallas kernels for 13% -> 15%
where the time goes in v4:
time: 321 us; the launch traced here: 316 us
  waiting for transfers between devices  146 us (45%)
  local copies, waits for them, and re-layouts  55.8 us (17%)
  Pallas kernels  46.2 us (14%)
  starting transfers between devices  21.5 us (7%)
  other arithmetic  17.8 us (6%)
  between operations  15.3 us (5%)
  matrix products  14.1 us (4%)
    ppermute x21, waiting for transfers between devices, shifted(): return lax.ppermute(x, axes, pairs)  84.6 us
    all_gather x1, waiting for transfers between devices, on_device(): lax.all_gather(lax.dynamic_slice_in_dim(down_weight, mine * part + LAST,...  61.2 us
    pallas_call x2, Pallas kernels, add_chunk(): pl.pallas_call(functools.partial(chunk_kernel, n_blocks, n_tensor, contra...  46.2 us
    unnamed x40, local copies, waits for them, and re-layouts  29.9 us
    ppermute x21, starting transfers between devices, shifted(): return lax.ppermute(x, axes, pairs)  21.4 us
    dynamic_slice x1, local copies, waits for them, and re-layouts, on_device(): columns = lax.dynamic_slice_in_dim(gate_pre, to * part, part, 1)  8.1 us
    optimization_barrier x3, local copies, waits for them, and re-layouts, on_device(): lax.optimization_barrier((right_part, doc_lens, cots, gates))  7.64 us
    another operation x3, other arithmetic, on_device(): factor = jnp.linalg.cholesky(damped)  6.52 us
  transfers between devices with their start and end apart: 23, of which 8 were waited for; matrix products, arithmetic and copies ran while one was open for 15% of the time, Pallas kernels for 15%

profile of v4, /device:TPU:0, one launch (start us, length us, event | category | flops | bytes accessed | tf_op | source)
XLA Modules:
  0.0 316.4 jit_solution(2213495339584122786)
XLA Ops:
  7.2 3.4 %constant_dynamic-slice_fusion.1 = bf16[1120,1024]{1,0:T(8,128)(2,1)} fusion(bf16[5504,1024]{1,0:T(8,128)(2,1)} %param.11, s32[]{:T(128)S(6)} %select_n.100), kind=kLoop, calls=%fused_computation.48 | loop fusion | bytes 4587524 | tf_op jit(solution)/shard_map/dynamic_slice | solution.py:134
  10.7 3.0 collective-permute-start.3
  15.2 44.5 %collective-permute-done.3.refs_4_ = bf16[512,2048]{1,0:T(8,128)(2,1)} collective-permute-done((bf16[512,2048]{1,0:T(8,128)(2,1)}, bf16[512,2048]{1,0:T(8,128)(2,1)}, u32[]{:S(2)}, u32[]{:S(2)}) %collective-permute-start.3) | collective-permute-done | bytes 2097184 | tf_op jit(solution)/shard_map/ppermute | solution.py:24
  59.7 1.7 collective-permute-start.4
  61.4 8.1 %constant_dynamic-slice_fusion.4 = (bf16[512,1376]{1,0:T(8,128)(2,1)}, bf16[512,1376]{1,0:T(8,128)(2,1)}, bf16[512,1376]{1,0:T(8,128)(2,1)}, bf16[512,1376]{1,0:T(8,128)(2,1)S(1)}) fusion(bf16[512,5504]{1,0:T(8,128)(2,1)} %param.10, s32[]{:T(128)S(6)} %select_n.98, s32[]{:T(128)S(6)} %select_n.97, s32[]{:T(128)S(6)} %select_n.95, s32[]{:T(128)S(6)} %select_n.93), kind=kLoop, calls=%fused_computation.51 | loop fusion | bytes 11272208 | tf_op jit(solution)/shard_map/dynamic_slice | solution.py:150
  69.5 2.7 copy.68
  72.2 2.5 copy.69
  77.0 29.8 %collective-permute-done.4.refs_5_ = bf16[512,2048]{1,0:T(8,128)(2,1)} collective-permute-done((bf16[512,2048]{1,0:T(8,128)(2,1)}, bf16[512,2048]{1,0:T(8,128)(2,1)}, u32[]{:S(2)}, u32[]{:S(2)}) %collective-permute-start.4) | collective-permute-done | bytes 2097184 | tf_op jit(solution)/shard_map/ppermute | solution.py:24
  106.8 2.6 copy.70
  110.9 1.9 constant_dynamic-slice_fusion.2
  112.8 2.0 copy.74
  114.8 61.2 %all-gather.3.cloned.1.call-done.refs_14_ = bf16[1120,4096]{1,0:T(8,128)(2,1)} async-done(((bf16[1120,1024]{1,0:T(8,128)(2,1)}), bf16[1120,4096]{1,0:T(8,128)(2,1)}) %all-gather.3.cloned.1.call-update) | async-done | bytes 9175056 | tf_op jit(solution)/shard_map/all_gather | solution.py:133
  176.0 1.6 constant_dynamic-slice_fusion.3
  177.6 1.8 copy.73.refs_12_
  181.5 3.1 fusion.33
  186.1 2.5 copy.56.refs_9_
  188.7 2.5 copy.57.refs_10_
  191.2 2.6 copy.58.refs_11_
  208.2 1.6 copy-done.7
  210.7 33.9 %shard_map.103.refs_13_ = f32[2048,32]{1,0:T(8,128)S(1)} custom-call(s32[1]{0:T(128)} %bitcast.side_ref, bf16[512,2048]{1,0:T(8,128)(2,1)S(1)} %copy-done.7, bf16[512,2048]{1,0:T(8,128)(2,1)} %collective-permute-done.refs_1_, bf16[512,2048]{1,0:T(8,128)(2,1)} %collective-permute-done.1.refs_2_, bf16[512,2048]{1,0:T(8,128)(2,1)} %collective-permute-done.2.refs_3_, ...), custom_call_target="tpu_custom_call" | custom-call | flops 18790481920 | bytes 30539776 | tf_op jit(solution)/shard_map/pallas_call | solution.py:98
  249.7 1.6 copy-done.8
  255.0 12.3 %shard_map.104 = f32[2048,32]{1,0:T(8,128)S(1)} custom-call(s32[1]{0:T(128)} %bitcast.side_ref, bf16[512,2048]{1,0:T(8,128)(2,1)S(1)} %copy-done.8, bf16[512,2048]{1,0:T(8,128)(2,1)} %collective-permute-done.refs_1_, bf16[512,2048]{1,0:T(8,128)(2,1)} %collective-permute-done.1.refs_2_, bf16[512,2048]{1,0:T(8,128)(2,1)} %collective-permute-done.2.refs_3_, ...), custom_call_target="tpu_custom_call" | custom-call | flops 4294967296 | bytes 19922944 | tf_op jit(solution)/shard_map/pallas_call | solution.py:98
  268.1 2.6 fusion.7
  272.8 2.6 fusion.4
  276.3 3.8 %collective-permute-done.16 = f32[16,1024]{1,0:T(8,128)S(1)} collective-permute-done((f32[16,1024]{1,0:T(8,128)S(1)}, f32[16,1024]{1,0:T(8,128)S(1)}, u32[]{:S(2)}, u32[]{:S(2)}) %collective-permute-start.16) | collective-permute-done | bytes 65568 | tf_op jit(solution)/shard_map/ppermute | solution.py:24
  282.5 3.0 collective-permute-start.20
  285.5 2.8 collective-permute-done.18
  288.3 1.9 collective-permute-done.19
  292.0 5.8 %cholesky.17 = f32[64,64]{1,0:T(8,128)S(1)} custom-call(f32[64,64]{1,0:T(8,128)S(1)} %fusion.27), custom_call_target="Cholesky" | custom-call | tf_op jit(solution)/shard_map/jit(cholesky)/cholesky | solution.py:199
  299.2 4.9 %custom-call.10 = f32[1,64,64]{1,2,0:T(8,128)S(1)} custom-call(f32[1,64,64]{2,1,0:T(8,128)S(1)} %fusion.21), custom_call_target="InvertDiagBlocksLowerTriangular" | custom-call | tf_op jit(solution)/shard_map/jit(_cho_solve)/triangular_solve | solution.py:201
  304.4 2.1 fusion.34
  306.6 2.0 convolution_divide_fusion
  (111 shorter events, 42.7 us)
Async XLA Ops:
  7.2 297.3 %copy-start = (f32[512,1024]{1,0:T(8,128)S(1)}, f32[512,1024]{1,0:T(8,128)}, u32[]{:S(2)}) copy-start(f32[512,1024]{1,0:T(8,128)} %param.15) | copy-start | bytes 6291460
  7.2 168.8 %all-gather.3.cloned.1.call-start = ((), (), s32[]{:S(2)}) async-start(), calls=%async_computation | async-start | bytes 11468800 | tf_op jit(solution)/shard_map/all_gather | solution.py:133
  10.6 235.0 %all-gather.5.cloned.1.call-start = ((), (), s32[]{:S(2)}) async-start(), calls=%async_computation.1 | async-start | bytes 2621440 | tf_op jit(solution)/shard_map/all_gather | solution.py:138
  10.7 49.0 %collective-permute-start.3 = (bf16[512,2048]{1,0:T(8,128)(2,1)}, bf16[512,2048]{1,0:T(8,128)(2,1)}, u32[]{:S(2)}, u32[]{:S(2)}) collective-permute-start(bf16[512,2048]{1,0:T(8,128)(2,1)} %refs_0_.1), channel_id=1, source_target_pairs={{0,16},{16,0},{1,17},{17,1},{2,18},{18,2},{3,19},{19,3},{4,20},{20... | collective-permute-start | bytes 6291464 | tf_op jit(solution)/shard_map/ppermute | solution.py:24
  13.7 63.0 %collective-permute-start = (bf16[512,2048]{1,0:T(8,128)(2,1)}, bf16[512,2048]{1,0:T(8,128)(2,1)}, u32[]{:S(2)}, u32[]{:S(2)}) collective-permute-start(bf16[512,2048]{1,0:T(8,128)(2,1)} %refs_0_.1), channel_id=1, source_target_pairs={{0,2},{2,0},{1,3},{3,1},{4,6},{6,4},{5,7},{7,5},{8,10},{10,8},{9,1... | collective-permute-start | bytes 6291464 | tf_op jit(solution)/shard_map/ppermute | solution.py:24
  59.7 47.1 %collective-permute-start.4 = (bf16[512,2048]{1,0:T(8,128)(2,1)}, bf16[512,2048]{1,0:T(8,128)(2,1)}, u32[]{:S(2)}, u32[]{:S(2)}) collective-permute-start(bf16[512,2048]{1,0:T(8,128)(2,1)} %collective-permute-done.3.refs_4_), channel_id=1, source_target_pairs={{0,2},{2,0},{1,3},{3,1},{4,6},{6,4},{5,7},{7,5},{8,10},{10,8},{9,1... | collective-permute-start | bytes 6291464 | tf_op jit(solution)/shard_map/ppermute | solution.py:24
  72.2 4.3 %collective-permute-start.7 = (bf16[512,1376]{0,1:T(8,128)(2,1)}, bf16[512,1376]{0,1:T(8,128)(2,1)}, u32[]{:S(2)}, u32[]{:S(2)}) collective-permute-start(bf16[512,1376]{0,1:T(8,128)(2,1)} %copy.68), channel_id=1, source_target_pairs={{0,1},{1,0},{16,17},{17,16},{2,3},{3,2},{18,19},{19,18},{4,5},{5,4... | collective-permute-start | bytes 4227080 | tf_op jit(solution)/shard_map/ppermute | solution.py:24
  74.7 34.7 %collective-permute-start.8 = (bf16[512,1376]{0,1:T(8,128)(2,1)}, bf16[512,1376]{0,1:T(8,128)(2,1)}, u32[]{:S(2)}, u32[]{:S(2)}) collective-permute-start(bf16[512,1376]{0,1:T(8,128)(2,1)} %copy.69), channel_id=1, source_target_pairs={{0,16},{1,17},{16,0},{17,1},{2,18},{3,19},{18,2},{19,3},{4,20},{5,... | collective-permute-start | bytes 4227080 | tf_op jit(solution)/shard_map/ppermute | solution.py:24
  76.2 108.4 %collective-permute-start.1 = (bf16[512,2048]{1,0:T(8,128)(2,1)}, bf16[512,2048]{1,0:T(8,128)(2,1)}, u32[]{:S(2)}, u32[]{:S(2)}) collective-permute-start(bf16[512,2048]{1,0:T(8,128)(2,1)} %refs_0_.1), channel_id=1, source_target_pairs={{0,1},{1,0},{2,3},{3,2},{4,5},{5,4},{6,7},{7,6},{8,9},{9,8},{10,11... | collective-permute-start | bytes 6291464 | tf_op jit(solution)/shard_map/ppermute | solution.py:24
  76.5 108.1 %collective-permute-start.5 = (bf16[512,2048]{1,0:T(8,128)(2,1)}, bf16[512,2048]{1,0:T(8,128)(2,1)}, u32[]{:S(2)}, u32[]{:S(2)}) collective-permute-start(bf16[512,2048]{1,0:T(8,128)(2,1)} %collective-permute-done.3.refs_4_), channel_id=1, source_target_pairs={{0,1},{1,0},{2,3},{3,2},{4,5},{5,4},{6,7},{7,6},{8,9},{9,8},{10,11... | collective-permute-start | bytes 6291464 | tf_op jit(solution)/shard_map/ppermute | solution.py:24
  76.8 107.9 %collective-permute-start.2 = (bf16[512,2048]{1,0:T(8,128)(2,1)}, bf16[512,2048]{1,0:T(8,128)(2,1)}, u32[]{:S(2)}, u32[]{:S(2)}) collective-permute-start(bf16[512,2048]{1,0:T(8,128)(2,1)} %collective-permute-done.refs_1_), channel_id=1, source_target_pairs={{0,1},{1,0},{2,3},{3,2},{4,5},{5,4},{6,7},{7,6},{8,9},{9,8},{10,11... | collective-permute-start | bytes 6291464 | tf_op jit(solution)/shard_map/ppermute | solution.py:24
  106.8 77.8 %collective-permute-start.6 = (bf16[512,2048]{1,0:T(8,128)(2,1)}, bf16[512,2048]{1,0:T(8,128)(2,1)}, u32[]{:S(2)}, u32[]{:S(2)}) collective-permute-start(bf16[512,2048]{1,0:T(8,128)(2,1)} %collective-permute-done.4.refs_5_), channel_id=1, source_target_pairs={{0,1},{1,0},{2,3},{3,2},{4,5},{5,4},{6,7},{7,6},{8,9},{9,8},{10,11... | collective-permute-start | bytes 6291464 | tf_op jit(solution)/shard_map/ppermute | solution.py:24
  109.4 75.2 %collective-permute-start.9 = (bf16[512,1376]{0,1:T(8,128)(2,1)}, bf16[512,1376]{0,1:T(8,128)(2,1)}, u32[]{:S(2)}, u32[]{:S(2)}) collective-permute-start(bf16[512,1376]{0,1:T(8,128)(2,1)} %copy.70), channel_id=1, source_target_pairs={{0,17},{1,16},{16,1},{17,0},{2,19},{3,18},{18,3},{19,2},{4,21},{5,... | collective-permute-start | bytes 4227080 | tf_op jit(solution)/shard_map/ppermute | solution.py:24
  184.6 15.7 %collective-permute-start.10 = (f32[512,32]{0,1:T(8,128)}, f32[512,32]{0,1:T(8,128)}, u32[]{:S(2)}, u32[]{:S(2)}) collective-permute-start(f32[512,32]{0,1:T(8,128)} %fusion.33), channel_id=1, source_target_pairs={{0,2},{2,0},{1,3},{3,1},{4,6},{6,4},{5,7},{7,5},{8,10},{10,8},{9,1... | collective-permute-start | bytes 196616 | tf_op jit(solution)/shard_map/ppermute | solution.py:24
  193.8 3.6 %collective-permute-start.12 = (s32[1,16]{1,0:T(1,128)}, s32[1,16]{1,0:T(1,128)}, u32[]{:S(2)}, u32[]{:S(2)}) collective-permute-start(s32[1,16]{1,0:T(1,128)} %param.14), channel_id=1, source_target_pairs={{0,16},{16,0},{1,17},{17,1},{2,18},{18,2},{3,19},{19,3},{4,20},{20... | collective-permute-start | bytes 200 | tf_op jit(solution)/shard_map/ppermute | solution.py:24
  201.9 65.7 %collective-permute-start.13 = (f32[512,32]{0,1:T(8,128)}, f32[512,32]{0,1:T(8,128)}, u32[]{:S(2)}, u32[]{:S(2)}) collective-permute-start(f32[512,32]{0,1:T(8,128)} %add.187), channel_id=1, source_target_pairs={{0,16},{1,17},{16,0},{17,1},{2,18},{3,19},{18,2},{19,3},{4,20},{5,... | collective-permute-start | bytes 196616 | tf_op jit(solution)/shard_map/ppermute | solution.py:24
  203.3 64.2 %collective-permute-start.14 = (f32[512,32]{0,1:T(8,128)}, f32[512,32]{0,1:T(8,128)}, u32[]{:S(2)}, u32[]{:S(2)}) collective-permute-start(f32[512,32]{0,1:T(8,128)} %add.187), channel_id=1, source_target_pairs={{0,17},{1,16},{16,1},{17,0},{2,19},{3,18},{18,3},{19,2},{4,21},{5,... | collective-permute-start | bytes 196616 | tf_op jit(solution)/shard_map/ppermute | solution.py:24
  203.4 69.4 %collective-permute-start.11 = (f32[512,32]{0,1:T(8,128)}, f32[512,32]{0,1:T(8,128)}, u32[]{:S(2)}, u32[]{:S(2)}) collective-permute-start(f32[512,32]{0,1:T(8,128)} %add.187), channel_id=1, source_target_pairs={{0,1},{1,0},{16,17},{17,16},{2,3},{3,2},{18,19},{19,18},{4,5},{5,4... | collective-permute-start | bytes 196616 | tf_op jit(solution)/shard_map/ppermute | solution.py:24
  204.1 1.4 copy-start.1
  205.4 1.4 copy-start.3
  208.2 1.6 copy-start.7
  245.6 1.4 copy-start.2
  249.7 1.6 copy-start.8
  251.3 1.6 copy-start.9
  267.4 5.4 %copy-start.14 = (f32[1024,16]{0,1:T(8,128)S(1)}, f32[1024,16]{0,1:T(8,128)}, u32[]{:S(2)}) copy-start(f32[1024,16]{0,1:T(8,128)} %fusion.19) | copy-start | bytes 196612
  271.0 4.6 %collective-permute-start.15 = (f32[16,1024]{1,0:T(8,128)S(1)}, f32[16,1024]{1,0:T(8,128)S(1)}, u32[]{:S(2)}, u32[]{:S(2)}) collective-permute-start(f32[16,1024]{1,0:T(8,128)S(1)} %reshape.90), channel_id=1, source_target_pairs={{0,16},{16,0},{1,17},{17,1},{2,18},{18,2},{3,19},{19,3},{4,20},{20... | collective-permute-start | bytes 196616 | tf_op jit(solution)/shard_map/ppermute | solution.py:24
  275.7 4.3 %collective-permute-start.16 = (f32[16,1024]{1,0:T(8,128)S(1)}, f32[16,1024]{1,0:T(8,128)S(1)}, u32[]{:S(2)}, u32[]{:S(2)}) collective-permute-start(f32[16,1024]{1,0:T(8,128)S(1)} %add.188), channel_id=1, source_target_pairs={{0,2},{2,0},{1,3},{3,1},{4,6},{6,4},{5,7},{7,5},{8,10},{10,8},{9,1... | collective-permute-start | bytes 196616 | tf_op jit(solution)/shard_map/ppermute | solution.py:24
  280.0 1.3 collective-permute-start.17
  281.4 27.2 %copy-start.16 = (f32[16,1024]{1,0:T(8,128)}, f32[16,1024]{1,0:T(8,128)S(1)}, u32[]{:S(2)}) copy-start(f32[16,1024]{1,0:T(8,128)S(1)} %get-tuple-element.38) | copy-start | bytes 196612
  281.4 6.8 %collective-permute-start.18 = (f32[16,1024]{1,0:T(8,128)S(1)}, f32[16,1024]{1,0:T(8,128)S(1)}, u32[]{:S(2)}, u32[]{:S(2)}) collective-permute-start(f32[16,1024]{1,0:T(8,128)S(1)} %get-tuple-element.38), channel_id=1, source_target_pairs={{0,4},{4,8},{8,12},{12,0},{1,5},{5,9},{9,13},{13,1},{2,6},{6,10},{... | collective-permute-start | bytes 196616 | tf_op jit(solution)/shard_map/ppermute | solution.py:24
  281.5 8.6 %collective-permute-start.19 = (f32[16,1024]{1,0:T(8,128)S(1)}, f32[16,1024]{1,0:T(8,128)S(1)}, u32[]{:S(2)}, u32[]{:S(2)}) collective-permute-start(f32[16,1024]{1,0:T(8,128)S(1)} %get-tuple-element.38), channel_id=1, source_target_pairs={{0,8},{4,12},{8,0},{12,4},{1,9},{5,13},{9,1},{13,5},{2,10},{6,14},... | collective-permute-start | bytes 196616 | tf_op jit(solution)/shard_map/ppermute | solution.py:24
  282.5 7.7 %collective-permute-start.20 = (f32[16,1024]{1,0:T(8,128)S(1)}, f32[16,1024]{1,0:T(8,128)S(1)}, u32[]{:S(2)}, u32[]{:S(2)}) collective-permute-start(f32[16,1024]{1,0:T(8,128)S(1)} %get-tuple-element.38), channel_id=1, source_target_pairs={{0,12},{4,0},{8,4},{12,8},{1,13},{5,1},{9,5},{13,9},{2,14},{6,2},{... | collective-permute-start | bytes 196616 | tf_op jit(solution)/shard_map/ppermute | solution.py:24
  (8 other events, 8.9 us)
Sparse Core Ops, SparseCore 0:
  10.7 165.1 all-gather.2
  177.5 43.8 all-gather.4

commit v5 on v3

--- a/solution.py
+++ b/solution.py
@@ -9,6 +9,7 @@
 
 HIGHEST = lax.Precision.HIGHEST
 LAST = 256
+LANES = 128
 
 
 def shifted(x, axes, sizes, shift):
@@ -84,6 +85,79 @@
     )(cot, gate, factor, before, weight)
 
 
+def dot3(a, b, dims):
+    a_high, b_high = a.astype(jnp.bfloat16), b.astype(jnp.bfloat16)
+    a_low = (a - a_high.astype(jnp.float32)).astype(jnp.bfloat16)
+    b_low = (b - b_high.astype(jnp.float32)).astype(jnp.bfloat16)
+    dot = functools.partial(
+        lax.dot_general, dimension_numbers=(dims, ((), ())), preferred_element_type=jnp.float32
+    )
+    return dot(a_high, b_high) + (dot(a_high, b_low) + dot(a_low, b_high))
+
+
+def final_kernel(n, share, place_ref, queries_ref, *refs):
+    pieces, (fisher_ref, scores_ref, every_ref) = refs[:n], refs[n:]
+    docs, width = pieces[0].shape
+    total = n * docs
+    stage, which = place_ref[0], place_ref[1]
+    for r in range(n):
+        at = pl.multiple_of(lax.rem(stage + (n - r), n) * docs, docs)
+        every_ref[pl.ds(at, docs), :] = pieces[r][...]
+    every = every_ref[...]
+    mean_diag = jnp.sum(jnp.sum(every * every, axis=1, keepdims=True), axis=0, keepdims=True) / width
+    scale = 1.0 / mean_diag
+    mine = every_ref[:, pl.ds(pl.multiple_of(which * share, share), share)]
+    fisher_ref[...] = dot3(mine, every, ((0,), (0,))) * scale
+
+    lanes = -(-(total + docs) // LANES) * LANES
+    tall = jnp.concatenate([every, jnp.zeros((lanes - total, width), jnp.float32)], axis=0)
+    row = lax.broadcasted_iota(jnp.int32, (total, lanes), 0)
+    lane = lax.broadcasted_iota(jnp.int32, (total, lanes), 1)
+    own = (lane >= total) & (lane - total == row - stage * docs) & (lane < total + docs)
+    table = dot3(every, tall, ((1,), (1,))) * scale + jnp.where((lane == row) | own, 1.0, 0.0)
+    products = dot3(every, queries_ref[...], ((1,), (1,)))
+
+    def pick(condition, x, axis):
+        return jnp.sum(jnp.where(condition, x, 0.0), axis=axis, keepdims=True)
+
+    def step(i, table):
+        k = 2 * i
+        left0 = pick(lane == k, table, 1)
+        left1 = pick(lane == k + 1, table, 1)
+        top0 = pick(row == k, table, 0)
+        top1 = pick(row == k + 1, table, 0)
+        column = row[:, :1]
+        a = pick(column == k, left0, 0)
+        b = pick(column == k, left1, 0)
+        c = pick(column == k + 1, left0, 0)
+        d = pick(column == k + 1, left1, 0)
+        inverse = 1.0 / (a * d - b * c)
+        new0 = (d * top0 - b * top1) * inverse
+        new1 = (a * top1 - c * top0) * inverse
+        table = table - left0 * new0 - left1 * new1
+        return jnp.where(row == k, new0, jnp.where(row == k + 1, new1, table))
+
+    table = lax.fori_loop(0, total // 2, step, table)
+    scores_ref[...] = dot3(table, products, ((0,), (0,)))[total:total + docs]
+
+
+def finish(stage, which, share, queries, pieces):
+    n = len(pieces)
+    docs, width = pieces[0].shape
+    in_vmem = pl.BlockSpec(memory_space=pltpu.VMEM)
+    return pl.pallas_call(
+        functools.partial(final_kernel, n, share),
+        out_shape=(
+            jax.ShapeDtypeStruct((share, width), jnp.float32),
+            jax.ShapeDtypeStruct((docs, queries.shape[0]), jnp.float32),
+        ),
+        in_specs=[pl.BlockSpec(memory_space=pltpu.SMEM)] + [in_vmem] * (n + 1),
+        out_specs=(in_vmem, in_vmem),
+        scratch_shapes=[pltpu.VMEM((n * docs, width), jnp.float32)],
+        compiler_params=pltpu.CompilerParams(vmem_limit_bytes=32 * 1024 * 1024),
+    )(jnp.stack([stage, which]).astype(jnp.int32), queries, *pieces)
+
+
 def on_device(inputs, cotangent, gate_pre, down_weight, proj_in, proj_out, doc_lens, queries):
     n_groups, n_seq = lax.axis_size("groups"), lax.axis_size("seq")
     n_dp, n_tensor = lax.axis_size("dp"), lax.axis_size("tensor")
@@ -107,32 +181,36 @@
     late = lax.all_gather(piece, "dp", axis=0, tiled=True)
 
     order = [(dg, ds) for dg in range(n_groups) for ds in range(n_seq)]
-    cots = []
+    right = sum_over(jnp.dot(inputs, proj_in, preferred_element_type=jnp.float32), "tensor")
+    rights = [right if dg == ds == 0 else shifted(right, pair, sizes, (dg, ds)) for dg, ds in order]
+    lens = [doc_lens if dg == 0 else shifted(doc_lens, "groups", (n_groups,), (dg,)) for dg in range(n_groups)]
+    rights, lens, cotangent, gate_pre = lax.optimization_barrier((rights, lens, cotangent, gate_pre))
+
+    cot = jnp.zeros((len(order) * rows, n_tensor * cotangent.shape[1]), cotangent.dtype)
+    gate_late = jnp.zeros((len(order) * rows, LAST), gate_pre.dtype)
+    gate_early = jnp.zeros((len(order) * rows, part - LAST), gate_pre.dtype)
+    placed = []
     for dg in range(n_groups):
         own = cotangent if dg == 0 else shifted(cotangent, "groups", (n_groups,), (dg,))
         pieces = [own if r == 0 else shifted(own, "tensor", (n_tensor,), (r,)) for r in range(n_tensor)]
         for ds in range(n_seq):
-            cots.append(in_order(
-                pieces if ds == 0 else [shifted(x, "seq", (n_seq,), (ds,)) for x in pieces], "tensor", 1
-            ))
-    gates = []
-    for dg, ds in order:
+            for r, piece in enumerate(pieces):
+                moved = piece if ds == 0 else shifted(piece, "seq", (n_seq,), (ds,))
+                placed.append((ds, dg, r, moved))
+    for ds, dg, r, piece in sorted(placed, key=lambda p: p[:3]):
+        at = ((side - r) % n_tensor) * piece.shape[1]
+        cot = lax.dynamic_update_slice(cot, piece, ((dg * n_seq + ds) * rows, at))
+    for number, (dg, ds) in enumerate(order):
         to = ((group + dg) % n_groups) * n_seq + (half + ds) % n_seq
         columns = lax.dynamic_slice_in_dim(gate_pre, to * part, part, 1)
-        gates.append(columns if dg == ds == 0 else shifted(columns, pair, sizes, (dg, ds)))
-
-    cot = jnp.concatenate(cots, axis=0)
-    gate = jnp.concatenate(gates, axis=0)
-    right_part = jnp.dot(inputs, proj_in, preferred_element_type=jnp.float32)
-    right_part, doc_lens, cot, gate = lax.optimization_barrier((right_part, doc_lens, cot, gate))
-    right = sum_over(right_part, "tensor")
-    rights = [right if dg == ds == 0 else shifted(right, pair, sizes, (dg, ds)) for dg, ds in order]
-    lens = [doc_lens if dg == 0 else shifted(doc_lens, "groups", (n_groups,), (dg,)) for dg in range(n_groups)]
+        piece = columns if dg == ds == 0 else shifted(columns, pair, sizes, (dg, ds))
+        gate_late = lax.dynamic_update_slice(gate_late, piece[:, :LAST], (number * rows, 0))
+        gate_early = lax.dynamic_update_slice(gate_early, piece[:, LAST:], (number * rows, 0))
 
     out_factor = lax.dynamic_slice_in_dim(proj_out, mine * part, part, 0)
     left = jnp.zeros((n_groups * n_seq * rows, rank), jnp.float32)
-    left = add_chunk(cot, gate[:, LAST:], out_factor[LAST:], left, early, 1, rows)
-    left = add_chunk(cot, gate[:, :LAST], out_factor[:LAST], left, late, 0, rows)
+    left = add_chunk(cot, gate_early, out_factor[LAST:], left, early, 1, rows)
+    left = add_chunk(cot, gate_late, out_factor[:LAST], left, late, 0, rows)
 
     parts = []
     for dg in range(n_groups):
@@ -153,29 +231,10 @@
         grads = grads + shifted(parts[dg], "groups", (n_groups,), (-dg,))
     doc_grads = sum_over(sum_over(grads, "tensor"), "seq")
 
-    every = gather_in_order(doc_grads, "dp", 0)
-    mean_diag = jnp.sum(every * every) / width
-    pieces = n_tensor * n_seq
-    share = width // pieces
-    which = side * n_seq + half
-    columns = lax.dynamic_slice_in_dim(every, which * share, share, 1)
-    fisher_rows = lax.dot_general(
-        columns, every, (((0,), (0,)), ((), ())), precision=HIGHEST, preferred_element_type=jnp.float32
-    ) / mean_diag
-
-    total = every.shape[0]
-    gram = lax.dot_general(
-        every, every, (((1,), (1,)), ((), ())), precision=HIGHEST, preferred_element_type=jnp.float32
-    )
-    damped = gram / mean_diag + jnp.eye(total, dtype=jnp.float32)
-    factor = jnp.linalg.cholesky(damped)
-    chosen = (jnp.arange(total)[:, None] == stage * docs + jnp.arange(docs)[None, :]).astype(jnp.float32)
-    solved = jax.scipy.linalg.cho_solve((factor, True), chosen)
-    products = lax.dot_general(
-        queries, every, (((1,), (1,)), ((), ())), precision=HIGHEST, preferred_element_type=jnp.float32
-    )
-    scores = jnp.dot(products, solved, precision=HIGHEST)
-    return (doc_grads, fisher_rows, scores)
+    stages = [doc_grads if r == 0 else shifted(doc_grads, "dp", (n_dp,), (r,)) for r in range(n_dp)]
+    share = width // (n_tensor * n_seq)
+    fisher_rows, scores = finish(stage, side * n_seq + half, share, queries, stages)
+    return (doc_grads, fisher_rows, scores.T)
 
 
 def solution(mesh):

time: 300 us -> 273 us (0.910)
  other arithmetic: 36.3 us -> 1.18 us
  local copies, waits for them, and re-layouts: 69.6 us -> 83.8 us
  matrix products: 14.2 us -> 4.27 us
  Pallas kernels: 38.2 us -> 45.4 us
  waiting for transfers between devices: 105 us -> 101 us
    concatenate x2 -> x0, other arithmetic: 20.3 us -> none  [the longest x1 13.7 us: on_device(): cot = jnp.concatenate(cots, axis=0)]
    ppermute x21, waiting for transfers between devices: 89.5 us -> 71.4 us  [shifted(): return lax.ppermute(x, axes, pairs)]
    all_gather x1, waiting for transfers between devices: 15 us -> 29.2 us  [on_device(): lax.all_gather(lax.dynamic_slice_in_dim(down_weight, mine * part + LAST,...]
    dynamic_update_slice x11 -> x16, local copies, waits for them, and re-layouts: 17.6 us -> 30.5 us  [the longest x8 24.4 us: on_device(): cot = lax.dynamic_update_slice(cot, piece, ((dg * n_seq + ds) * rows, at))]
    another operation x11 -> x7, other arithmetic: 13.6 us -> 1.03 us  [the longest x3 6.52 us: on_device(): factor = jnp.linalg.cholesky(damped)]
    another operation x6 -> x2, local copies, waits for them, and re-layouts: 8.55 us -> 0.17 us
    optimization_barrier x0 -> x1, local copies, waits for them, and re-layouts: none -> 8.3 us  [on_device(): lax.optimization_barrier((rights, lens, cotangent, gate_pre))]
    dot_general x5 -> x1, matrix products: 8.46 us -> 0.72 us  [on_device(): jnp.dot(inputs, proj_in, preferred_element_type=jnp.float32)]
  transfers between devices with their start and end apart: 23 -> 23, of which waited for: 11 -> 12; matrix products, arithmetic and copies ran while one was open for 31% -> 26% of each run, Pallas kernels for 13% -> 11%
where the time goes in v5:
time: 273 us; the launch traced here: 272 us
  waiting for transfers between devices  101 us (37%)
  local copies, waits for them, and re-layouts  83.8 us (31%)
  Pallas kernels  45.4 us (17%)
  starting transfers between devices  21.7 us (8%)
  between operations  14.6 us (5%)
  matrix products  4.27 us (2%)
    ppermute x21, waiting for transfers between devices, shifted(): return lax.ppermute(x, axes, pairs)  71.4 us
    pallas_call x2, Pallas kernels, add_chunk(): pl.pallas_call(functools.partial(chunk_kernel, contract), out_shape=jax.S...  38.3 us
    all_gather x1, waiting for transfers between devices, on_device(): lax.all_gather(lax.dynamic_slice_in_dim(down_weight, mine * part + LAST,...  29.2 us
    dynamic_update_slice x8, local copies, waits for them, and re-layouts, on_device(): cot = lax.dynamic_update_slice(cot, piece, ((dg * n_seq + ds) * rows, at))  24.4 us
    ppermute x21, starting transfers between devices, shifted(): return lax.ppermute(x, axes, pairs)  21.6 us
    unnamed x51, local copies, waits for them, and re-layouts  18.5 us
    slice x4, local copies, waits for them, and re-layouts, on_device(): piece[:, LAST:]  9.14 us
    optimization_barrier x1, local copies, waits for them, and re-layouts, on_device(): lax.optimization_barrier((rights, lens, cotangent, gate_pre))  8.3 us
  transfers between devices with their start and end apart: 23, of which 12 were waited for; matrix products, arithmetic and copies ran while one was open for 26% of the time, Pallas kernels for 11%

profile of v5, /device:TPU:0, one launch (start us, length us, event | category | flops | bytes accessed | tf_op | source)
XLA Modules:
  0.0 271.5 jit_solution(11788124720208509343)
XLA Ops:
  7.2 3.4 %constant_dynamic-slice_fusion.2 = bf16[1120,1024]{1,0:T(8,128)(2,1)} fusion(bf16[5504,1024]{1,0:T(8,128)(2,1)} %param.11, s32[]{:T(128)S(6)} %select_n.101), kind=kLoop, calls=%fused_computation.24 | loop fusion | bytes 4587524 | tf_op jit(solution)/shard_map/dynamic_slice | solution.py:177
  12.2 3.0 %collective-permute-start = (f32[512,32]{0,1:T(8,128)S(1)}, f32[512,32]{0,1:T(8,128)S(1)}, u32[]{:S(2)}, u32[]{:S(2)}) collective-permute-start(f32[512,32]{0,1:T(8,128)S(1)} %fusion.23), channel_id=1, source_target_pairs={{0,2},{2,0},{1,3},{3,1},{4,6},{6,4},{5,7},{7,5},{8,10},{10,8},{9,1... | collective-permute-start | bytes 196616 | tf_op jit(solution)/shard_map/ppermute | solution.py:25
  15.2 2.2 collective-permute-done
  17.5 2.1 collective-permute-start.2
  21.5 2.6 collective-permute-done.4
  30.4 8.3 %copy.44 = bf16[512,5504]{0,1:T(8,128)(2,1)} copy(bf16[512,5504]{1,0:T(8,128)(2,1)} %param.10) | data formatting | bytes 11272192 | tf_op jit(solution)/shard_map/optimization_barrier | solution.py:187
  38.7 4.0 %constant_dynamic-slice_fusion.5 = (bf16[512,1376]{0,1:T(8,128)(2,1)}, bf16[512,1376]{0,1:T(8,128)(2,1)}, bf16[512,1376]{0,1:T(8,128)(2,1)S(1)}) fusion(bf16[512,5504]{0,1:T(8,128)(2,1)} %copy.44, s32[]{:T(128)S(6)} %select_n.99, s32[]{:T(128)S(6)} %select_n.98, s32[]{:T(128)S(6)} %select_n.96), kind=kLoop, calls=%fused_computation.31 | loop fusion | bytes 8454156 | tf_op jit(solution)/shard_map/dynamic_slice | solution.py:205
  43.7 28.1 %collective-permute-done.6 = bf16[512,2048]{1,0:T(8,128)(2,1)} collective-permute-done((bf16[512,2048]{1,0:T(8,128)(2,1)}, bf16[512,2048]{1,0:T(8,128)(2,1)}, u32[]{:S(2)}, u32[]{:S(2)}) %collective-permute-start.6) | collective-permute-done | bytes 2097184 | tf_op jit(solution)/shard_map/ppermute | solution.py:25
  75.2 2.0 constant_dynamic-slice_fusion.8
  77.3 2.6 dynamic_update_slice.60
  80.6 1.9 broadcast_in_dim.4
  85.2 5.0 %copy-done.7 = bf16[2048,4096]{1,0:T(8,128)(2,1)} copy-done((bf16[2048,4096]{1,0:T(8,128)(2,1)}, bf16[2048,4096]{1,0:T(8,128)(2,1)S(1)}, u32[]{:S(2)}) %copy-start.7) | copy-done | bytes 16777240
  91.4 2.4 slice.51
  97.4 10.1 %collective-permute-done.13 = bf16[512,1376]{0,1:T(8,128)(2,1)} collective-permute-done((bf16[512,1376]{0,1:T(8,128)(2,1)}, bf16[512,1376]{0,1:T(8,128)(2,1)}, u32[]{:S(2)}, u32[]{:S(2)}) %collective-permute-start.13) | collective-permute-done | bytes 1409056 | tf_op jit(solution)/shard_map/ppermute | solution.py:25
  107.5 2.4 slice.52
  115.0 5.0 %collective-permute-done.7 = bf16[512,2048]{1,0:T(8,128)(2,1)} collective-permute-done((bf16[512,2048]{1,0:T(8,128)(2,1)}, bf16[512,2048]{1,0:T(8,128)(2,1)}, u32[]{:S(2)}, u32[]{:S(2)}) %collective-permute-start.7) | collective-permute-done | bytes 2097184 | tf_op jit(solution)/shard_map/ppermute | solution.py:25
  120.0 14.1 %collective-permute-done.14 = bf16[512,1376]{0,1:T(8,128)(2,1)} collective-permute-done((bf16[512,1376]{0,1:T(8,128)(2,1)}, bf16[512,1376]{0,1:T(8,128)(2,1)}, u32[]{:S(2)}, u32[]{:S(2)}) %collective-permute-start.14) | collective-permute-done | bytes 1409056 | tf_op jit(solution)/shard_map/ppermute | solution.py:25
  134.1 2.4 slice.53
  140.4 3.2 %constant_dynamic-update-slice_fusion.6 = bf16[2048,4096]{1,0:T(8,128)(2,1)} fusion(bf16[2048,4096]{1,0:T(8,128)(2,1)} %copy-done.7, bf16[512,2048]{1,0:T(8,128)(2,1)} %collective-permute-done.5, s32[]{:T(128)S(6)} %select_n.91), kind=kLoop, calls=%fused_computation.37 | loop fusion | bytes 4194308 | tf_op jit(solution)/shard_map/dynamic_update_slice | solution.py:202
  143.6 3.2 %constant_dynamic-update-slice_fusion.11 = bf16[2048,4096]{1,0:T(8,128)(2,1)} fusion(bf16[2048,4096]{1,0:T(8,128)(2,1)} %constant_dynamic-update-slice_fusion.6, bf16[512,2048]{1,0:T(8,128)(2,1)} %collective-permute-done.6, s32[]{:T(128)S(6)} %select_n.89), kind=kLoop, calls=%fused_computation.45 | loop fusion | bytes 4194308 | tf_op jit(solution)/shard_map/dynamic_update_slice | solution.py:202
  146.8 29.2 %all-gather.3.cloned.1.call-done.weight_ref = bf16[1120,4096]{1,0:T(8,128)(2,1)} async-done(((bf16[1120,1024]{1,0:T(8,128)(2,1)}), bf16[1120,4096]{1,0:T(8,128)(2,1)}) %all-gather.3.cloned.1.call-update) | async-done | bytes 9175056 | tf_op jit(solution)/shard_map/all_gather | solution.py:176
  176.0 3.2 %constant_dynamic-update-slice_fusion.10 = bf16[2048,4096]{1,0:T(8,128)(2,1)} fusion(bf16[2048,4096]{1,0:T(8,128)(2,1)} %constant_dynamic-update-slice_fusion.11, bf16[512,2048]{1,0:T(8,128)(2,1)} %collective-permute-done.7, s32[]{:T(128)S(6)} %select_n.91), kind=kLoop, calls=%fused_computation.44 | loop fusion | bytes 4194308 | tf_op jit(solution)/shard_map/dynamic_update_slice | solution.py:202
  179.2 3.2 %constant_dynamic-update-slice_fusion.13 = bf16[2048,4096]{1,0:T(8,128)(2,1)} fusion(bf16[2048,4096]{1,0:T(8,128)(2,1)} %constant_dynamic-update-slice_fusion.10, bf16[512,2048]{1,0:T(8,128)(2,1)} %collective-permute-done.8, s32[]{:T(128)S(6)} %select_n.89), kind=kLoop, calls=%fused_computation.47 | loop fusion | bytes 4194308 | tf_op jit(solution)/shard_map/dynamic_update_slice | solution.py:202
  182.4 3.5 %constant_dynamic-update-slice_fusion.12 = bf16[2048,4096]{1,0:T(8,128)(2,1)} fusion(bf16[2048,4096]{1,0:T(8,128)(2,1)} %constant_dynamic-update-slice_fusion.13, bf16[512,2048]{1,0:T(8,128)(2,1)} %collective-permute-done.9, s32[]{:T(128)S(6)} %select_n.91), kind=kLoop, calls=%fused_computation.46 | loop fusion | bytes 4194308 | tf_op jit(solution)/shard_map/dynamic_update_slice | solution.py:202
  185.9 3.2 %constant_dynamic-update-slice_fusion.9 = bf16[2048,4096]{1,0:T(8,128)(2,1)} fusion(bf16[2048,4096]{1,0:T(8,128)(2,1)} %constant_dynamic-update-slice_fusion.12, bf16[512,2048]{1,0:T(8,128)(2,1)} %collective-permute-done.10, s32[]{:T(128)S(6)} %select_n.89), kind=kLoop, calls=%fused_computation.43 | loop fusion | bytes 4194308 | tf_op jit(solution)/shard_map/dynamic_update_slice | solution.py:202
  189.1 3.1 %constant_dynamic-update-slice_fusion.8.cot_ref = bf16[2048,4096]{1,0:T(8,128)(2,1)} fusion(bf16[2048,4096]{1,0:T(8,128)(2,1)} %constant_dynamic-update-slice_fusion.9, bf16[512,2048]{1,0:T(8,128)(2,1)} %collective-permute-done.11, s32[]{:T(128)S(6)} %select_n.91), kind=kLoop, calls=%fused_computation.42 | loop fusion | bytes 4194308 | tf_op jit(solution)/shard_map/dynamic_update_slice | solution.py:202
  192.3 29.2 %shard_map.103.before_ref = f32[2048,32]{1,0:T(8,128)S(1)} custom-call(bf16[2048,4096]{1,0:T(8,128)(2,1)} %constant_dynamic-update-slice_fusion.8.cot_ref, bf16[2048,1120]{1,0:T(8,128)(2,1)S(1)} %bitcast.19, bf16[1120,32]{1,0:T(8,128)(2,1)S(1)} %copy.69.factor_ref, f32[2048,32]{1,0:T(8,128)S(1)} %broadcast_in_dim.5.before_ref, ...), custom_call_target="tpu_custom_call" | custom-call | flops 18790481920 | bytes 30539776 | tf_op jit(solution)/shard_map/pallas_call | solution.py:67
  225.4 9.1 %shard_map.104 = f32[2048,32]{1,0:T(8,128)S(1)} custom-call(bf16[2048,4096]{1,0:T(8,128)(2,1)} %constant_dynamic-update-slice_fusion.8.cot_ref, bf16[2048,256]{1,0:T(8,128)(2,1)S(1)} %constant_dynamic-update-slice_fusion.3.gate_ref, bf16[256,32]{1,0:T(8,128)(2,1)S(1)} %copy.65.factor_ref, f32[2048,32]{1,0:T(8,128)S(1)} %copy-done.5, ...), custom_call_target="tpu_custom_call" | custom-call | flops 4294967296 | bytes 19922944 | tf_op jit(solution)/shard_map/pallas_call | solution.py:67
  243.2 2.8 %collective-permute-done.16 = f32[16,1024]{1,0:T(8,128)S(1)} collective-permute-done((f32[16,1024]{1,0:T(8,128)S(1)}, f32[16,1024]{1,0:T(8,128)S(1)}, u32[]{:S(2)}, u32[]{:S(2)}) %collective-permute-start.16) | collective-permute-done | bytes 65568 | tf_op jit(solution)/shard_map/ppermute | solution.py:25
  248.3 3.0 %collective-permute-start.20 = (f32[16,1024]{1,0:T(8,128)S(1)}, f32[16,1024]{1,0:T(8,128)S(1)}, u32[]{:S(2)}, u32[]{:S(2)}) collective-permute-start(f32[16,1024]{1,0:T(8,128)S(1)} %add.161.refs_0_), channel_id=1, source_target_pairs={{0,12},{4,0},{8,4},{12,8},{1,13},{5,1},{9,5},{13,9},{2,14},{6,2},{... | collective-permute-start | bytes 196616 | tf_op jit(solution)/shard_map/ppermute | solution.py:25
  251.3 2.9 %collective-permute-done.18.refs_1_ = f32[16,1024]{1,0:T(8,128)S(1)} collective-permute-done((f32[16,1024]{1,0:T(8,128)S(1)}, f32[16,1024]{1,0:T(8,128)S(1)}, u32[]{:S(2)}, u32[]{:S(2)}) %collective-permute-start.18) | collective-permute-done | bytes 65568 | tf_op jit(solution)/shard_map/ppermute | solution.py:25
  257.7 7.0 %shard_map.105 = (f32[256,1024]{1,0:T(8,128)}, f32[16,512]{1,0:T(8,128)}) custom-call(s32[2]{0:T(128)S(1)} %pad_add_fusion.1.place_ref, f32[512,1024]{1,0:T(8,128)S(1)} %copy-done.2, f32[16,1024]{1,0:T(8,128)S(1)} %add.161.refs_0_, f32[16,1024]{1,0:T(8,128)S(1)} %collective-permute-done.18.refs_1_, f32[16,1024]{1,0:T(8,128)S(1)} %collective-permute-done.19.refs_2_, ...), custom_call_target="tpu_custom_call" | custom-call | tf_op jit(solution)/shard_map/pallas_call | solution.py:148
  (129 shorter events, 49.8 us)
Async XLA Ops:
  7.2 168.8 %all-gather.3.cloned.1.call-start = ((), (), s32[]{:S(2)}) async-start(), calls=%async_computation | async-start | bytes 11468800 | tf_op jit(solution)/shard_map/all_gather | solution.py:176
  10.6 9.1 %copy-start.12 = (s32[1,16]{1,0:T(1,128)S(1)}, s32[1,16]{1,0:T(1,128)}, u32[]{:S(2)}) copy-start(s32[1,16]{1,0:T(1,128)} %param.14) | copy-start | bytes 196
  10.6 211.9 %all-gather.5.cloned.1.call-start = ((), (), s32[]{:S(2)}) async-start(), calls=%async_computation.1 | async-start | bytes 2621440 | tf_op jit(solution)/shard_map/all_gather | solution.py:181
  12.2 5.2 %collective-permute-start = (f32[512,32]{0,1:T(8,128)S(1)}, f32[512,32]{0,1:T(8,128)S(1)}, u32[]{:S(2)}, u32[]{:S(2)}) collective-permute-start(f32[512,32]{0,1:T(8,128)S(1)} %fusion.23), channel_id=1, source_target_pairs={{0,2},{2,0},{1,3},{3,1},{4,6},{6,4},{5,7},{7,5},{8,10},{10,8},{9,1... | collective-permute-start | bytes 196616 | tf_op jit(solution)/shard_map/ppermute | solution.py:25
  17.5 6.6 %collective-permute-start.1 = (f32[512,32]{0,1:T(8,128)S(1)}, f32[512,32]{0,1:T(8,128)S(1)}, u32[]{:S(2)}, u32[]{:S(2)}) collective-permute-start(f32[512,32]{0,1:T(8,128)S(1)} %add.131), channel_id=1, source_target_pairs={{0,1},{1,0},{16,17},{17,16},{2,3},{3,2},{18,19},{19,18},{4,5},{5,4... | collective-permute-start | bytes 196616 | tf_op jit(solution)/shard_map/ppermute | solution.py:25
  17.5 6.5 %collective-permute-start.2 = (f32[512,32]{0,1:T(8,128)S(1)}, f32[512,32]{0,1:T(8,128)S(1)}, u32[]{:S(2)}, u32[]{:S(2)}) collective-permute-start(f32[512,32]{0,1:T(8,128)S(1)} %add.131), channel_id=1, source_target_pairs={{0,16},{1,17},{16,0},{17,1},{2,18},{3,19},{18,2},{19,3},{4,20},{5,... | collective-permute-start | bytes 196616 | tf_op jit(solution)/shard_map/ppermute | solution.py:25
  19.7 4.4 %collective-permute-start.3 = (f32[512,32]{0,1:T(8,128)S(1)}, f32[512,32]{0,1:T(8,128)S(1)}, u32[]{:S(2)}, u32[]{:S(2)}) collective-permute-start(f32[512,32]{0,1:T(8,128)S(1)} %add.131), channel_id=1, source_target_pairs={{0,17},{1,16},{16,1},{17,0},{2,19},{3,18},{18,3},{19,2},{4,21},{5,... | collective-permute-start | bytes 196616 | tf_op jit(solution)/shard_map/ppermute | solution.py:25
  19.7 4.3 %collective-permute-start.4 = (s32[1,16]{1,0:T(1,128)S(1)}, s32[1,16]{1,0:T(1,128)S(1)}, u32[]{:S(2)}, u32[]{:S(2)}) collective-permute-start(s32[1,16]{1,0:T(1,128)S(1)} %copy-done.12), channel_id=1, source_target_pairs={{0,16},{16,0},{1,17},{17,1},{2,18},{18,2},{3,19},{19,3},{4,20},{20... | collective-permute-start | bytes 200 | tf_op jit(solution)/shard_map/ppermute | solution.py:25
  24.0 14.7 %copy-start.13 = (f32[512,32]{0,1:T(8,128)}, f32[512,32]{0,1:T(8,128)S(1)}, u32[]{:S(2)}) copy-start(f32[512,32]{0,1:T(8,128)S(1)} %collective-permute-done.1) | copy-start | bytes 196612
  24.1 47.7 %collective-permute-start.6 = (bf16[512,2048]{1,0:T(8,128)(2,1)}, bf16[512,2048]{1,0:T(8,128)(2,1)}, u32[]{:S(2)}, u32[]{:S(2)}) collective-permute-start(bf16[512,2048]{1,0:T(8,128)(2,1)} %param.9), channel_id=1, source_target_pairs={{0,16},{16,0},{1,17},{17,1},{2,18},{18,2},{3,19},{19,3},{4,20},{20... | collective-permute-start | bytes 6291464 | tf_op jit(solution)/shard_map/ppermute | solution.py:25
  27.8 67.7 %collective-permute-start.5 = (bf16[512,2048]{1,0:T(8,128)(2,1)}, bf16[512,2048]{1,0:T(8,128)(2,1)}, u32[]{:S(2)}, u32[]{:S(2)}) collective-permute-start(bf16[512,2048]{1,0:T(8,128)(2,1)} %param.9), channel_id=1, source_target_pairs={{0,2},{2,0},{1,3},{3,1},{4,6},{6,4},{5,7},{7,5},{8,10},{10,8},{9,1... | collective-permute-start | bytes 6291464 | tf_op jit(solution)/shard_map/ppermute | solution.py:25
  42.7 41.7 %collective-permute-start.12 = (bf16[512,1376]{0,1:T(8,128)(2,1)S(1)}, bf16[512,1376]{0,1:T(8,128)(2,1)}, u32[]{:S(2)}, u32[]{:S(2)}) collective-permute-start(bf16[512,1376]{0,1:T(8,128)(2,1)S(1)} %get-tuple-element.31), channel_id=1, source_target_pairs={{0,1},{1,0},{16,17},{17,16},{2,3},{3,2},{18,19},{19,18},{4,5},{5,4... | collective-permute-start | bytes 4227080 | tf_op jit(solution)/shard_map/ppermute | solution.py:25
  71.8 48.2 %collective-permute-start.7 = (bf16[512,2048]{1,0:T(8,128)(2,1)}, bf16[512,2048]{1,0:T(8,128)(2,1)}, u32[]{:S(2)}, u32[]{:S(2)}) collective-permute-start(bf16[512,2048]{1,0:T(8,128)(2,1)} %collective-permute-done.6), channel_id=1, source_target_pairs={{0,2},{2,0},{1,3},{3,1},{4,6},{6,4},{5,7},{7,5},{8,10},{10,8},{9,1... | collective-permute-start | bytes 6291464 | tf_op jit(solution)/shard_map/ppermute | solution.py:25
  73.3 34.2 %collective-permute-start.13 = (bf16[512,1376]{0,1:T(8,128)(2,1)}, bf16[512,1376]{0,1:T(8,128)(2,1)}, u32[]{:S(2)}, u32[]{:S(2)}) collective-permute-start(bf16[512,1376]{0,1:T(8,128)(2,1)} %get-tuple-element.30), channel_id=1, source_target_pairs={{0,16},{1,17},{16,0},{17,1},{2,18},{3,19},{18,2},{19,3},{4,20},{5,... | collective-permute-start | bytes 4227080 | tf_op jit(solution)/shard_map/ppermute | solution.py:25
  74.7 59.4 %collective-permute-start.14 = (bf16[512,1376]{0,1:T(8,128)(2,1)}, bf16[512,1376]{0,1:T(8,128)(2,1)}, u32[]{:S(2)}, u32[]{:S(2)}) collective-permute-start(bf16[512,1376]{0,1:T(8,128)(2,1)} %get-tuple-element.29), channel_id=1, source_target_pairs={{0,17},{1,16},{16,1},{17,0},{2,19},{3,18},{18,3},{19,2},{4,21},{5,... | collective-permute-start | bytes 4227080 | tf_op jit(solution)/shard_map/ppermute | solution.py:25
  84.4 5.8 %copy-start.7 = (bf16[2048,4096]{1,0:T(8,128)(2,1)}, bf16[2048,4096]{1,0:T(8,128)(2,1)S(1)}, u32[]{:S(2)}) copy-start(bf16[2048,4096]{1,0:T(8,128)(2,1)S(1)} %constant_dynamic-update-slice_fusion.7) | copy-start | bytes 50331652
  84.4 94.7 %collective-permute-start.8 = (bf16[512,2048]{1,0:T(8,128)(2,1)}, bf16[512,2048]{1,0:T(8,128)(2,1)}, u32[]{:S(2)}, u32[]{:S(2)}) collective-permute-start(bf16[512,2048]{1,0:T(8,128)(2,1)} %param.9), channel_id=1, source_target_pairs={{0,1},{1,0},{2,3},{3,2},{4,5},{5,4},{6,7},{7,6},{8,9},{9,8},{10,11... | collective-permute-start | bytes 6291464 | tf_op jit(solution)/shard_map/ppermute | solution.py:25
  95.5 86.9 %collective-permute-start.9 = (bf16[512,2048]{1,0:T(8,128)(2,1)}, bf16[512,2048]{1,0:T(8,128)(2,1)}, u32[]{:S(2)}, u32[]{:S(2)}) collective-permute-start(bf16[512,2048]{1,0:T(8,128)(2,1)} %collective-permute-done.5), channel_id=1, source_target_pairs={{0,1},{1,0},{2,3},{3,2},{4,5},{5,4},{6,7},{7,6},{8,9},{9,8},{10,11... | collective-permute-start | bytes 6291464 | tf_op jit(solution)/shard_map/ppermute | solution.py:25
  111.5 74.4 %collective-permute-start.10 = (bf16[512,2048]{1,0:T(8,128)(2,1)}, bf16[512,2048]{1,0:T(8,128)(2,1)}, u32[]{:S(2)}, u32[]{:S(2)}) collective-permute-start(bf16[512,2048]{1,0:T(8,128)(2,1)} %collective-permute-done.6), channel_id=1, source_target_pairs={{0,1},{1,0},{2,3},{3,2},{4,5},{5,4},{6,7},{7,6},{8,9},{9,8},{10,11... | collective-permute-start | bytes 6291464 | tf_op jit(solution)/shard_map/ppermute | solution.py:25
  120.0 69.1 %collective-permute-start.11 = (bf16[512,2048]{1,0:T(8,128)(2,1)}, bf16[512,2048]{1,0:T(8,128)(2,1)}, u32[]{:S(2)}, u32[]{:S(2)}) collective-permute-start(bf16[512,2048]{1,0:T(8,128)(2,1)} %collective-permute-done.7), channel_id=1, source_target_pairs={{0,1},{1,0},{2,3},{3,2},{4,5},{5,4},{6,7},{7,6},{8,9},{9,8},{10,11... | collective-permute-start | bytes 6291464 | tf_op jit(solution)/shard_map/ppermute | solution.py:25
  182.4 9.9 %slice-start = ((s8[4718592]{0:T(1024)(128)(4,1)}), s8[4194304]{0:T(1024)(128)(4,1)S(1)}, s32[]{:S(2)}) async-start(s8[4718592]{0:T(1024)(128)(4,1)} %bitcast.18), calls=%async_computation.2 | async-start | bytes 8388608
  185.9 6.4 %slice-start.1 = ((s8[4718592]{0:T(1024)(128)(4,1)}), s8[524288]{0:T(1024)(128)(4,1)S(1)}, s32[]{:S(2)}) async-start(s8[4718592]{0:T(1024)(128)(4,1)} %bitcast.18), calls=%async_computation.3 | async-start | bytes 1048576
  234.6 4.5 %copy-start.10 = (f32[512,32]{0,1:T(8,128)S(1)}, f32[512,32]{0,1:T(8,128)}, u32[]{:S(2)}) copy-start(f32[512,32]{0,1:T(8,128)} %copy-done.9) | copy-start | bytes 196612
  234.6 4.5 %copy-start.11 = (f32[1024,16]{0,1:T(8,128)S(1)}, f32[1024,16]{0,1:T(8,128)}, u32[]{:S(2)}) copy-start(f32[1024,16]{0,1:T(8,128)} %fusion.18) | copy-start | bytes 196612
  237.4 4.3 %collective-permute-start.15 = (f32[16,1024]{1,0:T(8,128)S(1)}, f32[16,1024]{1,0:T(8,128)S(1)}, u32[]{:S(2)}, u32[]{:S(2)}) collective-permute-start(f32[16,1024]{1,0:T(8,128)S(1)} %reshape.68), channel_id=1, source_target_pairs={{0,16},{16,0},{1,17},{17,1},{2,18},{18,2},{3,19},{19,3},{4,20},{20... | collective-permute-start | bytes 196616 | tf_op jit(solution)/shard_map/ppermute | solution.py:25
  239.1 25.6 %copy-start.1 = (bf16[512,2048]{1,0:T(8,128)(2,1)S(1)}, bf16[512,2048]{1,0:T(8,128)(2,1)}, u32[]{:S(2)}) copy-start(bf16[512,2048]{1,0:T(8,128)(2,1)} %param.8) | copy-start | bytes 6291460
  241.7 4.3 %collective-permute-start.16 = (f32[16,1024]{1,0:T(8,128)S(1)}, f32[16,1024]{1,0:T(8,128)S(1)}, u32[]{:S(2)}, u32[]{:S(2)}) collective-permute-start(f32[16,1024]{1,0:T(8,128)S(1)} %add.159), channel_id=1, source_target_pairs={{0,2},{2,0},{1,3},{3,1},{4,6},{6,4},{5,7},{7,5},{8,10},{10,8},{9,1... | collective-permute-start | bytes 196616 | tf_op jit(solution)/shard_map/ppermute | solution.py:25
  246.0 1.3 collective-permute-start.17
  247.4 17.3 %copy-start.6 = (f32[16,1024]{1,0:T(8,128)}, f32[16,1024]{1,0:T(8,128)S(1)}, u32[]{:S(2)}) copy-start(f32[16,1024]{1,0:T(8,128)S(1)} %add.161.refs_0_) | copy-start | bytes 196612
  247.4 6.8 %collective-permute-start.18 = (f32[16,1024]{1,0:T(8,128)S(1)}, f32[16,1024]{1,0:T(8,128)S(1)}, u32[]{:S(2)}, u32[]{:S(2)}) collective-permute-start(f32[16,1024]{1,0:T(8,128)S(1)} %add.161.refs_0_), channel_id=1, source_target_pairs={{0,4},{4,8},{8,12},{12,0},{1,5},{5,9},{9,13},{13,1},{2,6},{6,10},{... | collective-permute-start | bytes 196616 | tf_op jit(solution)/shard_map/ppermute | solution.py:25
  247.4 8.6 %collective-permute-start.19 = (f32[16,1024]{1,0:T(8,128)S(1)}, f32[16,1024]{1,0:T(8,128)S(1)}, u32[]{:S(2)}, u32[]{:S(2)}) collective-permute-start(f32[16,1024]{1,0:T(8,128)S(1)} %add.161.refs_0_), channel_id=1, source_target_pairs={{0,8},{4,12},{8,0},{12,4},{1,9},{5,13},{9,1},{13,5},{2,10},{6,14},... | collective-permute-start | bytes 196616 | tf_op jit(solution)/shard_map/ppermute | solution.py:25
  248.3 7.8 %collective-permute-start.20 = (f32[16,1024]{1,0:T(8,128)S(1)}, f32[16,1024]{1,0:T(8,128)S(1)}, u32[]{:S(2)}, u32[]{:S(2)}) collective-permute-start(f32[16,1024]{1,0:T(8,128)S(1)} %add.161.refs_0_), channel_id=1, source_target_pairs={{0,12},{4,0},{8,4},{12,8},{1,13},{5,1},{9,5},{13,9},{2,14},{6,2},{... | collective-permute-start | bytes 196616 | tf_op jit(solution)/shard_map/ppermute | solution.py:25
  (12 other events, 21.3 us)
Sparse Core Ops, SparseCore 0:
  10.8 165.1 all-gather.2
  177.5 44.1 all-gather.4

commit v6 on v5

--- a/solution.py
+++ b/solution.py
@@ -8,7 +8,7 @@
 from jax.sharding import PartitionSpec as P
 
 HIGHEST = lax.Precision.HIGHEST
-LAST = 256
+LATE = 256
 LANES = 128
 
 
@@ -49,40 +49,52 @@
     return jnp.sum(gather_in_order(x[None], axis, 0), axis=0)
 
 
-def chunk_kernel(contract, cot_ref, gate_ref, factor_ref, before_ref, weight_ref, after_ref):
-    hidden = lax.dot_general(
-        cot_ref[...], weight_ref[...], (((1,), (contract,)), ((), ())), preferred_element_type=jnp.float32
-    )
-    gate = gate_ref[...].astype(jnp.float32)
+def chunk_kernel(n, skip, me_ref, cot_ref, gate_ref, factor_ref, before_ref, *rest):
+    slots, after_ref = rest[:n], rest[n]
+    height, columns = slots[0].shape
+    hidden = None
+    for r in range(n):
+        owner = lax.rem(me_ref[0] + (n - r), n)
+        block = cot_ref[:, pl.ds(pl.multiple_of(owner * columns, columns), columns)]
+        term = lax.dot_general(
+            block, slots[r][...], (((1,), (1,)), ((), ())), preferred_element_type=jnp.float32
+        )
+        hidden = term if hidden is None else hidden + term
+    gate = gate_ref[:, skip:skip + height].astype(jnp.float32)
     up_grad = (hidden * (gate / (1.0 + jnp.exp(-gate)))).astype(jnp.bfloat16)
     after_ref[...] = before_ref[...] + jnp.dot(
         up_grad, factor_ref[...], preferred_element_type=jnp.float32
     )
 
 
-def add_chunk(cot, gate, factor, before, weight, contract, tile):
+def add_chunk(me, cot, gate, low, factor, before, slots, tile):
     tokens, depth = cot.shape
-    height = gate.shape[1]
-    rank = factor.shape[1]
+    height, rank = factor.shape
+    aligned = low % height == 0 and height % LANES == 0
+    width, skip = (height, 0) if aligned else (gate.shape[1], low)
+    at = low // height if aligned else 0
+    n = len(slots)
     return pl.pallas_call(
-        functools.partial(chunk_kernel, contract),
+        functools.partial(chunk_kernel, n, skip),
         out_shape=jax.ShapeDtypeStruct((tokens, rank), jnp.float32),
-        grid=(tokens // tile,),
-        in_specs=[
-            pl.BlockSpec((tile, depth), lambda i: (i, 0)),
-            pl.BlockSpec((tile, height), lambda i: (i, 0)),
-            pl.BlockSpec((height, rank), lambda i: (0, 0)),
-            pl.BlockSpec((tile, rank), lambda i: (i, 0)),
-            pl.BlockSpec(weight.shape, lambda i: (0, 0)),
-        ],
-        out_specs=pl.BlockSpec((tile, rank), lambda i: (i, 0)),
-        compiler_params=pltpu.CompilerParams(vmem_limit_bytes=44 * 1024 * 1024),
+        grid_spec=pltpu.PrefetchScalarGridSpec(
+            num_scalar_prefetch=1,
+            grid=(tokens // tile,),
+            in_specs=[
+                pl.BlockSpec((tile, depth), lambda i, me: (i, 0)),
+                pl.BlockSpec((tile, width), lambda i, me: (i, at)),
+                pl.BlockSpec((height, rank), lambda i, me: (0, 0)),
+                pl.BlockSpec((tile, rank), lambda i, me: (i, 0)),
+            ] + [pl.BlockSpec(slots[0].shape, lambda i, me: (0, 0))] * n,
+            out_specs=pl.BlockSpec((tile, rank), lambda i, me: (i, 0)),
+        ),
+        compiler_params=pltpu.CompilerParams(vmem_limit_bytes=36 * 1024 * 1024),
         cost_estimate=pl.CostEstimate(
             flops=2 * tokens * depth * height,
             bytes_accessed=2 * (tokens * depth + height * depth + tokens * height),
             transcendentals=tokens * height,
         ),
-    )(cot, gate, factor, before, weight)
+    )(me, cot, gate, factor, before, *slots)
 
 
 def dot3(a, b, dims):
@@ -173,44 +185,55 @@
     sizes = (n_groups, n_seq)
     mine = group * n_seq + half
 
-    early = lax.all_gather(
-        lax.dynamic_slice_in_dim(down_weight, mine * part + LAST, part - LAST, 0), "dp", axis=1, tiled=True
-    )
-    piece = lax.dynamic_slice_in_dim(down_weight, mine * part, LAST, 0).T
-    piece, early = lax.optimization_barrier((piece, early))
-    late = lax.all_gather(piece, "dp", axis=0, tiled=True)
+    passed = LATE
+    spans = [(passed + LATE, part), (0, passed), (passed, passed + LATE)]
+    first, ringed, last = [
+        lax.dynamic_slice_in_dim(down_weight, mine * part + low, high - low, 0) for low, high in spans
+    ]
+    first = lax.all_gather(first, "dp", axis=1, tiled=True)
+    last, first = lax.optimization_barrier((last, first))
+    last = lax.all_gather(last, "dp", axis=1, tiled=True)
+    ring = [ringed]
+    for _ in range(n_dp - 1):
+        ring.append(shifted(ring[-1], "dp", (n_dp,), (1,)))
+    chunks = [[first], ring, [last]]
 
     order = [(dg, ds) for dg in range(n_groups) for ds in range(n_seq)]
-    right = sum_over(jnp.dot(inputs, proj_in, preferred_element_type=jnp.float32), "tensor")
-    rights = [right if dg == ds == 0 else shifted(right, pair, sizes, (dg, ds)) for dg, ds in order]
-    lens = [doc_lens if dg == 0 else shifted(doc_lens, "groups", (n_groups,), (dg,)) for dg in range(n_groups)]
-    rights, lens, cotangent, gate_pre = lax.optimization_barrier((rights, lens, cotangent, gate_pre))
-
     cot = jnp.zeros((len(order) * rows, n_tensor * cotangent.shape[1]), cotangent.dtype)
-    gate_late = jnp.zeros((len(order) * rows, LAST), gate_pre.dtype)
-    gate_early = jnp.zeros((len(order) * rows, part - LAST), gate_pre.dtype)
-    placed = []
+    gate = jnp.zeros((len(order) * rows, part), gate_pre.dtype)
+    placed, spots = [], []
     for dg in range(n_groups):
         own = cotangent if dg == 0 else shifted(cotangent, "groups", (n_groups,), (dg,))
         pieces = [own if r == 0 else shifted(own, "tensor", (n_tensor,), (r,)) for r in range(n_tensor)]
         for ds in range(n_seq):
             for r, piece in enumerate(pieces):
                 moved = piece if ds == 0 else shifted(piece, "seq", (n_seq,), (ds,))
-                placed.append((ds, dg, r, moved))
-    for ds, dg, r, piece in sorted(placed, key=lambda p: p[:3]):
+                placed.append(moved)
+                spots.append((ds, dg, r))
+    moved_gates = []
+    for dg, ds in order:
+        to = ((group + dg) % n_groups) * n_seq + (half + ds) % n_seq
+        columns = lax.dynamic_slice_in_dim(gate_pre, to * part, part, 1)
+        moved_gates.append(columns if dg == ds == 0 else shifted(columns, pair, sizes, (dg, ds)))
+    right_part = jnp.dot(inputs, proj_in, preferred_element_type=jnp.float32)
+    right_part, doc_lens, placed, moved_gates = lax.optimization_barrier(
+        (right_part, doc_lens, placed, moved_gates)
+    )
+    right = sum_over(right_part, "tensor")
+    rights = [right if dg == ds == 0 else shifted(right, pair, sizes, (dg, ds)) for dg, ds in order]
+    lens = [doc_lens if dg == 0 else shifted(doc_lens, "groups", (n_groups,), (dg,)) for dg in range(n_groups)]
+
+    for (ds, dg, r), piece in sorted(zip(spots, placed), key=lambda p: p[0]):
         at = ((side - r) % n_tensor) * piece.shape[1]
         cot = lax.dynamic_update_slice(cot, piece, ((dg * n_seq + ds) * rows, at))
-    for number, (dg, ds) in enumerate(order):
-        to = ((group + dg) % n_groups) * n_seq + (half + ds) % n_seq
-        columns = lax.dynamic_slice_in_dim(gate_pre, to * part, part, 1)
-        piece = columns if dg == ds == 0 else shifted(columns, pair, sizes, (dg, ds))
-        gate_late = lax.dynamic_update_slice(gate_late, piece[:, :LAST], (number * rows, 0))
-        gate_early = lax.dynamic_update_slice(gate_early, piece[:, LAST:], (number * rows, 0))
+    for number, piece in enumerate(moved_gates):
+        gate = lax.dynamic_update_slice(gate, piece, (number * rows, 0))
 
     out_factor = lax.dynamic_slice_in_dim(proj_out, mine * part, part, 0)
     left = jnp.zeros((n_groups * n_seq * rows, rank), jnp.float32)
-    left = add_chunk(cot, gate_early, out_factor[LAST:], left, early, 1, rows)
-    left = add_chunk(cot, gate_late, out_factor[:LAST], left, late, 0, rows)
+    me = jnp.reshape(stage, (1,)).astype(jnp.int32)
+    for slots, (low, high) in zip(chunks, spans):
+        left = add_chunk(me, cot, gate, low, out_factor[low:high], left, slots, rows)
 
     parts = []
     for dg in range(n_groups):

time: 273 us -> 339 us (1.24)
  waiting for transfers between devices: 101 us -> 137 us
  starting transfers between devices: 21.7 us -> 43.2 us
  matrix products: 4.27 us -> 7.7 us
    ppermute x21 -> x24, waiting for transfers between devices: 71.4 us -> 136 us  [shifted(): return lax.ppermute(x, axes, pairs)]
    all_gather x2, waiting for transfers between devices: 29.2 us -> 1.52 us  [the longest x1 1.52 us: on_device(): last = lax.all_gather(last, 'dp', axis=1, tiled=True)]
    ppermute x21 -> x24, starting transfers between devices: 21.6 us -> 43.1 us  [shifted(): return lax.ppermute(x, axes, pairs)]
    slice x10 -> x2, local copies, waits for them, and re-layouts: 15 us -> 1.82 us  [on_device(): out_factor[low:high]]
    dynamic_slice x1, local copies, waits for them, and re-layouts: 4 us -> 8.13 us  [on_device(): columns = lax.dynamic_slice_in_dim(gate_pre, to * part, part, 1)]
    broadcast_in_dim x1, local copies, waits for them, and re-layouts: 1.91 us -> 6 us  [on_device(): jnp.zeros((len(order) * rows, n_tensor * cotangent.shape[1]), cotangent.d...]
    unnamed x51 -> x56, local copies, waits for them, and re-layouts: 18.5 us -> 22.1 us
    dynamic_update_slice x8 -> x4, local copies, waits for them, and re-layouts: 6.07 us -> 8.15 us  [on_device(): gate = lax.dynamic_update_slice(gate, piece, (number * rows, 0))]
  transfers between devices with their start and end apart: 23 -> 26, of which waited for: 12 -> 8; matrix products, arithmetic and copies ran while one was open for 26% -> 23% of each run, Pallas kernels for 11% -> 12%
where the time goes in v6:
time: 339 us; the launch traced here: 338 us
  waiting for transfers between devices  137 us (40%)
  local copies, waits for them, and re-layouts  84.7 us (25%)
  Pallas kernels  47.1 us (14%)
  starting transfers between devices  43.2 us (13%)
  between operations  14.4 us (4%)
  matrix products  7.7 us (2%)
    ppermute x24, waiting for transfers between devices, shifted(): return lax.ppermute(x, axes, pairs)  136 us
    ppermute x24, starting transfers between devices, shifted(): return lax.ppermute(x, axes, pairs)  43.1 us
    pallas_call x3, Pallas kernels, add_chunk(): pl.pallas_call(functools.partial(chunk_kernel, n, skip), out_shape=jax.Sh...  40 us
    dynamic_update_slice x8, local copies, waits for them, and re-layouts, on_device(): cot = lax.dynamic_update_slice(cot, piece, ((dg * n_seq + ds) * rows, at))  24.7 us
    unnamed x56, local copies, waits for them, and re-layouts  22.1 us
    dynamic_update_slice x4, local copies, waits for them, and re-layouts, on_device(): gate = lax.dynamic_update_slice(gate, piece, (number * rows, 0))  8.15 us
    dynamic_slice x1, local copies, waits for them, and re-layouts, on_device(): columns = lax.dynamic_slice_in_dim(gate_pre, to * part, part, 1)  8.13 us
    optimization_barrier x3, local copies, waits for them, and re-layouts, on_device(): lax.optimization_barrier((right_part, doc_lens, placed, moved_gates))  7.75 us
  transfers between devices with their start and end apart: 26, of which 8 were waited for; matrix products, arithmetic and copies ran while one was open for 23% of the time, Pallas kernels for 12%

profile of v6, /device:TPU:0, one launch (start us, length us, event | category | flops | bytes accessed | tf_op | source)
XLA Modules:
  0.0 337.8 jit_solution(9468288483634294074)
XLA Ops:
  7.2 3.0 constant_dynamic-slice_fusion.3
  10.3 3.0 collective-permute-start.3
  14.8 44.5 %collective-permute-done.3 = bf16[512,2048]{1,0:T(8,128)(2,1)} collective-permute-done((bf16[512,2048]{1,0:T(8,128)(2,1)}, bf16[512,2048]{1,0:T(8,128)(2,1)}, u32[]{:S(2)}, u32[]{:S(2)}) %collective-permute-start.3) | collective-permute-done | bytes 2097184 | tf_op jit(solution)/shard_map/ppermute | solution.py:25
  61.0 8.1 %constant_dynamic-slice_fusion.6 = (bf16[512,1376]{1,0:T(8,128)(2,1)}, bf16[512,1376]{1,0:T(8,128)(2,1)}, bf16[512,1376]{1,0:T(8,128)(2,1)S(1)}, bf16[512,1376]{1,0:T(8,128)(2,1)}) fusion(bf16[512,5504]{1,0:T(8,128)(2,1)} %param.10, s32[]{:T(128)S(6)} %select_n.98, s32[]{:T(128)S(6)} %select_n.97, s32[]{:T(128)S(6)} %select_n.95, s32[]{:T(128)S(6)} %select_n.93), kind=kLoop, calls=%fused_computation.34 | loop fusion | bytes 11272208 | tf_op jit(solution)/shard_map/dynamic_slice | solution.py:216
  78.5 22.0 %collective-permute-done.10.rest_1_ = bf16[256,1024]{1,0:T(8,128)(2,1)S(1)} collective-permute-done((bf16[256,1024]{1,0:T(8,128)(2,1)S(1)}, bf16[256,1024]{1,0:T(8,128)(2,1)S(1)}, u32[]{:S(2)}, u32[]{:S(2)}) %collective-permute-start.10) | collective-permute-done | bytes 524320 | tf_op jit(solution)/shard_map/ppermute | solution.py:25
  100.5 8.3 %collective-permute-start.11 = (bf16[256,1024]{1,0:T(8,128)(2,1)S(1)}, bf16[256,1024]{1,0:T(8,128)(2,1)S(1)}, u32[]{:S(2)}, u32[]{:S(2)}) collective-permute-start(bf16[256,1024]{1,0:T(8,128)(2,1)S(1)} %collective-permute-done.10.rest_1_), channel_id=1, source_target_pairs={{0,4},{4,8},{8,12},{12,0},{1,5},{5,9},{9,13},{13,1},{2,6},{6,10},{... | collective-permute-start | bytes 1572872 | tf_op jit(solution)/shard_map/ppermute | solution.py:25
  108.8 34.1 %collective-permute-done.11.rest_2_ = bf16[256,1024]{1,0:T(8,128)(2,1)S(1)} collective-permute-done((bf16[256,1024]{1,0:T(8,128)(2,1)S(1)}, bf16[256,1024]{1,0:T(8,128)(2,1)S(1)}, u32[]{:S(2)}, u32[]{:S(2)}) %collective-permute-start.11) | collective-permute-done | bytes 524320 | tf_op jit(solution)/shard_map/ppermute | solution.py:25
  153.0 27.6 %collective-permute-done.9 = bf16[512,1376]{0,1:T(8,128)(2,1)} collective-permute-done((bf16[512,1376]{0,1:T(8,128)(2,1)}, bf16[512,1376]{0,1:T(8,128)(2,1)}, u32[]{:S(2)}, u32[]{:S(2)}) %collective-permute-start.9) | collective-permute-done | bytes 1409056 | tf_op jit(solution)/shard_map/ppermute | solution.py:25
  180.6 8.6 %collective-permute-start.12 = (bf16[256,1024]{1,0:T(8,128)(2,1)S(1)}, bf16[256,1024]{1,0:T(8,128)(2,1)S(1)}, u32[]{:S(2)}, u32[]{:S(2)}) collective-permute-start(bf16[256,1024]{1,0:T(8,128)(2,1)S(1)} %copy-done.12), channel_id=1, source_target_pairs={{0,4},{4,8},{8,12},{12,0},{1,5},{5,9},{9,13},{13,1},{2,6},{6,10},{... | collective-permute-start | bytes 1572872 | tf_op jit(solution)/shard_map/ppermute | solution.py:25
  194.3 2.6 copy.43
  198.6 2.9 dynamic_update_slice.44
  201.6 6.0 %broadcast_in_dim.4 = bf16[2048,4096]{1,0:T(8,128)(2,1)} broadcast(bf16[]{:T(256)} %constant.94.clone.1), dimensions={} | broadcast | bytes 16777218 | tf_op jit(solution)/shard_map/broadcast_in_dim | solution.py:202
  209.2 3.2 constant_dynamic-update-slice_fusion.3
  212.5 3.3 constant_dynamic-update-slice_fusion.8
  215.7 3.3 constant_dynamic-update-slice_fusion.7
  219.0 3.3 constant_dynamic-update-slice_fusion.10
  222.3 3.3 constant_dynamic-update-slice_fusion.9
  225.6 3.3 constant_dynamic-update-slice_fusion.6
  228.9 3.4 constant_dynamic-update-slice_fusion.5.cot_ref
  233.5 2.7 constant_dynamic-update-slice_fusion.1
  243.0 2.9 copy-done.2
  245.9 3.0 copy-done.17
  248.9 21.7 %shard_map.103.before_ref = f32[2048,32]{1,0:T(8,128)S(1)} custom-call(s32[1]{0:T(128)} %bitcast.me_ref, bf16[2048,4096]{1,0:T(8,128)(2,1)} %constant_dynamic-update-slice_fusion.5.cot_ref, bf16[2048,1376]{1,0:T(8,128)(2,1)S(1)} %copy-done.2, bf16[864,32]{1,0:T(8,128)(2,1)S(1)} %copy.57.factor_ref, f32[2048,32]{1,0:T(8,128)S(1)} %broadcast_in_dim.5.before_ref, ...), custom_call_target="tpu_custom_call" | custom-call | flops 14495514624 | bytes 27394048 | tf_op jit(solution)/shard_map/pallas_call | solution.py:77
  272.5 9.1 %shard_map.104.before_ref = f32[2048,32]{1,0:T(8,128)S(1)} custom-call(s32[1]{0:T(128)} %bitcast.me_ref, bf16[2048,4096]{1,0:T(8,128)(2,1)} %constant_dynamic-update-slice_fusion.5.cot_ref, bf16[2048,1376]{1,0:T(8,128)(2,1)S(1)} %copy-done.3, bf16[256,32]{1,0:T(8,128)(2,1)S(1)} %copy.56.factor_ref, f32[2048,32]{1,0:T(8,128)S(1)} %shard_map.103.before_ref, ...), custom_call_target="tpu_custom_call" | custom-call | flops 4294967296 | bytes 19922944 | tf_op jit(solution)/shard_map/pallas_call | solution.py:77
  283.1 2.6 copy-done.4
  287.4 9.3 %shard_map.105 = f32[2048,32]{1,0:T(8,128)S(1)} custom-call(s32[1]{0:T(128)} %bitcast.me_ref, bf16[2048,4096]{1,0:T(8,128)(2,1)} %constant_dynamic-update-slice_fusion.5.cot_ref, bf16[2048,1376]{1,0:T(8,128)(2,1)S(1)} %copy-done.4, bf16[256,32]{1,0:T(8,128)(2,1)S(1)} %copy.55.factor_ref, f32[2048,32]{1,0:T(8,128)S(1)} %shard_map.104.before_ref, ...), custom_call_target="tpu_custom_call" | custom-call | flops 4294967296 | bytes 19922944 | tf_op jit(solution)/shard_map/pallas_call | solution.py:77
  297.5 2.6 fusion.7
  302.1 2.8 fusion.4
  306.7 2.8 collective-permute-done.19
  310.8 5.4 %collective-permute-start.21 = (f32[16,1024]{1,0:T(8,128)S(1)}, f32[16,1024]{1,0:T(8,128)S(1)}, u32[]{:S(2)}, u32[]{:S(2)}) collective-permute-start(f32[16,1024]{1,0:T(8,128)S(1)} %add.169.refs_0_), channel_id=1, source_target_pairs={{0,4},{4,8},{8,12},{12,0},{1,5},{5,9},{9,13},{13,1},{2,6},{6,10},{... | collective-permute-start | bytes 196616 | tf_op jit(solution)/shard_map/ppermute | solution.py:25
  318.8 3.6 %collective-permute-done.22.refs_2_ = f32[16,1024]{1,0:T(8,128)S(1)} collective-permute-done((f32[16,1024]{1,0:T(8,128)S(1)}, f32[16,1024]{1,0:T(8,128)S(1)}, u32[]{:S(2)}, u32[]{:S(2)}) %collective-permute-start.22) | collective-permute-done | bytes 65568 | tf_op jit(solution)/shard_map/ppermute | solution.py:25
  324.0 7.0 %shard_map.106 = (f32[256,1024]{1,0:T(8,128)}, f32[16,512]{1,0:T(8,128)}) custom-call(s32[2]{0:T(128)S(1)} %pad_add_fusion.1.place_ref, f32[512,1024]{1,0:T(8,128)S(1)} %copy-done.6, f32[16,1024]{1,0:T(8,128)S(1)} %add.169.refs_0_, f32[16,1024]{1,0:T(8,128)S(1)} %collective-permute-done.21.refs_1_, f32[16,1024]{1,0:T(8,128)S(1)} %collective-permute-done.22.refs_2_, ...), custom_call_target="tpu_custom_call" | custom-call | tf_op jit(solution)/shard_map/pallas_call | solution.py:160
  (130 shorter events, 54.0 us)
Async XLA Ops:
  7.2 143.5 %copy-start = (bf16[512,2048]{1,0:T(8,128)(2,1)S(1)}, bf16[512,2048]{1,0:T(8,128)(2,1)}, u32[]{:S(2)}) copy-start(bf16[512,2048]{1,0:T(8,128)(2,1)} %param.8) | copy-start | bytes 6291460
  7.2 225.1 %all-gather.3.cloned.1.call-start = ((), (), s32[]{:S(2)}) async-start(), calls=%async_computation | async-start | bytes 8847360 | tf_op jit(solution)/shard_map/all_gather | solution.py:193
  10.3 272.9 %all-gather.5.cloned.1.call-start = ((), (), s32[]{:S(2)}) async-start(), calls=%async_computation.1 | async-start | bytes 2621440 | tf_op jit(solution)/shard_map/all_gather | solution.py:195
  10.3 49.0 %collective-permute-start.3 = (bf16[512,2048]{1,0:T(8,128)(2,1)}, bf16[512,2048]{1,0:T(8,128)(2,1)}, u32[]{:S(2)}, u32[]{:S(2)}) collective-permute-start(bf16[512,2048]{1,0:T(8,128)(2,1)} %param.9), channel_id=1, source_target_pairs={{0,16},{16,0},{1,17},{17,1},{2,18},{18,2},{3,19},{19,3},{4,20},{20... | collective-permute-start | bytes 6291464 | tf_op jit(solution)/shard_map/ppermute | solution.py:25
  13.3 130.8 %collective-permute-start = (bf16[512,2048]{1,0:T(8,128)(2,1)}, bf16[512,2048]{1,0:T(8,128)(2,1)}, u32[]{:S(2)}, u32[]{:S(2)}) collective-permute-start(bf16[512,2048]{1,0:T(8,128)(2,1)} %param.9), channel_id=1, source_target_pairs={{0,2},{2,0},{1,3},{3,1},{4,6},{6,4},{5,7},{7,5},{8,10},{10,8},{9,1... | collective-permute-start | bytes 6291464 | tf_op jit(solution)/shard_map/ppermute | solution.py:25
  59.3 85.0 %collective-permute-start.4 = (bf16[512,2048]{1,0:T(8,128)(2,1)}, bf16[512,2048]{1,0:T(8,128)(2,1)}, u32[]{:S(2)}, u32[]{:S(2)}) collective-permute-start(bf16[512,2048]{1,0:T(8,128)(2,1)} %collective-permute-done.3), channel_id=1, source_target_pairs={{0,2},{2,0},{1,3},{3,1},{4,6},{6,4},{5,7},{7,5},{8,10},{10,8},{9,1... | collective-permute-start | bytes 6291464 | tf_op jit(solution)/shard_map/ppermute | solution.py:25
  70.7 73.0 %collective-permute-start.7 = (bf16[512,1376]{0,1:T(8,128)(2,1)}, bf16[512,1376]{0,1:T(8,128)(2,1)}, u32[]{:S(2)}, u32[]{:S(2)}) collective-permute-start(bf16[512,1376]{0,1:T(8,128)(2,1)} %copy.51), channel_id=1, source_target_pairs={{0,1},{1,0},{16,17},{17,16},{2,3},{3,2},{18,19},{19,18},{4,5},{5,4... | collective-permute-start | bytes 4227080 | tf_op jit(solution)/shard_map/ppermute | solution.py:25
  72.7 74.5 %copy-start.7 = (bf16[256,1024]{1,0:T(8,128)(2,1)}, bf16[256,1024]{1,0:T(8,128)(2,1)S(1)}, u32[]{:S(2)}) copy-start(bf16[256,1024]{1,0:T(8,128)(2,1)S(1)} %get-tuple-element.41.rest_0_) | copy-start | bytes 1572868
  72.7 27.7 %collective-permute-start.10 = (bf16[256,1024]{1,0:T(8,128)(2,1)S(1)}, bf16[256,1024]{1,0:T(8,128)(2,1)S(1)}, u32[]{:S(2)}, u32[]{:S(2)}) collective-permute-start(bf16[256,1024]{1,0:T(8,128)(2,1)S(1)} %get-tuple-element.41.rest_0_), channel_id=1, source_target_pairs={{0,4},{4,8},{8,12},{12,0},{1,5},{5,9},{9,13},{13,1},{2,6},{6,10},{... | collective-permute-start | bytes 1572872 | tf_op jit(solution)/shard_map/ppermute | solution.py:25
  77.0 70.3 %collective-permute-start.8 = (bf16[512,1376]{0,1:T(8,128)(2,1)}, bf16[512,1376]{0,1:T(8,128)(2,1)}, u32[]{:S(2)}, u32[]{:S(2)}) collective-permute-start(bf16[512,1376]{0,1:T(8,128)(2,1)} %copy.52), channel_id=1, source_target_pairs={{0,16},{1,17},{16,0},{17,1},{2,18},{3,19},{18,2},{19,3},{4,20},{5,... | collective-permute-start | bytes 4227080 | tf_op jit(solution)/shard_map/ppermute | solution.py:25
  100.5 52.5 %copy-start.9 = (bf16[256,1024]{1,0:T(8,128)(2,1)}, bf16[256,1024]{1,0:T(8,128)(2,1)S(1)}, u32[]{:S(2)}) copy-start(bf16[256,1024]{1,0:T(8,128)(2,1)S(1)} %collective-permute-done.10.rest_1_) | copy-start | bytes 1572868
  100.5 42.4 %collective-permute-start.11 = (bf16[256,1024]{1,0:T(8,128)(2,1)S(1)}, bf16[256,1024]{1,0:T(8,128)(2,1)S(1)}, u32[]{:S(2)}, u32[]{:S(2)}) collective-permute-start(bf16[256,1024]{1,0:T(8,128)(2,1)S(1)} %collective-permute-done.10.rest_1_), channel_id=1, source_target_pairs={{0,4},{4,8},{8,12},{12,0},{1,5},{5,9},{9,13},{13,1},{2,6},{6,10},{... | collective-permute-start | bytes 1572872 | tf_op jit(solution)/shard_map/ppermute | solution.py:25
  143.7 45.5 %collective-permute-start.1 = (bf16[512,2048]{1,0:T(8,128)(2,1)}, bf16[512,2048]{1,0:T(8,128)(2,1)}, u32[]{:S(2)}, u32[]{:S(2)}) collective-permute-start(bf16[512,2048]{1,0:T(8,128)(2,1)} %param.9), channel_id=1, source_target_pairs={{0,1},{1,0},{2,3},{3,2},{4,5},{5,4},{6,7},{7,6},{8,9},{9,8},{10,11... | collective-permute-start | bytes 6291464 | tf_op jit(solution)/shard_map/ppermute | solution.py:25
  143.7 45.5 %collective-permute-start.5 = (bf16[512,2048]{1,0:T(8,128)(2,1)}, bf16[512,2048]{1,0:T(8,128)(2,1)}, u32[]{:S(2)}, u32[]{:S(2)}) collective-permute-start(bf16[512,2048]{1,0:T(8,128)(2,1)} %collective-permute-done.3), channel_id=1, source_target_pairs={{0,1},{1,0},{2,3},{3,2},{4,5},{5,4},{6,7},{7,6},{8,9},{9,8},{10,11... | collective-permute-start | bytes 6291464 | tf_op jit(solution)/shard_map/ppermute | solution.py:25
  144.2 45.0 %collective-permute-start.2 = (bf16[512,2048]{1,0:T(8,128)(2,1)}, bf16[512,2048]{1,0:T(8,128)(2,1)}, u32[]{:S(2)}, u32[]{:S(2)}) collective-permute-start(bf16[512,2048]{1,0:T(8,128)(2,1)} %collective-permute-done), channel_id=1, source_target_pairs={{0,1},{1,0},{2,3},{3,2},{4,5},{5,4},{6,7},{7,6},{8,9},{9,8},{10,11... | collective-permute-start | bytes 6291464 | tf_op jit(solution)/shard_map/ppermute | solution.py:25
  144.3 45.0 %collective-permute-start.6 = (bf16[512,2048]{1,0:T(8,128)(2,1)}, bf16[512,2048]{1,0:T(8,128)(2,1)}, u32[]{:S(2)}, u32[]{:S(2)}) collective-permute-start(bf16[512,2048]{1,0:T(8,128)(2,1)} %collective-permute-done.4), channel_id=1, source_target_pairs={{0,1},{1,0},{2,3},{3,2},{4,5},{5,4},{6,7},{7,6},{8,9},{9,8},{10,11... | collective-permute-start | bytes 6291464 | tf_op jit(solution)/shard_map/ppermute | solution.py:25
  147.2 33.3 %copy-start.12 = (bf16[256,1024]{1,0:T(8,128)(2,1)S(1)}, bf16[256,1024]{1,0:T(8,128)(2,1)}, u32[]{:S(2)}) copy-start(bf16[256,1024]{1,0:T(8,128)(2,1)} %copy-done.11) | copy-start | bytes 1572868
  147.2 33.3 %collective-permute-start.9 = (bf16[512,1376]{0,1:T(8,128)(2,1)}, bf16[512,1376]{0,1:T(8,128)(2,1)}, u32[]{:S(2)}, u32[]{:S(2)}) collective-permute-start(bf16[512,1376]{0,1:T(8,128)(2,1)} %copy.53), channel_id=1, source_target_pairs={{0,17},{1,16},{16,1},{17,0},{2,19},{3,18},{18,3},{19,2},{4,21},{5,... | collective-permute-start | bytes 4227080 | tf_op jit(solution)/shard_map/ppermute | solution.py:25
  180.6 90.1 %collective-permute-start.12 = (bf16[256,1024]{1,0:T(8,128)(2,1)S(1)}, bf16[256,1024]{1,0:T(8,128)(2,1)S(1)}, u32[]{:S(2)}, u32[]{:S(2)}) collective-permute-start(bf16[256,1024]{1,0:T(8,128)(2,1)S(1)} %copy-done.12), channel_id=1, source_target_pairs={{0,4},{4,8},{8,12},{12,0},{1,5},{5,9},{9,13},{13,1},{2,6},{6,10},{... | collective-permute-start | bytes 1572872 | tf_op jit(solution)/shard_map/ppermute | solution.py:25
  197.0 42.3 %collective-permute-start.13 = (f32[512,32]{0,1:T(8,128)}, f32[512,32]{0,1:T(8,128)}, u32[]{:S(2)}, u32[]{:S(2)}) collective-permute-start(f32[512,32]{0,1:T(8,128)} %fusion.23), channel_id=1, source_target_pairs={{0,2},{2,0},{1,3},{3,1},{4,6},{6,4},{5,7},{7,5},{8,10},{10,8},{9,1... | collective-permute-start | bytes 196616 | tf_op jit(solution)/shard_map/ppermute | solution.py:25
  197.0 40.7 %collective-permute-start.15 = (s32[1,16]{1,0:T(1,128)S(1)}, s32[1,16]{1,0:T(1,128)S(1)}, u32[]{:S(2)}, u32[]{:S(2)}) collective-permute-start(s32[1,16]{1,0:T(1,128)S(1)} %copy-done.24), channel_id=1, source_target_pairs={{0,16},{16,0},{1,17},{17,1},{2,18},{18,2},{3,19},{19,3},{4,20},{20... | collective-permute-start | bytes 200 | tf_op jit(solution)/shard_map/ppermute | solution.py:25
  240.8 56.1 %collective-permute-start.16 = (f32[512,32]{0,1:T(8,128)}, f32[512,32]{0,1:T(8,128)}, u32[]{:S(2)}, u32[]{:S(2)}) collective-permute-start(f32[512,32]{0,1:T(8,128)} %add.166), channel_id=1, source_target_pairs={{0,16},{1,17},{16,0},{17,1},{2,18},{3,19},{18,2},{19,3},{4,20},{5,... | collective-permute-start | bytes 196616 | tf_op jit(solution)/shard_map/ppermute | solution.py:25
  241.3 55.6 %collective-permute-start.17 = (f32[512,32]{0,1:T(8,128)}, f32[512,32]{0,1:T(8,128)}, u32[]{:S(2)}, u32[]{:S(2)}) collective-permute-start(f32[512,32]{0,1:T(8,128)} %add.166), channel_id=1, source_target_pairs={{0,17},{1,16},{16,1},{17,0},{2,19},{3,18},{18,3},{19,2},{4,21},{5,... | collective-permute-start | bytes 196616 | tf_op jit(solution)/shard_map/ppermute | solution.py:25
  241.7 60.4 %collective-permute-start.14 = (f32[512,32]{0,1:T(8,128)}, f32[512,32]{0,1:T(8,128)}, u32[]{:S(2)}, u32[]{:S(2)}) collective-permute-start(f32[512,32]{0,1:T(8,128)} %add.166), channel_id=1, source_target_pairs={{0,1},{1,0},{16,17},{17,16},{2,3},{3,2},{18,19},{19,18},{4,5},{5,4... | collective-permute-start | bytes 196616 | tf_op jit(solution)/shard_map/ppermute | solution.py:25
  248.9 22.6 %copy-start.13 = (bf16[256,1024]{1,0:T(8,128)(2,1)S(1)}, bf16[256,1024]{1,0:T(8,128)(2,1)}, u32[]{:S(2)}) copy-start(bf16[256,1024]{1,0:T(8,128)(2,1)} %copy-done.11) | copy-start | bytes 1572868
  300.3 4.8 %collective-permute-start.18 = (f32[16,1024]{1,0:T(8,128)S(1)}, f32[16,1024]{1,0:T(8,128)S(1)}, u32[]{:S(2)}, u32[]{:S(2)}) collective-permute-start(f32[16,1024]{1,0:T(8,128)S(1)} %reshape.72), channel_id=1, source_target_pairs={{0,16},{16,0},{1,17},{17,1},{2,18},{18,2},{3,19},{19,3},{4,20},{20... | collective-permute-start | bytes 196616 | tf_op jit(solution)/shard_map/ppermute | solution.py:25
  302.1 28.9 %copy-start.1 = (bf16[512,2048]{1,0:T(8,128)(2,1)S(1)}, bf16[512,2048]{1,0:T(8,128)(2,1)}, u32[]{:S(2)}) copy-start(bf16[512,2048]{1,0:T(8,128)(2,1)} %param.8) | copy-start | bytes 6291460
  305.2 4.3 %collective-permute-start.19 = (f32[16,1024]{1,0:T(8,128)S(1)}, f32[16,1024]{1,0:T(8,128)S(1)}, u32[]{:S(2)}, u32[]{:S(2)}) collective-permute-start(f32[16,1024]{1,0:T(8,128)S(1)} %add.167), channel_id=1, source_target_pairs={{0,2},{2,0},{1,3},{3,1},{4,6},{6,4},{5,7},{7,5},{8,10},{10,8},{9,1... | collective-permute-start | bytes 196616 | tf_op jit(solution)/shard_map/ppermute | solution.py:25
  309.5 1.3 collective-permute-start.20
  310.8 8.0 %collective-permute-start.21 = (f32[16,1024]{1,0:T(8,128)S(1)}, f32[16,1024]{1,0:T(8,128)S(1)}, u32[]{:S(2)}, u32[]{:S(2)}) collective-permute-start(f32[16,1024]{1,0:T(8,128)S(1)} %add.169.refs_0_), channel_id=1, source_target_pairs={{0,4},{4,8},{8,12},{12,0},{1,5},{5,9},{9,13},{13,1},{2,6},{6,10},{... | collective-permute-start | bytes 196616 | tf_op jit(solution)/shard_map/ppermute | solution.py:25
  316.3 6.1 %collective-permute-start.22 = (f32[16,1024]{1,0:T(8,128)S(1)}, f32[16,1024]{1,0:T(8,128)S(1)}, u32[]{:S(2)}, u32[]{:S(2)}) collective-permute-start(f32[16,1024]{1,0:T(8,128)S(1)} %add.169.refs_0_), channel_id=1, source_target_pairs={{0,8},{4,12},{8,0},{12,4},{1,9},{5,13},{9,1},{13,5},{2,10},{6,14},... | collective-permute-start | bytes 196616 | tf_op jit(solution)/shard_map/ppermute | solution.py:25
  316.3 6.1 %collective-permute-start.23 = (f32[16,1024]{1,0:T(8,128)S(1)}, f32[16,1024]{1,0:T(8,128)S(1)}, u32[]{:S(2)}, u32[]{:S(2)}) collective-permute-start(f32[16,1024]{1,0:T(8,128)S(1)} %add.169.refs_0_), channel_id=1, source_target_pairs={{0,12},{4,0},{8,4},{12,8},{1,13},{5,1},{9,5},{13,9},{2,14},{6,2},{... | collective-permute-start | bytes 196616 | tf_op jit(solution)/shard_map/ppermute | solution.py:25
  (19 other events, 127.5 us)
Sparse Core Ops, SparseCore 0:
  10.4 153.2 all-gather.2
  232.4 50.6 all-gather.4

commit v7 on v6

--- a/solution.py
+++ b/solution.py
@@ -8,7 +8,7 @@
 from jax.sharding import PartitionSpec as P
 
 HIGHEST = lax.Precision.HIGHEST
-LATE = 256
+CUTS = (0, 512, 768, 1024)
 LANES = 128
 
 
@@ -74,6 +74,14 @@
     width, skip = (height, 0) if aligned else (gate.shape[1], low)
     at = low // height if aligned else 0
     n = len(slots)
+    columns = slots[0].shape[1]
+    if low % height:
+        slots = [slot if slot.shape[0] == height else slot[low:low + height] for slot in slots]
+
+    def weight_spec(slot):
+        block = 0 if slot.shape[0] == height else low // height
+        return pl.BlockSpec((height, columns), lambda i, me: (block, 0))
+
     return pl.pallas_call(
         functools.partial(chunk_kernel, n, skip),
         out_shape=jax.ShapeDtypeStruct((tokens, rank), jnp.float32),
@@ -85,7 +93,7 @@
                 pl.BlockSpec((tile, width), lambda i, me: (i, at)),
                 pl.BlockSpec((height, rank), lambda i, me: (0, 0)),
                 pl.BlockSpec((tile, rank), lambda i, me: (i, 0)),
-            ] + [pl.BlockSpec(slots[0].shape, lambda i, me: (0, 0))] * n,
+            ] + [weight_spec(slot) for slot in slots],
             out_specs=pl.BlockSpec((tile, rank), lambda i, me: (i, 0)),
         ),
         compiler_params=pltpu.CompilerParams(vmem_limit_bytes=36 * 1024 * 1024),
@@ -185,49 +193,79 @@
     sizes = (n_groups, n_seq)
     mine = group * n_seq + half
 
-    passed = LATE
-    spans = [(passed + LATE, part), (0, passed), (passed, passed + LATE)]
-    first, ringed, last = [
-        lax.dynamic_slice_in_dim(down_weight, mine * part + low, high - low, 0) for low, high in spans
+    lows = [low for low in CUTS if low < part]
+    spans = list(zip(lows, lows[1:] + [part]))
+    spans = spans[:1] + spans[3:] + spans[1:3]
+    ring = [lax.dynamic_slice_in_dim(down_weight, mine * part, part, 0)]
+
+    def across(x, ds):
+        return shifted(x, "seq", (n_seq,), (ds,))
+
+    order = [(dg, ds) for dg in range(n_groups) for ds in range(n_seq)]
+
+    def unit_columns(dg, ds):
+        to = ((group + dg) % n_groups) * n_seq + (half + ds) % n_seq
+        return lax.dynamic_slice_in_dim(gate_pre, to * part, part, 1)
+
+    cots = {(0, 0, 0): cotangent}
+    for dg in range(1, n_groups):
+        cots[dg, 0, 0] = shifted(cotangent, "groups", (n_groups,), (dg,))
+    for r in range(1, n_tensor):
+        cots[0, 0, r] = shifted(cotangent, "tensor", (n_tensor,), (r,))
+    sheets = {
+        dg: jnp.concatenate([unit_columns(dg, ds) for ds in range(n_seq)], axis=0)
+        for dg in range(n_groups)
+    }
+    for dg in range(1, n_groups):
+        sheets[dg] = shifted(sheets[dg], "groups", (n_groups,), (dg,))
+    turned = shifted(ring[-1], "dp", (n_dp,), (1,))
+    turned, cots = lax.optimization_barrier((turned, cots))
+    ring.append(turned)
+
+    gates, more = {}, {}
+
+    def spread(dg, sheet):
+        for ds in range(n_seq):
+            x = sheet[ds * rows:(ds + 1) * rows]
+            gates[dg, ds] = x if ds == 0 else across(x, ds)
+
+    spread(0, sheets[0])
+    for (dg, _, r), x in cots.items():
+        for ds in range(1, n_seq):
+            more[dg, ds, r] = across(x, ds)
+    for dg in range(1, n_groups):
+        for r in range(1, n_tensor):
+            more[dg, 0, r] = shifted(cots[dg, 0, 0], "tensor", (n_tensor,), (r,))
+    right_part = jnp.dot(inputs, proj_in, preferred_element_type=jnp.float32)
+    turned = shifted(ring[-1], "dp", (n_dp,), (1,)) if n_dp > 3 else ring.pop()
+    turned, cots, more, sheets, right_part, doc_lens = lax.optimization_barrier(
+        (turned, cots, more, sheets, right_part, doc_lens)
+    )
+    ring.append(turned)
+    cots.update(more)
+
+    for dg in range(1, n_groups):
+        for r in range(1, n_tensor):
+            for ds in range(1, n_seq):
+                cots[dg, ds, r] = across(cots[dg, 0, r], ds)
+        spread(dg, sheets[dg])
+    while len(ring) < n_dp - 1:
+        ring.append(shifted(ring[-1], "dp", (n_dp,), (1,)))
+    chunks = [
+        ring + ([shifted(ring[-1][low:high], "dp", (n_dp,), (1,))] if n_dp > 1 else [])
+        for low, high in spans
     ]
-    first = lax.all_gather(first, "dp", axis=1, tiled=True)
-    last, first = lax.optimization_barrier((last, first))
-    last = lax.all_gather(last, "dp", axis=1, tiled=True)
-    ring = [ringed]
-    for _ in range(n_dp - 1):
-        ring.append(shifted(ring[-1], "dp", (n_dp,), (1,)))
-    chunks = [[first], ring, [last]]
-
-    order = [(dg, ds) for dg in range(n_groups) for ds in range(n_seq)]
-    cot = jnp.zeros((len(order) * rows, n_tensor * cotangent.shape[1]), cotangent.dtype)
-    gate = jnp.zeros((len(order) * rows, part), gate_pre.dtype)
-    placed, spots = [], []
-    for dg in range(n_groups):
-        own = cotangent if dg == 0 else shifted(cotangent, "groups", (n_groups,), (dg,))
-        pieces = [own if r == 0 else shifted(own, "tensor", (n_tensor,), (r,)) for r in range(n_tensor)]
-        for ds in range(n_seq):
-            for r, piece in enumerate(pieces):
-                moved = piece if ds == 0 else shifted(piece, "seq", (n_seq,), (ds,))
-                placed.append(moved)
-                spots.append((ds, dg, r))
-    moved_gates = []
-    for dg, ds in order:
-        to = ((group + dg) % n_groups) * n_seq + (half + ds) % n_seq
-        columns = lax.dynamic_slice_in_dim(gate_pre, to * part, part, 1)
-        moved_gates.append(columns if dg == ds == 0 else shifted(columns, pair, sizes, (dg, ds)))
-    right_part = jnp.dot(inputs, proj_in, preferred_element_type=jnp.float32)
-    right_part, doc_lens, placed, moved_gates = lax.optimization_barrier(
-        (right_part, doc_lens, placed, moved_gates)
-    )
     right = sum_over(right_part, "tensor")
     rights = [right if dg == ds == 0 else shifted(right, pair, sizes, (dg, ds)) for dg, ds in order]
     lens = [doc_lens if dg == 0 else shifted(doc_lens, "groups", (n_groups,), (dg,)) for dg in range(n_groups)]
 
-    for (ds, dg, r), piece in sorted(zip(spots, placed), key=lambda p: p[0]):
-        at = ((side - r) % n_tensor) * piece.shape[1]
-        cot = lax.dynamic_update_slice(cot, piece, ((dg * n_seq + ds) * rows, at))
-    for number, piece in enumerate(moved_gates):
-        gate = lax.dynamic_update_slice(gate, piece, (number * rows, 0))
+    cot = jnp.zeros((len(order) * rows, n_tensor * cotangent.shape[1]), cotangent.dtype)
+    gate = jnp.zeros((len(order) * rows, part), gate_pre.dtype)
+    for (dg, ds, r), block in sorted(cots.items(), key=lambda item: (item[0][1] * item[0][0] * item[0][2], item[0])):
+        at = ((side - r) % n_tensor) * cotangent.shape[1]
+        cot = lax.dynamic_update_slice(cot, block, ((dg * n_seq + ds) * rows, at))
+    for number, place in enumerate(order):
+        gate = lax.dynamic_update_slice(gate, gates[place], (number * rows, 0))
 
     out_factor = lax.dynamic_slice_in_dim(proj_out, mine * part, part, 0)
     left = jnp.zeros((n_groups * n_seq * rows, rank), jnp.float32)

time: 339 us -> 284 us (0.84)
  waiting for transfers between devices: 137 us -> 102 us
  starting transfers between devices: 43.2 us -> 23.5 us
  between operations: 14.4 us -> 1 us
  local copies, waits for them, and re-layouts: 84.7 us -> 94.7 us
  Pallas kernels: 47.1 us -> 52.7 us
  matrix products: 7.7 us -> 4.28 us
    ppermute x24 -> x27, waiting for transfers between devices: 136 us -> 102 us  [shifted(): return lax.ppermute(x, axes, pairs)]
    ppermute x24 -> x27, starting transfers between devices: 43.1 us -> 23.5 us  [shifted(): return lax.ppermute(x, axes, pairs)]
    slice x0 -> x6, local copies, waits for them, and re-layouts: none -> 11.4 us  [the longest x2 4.55 us: on_device(): ring[-1][low:high]]
    pallas_call x3 -> x4, Pallas kernels: 40 us -> 45.7 us  [add_chunk(): pl.pallas_call(functools.partial(chunk_kernel, n, skip), out_shape=jax.Sh...]
    ppermute x0 -> x2, local copies, waits for them, and re-layouts: none -> 4.36 us  [shifted(): return lax.ppermute(x, axes, pairs)]
    concatenate x0 -> x1, other arithmetic: none -> 3.69 us  [on_device(): jnp.concatenate([unit_columns(dg, ds) for ds in range(n_seq)], axis=0)]
    optimization_barrier x3 -> x1, local copies, waits for them, and re-layouts: 7.75 us -> 4.58 us  [on_device(): lax.optimization_barrier((turned, cots, more, sheets, right_part, doc_lens))]
    unnamed x56 -> x39, local copies, waits for them, and re-layouts: 22.1 us -> 19.3 us
  transfers between devices with their start and end apart: 26 -> 27, of which waited for: 8 -> 12; matrix products, arithmetic and copies ran while one was open for 23% -> 34% of each run, Pallas kernels for 12% -> 16%
where the time goes in v7:
time: 284 us; the launch traced here: 283 us
  waiting for transfers between devices  102 us (36%)
  local copies, waits for them, and re-layouts  94.7 us (33%)
  Pallas kernels  52.7 us (19%)
  starting transfers between devices  23.5 us (8%)
  matrix products  4.28 us (2%)
  other arithmetic  4.24 us (1%)
    ppermute x27, waiting for transfers between devices, shifted(): return lax.ppermute(x, axes, pairs)  102 us
    pallas_call x4, Pallas kernels, add_chunk(): pl.pallas_call(functools.partial(chunk_kernel, n, skip), out_shape=jax.Sh...  45.7 us
    dynamic_update_slice x8, local copies, waits for them, and re-layouts, on_device(): cot = lax.dynamic_update_slice(cot, block, ((dg * n_seq + ds) * rows, at))  23.9 us
    ppermute x27, starting transfers between devices, shifted(): return lax.ppermute(x, axes, pairs)  23.5 us
    unnamed x39, local copies, waits for them, and re-layouts  19.3 us
    dynamic_slice x1, local copies, waits for them, and re-layouts, unit_columns(): return lax.dynamic_slice_in_dim(gate_pre, to * part, part, 1)  8.04 us
    dynamic_update_slice x4, local copies, waits for them, and re-layouts, on_device(): gate = lax.dynamic_update_slice(gate, gates[place], (number * rows, 0))  7.9 us
    pallas_call x1, Pallas kernels, finish(): pl.pallas_call(functools.partial(final_kernel, n, share), out_shape=(jax....  7.01 us
  transfers between devices with their start and end apart: 27, of which 12 were waited for; matrix products, arithmetic and copies ran while one was open for 34% of the time, Pallas kernels for 16%

profile of v7, /device:TPU:0, one launch (start us, length us, event | category | flops | bytes accessed | tf_op | source)
XLA Modules:
  0.0 282.7 jit_solution(839367691099927476)
XLA Ops:
  0.6 3.0 %collective-permute-start.1 = (bf16[512,2048]{1,0:T(8,128)(2,1)}, bf16[512,2048]{1,0:T(8,128)(2,1)}, u32[]{:S(2)}, u32[]{:S(2)}) collective-permute-start(bf16[512,2048]{1,0:T(8,128)(2,1)} %param.9), channel_id=1, source_target_pairs={{0,2},{2,0},{1,3},{3,1},{4,6},{6,4},{5,7},{7,5},{8,10},{10,8},{9,1... | collective-permute-start | bytes 6291464 | tf_op jit(solution)/shard_map/ppermute | solution.py:25
  5.2 3.6 %constant_dynamic-slice_fusion.9.rest_0_ = bf16[1376,1024]{1,0:T(8,128)(2,1)} fusion(bf16[5504,1024]{1,0:T(8,128)(2,1)} %param.11, s32[]{:T(128)S(6)} %select_n.85), kind=kLoop, calls=%fused_computation.38 | loop fusion | bytes 5636100 | tf_op jit(solution)/shard_map/dynamic_slice | solution.py:199
  10.3 8.0 %constant_dynamic-slice_fusion.5 = (bf16[512,1376]{1,0:T(8,128)(2,1)}, bf16[512,1376]{1,0:T(8,128)(2,1)}, bf16[512,1376]{1,0:T(8,128)(2,1)}, bf16[512,1376]{1,0:T(8,128)(2,1)S(1)}) fusion(bf16[512,5504]{1,0:T(8,128)(2,1)} %param.10, s32[]{:T(128)S(6)} %select_n.97, s32[]{:T(128)S(6)} %select_n.90, s32[]{:T(128)S(6)} %select_n.88, s32[]{:T(128)S(6)} %select_n.96), kind=kLoop, calls=%fused_computation.32 | loop fusion | bytes 11272208 | tf_op jit(solution)/shard_map/dynamic_slice | solution.py:208
  23.5 3.7 %pad_maximum_fusion = bf16[1024,1376]{0,1:T(8,128)(2,1)} fusion(bf16[512,1376]{0,1:T(8,128)(2,1)} %copy.52, bf16[512,1376]{0,1:T(8,128)(2,1)} %copy.51), kind=kLoop, calls=%fused_computation | loop fusion | flops 5636096 | bytes 5636096 | tf_op jit(solution)/shard_map/concatenate | solution.py:216
  30.3 19.3 %collective-permute-done.1 = bf16[512,2048]{1,0:T(8,128)(2,1)} collective-permute-done((bf16[512,2048]{1,0:T(8,128)(2,1)}, bf16[512,2048]{1,0:T(8,128)(2,1)}, u32[]{:S(2)}, u32[]{:S(2)}) %collective-permute-start.1) | collective-permute-done | bytes 2097184 | tf_op jit(solution)/shard_map/ppermute | solution.py:25
  49.6 2.9 %collective-permute-done.2 = bf16[512,2048]{1,0:T(8,128)(2,1)} collective-permute-done((bf16[512,2048]{1,0:T(8,128)(2,1)}, bf16[512,2048]{1,0:T(8,128)(2,1)}, u32[]{:S(2)}, u32[]{:S(2)}) %collective-permute-start.2) | collective-permute-done | bytes 2097184 | tf_op jit(solution)/shard_map/ppermute | solution.py:25
  52.5 20.7 %collective-permute-done.rest_1_ = bf16[1376,1024]{1,0:T(8,128)(2,1)} collective-permute-done((bf16[1376,1024]{1,0:T(8,128)(2,1)}, bf16[1376,1024]{1,0:T(8,128)(2,1)}, u32[]{:S(2)}, u32[]{:S(2)}) %collective-permute-start) | collective-permute-done | bytes 2818080 | tf_op jit(solution)/shard_map/ppermute | solution.py:25
  74.2 37.2 %collective-permute-done.8 = bf16[1024,1376]{0,1:T(8,128)(2,1)} collective-permute-done((bf16[1024,1376]{0,1:T(8,128)(2,1)}, bf16[1024,1376]{0,1:T(8,128)(2,1)}, u32[]{:S(2)}, u32[]{:S(2)}) %collective-permute-start.8) | collective-permute-done | bytes 2818080 | tf_op jit(solution)/shard_map/ppermute | solution.py:25
  121.0 2.9 %dynamic_update_slice.44 = bf16[2048,1376]{1,0:T(8,128)(2,1)} pad(bf16[512,1376]{1,0:T(8,128)(2,1)S(1)} %get-tuple-element.42, bf16[]{:T(256)} %constant.91.clone.1), padding=0_1536x0_0 | pad | bytes 7045122 | tf_op jit(solution)/shard_map/dynamic_update_slice | solution.py:268
  130.9 5.8 %collective-permute-done.3.rest_2_ = bf16[1376,1024]{1,0:T(8,128)(2,1)} collective-permute-done((bf16[1376,1024]{1,0:T(8,128)(2,1)}, bf16[1376,1024]{1,0:T(8,128)(2,1)}, u32[]{:S(2)}, u32[]{:S(2)}) %collective-permute-start.3) | collective-permute-done | bytes 2818080 | tf_op jit(solution)/shard_map/ppermute | solution.py:25
  139.8 6.2 %broadcast_in_dim.4 = bf16[2048,4096]{1,0:T(8,128)(2,1)} broadcast(bf16[]{:T(256)} %constant.91.clone.1), dimensions={} | broadcast | bytes 16777218 | tf_op jit(solution)/shard_map/broadcast_in_dim | solution.py:262
  147.4 3.2 %constant_dynamic-update-slice_fusion.2 = bf16[2048,4096]{1,0:T(8,128)(2,1)} fusion(bf16[2048,4096]{1,0:T(8,128)(2,1)} %constant_dynamic-update-slice_fusion.3, bf16[512,2048]{1,0:T(8,128)(2,1)} %collective-permute-done.1, s32[]{:T(128)S(6)} %select_n.94), kind=kLoop, calls=%fused_computation.34 | loop fusion | bytes 4194308 | tf_op jit(solution)/shard_map/dynamic_update_slice | solution.py:266
  150.6 3.2 %constant_dynamic-update-slice_fusion.9 = bf16[2048,4096]{1,0:T(8,128)(2,1)} fusion(bf16[2048,4096]{1,0:T(8,128)(2,1)} %constant_dynamic-update-slice_fusion.2, bf16[512,2048]{1,0:T(8,128)(2,1)} %collective-permute-done.4, s32[]{:T(128)S(6)} %select_n.92), kind=kLoop, calls=%fused_computation.46 | loop fusion | bytes 4194308 | tf_op jit(solution)/shard_map/dynamic_update_slice | solution.py:266
  153.7 3.2 %constant_dynamic-update-slice_fusion.8 = bf16[2048,4096]{1,0:T(8,128)(2,1)} fusion(bf16[2048,4096]{1,0:T(8,128)(2,1)} %constant_dynamic-update-slice_fusion.9, bf16[512,2048]{1,0:T(8,128)(2,1)} %collective-permute-done.5, s32[]{:T(128)S(6)} %select_n.94), kind=kLoop, calls=%fused_computation.45 | loop fusion | bytes 4194308 | tf_op jit(solution)/shard_map/dynamic_update_slice | solution.py:266
  156.9 3.2 %constant_dynamic-update-slice_fusion.7 = bf16[2048,4096]{1,0:T(8,128)(2,1)} fusion(bf16[2048,4096]{1,0:T(8,128)(2,1)} %constant_dynamic-update-slice_fusion.8, bf16[512,2048]{1,0:T(8,128)(2,1)} %collective-permute-done.2, s32[]{:T(128)S(6)} %select_n.92), kind=kLoop, calls=%fused_computation.44 | loop fusion | bytes 4194308 | tf_op jit(solution)/shard_map/dynamic_update_slice | solution.py:266
  160.1 3.2 %constant_dynamic-update-slice_fusion.6 = bf16[2048,4096]{1,0:T(8,128)(2,1)} fusion(bf16[2048,4096]{1,0:T(8,128)(2,1)} %constant_dynamic-update-slice_fusion.7, bf16[512,2048]{1,0:T(8,128)(2,1)} %collective-permute-done.6, s32[]{:T(128)S(6)} %select_n.94), kind=kLoop, calls=%fused_computation.43 | loop fusion | bytes 4194308 | tf_op jit(solution)/shard_map/dynamic_update_slice | solution.py:266
  165.5 4.6 %copy.42 = bf16[1024,1376]{1,0:T(8,128)(2,1)} copy(bf16[1024,1376]{0,1:T(8,128)(2,1)} %collective-permute-done.8) | data formatting | bytes 5636096 | tf_op jit(solution)/shard_map/optimization_barrier | solution.py:241
  174.4 3.4 %constant_dynamic-update-slice_fusion.5 = bf16[2048,4096]{1,0:T(8,128)(2,1)} fusion(bf16[2048,4096]{1,0:T(8,128)(2,1)} %constant_dynamic-update-slice_fusion.6, bf16[512,2048]{1,0:T(8,128)(2,1)} %collective-permute-done.7, s32[]{:T(128)S(6)} %select_n.92), kind=kLoop, calls=%fused_computation.42 | loop fusion | bytes 4194308 | tf_op jit(solution)/shard_map/dynamic_update_slice | solution.py:266
  180.4 3.0 %collective-permute-done.16 = f32[512,32]{0,1:T(8,128)S(1)} collective-permute-done((f32[512,32]{0,1:T(8,128)S(1)}, f32[512,32]{0,1:T(8,128)S(1)}, u32[]{:S(2)}, u32[]{:S(2)}) %collective-permute-start.16) | collective-permute-done | bytes 65568 | tf_op jit(solution)/shard_map/ppermute | solution.py:25
  184.3 4.2 %collective-permute-start.15 = (bf16[256,1024]{1,0:T(8,128)(2,1)}, bf16[256,1024]{1,0:T(8,128)(2,1)}, u32[]{:S(2)}, u32[]{:S(2)}) collective-permute-start(bf16[256,1024]{1,0:T(8,128)(2,1)} %get-tuple-element.43), channel_id=1, source_target_pairs={{0,4},{4,8},{8,12},{12,0},{1,5},{5,9},{9,13},{13,1},{2,6},{6,10},{... | collective-permute-start | bytes 1572872 | tf_op jit(solution)/shard_map/ppermute | solution.py:25
  191.0 2.6 constant_dynamic-update-slice_fusion.gate_ref
  195.1 3.1 %constant_dynamic-update-slice_fusion.4.cot_ref = bf16[2048,4096]{1,0:T(8,128)(2,1)} fusion(bf16[2048,4096]{1,0:T(8,128)(2,1)} %constant_dynamic-update-slice_fusion.5, bf16[512,2048]{1,0:T(8,128)(2,1)} %collective-permute-done.9, s32[]{:T(128)S(6)} %select_n.94), kind=kLoop, calls=%fused_computation.41 | loop fusion | bytes 4194308 | tf_op jit(solution)/shard_map/dynamic_update_slice | solution.py:266
  198.3 3.4 %collective-permute-done.12.rest_3_ = bf16[512,1024]{1,0:T(8,128)(2,1)S(1)} collective-permute-done((bf16[512,1024]{1,0:T(8,128)(2,1)}, bf16[512,1024]{1,0:T(8,128)(2,1)S(1)}, u32[]{:S(2)}, u32[]{:S(2)}) %collective-permute-start.12) | collective-permute-done | bytes 1048608 | tf_op jit(solution)/shard_map/ppermute | solution.py:25
  202.7 2.6 copy-done.2
  206.6 13.7 %shard_map.103.before_ref = f32[2048,32]{1,0:T(8,128)S(1)} custom-call(s32[1]{0:T(128)} %bitcast.me_ref, bf16[2048,4096]{1,0:T(8,128)(2,1)} %constant_dynamic-update-slice_fusion.4.cot_ref, bf16[2048,1376]{1,0:T(8,128)(2,1)S(1)} %copy-done.2, bf16[512,32]{1,0:T(8,128)(2,1)S(1)} %copy-done.7, f32[2048,32]{1,0:T(8,128)S(1)} %broadcast_in_dim.5.before_ref, ...), custom_call_target="tpu_custom_call" | custom-call | flops 8589934592 | bytes 23068672 | tf_op jit(solution)/shard_map/pallas_call | solution.py:85
  221.0 12.7 %shard_map.104.before_ref = f32[2048,32]{1,0:T(8,128)S(1)} custom-call(s32[1]{0:T(128)} %bitcast.me_ref, bf16[2048,4096]{1,0:T(8,128)(2,1)} %constant_dynamic-update-slice_fusion.4.cot_ref, bf16[2048,1376]{1,0:T(8,128)(2,1)S(1)} %copy-done.2, bf16[352,32]{1,0:T(8,128)(2,1)S(1)} %copy-done.8, f32[2048,32]{1,0:T(8,128)S(1)} %shard_map.103.before_ref, ...), custom_call_target="tpu_custom_call" | custom-call | flops 5905580032 | bytes 21102592 | tf_op jit(solution)/shard_map/pallas_call | solution.py:85
  233.7 9.7 %shard_map.105.before_ref = f32[2048,32]{1,0:T(8,128)S(1)} custom-call(s32[1]{0:T(128)} %bitcast.me_ref, bf16[2048,4096]{1,0:T(8,128)(2,1)} %constant_dynamic-update-slice_fusion.4.cot_ref, bf16[2048,1376]{1,0:T(8,128)(2,1)S(1)} %copy-done.2, bf16[256,32]{1,0:T(8,128)(2,1)S(1)} %copy-done.10, f32[2048,32]{1,0:T(8,128)S(1)} %shard_map.104.before_ref, ...), custom_call_target="tpu_custom_call" | custom-call | flops 4294967296 | bytes 19922944 | tf_op jit(solution)/shard_map/pallas_call | solution.py:85
  243.4 9.7 %shard_map.106 = f32[2048,32]{1,0:T(8,128)S(1)} custom-call(s32[1]{0:T(128)} %bitcast.me_ref, bf16[2048,4096]{1,0:T(8,128)(2,1)} %constant_dynamic-update-slice_fusion.4.cot_ref, bf16[2048,1376]{1,0:T(8,128)(2,1)S(1)} %copy-done.2, bf16[256,32]{1,0:T(8,128)(2,1)S(1)} %copy-done.9, f32[2048,32]{1,0:T(8,128)S(1)} %shard_map.105.before_ref, ...), custom_call_target="tpu_custom_call" | custom-call | flops 4294967296 | bytes 19922944 | tf_op jit(solution)/shard_map/pallas_call | solution.py:85
  260.7 3.3 %collective-permute-done.22 = f32[16,1024]{1,0:T(8,128)S(1)} collective-permute-done((f32[16,1024]{1,0:T(8,128)S(1)}, f32[16,1024]{1,0:T(8,128)S(1)}, u32[]{:S(2)}, u32[]{:S(2)}) %collective-permute-start.22) | collective-permute-done | bytes 65568 | tf_op jit(solution)/shard_map/ppermute | solution.py:25
  265.6 3.6 %collective-permute-start.26 = (f32[16,1024]{1,0:T(8,128)S(1)}, f32[16,1024]{1,0:T(8,128)S(1)}, u32[]{:S(2)}, u32[]{:S(2)}) collective-permute-start(f32[16,1024]{1,0:T(8,128)S(1)} %add.149.refs_0_), channel_id=1, source_target_pairs={{0,12},{4,0},{8,4},{12,8},{1,13},{5,1},{9,5},{13,9},{2,14},{6,2},{... | collective-permute-start | bytes 196616 | tf_op jit(solution)/shard_map/ppermute | solution.py:25
  269.3 2.9 %collective-permute-done.24.refs_1_ = f32[16,1024]{1,0:T(8,128)S(1)} collective-permute-done((f32[16,1024]{1,0:T(8,128)S(1)}, f32[16,1024]{1,0:T(8,128)S(1)}, u32[]{:S(2)}, u32[]{:S(2)}) %collective-permute-start.24) | collective-permute-done | bytes 65568 | tf_op jit(solution)/shard_map/ppermute | solution.py:25
  275.7 7.0 %shard_map.107 = (f32[256,1024]{1,0:T(8,128)}, f32[16,512]{1,0:T(8,128)}) custom-call(s32[2]{0:T(128)S(1)} %pad_add_fusion.1.place_ref, f32[512,1024]{1,0:T(8,128)S(1)} %copy-done.4, f32[16,1024]{1,0:T(8,128)S(1)} %add.149.refs_0_, f32[16,1024]{1,0:T(8,128)S(1)} %collective-permute-done.24.refs_1_, f32[16,1024]{1,0:T(8,128)S(1)} %collective-permute-done.25.refs_2_, ...), custom_call_target="tpu_custom_call" | custom-call | tf_op jit(solution)/shard_map/pallas_call | solution.py:168
  (121 shorter events, 63.1 us)
Async XLA Ops:
  0.6 125.3 %copy-start = (bf16[512,2048]{1,0:T(8,128)(2,1)S(1)}, bf16[512,2048]{1,0:T(8,128)(2,1)}, u32[]{:S(2)}) copy-start(bf16[512,2048]{1,0:T(8,128)(2,1)} %param.8) | copy-start | bytes 6291460
  0.6 49.0 %collective-permute-start.1 = (bf16[512,2048]{1,0:T(8,128)(2,1)}, bf16[512,2048]{1,0:T(8,128)(2,1)}, u32[]{:S(2)}, u32[]{:S(2)}) collective-permute-start(bf16[512,2048]{1,0:T(8,128)(2,1)} %param.9), channel_id=1, source_target_pairs={{0,2},{2,0},{1,3},{3,1},{4,6},{6,4},{5,7},{7,5},{8,10},{10,8},{9,1... | collective-permute-start | bytes 6291464 | tf_op jit(solution)/shard_map/ppermute | solution.py:25
  3.7 48.9 %collective-permute-start.2 = (bf16[512,2048]{1,0:T(8,128)(2,1)}, bf16[512,2048]{1,0:T(8,128)(2,1)}, u32[]{:S(2)}, u32[]{:S(2)}) collective-permute-start(bf16[512,2048]{1,0:T(8,128)(2,1)} %param.9), channel_id=1, source_target_pairs={{0,16},{16,0},{1,17},{17,1},{2,18},{18,2},{3,19},{19,3},{4,20},{20... | collective-permute-start | bytes 6291464 | tf_op jit(solution)/shard_map/ppermute | solution.py:25
  8.8 64.4 %collective-permute-start = (bf16[1376,1024]{1,0:T(8,128)(2,1)}, bf16[1376,1024]{1,0:T(8,128)(2,1)}, u32[]{:S(2)}, u32[]{:S(2)}) collective-permute-start(bf16[1376,1024]{1,0:T(8,128)(2,1)} %constant_dynamic-slice_fusion.9.rest_0_), channel_id=1, source_target_pairs={{0,4},{4,8},{8,12},{12,0},{1,5},{5,9},{9,13},{13,1},{2,6},{6,10},{... | collective-permute-start | bytes 8454152 | tf_op jit(solution)/shard_map/ppermute | solution.py:25
  27.2 84.2 %collective-permute-start.8 = (bf16[1024,1376]{0,1:T(8,128)(2,1)}, bf16[1024,1376]{0,1:T(8,128)(2,1)}, u32[]{:S(2)}, u32[]{:S(2)}) collective-permute-start(bf16[1024,1376]{0,1:T(8,128)(2,1)} %pad_maximum_fusion), channel_id=1, source_target_pairs={{0,16},{16,0},{1,17},{17,1},{2,18},{18,2},{3,19},{19,3},{4,20},{20... | collective-permute-start | bytes 8454152 | tf_op jit(solution)/shard_map/ppermute | solution.py:25
  30.3 43.5 %collective-permute-start.10 = (bf16[512,1376]{0,1:T(8,128)(2,1)}, bf16[512,1376]{0,1:T(8,128)(2,1)}, u32[]{:S(2)}, u32[]{:S(2)}) collective-permute-start(bf16[512,1376]{0,1:T(8,128)(2,1)} %copy.53), channel_id=1, source_target_pairs={{0,1},{1,0},{2,3},{3,2},{4,5},{5,4},{6,7},{7,6},{8,9},{9,8},{10,11... | collective-permute-start | bytes 4227080 | tf_op jit(solution)/shard_map/ppermute | solution.py:25
  73.2 63.5 %collective-permute-start.3 = (bf16[1376,1024]{1,0:T(8,128)(2,1)}, bf16[1376,1024]{1,0:T(8,128)(2,1)}, u32[]{:S(2)}, u32[]{:S(2)}) collective-permute-start(bf16[1376,1024]{1,0:T(8,128)(2,1)} %collective-permute-done.rest_1_), channel_id=1, source_target_pairs={{0,4},{4,8},{8,12},{12,0},{1,5},{5,9},{9,13},{13,1},{2,6},{6,10},{... | collective-permute-start | bytes 8454152 | tf_op jit(solution)/shard_map/ppermute | solution.py:25
  73.2 57.7 %collective-permute-start.6 = (bf16[512,2048]{1,0:T(8,128)(2,1)}, bf16[512,2048]{1,0:T(8,128)(2,1)}, u32[]{:S(2)}, u32[]{:S(2)}) collective-permute-start(bf16[512,2048]{1,0:T(8,128)(2,1)} %collective-permute-done.2), channel_id=1, source_target_pairs={{0,2},{2,0},{1,3},{3,1},{4,6},{6,4},{5,7},{7,5},{8,10},{10,8},{9,1... | collective-permute-start | bytes 6291464 | tf_op jit(solution)/shard_map/ppermute | solution.py:25
  73.7 57.2 %collective-permute-start.7 = (bf16[512,2048]{1,0:T(8,128)(2,1)}, bf16[512,2048]{1,0:T(8,128)(2,1)}, u32[]{:S(2)}, u32[]{:S(2)}) collective-permute-start(bf16[512,2048]{1,0:T(8,128)(2,1)} %collective-permute-done.2), channel_id=1, source_target_pairs={{0,1},{1,0},{2,3},{3,2},{4,5},{5,4},{6,7},{7,6},{8,9},{9,8},{10,11... | collective-permute-start | bytes 6291464 | tf_op jit(solution)/shard_map/ppermute | solution.py:25
  73.7 57.2 %collective-permute-start.4 = (bf16[512,2048]{1,0:T(8,128)(2,1)}, bf16[512,2048]{1,0:T(8,128)(2,1)}, u32[]{:S(2)}, u32[]{:S(2)}) collective-permute-start(bf16[512,2048]{1,0:T(8,128)(2,1)} %param.9), channel_id=1, source_target_pairs={{0,1},{1,0},{2,3},{3,2},{4,5},{5,4},{6,7},{7,6},{8,9},{9,8},{10,11... | collective-permute-start | bytes 6291464 | tf_op jit(solution)/shard_map/ppermute | solution.py:25
  111.4 19.5 %collective-permute-start.5 = (bf16[512,2048]{1,0:T(8,128)(2,1)}, bf16[512,2048]{1,0:T(8,128)(2,1)}, u32[]{:S(2)}, u32[]{:S(2)}) collective-permute-start(bf16[512,2048]{1,0:T(8,128)(2,1)} %collective-permute-done.1), channel_id=1, source_target_pairs={{0,1},{1,0},{2,3},{3,2},{4,5},{5,4},{6,7},{7,6},{8,9},{9,8},{10,11... | collective-permute-start | bytes 6291464 | tf_op jit(solution)/shard_map/ppermute | solution.py:25
  136.7 56.9 %collective-permute-start.9 = (bf16[512,2048]{1,0:T(8,128)(2,1)}, bf16[512,2048]{1,0:T(8,128)(2,1)}, u32[]{:S(2)}, u32[]{:S(2)}) collective-permute-start(bf16[512,2048]{1,0:T(8,128)(2,1)} %collective-permute-done.6), channel_id=1, source_target_pairs={{0,1},{1,0},{2,3},{3,2},{4,5},{5,4},{6,7},{7,6},{8,9},{9,8},{10,11... | collective-permute-start | bytes 6291464 | tf_op jit(solution)/shard_map/ppermute | solution.py:25
  139.2 45.0 %collective-permute-start.11 = (bf16[512,1376]{0,1:T(8,128)(2,1)}, bf16[512,1376]{0,1:T(8,128)(2,1)}, u32[]{:S(2)}, u32[]{:S(2)}) collective-permute-start(bf16[512,1376]{0,1:T(8,128)(2,1)} %slice.44), channel_id=1, source_target_pairs={{0,1},{1,0},{2,3},{3,2},{4,5},{5,4},{6,7},{7,6},{8,9},{9,8},{10,11... | collective-permute-start | bytes 4227080 | tf_op jit(solution)/shard_map/ppermute | solution.py:25
  173.5 28.1 %collective-permute-start.12 = (bf16[512,1024]{1,0:T(8,128)(2,1)}, bf16[512,1024]{1,0:T(8,128)(2,1)S(1)}, u32[]{:S(2)}, u32[]{:S(2)}) collective-permute-start(bf16[512,1024]{1,0:T(8,128)(2,1)} %slice.49), channel_id=1, source_target_pairs={{0,4},{4,8},{8,12},{12,0},{1,5},{5,9},{9,13},{13,1},{2,6},{6,10},{... | collective-permute-start | bytes 3145736 | tf_op jit(solution)/shard_map/ppermute | solution.py:25
  173.6 46.7 %collective-permute-start.13 = (bf16[352,1024]{1,0:T(8,128)(2,1)S(1)}, bf16[352,1024]{1,0:T(8,128)(2,1)}, u32[]{:S(2)}, u32[]{:S(2)}) collective-permute-start(bf16[352,1024]{1,0:T(8,128)(2,1)S(1)} %slice.52.rest_2_), channel_id=1, source_target_pairs={{0,4},{4,8},{8,12},{12,0},{1,5},{5,9},{9,13},{13,1},{2,6},{6,10},{... | collective-permute-start | bytes 2162696 | tf_op jit(solution)/shard_map/ppermute | solution.py:25
  173.7 5.4 %collective-permute-start.18 = (s32[1,16]{1,0:T(1,128)S(1)}, s32[1,16]{1,0:T(1,128)S(1)}, u32[]{:S(2)}, u32[]{:S(2)}) collective-permute-start(s32[1,16]{1,0:T(1,128)S(1)} %copy-done.15), channel_id=1, source_target_pairs={{0,16},{16,0},{1,17},{17,1},{2,18},{18,2},{3,19},{19,3},{4,20},{20... | collective-permute-start | bytes 200 | tf_op jit(solution)/shard_map/ppermute | solution.py:25
  179.1 4.3 %collective-permute-start.16 = (f32[512,32]{0,1:T(8,128)S(1)}, f32[512,32]{0,1:T(8,128)S(1)}, u32[]{:S(2)}, u32[]{:S(2)}) collective-permute-start(f32[512,32]{0,1:T(8,128)S(1)} %fusion.24), channel_id=1, source_target_pairs={{0,2},{2,0},{1,3},{3,1},{4,6},{6,4},{5,7},{7,5},{8,10},{10,8},{9,1... | collective-permute-start | bytes 196616 | tf_op jit(solution)/shard_map/ppermute | solution.py:25
  183.4 50.3 %collective-permute-start.14 = (bf16[256,1024]{1,0:T(8,128)(2,1)}, bf16[256,1024]{1,0:T(8,128)(2,1)}, u32[]{:S(2)}, u32[]{:S(2)}) collective-permute-start(bf16[256,1024]{1,0:T(8,128)(2,1)} %get-tuple-element.44), channel_id=1, source_target_pairs={{0,4},{4,8},{8,12},{12,0},{1,5},{5,9},{9,13},{13,1},{2,6},{6,10},{... | collective-permute-start | bytes 1572872 | tf_op jit(solution)/shard_map/ppermute | solution.py:25
  184.3 59.1 %collective-permute-start.15 = (bf16[256,1024]{1,0:T(8,128)(2,1)}, bf16[256,1024]{1,0:T(8,128)(2,1)}, u32[]{:S(2)}, u32[]{:S(2)}) collective-permute-start(bf16[256,1024]{1,0:T(8,128)(2,1)} %get-tuple-element.43), channel_id=1, source_target_pairs={{0,4},{4,8},{8,12},{12,0},{1,5},{5,9},{9,13},{13,1},{2,6},{6,10},{... | collective-permute-start | bytes 1572872 | tf_op jit(solution)/shard_map/ppermute | solution.py:25
  193.6 59.7 %collective-permute-start.19 = (f32[512,32]{0,1:T(8,128)S(1)}, f32[512,32]{0,1:T(8,128)S(1)}, u32[]{:S(2)}, u32[]{:S(2)}) collective-permute-start(f32[512,32]{0,1:T(8,128)S(1)} %add.146), channel_id=1, source_target_pairs={{0,16},{1,17},{16,0},{17,1},{2,18},{3,19},{18,2},{19,3},{4,20},{5,... | collective-permute-start | bytes 196616 | tf_op jit(solution)/shard_map/ppermute | solution.py:25
  202.6 50.7 %collective-permute-start.20 = (f32[512,32]{0,1:T(8,128)S(1)}, f32[512,32]{0,1:T(8,128)S(1)}, u32[]{:S(2)}, u32[]{:S(2)}) collective-permute-start(f32[512,32]{0,1:T(8,128)S(1)} %add.146), channel_id=1, source_target_pairs={{0,17},{1,16},{16,1},{17,0},{2,19},{3,18},{18,3},{19,2},{4,21},{5,... | collective-permute-start | bytes 196616 | tf_op jit(solution)/shard_map/ppermute | solution.py:25
  206.5 14.4 %copy-start.3 = (bf16[352,1024]{1,0:T(8,128)(2,1)S(1)}, bf16[352,1024]{1,0:T(8,128)(2,1)}, u32[]{:S(2)}) copy-start(bf16[352,1024]{1,0:T(8,128)(2,1)} %constant_dynamic-slice_fusion.3.rest_0_) | copy-start | bytes 2162692
  206.6 14.4 %copy-start.8 = (bf16[352,32]{1,0:T(8,128)(2,1)S(1)}, bf16[352,32]{1,0:T(8,128)(2,1)}, u32[]{:S(2)}) copy-start(bf16[352,32]{1,0:T(8,128)(2,1)} %copy.57.factor_ref) | copy-start | bytes 67588
  220.3 36.8 %collective-permute-start.17 = (f32[512,32]{0,1:T(8,128)S(1)}, f32[512,32]{0,1:T(8,128)S(1)}, u32[]{:S(2)}, u32[]{:S(2)}) collective-permute-start(f32[512,32]{0,1:T(8,128)S(1)} %add.146), channel_id=1, source_target_pairs={{0,1},{1,0},{16,17},{17,16},{2,3},{3,2},{18,19},{19,18},{4,5},{5,4... | collective-permute-start | bytes 196616 | tf_op jit(solution)/shard_map/ppermute | solution.py:25
  255.2 27.5 %copy-start.1 = (bf16[512,2048]{1,0:T(8,128)(2,1)S(1)}, bf16[512,2048]{1,0:T(8,128)(2,1)}, u32[]{:S(2)}) copy-start(bf16[512,2048]{1,0:T(8,128)(2,1)} %param.8) | copy-start | bytes 6291460
  255.3 4.3 %collective-permute-start.21 = (f32[16,1024]{1,0:T(8,128)S(1)}, f32[16,1024]{1,0:T(8,128)S(1)}, u32[]{:S(2)}, u32[]{:S(2)}) collective-permute-start(f32[16,1024]{1,0:T(8,128)S(1)} %reshape.72), channel_id=1, source_target_pairs={{0,16},{16,0},{1,17},{17,1},{2,18},{18,2},{3,19},{19,3},{4,20},{20... | collective-permute-start | bytes 196616 | tf_op jit(solution)/shard_map/ppermute | solution.py:25
  259.7 4.3 %collective-permute-start.22 = (f32[16,1024]{1,0:T(8,128)S(1)}, f32[16,1024]{1,0:T(8,128)S(1)}, u32[]{:S(2)}, u32[]{:S(2)}) collective-permute-start(f32[16,1024]{1,0:T(8,128)S(1)} %add.147), channel_id=1, source_target_pairs={{0,2},{2,0},{1,3},{3,1},{4,6},{6,4},{5,7},{7,5},{8,10},{10,8},{9,1... | collective-permute-start | bytes 196616 | tf_op jit(solution)/shard_map/ppermute | solution.py:25
  264.0 1.3 collective-permute-start.23
  265.4 17.3 %copy-start.11 = (f32[16,1024]{1,0:T(8,128)}, f32[16,1024]{1,0:T(8,128)S(1)}, u32[]{:S(2)}) copy-start(f32[16,1024]{1,0:T(8,128)S(1)} %add.149.refs_0_) | copy-start | bytes 196612
  265.4 6.8 %collective-permute-start.24 = (f32[16,1024]{1,0:T(8,128)S(1)}, f32[16,1024]{1,0:T(8,128)S(1)}, u32[]{:S(2)}, u32[]{:S(2)}) collective-permute-start(f32[16,1024]{1,0:T(8,128)S(1)} %add.149.refs_0_), channel_id=1, source_target_pairs={{0,4},{4,8},{8,12},{12,0},{1,5},{5,9},{9,13},{13,1},{2,6},{6,10},{... | collective-permute-start | bytes 196616 | tf_op jit(solution)/shard_map/ppermute | solution.py:25
  265.4 8.6 %collective-permute-start.25 = (f32[16,1024]{1,0:T(8,128)S(1)}, f32[16,1024]{1,0:T(8,128)S(1)}, u32[]{:S(2)}, u32[]{:S(2)}) collective-permute-start(f32[16,1024]{1,0:T(8,128)S(1)} %add.149.refs_0_), channel_id=1, source_target_pairs={{0,8},{4,12},{8,0},{12,4},{1,9},{5,13},{9,1},{13,5},{2,10},{6,14},... | collective-permute-start | bytes 196616 | tf_op jit(solution)/shard_map/ppermute | solution.py:25
  265.6 8.4 %collective-permute-start.26 = (f32[16,1024]{1,0:T(8,128)S(1)}, f32[16,1024]{1,0:T(8,128)S(1)}, u32[]{:S(2)}, u32[]{:S(2)}) collective-permute-start(f32[16,1024]{1,0:T(8,128)S(1)} %add.149.refs_0_), channel_id=1, source_target_pairs={{0,12},{4,0},{8,4},{12,8},{1,13},{5,1},{9,5},{13,9},{2,14},{6,2},{... | collective-permute-start | bytes 196616 | tf_op jit(solution)/shard_map/ppermute | solution.py:25
  (11 other events, 57.1 us)

commit v8 on v7

--- a/solution.py
+++ b/solution.py
@@ -203,6 +203,10 @@
 
     order = [(dg, ds) for dg in range(n_groups) for ds in range(n_seq)]
 
+    def place(cot, dg, ds, r, block):
+        at = ((side - r) % n_tensor) * block.shape[1]
+        return lax.dynamic_update_slice(cot, block, ((dg * n_seq + ds) * rows, at))
+
     def unit_columns(dg, ds):
         to = ((group + dg) % n_groups) * n_seq + (half + ds) % n_seq
         return lax.dynamic_slice_in_dim(gate_pre, to * part, part, 1)
@@ -237,41 +241,46 @@
         for r in range(1, n_tensor):
             more[dg, 0, r] = shifted(cots[dg, 0, 0], "tensor", (n_tensor,), (r,))
     right_part = jnp.dot(inputs, proj_in, preferred_element_type=jnp.float32)
+    out_factor = lax.dynamic_slice_in_dim(proj_out, mine * part, part, 0)
+    factors = [out_factor[low:high] for low, high in spans]
+    cot = jnp.zeros((len(order) * rows, n_tensor * cotangent.shape[1]), cotangent.dtype)
+    for r in range(n_tensor):
+        cot = place(cot, 0, 0, r, cots[0, 0, r])
     turned = shifted(ring[-1], "dp", (n_dp,), (1,)) if n_dp > 3 else ring.pop()
-    turned, cots, more, sheets, right_part, doc_lens = lax.optimization_barrier(
-        (turned, cots, more, sheets, right_part, doc_lens)
+    turned, cot, cots, more, sheets, right_part, doc_lens, factors = lax.optimization_barrier(
+        (turned, cot, cots, more, sheets, right_part, doc_lens, factors)
     )
     ring.append(turned)
     cots.update(more)
 
+    while len(ring) < n_dp - 1:
+        ring.append(shifted(ring[-1], "dp", (n_dp,), (1,)))
+    cuts = [ring[-1][low:high] for low, high in spans]
+    cuts, cot, cots, sheets, right_part, doc_lens = lax.optimization_barrier(
+        (cuts, cot, cots, sheets, right_part, doc_lens)
+    )
+    turned = [shifted(cut, "dp", (n_dp,), (1,)) for cut in cuts]
     for dg in range(1, n_groups):
         for r in range(1, n_tensor):
             for ds in range(1, n_seq):
                 cots[dg, ds, r] = across(cots[dg, 0, r], ds)
         spread(dg, sheets[dg])
-    while len(ring) < n_dp - 1:
-        ring.append(shifted(ring[-1], "dp", (n_dp,), (1,)))
-    chunks = [
-        ring + ([shifted(ring[-1][low:high], "dp", (n_dp,), (1,))] if n_dp > 1 else [])
-        for low, high in spans
-    ]
+    chunks = [ring + [block] for block in turned]
     right = sum_over(right_part, "tensor")
     rights = [right if dg == ds == 0 else shifted(right, pair, sizes, (dg, ds)) for dg, ds in order]
     lens = [doc_lens if dg == 0 else shifted(doc_lens, "groups", (n_groups,), (dg,)) for dg in range(n_groups)]
 
-    cot = jnp.zeros((len(order) * rows, n_tensor * cotangent.shape[1]), cotangent.dtype)
     gate = jnp.zeros((len(order) * rows, part), gate_pre.dtype)
-    for (dg, ds, r), block in sorted(cots.items(), key=lambda item: (item[0][1] * item[0][0] * item[0][2], item[0])):
-        at = ((side - r) % n_tensor) * cotangent.shape[1]
-        cot = lax.dynamic_update_slice(cot, block, ((dg * n_seq + ds) * rows, at))
-    for number, place in enumerate(order):
-        gate = lax.dynamic_update_slice(gate, gates[place], (number * rows, 0))
-
-    out_factor = lax.dynamic_slice_in_dim(proj_out, mine * part, part, 0)
+    for (dg, ds, r), block in sorted(cots.items(), key=lambda item: (item[0][0] * item[0][2], item[0])):
+        if (dg, ds) != (0, 0):
+            cot = place(cot, dg, ds, r, block)
+    for number, block in enumerate(order):
+        gate = lax.dynamic_update_slice(gate, gates[block], (number * rows, 0))
+
     left = jnp.zeros((n_groups * n_seq * rows, rank), jnp.float32)
     me = jnp.reshape(stage, (1,)).astype(jnp.int32)
-    for slots, (low, high) in zip(chunks, spans):
-        left = add_chunk(me, cot, gate, low, out_factor[low:high], left, slots, rows)
+    for slots, (low, high), factor in zip(chunks, spans, factors):
+        left = add_chunk(me, cot, gate, low, factor, left, slots, rows)
 
     parts = []
     for dg in range(n_groups):

time: 284 us -> 277 us (0.975)
  waiting for transfers between devices: 102 us -> 93.5 us
    ppermute x27, waiting for transfers between devices: 102 us -> 93.5 us  [shifted(): return lax.ppermute(x, axes, pairs)]
    unnamed x39 -> x35, local copies, waits for them, and re-layouts: 19.3 us -> 14.2 us
    optimization_barrier x1 -> x5, local copies, waits for them, and re-layouts: 4.58 us -> 9.7 us  [the longest x4 5.17 us: on_device(): lax.optimization_barrier((turned, cot, cots, more, sheets, right_part, do...]
    slice x5 -> x6, local copies, waits for them, and re-layouts: 8.96 us -> 10.1 us  [the longest x3 5.71 us: on_device(): cuts = [ring[-1][low:high] for low, high in spans]]
  transfers between devices with their start and end apart: 27 -> 27, of which waited for: 12 -> 11; matrix products, arithmetic and copies ran while one was open for 34% -> 32% of each run, Pallas kernels for 16% -> 17%
where the time goes in v8:
time: 277 us; the launch traced here: 276 us
  local copies, waits for them, and re-layouts  95.5 us (34%)
  waiting for transfers between devices  93.5 us (34%)
  Pallas kernels  52.7 us (19%)
  starting transfers between devices  24.5 us (9%)
  matrix products  4.28 us (2%)
  other arithmetic  4.25 us (2%)
    ppermute x27, waiting for transfers between devices, shifted(): return lax.ppermute(x, axes, pairs)  93.5 us
    pallas_call x4, Pallas kernels, add_chunk(): pl.pallas_call(functools.partial(chunk_kernel, n, skip), out_shape=jax.Sh...  45.7 us
    dynamic_update_slice x8, local copies, waits for them, and re-layouts, place(): return lax.dynamic_update_slice(cot, block, ((dg * n_seq + ds) * rows, at))  24.7 us
    ppermute x27, starting transfers between devices, shifted(): return lax.ppermute(x, axes, pairs)  24.5 us
    unnamed x35, local copies, waits for them, and re-layouts  14.2 us
    dynamic_slice x1, local copies, waits for them, and re-layouts, unit_columns(): return lax.dynamic_slice_in_dim(gate_pre, to * part, part, 1)  8.11 us
    dynamic_update_slice x4, local copies, waits for them, and re-layouts, on_device(): gate = lax.dynamic_update_slice(gate, gates[block], (number * rows, 0))  7.89 us
    pallas_call x1, Pallas kernels, finish(): pl.pallas_call(functools.partial(final_kernel, n, share), out_shape=(jax....  7.02 us
  transfers between devices with their start and end apart: 27, of which 11 were waited for; matrix products, arithmetic and copies ran while one was open for 32% of the time, Pallas kernels for 17%

profile of v8, /device:TPU:0, one launch (start us, length us, event | category | flops | bytes accessed | tf_op | source)
XLA Modules:
  0.0 275.7 jit_solution(10994575304044543053)
XLA Ops:
  0.6 3.0 %collective-permute-start.1 = (bf16[512,2048]{1,0:T(8,128)(2,1)}, bf16[512,2048]{1,0:T(8,128)(2,1)}, u32[]{:S(2)}, u32[]{:S(2)}) collective-permute-start(bf16[512,2048]{1,0:T(8,128)(2,1)} %param.9), channel_id=1, source_target_pairs={{0,2},{2,0},{1,3},{3,1},{4,6},{6,4},{5,7},{7,5},{8,10},{10,8},{9,1... | collective-permute-start | bytes 6291464 | tf_op jit(solution)/shard_map/ppermute | solution.py:25
  5.2 3.6 %constant_dynamic-slice_fusion.9.rest_0_ = bf16[1376,1024]{1,0:T(8,128)(2,1)} fusion(bf16[5504,1024]{1,0:T(8,128)(2,1)} %param.11, s32[]{:T(128)S(6)} %select_n.85), kind=kLoop, calls=%fused_computation.38 | loop fusion | bytes 5636100 | tf_op jit(solution)/shard_map/dynamic_slice | solution.py:199
  10.3 8.1 %constant_dynamic-slice_fusion.4 = (bf16[512,1376]{1,0:T(8,128)(2,1)}, bf16[512,1376]{1,0:T(8,128)(2,1)}, bf16[512,1376]{1,0:T(8,128)(2,1)}, bf16[512,1376]{1,0:T(8,128)(2,1)S(1)}) fusion(bf16[512,5504]{1,0:T(8,128)(2,1)} %param.10, s32[]{:T(128)S(6)} %select_n.97, s32[]{:T(128)S(6)} %select_n.94, s32[]{:T(128)S(6)} %select_n.92, s32[]{:T(128)S(6)} %select_n.96), kind=kLoop, calls=%fused_computation.31 | loop fusion | bytes 11272208 | tf_op jit(solution)/shard_map/dynamic_slice | solution.py:212
  18.4 2.6 copy.51
  21.0 2.6 copy.52
  23.6 3.7 %pad_maximum_fusion = bf16[1024,1376]{0,1:T(8,128)(2,1)} fusion(bf16[512,1376]{0,1:T(8,128)(2,1)} %copy.52, bf16[512,1376]{0,1:T(8,128)(2,1)} %copy.51), kind=kLoop, calls=%fused_computation | loop fusion | flops 5636096 | bytes 5636096 | tf_op jit(solution)/shard_map/concatenate | solution.py:220
  27.8 2.6 copy.58
  30.4 19.2 %collective-permute-done.1 = bf16[512,2048]{1,0:T(8,128)(2,1)} collective-permute-done((bf16[512,2048]{1,0:T(8,128)(2,1)}, bf16[512,2048]{1,0:T(8,128)(2,1)}, u32[]{:S(2)}, u32[]{:S(2)}) %collective-permute-start.1) | collective-permute-done | bytes 2097184 | tf_op jit(solution)/shard_map/ppermute | solution.py:25
  49.6 2.9 %collective-permute-done.2 = bf16[512,2048]{1,0:T(8,128)(2,1)} collective-permute-done((bf16[512,2048]{1,0:T(8,128)(2,1)}, bf16[512,2048]{1,0:T(8,128)(2,1)}, u32[]{:S(2)}, u32[]{:S(2)}) %collective-permute-start.2) | collective-permute-done | bytes 2097184 | tf_op jit(solution)/shard_map/ppermute | solution.py:25
  52.5 20.7 %collective-permute-done.rest_1_ = bf16[1376,1024]{1,0:T(8,128)(2,1)} collective-permute-done((bf16[1376,1024]{1,0:T(8,128)(2,1)}, bf16[1376,1024]{1,0:T(8,128)(2,1)}, u32[]{:S(2)}, u32[]{:S(2)}) %collective-permute-start) | collective-permute-done | bytes 2818080 | tf_op jit(solution)/shard_map/ppermute | solution.py:25
  74.2 37.2 %collective-permute-done.8 = bf16[1024,1376]{0,1:T(8,128)(2,1)} collective-permute-done((bf16[1024,1376]{0,1:T(8,128)(2,1)}, bf16[1024,1376]{0,1:T(8,128)(2,1)}, u32[]{:S(2)}, u32[]{:S(2)}) %collective-permute-start.8) | collective-permute-done | bytes 2818080 | tf_op jit(solution)/shard_map/ppermute | solution.py:25
  121.0 2.8 %dynamic_update_slice.44 = bf16[2048,1376]{1,0:T(8,128)(2,1)} pad(bf16[512,1376]{1,0:T(8,128)(2,1)S(1)} %get-tuple-element.74, bf16[]{:T(256)} %constant.97.clone.1), padding=0_1536x0_0 | pad | bytes 7045122 | tf_op jit(solution)/shard_map/dynamic_update_slice | solution.py:278
  130.9 6.0 %broadcast_in_dim.4 = bf16[2048,4096]{1,0:T(8,128)(2,1)} broadcast(bf16[]{:T(256)} %constant.97.clone.1), dimensions={} | broadcast | bytes 16777218 | tf_op jit(solution)/shard_map/broadcast_in_dim | solution.py:246
  138.5 3.3 %constant_dynamic-update-slice_fusion.2 = bf16[2048,4096]{1,0:T(8,128)(2,1)} fusion(bf16[2048,4096]{1,0:T(8,128)(2,1)} %constant_dynamic-update-slice_fusion.3, bf16[512,2048]{1,0:T(8,128)(2,1)} %collective-permute-done.1, s32[]{:T(128)S(6)} %select_n.89), kind=kLoop, calls=%fused_computation.36 | loop fusion | bytes 4194308 | tf_op jit(solution)/shard_map/dynamic_update_slice | solution.py:208
  155.3 3.3 %constant_dynamic-update-slice_fusion.9 = bf16[2048,4096]{1,0:T(8,128)(2,1)} fusion(bf16[2048,4096]{1,0:T(8,128)(2,1)} %constant_dynamic-update-slice_fusion.2, bf16[512,2048]{1,0:T(8,128)(2,1)} %collective-permute-done.4, s32[]{:T(128)S(6)} %select_n.87), kind=kLoop, calls=%fused_computation.46 | loop fusion | bytes 4194308 | tf_op jit(solution)/shard_map/dynamic_update_slice | solution.py:208
  158.5 3.3 %constant_dynamic-update-slice_fusion.8 = bf16[2048,4096]{1,0:T(8,128)(2,1)} fusion(bf16[2048,4096]{1,0:T(8,128)(2,1)} %constant_dynamic-update-slice_fusion.9, bf16[512,2048]{1,0:T(8,128)(2,1)} %collective-permute-done.5, s32[]{:T(128)S(6)} %select_n.89), kind=kLoop, calls=%fused_computation.45 | loop fusion | bytes 4194308 | tf_op jit(solution)/shard_map/dynamic_update_slice | solution.py:208
  161.8 3.3 %constant_dynamic-update-slice_fusion.7 = bf16[2048,4096]{1,0:T(8,128)(2,1)} fusion(bf16[2048,4096]{1,0:T(8,128)(2,1)} %constant_dynamic-update-slice_fusion.8, bf16[512,2048]{1,0:T(8,128)(2,1)} %collective-permute-done.2, s32[]{:T(128)S(6)} %select_n.87), kind=kLoop, calls=%fused_computation.44 | loop fusion | bytes 4194308 | tf_op jit(solution)/shard_map/dynamic_update_slice | solution.py:208
  165.0 3.3 %constant_dynamic-update-slice_fusion.5 = bf16[2048,4096]{1,0:T(8,128)(2,1)} fusion(bf16[2048,4096]{1,0:T(8,128)(2,1)} %constant_dynamic-update-slice_fusion.7, bf16[512,2048]{1,0:T(8,128)(2,1)} %collective-permute-done.7, s32[]{:T(128)S(6)} %select_n.87), kind=kLoop, calls=%fused_computation.42 | loop fusion | bytes 4194308 | tf_op jit(solution)/shard_map/dynamic_update_slice | solution.py:208
  168.4 4.5 %copy.43 = bf16[1024,1376]{1,0:T(8,128)(2,1)} copy(bf16[1024,1376]{0,1:T(8,128)(2,1)} %collective-permute-done.8) | data formatting | bytes 5636096 | tf_op jit(solution)/shard_map/optimization_barrier | solution.py:259
  173.0 3.4 %constant_dynamic-update-slice_fusion.6 = bf16[2048,4096]{1,0:T(8,128)(2,1)} fusion(bf16[2048,4096]{1,0:T(8,128)(2,1)} %constant_dynamic-update-slice_fusion.5, bf16[512,2048]{1,0:T(8,128)(2,1)} %collective-permute-done.6, s32[]{:T(128)S(6)} %select_n.89), kind=kLoop, calls=%fused_computation.43 | loop fusion | bytes 4194308 | tf_op jit(solution)/shard_map/dynamic_update_slice | solution.py:208
  178.7 3.4 %collective-permute-done.16 = f32[512,32]{0,1:T(8,128)S(1)} collective-permute-done((f32[512,32]{0,1:T(8,128)S(1)}, f32[512,32]{0,1:T(8,128)S(1)}, u32[]{:S(2)}, u32[]{:S(2)}) %collective-permute-start.16) | collective-permute-done | bytes 65568 | tf_op jit(solution)/shard_map/ppermute | solution.py:25
  186.7 2.6 constant_dynamic-update-slice_fusion.gate_ref
  189.8 3.3 %constant_dynamic-update-slice_fusion.4.cot_ref = bf16[2048,4096]{1,0:T(8,128)(2,1)} fusion(bf16[2048,4096]{1,0:T(8,128)(2,1)} %constant_dynamic-update-slice_fusion.6, bf16[512,2048]{1,0:T(8,128)(2,1)} %collective-permute-done.9, s32[]{:T(128)S(6)} %select_n.89), kind=kLoop, calls=%fused_computation.41 | loop fusion | bytes 4194308 | tf_op jit(solution)/shard_map/dynamic_update_slice | solution.py:208
  194.2 2.6 copy-done.2
  198.0 13.7 %shard_map.103.before_ref = f32[2048,32]{1,0:T(8,128)S(1)} custom-call(s32[1]{0:T(128)} %bitcast.me_ref, bf16[2048,4096]{1,0:T(8,128)(2,1)} %constant_dynamic-update-slice_fusion.4.cot_ref, bf16[2048,1376]{1,0:T(8,128)(2,1)S(1)} %copy-done.2, bf16[512,32]{1,0:T(8,128)(2,1)S(1)} %copy-done.7, f32[2048,32]{1,0:T(8,128)S(1)} %broadcast_in_dim.5.before_ref, ...), custom_call_target="tpu_custom_call" | custom-call | flops 8589934592 | bytes 23068672 | tf_op jit(solution)/shard_map/pallas_call | solution.py:85
  213.5 12.7 %shard_map.104.before_ref = f32[2048,32]{1,0:T(8,128)S(1)} custom-call(s32[1]{0:T(128)} %bitcast.me_ref, bf16[2048,4096]{1,0:T(8,128)(2,1)} %constant_dynamic-update-slice_fusion.4.cot_ref, bf16[2048,1376]{1,0:T(8,128)(2,1)S(1)} %copy-done.2, bf16[352,32]{1,0:T(8,128)(2,1)S(1)} %copy-done.8, f32[2048,32]{1,0:T(8,128)S(1)} %shard_map.103.before_ref, ...), custom_call_target="tpu_custom_call" | custom-call | flops 5905580032 | bytes 21102592 | tf_op jit(solution)/shard_map/pallas_call | solution.py:85
  226.2 9.7 %shard_map.105.before_ref = f32[2048,32]{1,0:T(8,128)S(1)} custom-call(s32[1]{0:T(128)} %bitcast.me_ref, bf16[2048,4096]{1,0:T(8,128)(2,1)} %constant_dynamic-update-slice_fusion.4.cot_ref, bf16[2048,1376]{1,0:T(8,128)(2,1)S(1)} %copy-done.2, bf16[256,32]{1,0:T(8,128)(2,1)S(1)} %copy-done.10, f32[2048,32]{1,0:T(8,128)S(1)} %shard_map.104.before_ref, ...), custom_call_target="tpu_custom_call" | custom-call | flops 4294967296 | bytes 19922944 | tf_op jit(solution)/shard_map/pallas_call | solution.py:85
  235.9 9.7 %shard_map.106 = f32[2048,32]{1,0:T(8,128)S(1)} custom-call(s32[1]{0:T(128)} %bitcast.me_ref, bf16[2048,4096]{1,0:T(8,128)(2,1)} %constant_dynamic-update-slice_fusion.4.cot_ref, bf16[2048,1376]{1,0:T(8,128)(2,1)S(1)} %copy-done.2, bf16[256,32]{1,0:T(8,128)(2,1)S(1)} %copy-done.9, f32[2048,32]{1,0:T(8,128)S(1)} %shard_map.105.before_ref, ...), custom_call_target="tpu_custom_call" | custom-call | flops 4294967296 | bytes 19922944 | tf_op jit(solution)/shard_map/pallas_call | solution.py:85
  252.8 3.7 %collective-permute-done.22 = f32[16,1024]{1,0:T(8,128)S(1)} collective-permute-done((f32[16,1024]{1,0:T(8,128)S(1)}, f32[16,1024]{1,0:T(8,128)S(1)}, u32[]{:S(2)}, u32[]{:S(2)}) %collective-permute-start.22) | collective-permute-done | bytes 65568 | tf_op jit(solution)/shard_map/ppermute | solution.py:25
  259.5 2.6 collective-permute-start.25
  264.2 2.7 collective-permute-done.25.refs_2_
  268.7 7.0 %shard_map.107 = (f32[256,1024]{1,0:T(8,128)}, f32[16,512]{1,0:T(8,128)}) custom-call(s32[2]{0:T(128)S(1)} %pad_add_fusion.1.place_ref, f32[512,1024]{1,0:T(8,128)S(1)} %copy-done.4, f32[16,1024]{1,0:T(8,128)S(1)} %add.149.refs_0_, f32[16,1024]{1,0:T(8,128)S(1)} %collective-permute-done.24.refs_1_, f32[16,1024]{1,0:T(8,128)S(1)} %collective-permute-done.25.refs_2_, ...), custom_call_target="tpu_custom_call" | custom-call | tf_op jit(solution)/shard_map/pallas_call | solution.py:168
  (121 shorter events, 61.8 us)
Async XLA Ops:
  0.6 125.3 %copy-start = (bf16[512,2048]{1,0:T(8,128)(2,1)S(1)}, bf16[512,2048]{1,0:T(8,128)(2,1)}, u32[]{:S(2)}) copy-start(bf16[512,2048]{1,0:T(8,128)(2,1)} %param.8) | copy-start | bytes 6291460
  0.6 49.0 %collective-permute-start.1 = (bf16[512,2048]{1,0:T(8,128)(2,1)}, bf16[512,2048]{1,0:T(8,128)(2,1)}, u32[]{:S(2)}, u32[]{:S(2)}) collective-permute-start(bf16[512,2048]{1,0:T(8,128)(2,1)} %param.9), channel_id=1, source_target_pairs={{0,2},{2,0},{1,3},{3,1},{4,6},{6,4},{5,7},{7,5},{8,10},{10,8},{9,1... | collective-permute-start | bytes 6291464 | tf_op jit(solution)/shard_map/ppermute | solution.py:25
  3.7 48.9 %collective-permute-start.2 = (bf16[512,2048]{1,0:T(8,128)(2,1)}, bf16[512,2048]{1,0:T(8,128)(2,1)}, u32[]{:S(2)}, u32[]{:S(2)}) collective-permute-start(bf16[512,2048]{1,0:T(8,128)(2,1)} %param.9), channel_id=1, source_target_pairs={{0,16},{16,0},{1,17},{17,1},{2,18},{18,2},{3,19},{19,3},{4,20},{20... | collective-permute-start | bytes 6291464 | tf_op jit(solution)/shard_map/ppermute | solution.py:25
  8.8 64.4 %collective-permute-start = (bf16[1376,1024]{1,0:T(8,128)(2,1)}, bf16[1376,1024]{1,0:T(8,128)(2,1)}, u32[]{:S(2)}, u32[]{:S(2)}) collective-permute-start(bf16[1376,1024]{1,0:T(8,128)(2,1)} %constant_dynamic-slice_fusion.9.rest_0_), channel_id=1, source_target_pairs={{0,4},{4,8},{8,12},{12,0},{1,5},{5,9},{9,13},{13,1},{2,6},{6,10},{... | collective-permute-start | bytes 8454152 | tf_op jit(solution)/shard_map/ppermute | solution.py:25
  27.3 84.2 %collective-permute-start.8 = (bf16[1024,1376]{0,1:T(8,128)(2,1)}, bf16[1024,1376]{0,1:T(8,128)(2,1)}, u32[]{:S(2)}, u32[]{:S(2)}) collective-permute-start(bf16[1024,1376]{0,1:T(8,128)(2,1)} %pad_maximum_fusion), channel_id=1, source_target_pairs={{0,16},{16,0},{1,17},{17,1},{2,18},{18,2},{3,19},{19,3},{4,20},{20... | collective-permute-start | bytes 8454152 | tf_op jit(solution)/shard_map/ppermute | solution.py:25
  30.4 43.4 %collective-permute-start.10 = (bf16[512,1376]{0,1:T(8,128)(2,1)}, bf16[512,1376]{0,1:T(8,128)(2,1)}, u32[]{:S(2)}, u32[]{:S(2)}) collective-permute-start(bf16[512,1376]{0,1:T(8,128)(2,1)} %copy.58), channel_id=1, source_target_pairs={{0,1},{1,0},{2,3},{3,2},{4,5},{5,4},{6,7},{7,6},{8,9},{9,8},{10,11... | collective-permute-start | bytes 4227080 | tf_op jit(solution)/shard_map/ppermute | solution.py:25
  73.2 68.6 %collective-permute-start.3 = (bf16[1376,1024]{1,0:T(8,128)(2,1)}, bf16[1376,1024]{1,0:T(8,128)(2,1)}, u32[]{:S(2)}, u32[]{:S(2)}) collective-permute-start(bf16[1376,1024]{1,0:T(8,128)(2,1)} %collective-permute-done.rest_1_), channel_id=1, source_target_pairs={{0,4},{4,8},{8,12},{12,0},{1,5},{5,9},{9,13},{13,1},{2,6},{6,10},{... | collective-permute-start | bytes 8454152 | tf_op jit(solution)/shard_map/ppermute | solution.py:25
  73.2 68.6 %collective-permute-start.4 = (bf16[512,2048]{1,0:T(8,128)(2,1)}, bf16[512,2048]{1,0:T(8,128)(2,1)}, u32[]{:S(2)}, u32[]{:S(2)}) collective-permute-start(bf16[512,2048]{1,0:T(8,128)(2,1)} %param.9), channel_id=1, source_target_pairs={{0,1},{1,0},{2,3},{3,2},{4,5},{5,4},{6,7},{7,6},{8,9},{9,8},{10,11... | collective-permute-start | bytes 6291464 | tf_op jit(solution)/shard_map/ppermute | solution.py:25
  73.2 68.6 %collective-permute-start.5 = (bf16[512,2048]{1,0:T(8,128)(2,1)}, bf16[512,2048]{1,0:T(8,128)(2,1)}, u32[]{:S(2)}, u32[]{:S(2)}) collective-permute-start(bf16[512,2048]{1,0:T(8,128)(2,1)} %collective-permute-done.1), channel_id=1, source_target_pairs={{0,1},{1,0},{2,3},{3,2},{4,5},{5,4},{6,7},{7,6},{8,9},{9,8},{10,11... | collective-permute-start | bytes 6291464 | tf_op jit(solution)/shard_map/ppermute | solution.py:25
  73.7 68.1 %collective-permute-start.6 = (bf16[512,2048]{1,0:T(8,128)(2,1)}, bf16[512,2048]{1,0:T(8,128)(2,1)}, u32[]{:S(2)}, u32[]{:S(2)}) collective-permute-start(bf16[512,2048]{1,0:T(8,128)(2,1)} %collective-permute-done.2), channel_id=1, source_target_pairs={{0,2},{2,0},{1,3},{3,1},{4,6},{6,4},{5,7},{7,5},{8,10},{10,8},{9,1... | collective-permute-start | bytes 6291464 | tf_op jit(solution)/shard_map/ppermute | solution.py:25
  111.4 30.3 %collective-permute-start.7 = (bf16[512,2048]{1,0:T(8,128)(2,1)}, bf16[512,2048]{1,0:T(8,128)(2,1)}, u32[]{:S(2)}, u32[]{:S(2)}) collective-permute-start(bf16[512,2048]{1,0:T(8,128)(2,1)} %collective-permute-done.2), channel_id=1, source_target_pairs={{0,1},{1,0},{2,3},{3,2},{4,5},{5,4},{6,7},{7,6},{8,9},{9,8},{10,11... | collective-permute-start | bytes 6291464 | tf_op jit(solution)/shard_map/ppermute | solution.py:25
  150.1 33.6 %collective-permute-start.11 = (bf16[512,1376]{0,1:T(8,128)(2,1)}, bf16[512,1376]{0,1:T(8,128)(2,1)}, u32[]{:S(2)}, u32[]{:S(2)}) collective-permute-start(bf16[512,1376]{0,1:T(8,128)(2,1)} %slice.52), channel_id=1, source_target_pairs={{0,1},{1,0},{2,3},{3,2},{4,5},{5,4},{6,7},{7,6},{8,9},{9,8},{10,11... | collective-permute-start | bytes 4227080 | tf_op jit(solution)/shard_map/ppermute | solution.py:25
  150.6 38.7 %collective-permute-start.9 = (bf16[512,2048]{1,0:T(8,128)(2,1)}, bf16[512,2048]{1,0:T(8,128)(2,1)}, u32[]{:S(2)}, u32[]{:S(2)}) collective-permute-start(bf16[512,2048]{1,0:T(8,128)(2,1)} %collective-permute-done.6), channel_id=1, source_target_pairs={{0,1},{1,0},{2,3},{3,2},{4,5},{5,4},{6,7},{7,6},{8,9},{9,8},{10,11... | collective-permute-start | bytes 6291464 | tf_op jit(solution)/shard_map/ppermute | solution.py:25
  150.6 42.5 %collective-permute-start.12 = (bf16[512,1024]{1,0:T(8,128)(2,1)}, bf16[512,1024]{1,0:T(8,128)(2,1)S(1)}, u32[]{:S(2)}, u32[]{:S(2)}) collective-permute-start(bf16[512,1024]{1,0:T(8,128)(2,1)} %slice.47), channel_id=1, source_target_pairs={{0,4},{4,8},{8,12},{12,0},{1,5},{5,9},{9,13},{13,1},{2,6},{6,10},{... | collective-permute-start | bytes 3145736 | tf_op jit(solution)/shard_map/ppermute | solution.py:25
  152.2 59.6 %collective-permute-start.13 = (bf16[352,1024]{1,0:T(8,128)(2,1)S(1)}, bf16[352,1024]{1,0:T(8,128)(2,1)}, u32[]{:S(2)}, u32[]{:S(2)}) collective-permute-start(bf16[352,1024]{1,0:T(8,128)(2,1)S(1)} %slice.48.rest_2_), channel_id=1, source_target_pairs={{0,4},{4,8},{8,12},{12,0},{1,5},{5,9},{9,13},{13,1},{2,6},{6,10},{... | collective-permute-start | bytes 2162696 | tf_op jit(solution)/shard_map/ppermute | solution.py:25
  153.7 24.0 %collective-permute-start.18 = (s32[1,16]{1,0:T(1,128)S(1)}, s32[1,16]{1,0:T(1,128)S(1)}, u32[]{:S(2)}, u32[]{:S(2)}) collective-permute-start(s32[1,16]{1,0:T(1,128)S(1)} %copy-done.15), channel_id=1, source_target_pairs={{0,16},{16,0},{1,17},{17,1},{2,18},{18,2},{3,19},{19,3},{4,20},{20... | collective-permute-start | bytes 200 | tf_op jit(solution)/shard_map/ppermute | solution.py:25
  177.8 4.3 %collective-permute-start.16 = (f32[512,32]{0,1:T(8,128)S(1)}, f32[512,32]{0,1:T(8,128)S(1)}, u32[]{:S(2)}, u32[]{:S(2)}) collective-permute-start(f32[512,32]{0,1:T(8,128)S(1)} %fusion.24), channel_id=1, source_target_pairs={{0,2},{2,0},{1,3},{3,1},{4,6},{6,4},{5,7},{7,5},{8,10},{10,8},{9,1... | collective-permute-start | bytes 196616 | tf_op jit(solution)/shard_map/ppermute | solution.py:25
  182.1 44.1 %collective-permute-start.14 = (bf16[256,1024]{1,0:T(8,128)(2,1)}, bf16[256,1024]{1,0:T(8,128)(2,1)}, u32[]{:S(2)}, u32[]{:S(2)}) collective-permute-start(bf16[256,1024]{1,0:T(8,128)(2,1)} %get-tuple-element.63), channel_id=1, source_target_pairs={{0,4},{4,8},{8,12},{12,0},{1,5},{5,9},{9,13},{13,1},{2,6},{6,10},{... | collective-permute-start | bytes 1572872 | tf_op jit(solution)/shard_map/ppermute | solution.py:25
  183.7 52.2 %collective-permute-start.15 = (bf16[256,1024]{1,0:T(8,128)(2,1)}, bf16[256,1024]{1,0:T(8,128)(2,1)}, u32[]{:S(2)}, u32[]{:S(2)}) collective-permute-start(bf16[256,1024]{1,0:T(8,128)(2,1)} %get-tuple-element.64), channel_id=1, source_target_pairs={{0,4},{4,8},{8,12},{12,0},{1,5},{5,9},{9,13},{13,1},{2,6},{6,10},{... | collective-permute-start | bytes 1572872 | tf_op jit(solution)/shard_map/ppermute | solution.py:25
  189.3 56.5 %collective-permute-start.19 = (f32[512,32]{0,1:T(8,128)S(1)}, f32[512,32]{0,1:T(8,128)S(1)}, u32[]{:S(2)}, u32[]{:S(2)}) collective-permute-start(f32[512,32]{0,1:T(8,128)S(1)} %add.146), channel_id=1, source_target_pairs={{0,16},{1,17},{16,0},{17,1},{2,18},{3,19},{18,2},{19,3},{4,20},{5,... | collective-permute-start | bytes 196616 | tf_op jit(solution)/shard_map/ppermute | solution.py:25
  194.1 51.7 %collective-permute-start.20 = (f32[512,32]{0,1:T(8,128)S(1)}, f32[512,32]{0,1:T(8,128)S(1)}, u32[]{:S(2)}, u32[]{:S(2)}) collective-permute-start(f32[512,32]{0,1:T(8,128)S(1)} %add.146), channel_id=1, source_target_pairs={{0,17},{1,16},{16,1},{17,0},{2,19},{3,18},{18,3},{19,2},{4,21},{5,... | collective-permute-start | bytes 196616 | tf_op jit(solution)/shard_map/ppermute | solution.py:25
  198.0 15.5 %copy-start.3 = (bf16[352,1024]{1,0:T(8,128)(2,1)S(1)}, bf16[352,1024]{1,0:T(8,128)(2,1)}, u32[]{:S(2)}) copy-start(bf16[352,1024]{1,0:T(8,128)(2,1)} %constant_dynamic-slice_fusion.3.rest_0_) | copy-start | bytes 2162692
  198.0 15.5 %copy-start.8 = (bf16[352,32]{1,0:T(8,128)(2,1)S(1)}, bf16[352,32]{1,0:T(8,128)(2,1)}, u32[]{:S(2)}) copy-start(bf16[352,32]{1,0:T(8,128)(2,1)} %copy.55.factor_ref) | copy-start | bytes 67588
  211.8 36.8 %collective-permute-start.17 = (f32[512,32]{0,1:T(8,128)S(1)}, f32[512,32]{0,1:T(8,128)S(1)}, u32[]{:S(2)}, u32[]{:S(2)}) collective-permute-start(f32[512,32]{0,1:T(8,128)S(1)} %add.146), channel_id=1, source_target_pairs={{0,1},{1,0},{16,17},{17,16},{2,3},{3,2},{18,19},{19,18},{4,5},{5,4... | collective-permute-start | bytes 196616 | tf_op jit(solution)/shard_map/ppermute | solution.py:25
  247.7 28.0 %copy-start.1 = (bf16[512,2048]{1,0:T(8,128)(2,1)S(1)}, bf16[512,2048]{1,0:T(8,128)(2,1)}, u32[]{:S(2)}) copy-start(bf16[512,2048]{1,0:T(8,128)(2,1)} %param.8) | copy-start | bytes 6291460
  247.8 4.3 %collective-permute-start.21 = (f32[16,1024]{1,0:T(8,128)S(1)}, f32[16,1024]{1,0:T(8,128)S(1)}, u32[]{:S(2)}, u32[]{:S(2)}) collective-permute-start(f32[16,1024]{1,0:T(8,128)S(1)} %reshape.72), channel_id=1, source_target_pairs={{0,16},{16,0},{1,17},{17,1},{2,18},{18,2},{3,19},{19,3},{4,20},{20... | collective-permute-start | bytes 196616 | tf_op jit(solution)/shard_map/ppermute | solution.py:25
  252.2 4.3 %collective-permute-start.22 = (f32[16,1024]{1,0:T(8,128)S(1)}, f32[16,1024]{1,0:T(8,128)S(1)}, u32[]{:S(2)}, u32[]{:S(2)}) collective-permute-start(f32[16,1024]{1,0:T(8,128)S(1)} %add.147), channel_id=1, source_target_pairs={{0,2},{2,0},{1,3},{3,1},{4,6},{6,4},{5,7},{7,5},{8,10},{10,8},{9,1... | collective-permute-start | bytes 196616 | tf_op jit(solution)/shard_map/ppermute | solution.py:25
  256.5 1.3 collective-permute-start.23
  257.9 17.8 %copy-start.11 = (f32[16,1024]{1,0:T(8,128)}, f32[16,1024]{1,0:T(8,128)S(1)}, u32[]{:S(2)}) copy-start(f32[16,1024]{1,0:T(8,128)S(1)} %add.149.refs_0_) | copy-start | bytes 196612
  257.9 6.3 %collective-permute-start.24 = (f32[16,1024]{1,0:T(8,128)S(1)}, f32[16,1024]{1,0:T(8,128)S(1)}, u32[]{:S(2)}, u32[]{:S(2)}) collective-permute-start(f32[16,1024]{1,0:T(8,128)S(1)} %add.149.refs_0_), channel_id=1, source_target_pairs={{0,4},{4,8},{8,12},{12,0},{1,5},{5,9},{9,13},{13,1},{2,6},{6,10},{... | collective-permute-start | bytes 196616 | tf_op jit(solution)/shard_map/ppermute | solution.py:25
  259.5 7.3 %collective-permute-start.25 = (f32[16,1024]{1,0:T(8,128)S(1)}, f32[16,1024]{1,0:T(8,128)S(1)}, u32[]{:S(2)}, u32[]{:S(2)}) collective-permute-start(f32[16,1024]{1,0:T(8,128)S(1)} %add.149.refs_0_), channel_id=1, source_target_pairs={{0,8},{4,12},{8,0},{12,4},{1,9},{5,13},{9,1},{13,5},{2,10},{6,14},... | collective-permute-start | bytes 196616 | tf_op jit(solution)/shard_map/ppermute | solution.py:25
  262.1 5.0 %collective-permute-start.26 = (f32[16,1024]{1,0:T(8,128)S(1)}, f32[16,1024]{1,0:T(8,128)S(1)}, u32[]{:S(2)}, u32[]{:S(2)}) collective-permute-start(f32[16,1024]{1,0:T(8,128)S(1)} %add.149.refs_0_), channel_id=1, source_target_pairs={{0,12},{4,0},{8,4},{12,8},{1,13},{5,1},{9,5},{13,9},{2,14},{6,2},{... | collective-permute-start | bytes 196616 | tf_op jit(solution)/shard_map/ppermute | solution.py:25
  (11 other events, 59.4 us)

commit v9 on v8

--- a/solution.py
+++ b/solution.py
@@ -188,15 +188,20 @@
     docs = doc_lens.shape[1]
     rank = proj_in.shape[1]
     width = rank * rank
-    part = units // (n_groups * n_seq)
+    part = min(units, -(-units // (n_groups * n_seq * LANES)) * LANES)
     pair = ("groups", "seq")
     sizes = (n_groups, n_seq)
     mine = group * n_seq + half
 
+    def first_unit(who):
+        return jnp.minimum(who * part, units - part)
+
+    start = first_unit(mine)
+
     lows = [low for low in CUTS if low < part]
     spans = list(zip(lows, lows[1:] + [part]))
     spans = spans[:1] + spans[3:] + spans[1:3]
-    ring = [lax.dynamic_slice_in_dim(down_weight, mine * part, part, 0)]
+    ring = [lax.dynamic_slice_in_dim(down_weight, start, part, 0)]
 
     def across(x, ds):
         return shifted(x, "seq", (n_seq,), (ds,))
@@ -209,7 +214,7 @@
 
     def unit_columns(dg, ds):
         to = ((group + dg) % n_groups) * n_seq + (half + ds) % n_seq
-        return lax.dynamic_slice_in_dim(gate_pre, to * part, part, 1)
+        return lax.dynamic_slice_in_dim(gate_pre, first_unit(to), part, 1)
 
     cots = {(0, 0, 0): cotangent}
     for dg in range(1, n_groups):
@@ -220,6 +225,8 @@
         dg: jnp.concatenate([unit_columns(dg, ds) for ds in range(n_seq)], axis=0)
         for dg in range(n_groups)
     }
+    beside = (0, 0, n_tensor - 1)
+    sheets, cots[beside] = lax.optimization_barrier((sheets, cots[beside]))
     for dg in range(1, n_groups):
         sheets[dg] = shifted(sheets[dg], "groups", (n_groups,), (dg,))
     turned = shifted(ring[-1], "dp", (n_dp,), (1,))
@@ -241,7 +248,9 @@
         for r in range(1, n_tensor):
             more[dg, 0, r] = shifted(cots[dg, 0, 0], "tensor", (n_tensor,), (r,))
     right_part = jnp.dot(inputs, proj_in, preferred_element_type=jnp.float32)
-    out_factor = lax.dynamic_slice_in_dim(proj_out, mine * part, part, 0)
+    out_factor = lax.dynamic_slice_in_dim(proj_out, start, part, 0)
+    once = start + jnp.arange(part, dtype=jnp.int32) >= mine * part
+    out_factor = jnp.where(once[:, None], out_factor, 0).astype(proj_out.dtype)
     factors = [out_factor[low:high] for low, high in spans]
     cot = jnp.zeros((len(order) * rows, n_tensor * cotangent.shape[1]), cotangent.dtype)
     for r in range(n_tensor):

time: 277 us -> 270 us (0.975)
  local copies, waits for them, and re-layouts: 95.5 us -> 74.3 us
  waiting for transfers between devices: 93.5 us -> 100 us
  other arithmetic: 4.25 us -> 7.71 us
    optimization_barrier x5 -> x0, local copies, waits for them, and re-layouts: 9.7 us -> none  [the longest x4 5.17 us: on_device(): lax.optimization_barrier((turned, cot, cots, more, sheets, right_part, do...]
    ppermute x27, waiting for transfers between devices: 93.5 us -> 100 us  [shifted(): return lax.ppermute(x, axes, pairs)]
    dynamic_update_slice x4 -> x3, local copies, waits for them, and re-layouts: 7.89 us -> 3.21 us  [on_device(): gate = lax.dynamic_update_slice(gate, gates[block], (number * rows, 0))]
    unnamed x35 -> x29, local copies, waits for them, and re-layouts: 14.2 us -> 9.54 us
    ppermute x2 -> x0, local copies, waits for them, and re-layouts: 4.35 us -> none  [shifted(): return lax.ppermute(x, axes, pairs)]
    slice x3, local copies, waits for them, and re-layouts: 4.41 us -> 0.9 us  [on_device(): factors = [out_factor[low:high] for low, high in spans]]
    dynamic_slice x2 -> x3, local copies, waits for them, and re-layouts: 11.7 us -> 12.1 us  [the longest x1 6.05 us: unit_columns(): return lax.dynamic_slice_in_dim(gate_pre, first_unit(to), part, 1)]
  transfers between devices with their start and end apart: 27 -> 27, of which waited for: 11 -> 11; matrix products, arithmetic and copies ran while one was open for 32% -> 25% of each run, Pallas kernels for 17% -> 17%
where the time goes in v9:
time: 270 us; the launch traced here: 269 us
  waiting for transfers between devices  100 us (37%)
  local copies, waits for them, and re-layouts  74.3 us (28%)
  Pallas kernels  52.7 us (20%)
  starting transfers between devices  26.2 us (10%)
  other arithmetic  7.71 us (3%)
  matrix products  6.85 us (3%)
    ppermute x27, waiting for transfers between devices, shifted(): return lax.ppermute(x, axes, pairs)  100 us
    pallas_call x4, Pallas kernels, add_chunk(): pl.pallas_call(functools.partial(chunk_kernel, n, skip), out_shape=jax.Sh...  45.6 us
    dynamic_update_slice x8, local copies, waits for them, and re-layouts, place(): return lax.dynamic_update_slice(cot, block, ((dg * n_seq + ds) * rows, at))  26.4 us
    ppermute x27, starting transfers between devices, shifted(): return lax.ppermute(x, axes, pairs)  26.2 us
    unnamed x29, local copies, waits for them, and re-layouts  9.54 us
    pallas_call x1, Pallas kernels, finish(): pl.pallas_call(functools.partial(final_kernel, n, share), out_shape=(jax....  7.02 us
    slice x3, local copies, waits for them, and re-layouts, on_device(): cuts = [ring[-1][low:high] for low, high in spans]  6.6 us
    dynamic_slice x1, local copies, waits for them, and re-layouts, unit_columns(): return lax.dynamic_slice_in_dim(gate_pre, first_unit(to), part, 1)  6.05 us
  transfers between devices with their start and end apart: 27, of which 11 were waited for; matrix products, arithmetic and copies ran while one was open for 25% of the time, Pallas kernels for 17%

profile of v9, /device:TPU:0, one launch (start us, length us, event | category | flops | bytes accessed | tf_op | source)
XLA Modules:
  0.0 268.7 jit_solution(15352394746899880374)
XLA Ops:
  0.7 4.4 %constant_dynamic-slice_fusion.6.rest_0_ = bf16[1408,1024]{1,0:T(8,128)(2,1)} fusion(bf16[5504,1024]{1,0:T(8,128)(2,1)} %param.11, s32[]{:T(128)S(6)} %select_n.89), kind=kLoop, calls=%fused_computation.38 | loop fusion | bytes 5767172 | tf_op jit(solution)/shard_map/dynamic_slice | solution.py:204
  5.1 3.0 %collective-permute-start = (bf16[1408,1024]{1,0:T(8,128)(2,1)}, bf16[1408,1024]{1,0:T(8,128)(2,1)}, u32[]{:S(2)}, u32[]{:S(2)}) collective-permute-start(bf16[1408,1024]{1,0:T(8,128)(2,1)} %constant_dynamic-slice_fusion.6.rest_0_), channel_id=1, source_target_pairs={{0,4},{4,8},{8,12},{12,0},{1,5},{5,9},{9,13},{13,1},{2,6},{6,10},{... | collective-permute-start | bytes 8650760 | tf_op jit(solution)/shard_map/ppermute | solution.py:25
  11.1 6.0 %constant_dynamic-slice_fusion.3 = (bf16[512,1408]{1,0:T(8,128)(2,1)S(1)}, bf16[512,1408]{1,0:T(8,128)(2,1)S(1)}, bf16[512,1408]{1,0:T(8,128)(2,1)S(1)}, bf16[512,1408]{1,0:T(8,128)(2,1)S(1)}) fusion(bf16[512,5504]{1,0:T(8,128)(2,1)} %param.10, s32[]{:T(128)S(6)} %select_n.96, s32[]{:T(128)S(6)} %select_n.94, s32[]{:T(128)S(6)} %select_n.92, s32[]{:T(128)S(6)} %select_n.97), kind=kLoop, calls=%fused_computation.35 | loop fusion | bytes 11534352 | tf_op jit(solution)/shard_map/dynamic_slice | solution.py:217
  17.2 5.9 %pad_maximum_fusion = (bf16[1024,1408]{1,0:T(8,128)(2,1)S(1)}, bf16[1024,1408]{1,0:T(8,128)(2,1)}) fusion(bf16[512,1408]{1,0:T(8,128)(2,1)S(1)} %get-tuple-element.78, bf16[512,1408]{1,0:T(8,128)(2,1)S(1)} %get-tuple-element.79, bf16[512,1408]{1,0:T(8,128)(2,1)S(1)} %get-tuple-element.80, bf16[512,1408]{1,0:T(8,128)(2,1)S(1)} %get-tuple-element.77), kind=kLoop, calls=%fused_computation | loop fusion | flops 11534336 | bytes 11534336 | tf_op jit(solution)/shard_map/concatenate | solution.py:225
  23.1 32.4 %collective-permute-done.1 = bf16[512,2048]{1,0:T(8,128)(2,1)} collective-permute-done((bf16[512,2048]{1,0:T(8,128)(2,1)}, bf16[512,2048]{1,0:T(8,128)(2,1)}, u32[]{:S(2)}, u32[]{:S(2)}) %collective-permute-start.1) | collective-permute-done | bytes 2097184 | tf_op jit(solution)/shard_map/ppermute | solution.py:25
  56.7 16.2 %collective-permute-done.rest_1_ = bf16[1408,1024]{1,0:T(8,128)(2,1)} collective-permute-done((bf16[1408,1024]{1,0:T(8,128)(2,1)}, bf16[1408,1024]{1,0:T(8,128)(2,1)}, u32[]{:S(2)}, u32[]{:S(2)}) %collective-permute-start) | collective-permute-done | bytes 2883616 | tf_op jit(solution)/shard_map/ppermute | solution.py:25
  91.3 6.0 %broadcast_in_dim.16 = bf16[2048,4096]{1,0:T(8,128)(2,1)} broadcast(bf16[]{:T(256)} %constant.100.clone.1), dimensions={} | broadcast | bytes 16777218 | tf_op jit(solution)/shard_map/broadcast_in_dim | solution.py:255
  97.3 3.2 %constant_dynamic-update-slice_fusion.3 = bf16[2048,4096]{1,0:T(8,128)(2,1)} fusion(bf16[2048,4096]{1,0:T(8,128)(2,1)} %broadcast_in_dim.16, bf16[512,2048]{1,0:T(8,128)(2,1)} %param.9, s32[]{:T(128)S(6)} %select_n.99), kind=kLoop, calls=%fused_computation.33 | loop fusion | bytes 4194308 | tf_op jit(solution)/shard_map/dynamic_update_slice | solution.py:213
  100.5 3.3 %constant_dynamic-update-slice_fusion.2 = bf16[2048,4096]{1,0:T(8,128)(2,1)} fusion(bf16[2048,4096]{1,0:T(8,128)(2,1)} %constant_dynamic-update-slice_fusion.3, bf16[512,2048]{1,0:T(8,128)(2,1)} %collective-permute-done.1, s32[]{:T(128)S(6)} %select_n.101), kind=kLoop, calls=%fused_computation.32 | loop fusion | bytes 4194308 | tf_op jit(solution)/shard_map/dynamic_update_slice | solution.py:213
  104.0 23.7 %collective-permute-done.6 = bf16[512,2048]{1,0:T(8,128)(2,1)} collective-permute-done((bf16[512,2048]{1,0:T(8,128)(2,1)}, bf16[512,2048]{1,0:T(8,128)(2,1)}, u32[]{:S(2)}, u32[]{:S(2)}) %collective-permute-start.6) | collective-permute-done | bytes 2097184 | tf_op jit(solution)/shard_map/ppermute | solution.py:25
  127.8 12.2 %collective-permute-done.8 = bf16[1024,1408]{1,0:T(8,128)(2,1)} collective-permute-done((bf16[1024,1408]{1,0:T(8,128)(2,1)}, bf16[1024,1408]{1,0:T(8,128)(2,1)}, u32[]{:S(2)}, u32[]{:S(2)}) %collective-permute-start.8) | collective-permute-done | bytes 2883616 | tf_op jit(solution)/shard_map/ppermute | solution.py:25
  139.9 3.0 %collective-permute-done.3.rest_2_ = bf16[1408,1024]{1,0:T(8,128)(2,1)} collective-permute-done((bf16[1408,1024]{1,0:T(8,128)(2,1)}, bf16[1408,1024]{1,0:T(8,128)(2,1)}, u32[]{:S(2)}, u32[]{:S(2)}) %collective-permute-start.3) | collective-permute-done | bytes 2883616 | tf_op jit(solution)/shard_map/ppermute | solution.py:25
  149.6 3.1 %fusion.22 = (bf16[512,1408]{1,0:T(8,128)(2,1)}, bf16[2048,1408]{1,0:T(8,128)(2,1)S(1)}) fusion(bf16[1024,1408]{1,0:T(8,128)(2,1)} %collective-permute-done.8, bf16[2048,1408]{1,0:T(8,128)(2,1)S(1)} %constant_dynamic-update-slice_fusion.1), kind=kLoop, calls=%fused_computation.50 | loop fusion | bytes 5767168 | tf_op jit(solution)/shard_map/slice | solution.py:240
  153.8 4.1 %constant_dynamic-update-slice_fusion.9 = bf16[2048,4096]{1,0:T(8,128)(2,1)} fusion(bf16[2048,4096]{1,0:T(8,128)(2,1)} %constant_dynamic-update-slice_fusion.2, bf16[512,2048]{1,0:T(8,128)(2,1)} %collective-permute-done.4, s32[]{:T(128)S(6)} %select_n.99), kind=kLoop, calls=%fused_computation.46 | loop fusion | bytes 4194308 | tf_op jit(solution)/shard_map/dynamic_update_slice | solution.py:213
  157.9 3.2 %constant_dynamic-update-slice_fusion.8 = bf16[2048,4096]{1,0:T(8,128)(2,1)} fusion(bf16[2048,4096]{1,0:T(8,128)(2,1)} %constant_dynamic-update-slice_fusion.9, bf16[512,2048]{1,0:T(8,128)(2,1)} %collective-permute-done.5, s32[]{:T(128)S(6)} %select_n.101), kind=kLoop, calls=%fused_computation.45 | loop fusion | bytes 4194308 | tf_op jit(solution)/shard_map/dynamic_update_slice | solution.py:213
  161.2 3.2 %constant_dynamic-update-slice_fusion.7 = bf16[2048,4096]{1,0:T(8,128)(2,1)} fusion(bf16[2048,4096]{1,0:T(8,128)(2,1)} %constant_dynamic-update-slice_fusion.8, bf16[512,2048]{1,0:T(8,128)(2,1)} %collective-permute-done.2, s32[]{:T(128)S(6)} %select_n.99), kind=kLoop, calls=%fused_computation.44 | loop fusion | bytes 4194308 | tf_op jit(solution)/shard_map/dynamic_update_slice | solution.py:213
  164.4 3.1 %constant_dynamic-update-slice_fusion.5 = bf16[2048,4096]{1,0:T(8,128)(2,1)} fusion(bf16[2048,4096]{1,0:T(8,128)(2,1)} %constant_dynamic-update-slice_fusion.7, bf16[512,2048]{1,0:T(8,128)(2,1)} %collective-permute-done.7, s32[]{:T(128)S(6)} %select_n.99), kind=kLoop, calls=%fused_computation.42 | loop fusion | bytes 4194308 | tf_op jit(solution)/shard_map/dynamic_update_slice | solution.py:213
  167.5 3.2 %constant_dynamic-update-slice_fusion.6 = bf16[2048,4096]{1,0:T(8,128)(2,1)} fusion(bf16[2048,4096]{1,0:T(8,128)(2,1)} %constant_dynamic-update-slice_fusion.5, bf16[512,2048]{1,0:T(8,128)(2,1)} %collective-permute-done.6, s32[]{:T(128)S(6)} %select_n.101), kind=kLoop, calls=%fused_computation.43 | loop fusion | bytes 4194308 | tf_op jit(solution)/shard_map/dynamic_update_slice | solution.py:213
  175.3 4.1 %collective-permute-start.15 = (bf16[256,1024]{1,0:T(8,128)(2,1)}, bf16[256,1024]{1,0:T(8,128)(2,1)S(1)}, u32[]{:S(2)}, u32[]{:S(2)}) collective-permute-start(bf16[256,1024]{1,0:T(8,128)(2,1)} %get-tuple-element.70), channel_id=1, source_target_pairs={{0,4},{4,8},{8,12},{12,0},{1,5},{5,9},{9,13},{13,1},{2,6},{6,10},{... | collective-permute-start | bytes 1572872 | tf_op jit(solution)/shard_map/ppermute | solution.py:25
  179.4 2.6 constant_dynamic-update-slice_fusion.gate_ref
  183.5 3.1 %constant_dynamic-update-slice_fusion.4.cot_ref = bf16[2048,4096]{1,0:T(8,128)(2,1)} fusion(bf16[2048,4096]{1,0:T(8,128)(2,1)} %constant_dynamic-update-slice_fusion.6, bf16[512,2048]{1,0:T(8,128)(2,1)} %collective-permute-done.9, s32[]{:T(128)S(6)} %select_n.101), kind=kLoop, calls=%fused_computation.41 | loop fusion | bytes 4194308 | tf_op jit(solution)/shard_map/dynamic_update_slice | solution.py:213
  187.7 2.6 copy-done.3
  191.5 13.7 %shard_map.103.before_ref = f32[2048,32]{1,0:T(8,128)S(1)} custom-call(s32[1]{0:T(128)} %bitcast.me_ref, bf16[2048,4096]{1,0:T(8,128)(2,1)} %constant_dynamic-update-slice_fusion.4.cot_ref, bf16[2048,1408]{1,0:T(8,128)(2,1)S(1)} %copy-done.3, bf16[512,32]{1,0:T(8,128)(2,1)S(1)} %slice.65.factor_ref, f32[2048,32]{1,0:T(8,128)S(1)} %broadcast_in_dim.19.before_ref, ...), custom_call_target="tpu_custom_call" | custom-call | flops 8589934592 | bytes 23068672 | tf_op jit(solution)/shard_map/pallas_call | solution.py:85
  206.0 12.9 %shard_map.104.before_ref = f32[2048,32]{1,0:T(8,128)S(1)} custom-call(s32[1]{0:T(128)} %bitcast.me_ref, bf16[2048,4096]{1,0:T(8,128)(2,1)} %constant_dynamic-update-slice_fusion.4.cot_ref, bf16[2048,1408]{1,0:T(8,128)(2,1)S(1)} %copy-done.3, bf16[384,32]{1,0:T(8,128)(2,1)S(1)} %slice.66.factor_ref, f32[2048,32]{1,0:T(8,128)S(1)} %shard_map.103.before_ref, ...), custom_call_target="tpu_custom_call" | custom-call | flops 6442450944 | bytes 21495808 | tf_op jit(solution)/shard_map/pallas_call | solution.py:85
  218.9 9.5 %shard_map.105.before_ref = f32[2048,32]{1,0:T(8,128)S(1)} custom-call(s32[1]{0:T(128)} %bitcast.me_ref, bf16[2048,4096]{1,0:T(8,128)(2,1)} %constant_dynamic-update-slice_fusion.4.cot_ref, bf16[2048,1408]{1,0:T(8,128)(2,1)S(1)} %copy-done.3, bf16[256,32]{1,0:T(8,128)(2,1)S(1)} %get-tuple-element.64.factor_ref, f32[2048,32]{1,0:T(8,128)S(1)} %shard_map.104.before_ref, ...), custom_call_target="tpu_custom_call" | custom-call | flops 4294967296 | bytes 19922944 | tf_op jit(solution)/shard_map/pallas_call | solution.py:85
  228.4 9.5 %shard_map.106 = f32[2048,32]{1,0:T(8,128)S(1)} custom-call(s32[1]{0:T(128)} %bitcast.me_ref, bf16[2048,4096]{1,0:T(8,128)(2,1)} %constant_dynamic-update-slice_fusion.4.cot_ref, bf16[2048,1408]{1,0:T(8,128)(2,1)S(1)} %copy-done.3, bf16[256,32]{1,0:T(8,128)(2,1)S(1)} %get-tuple-element.63.factor_ref, f32[2048,32]{1,0:T(8,128)S(1)} %shard_map.105.before_ref, ...), custom_call_target="tpu_custom_call" | custom-call | flops 4294967296 | bytes 19922944 | tf_op jit(solution)/shard_map/pallas_call | solution.py:85
  238.2 2.6 fusion.7
  242.8 2.6 fusion.4
  247.3 2.8 %collective-permute-done.22 = f32[16,1024]{1,0:T(8,128)S(1)} collective-permute-done((f32[16,1024]{1,0:T(8,128)S(1)}, f32[16,1024]{1,0:T(8,128)S(1)}, u32[]{:S(2)}, u32[]{:S(2)}) %collective-permute-start.22) | collective-permute-done | bytes 65568 | tf_op jit(solution)/shard_map/ppermute | solution.py:25
  252.0 3.3 %collective-permute-start.26 = (f32[16,1024]{1,0:T(8,128)S(1)}, f32[16,1024]{1,0:T(8,128)S(1)}, u32[]{:S(2)}, u32[]{:S(2)}) collective-permute-start(f32[16,1024]{1,0:T(8,128)S(1)} %add.161.refs_0_), channel_id=1, source_target_pairs={{0,12},{4,0},{8,4},{12,8},{1,13},{5,1},{9,5},{13,9},{2,14},{6,2},{... | collective-permute-start | bytes 196616 | tf_op jit(solution)/shard_map/ppermute | solution.py:25
  255.3 2.9 %collective-permute-done.24.refs_1_ = f32[16,1024]{1,0:T(8,128)S(1)} collective-permute-done((f32[16,1024]{1,0:T(8,128)S(1)}, f32[16,1024]{1,0:T(8,128)S(1)}, u32[]{:S(2)}, u32[]{:S(2)}) %collective-permute-start.24) | collective-permute-done | bytes 65568 | tf_op jit(solution)/shard_map/ppermute | solution.py:25
  261.7 7.0 %shard_map.107 = (f32[256,1024]{1,0:T(8,128)}, f32[16,512]{1,0:T(8,128)}) custom-call(s32[2]{0:T(128)S(1)} %pad_add_fusion.1.place_ref, f32[512,1024]{1,0:T(8,128)S(1)} %copy-done.5, f32[16,1024]{1,0:T(8,128)S(1)} %add.161.refs_0_, f32[16,1024]{1,0:T(8,128)S(1)} %collective-permute-done.24.refs_1_, f32[16,1024]{1,0:T(8,128)S(1)} %collective-permute-done.25.refs_2_, ...), custom_call_target="tpu_custom_call" | custom-call | tf_op jit(solution)/shard_map/pallas_call | solution.py:168
  (111 shorter events, 49.0 us)
Async XLA Ops:
  0.6 86.5 %copy-start = (bf16[512,2048]{1,0:T(8,128)(2,1)S(1)}, bf16[512,2048]{1,0:T(8,128)(2,1)}, u32[]{:S(2)}) copy-start(bf16[512,2048]{1,0:T(8,128)(2,1)} %param.8) | copy-start | bytes 6291460
  5.1 67.8 %collective-permute-start = (bf16[1408,1024]{1,0:T(8,128)(2,1)}, bf16[1408,1024]{1,0:T(8,128)(2,1)}, u32[]{:S(2)}, u32[]{:S(2)}) collective-permute-start(bf16[1408,1024]{1,0:T(8,128)(2,1)} %constant_dynamic-slice_fusion.6.rest_0_), channel_id=1, source_target_pairs={{0,4},{4,8},{8,12},{12,0},{1,5},{5,9},{9,13},{13,1},{2,6},{6,10},{... | collective-permute-start | bytes 8650760 | tf_op jit(solution)/shard_map/ppermute | solution.py:25
  8.1 47.4 %collective-permute-start.1 = (bf16[512,2048]{1,0:T(8,128)(2,1)}, bf16[512,2048]{1,0:T(8,128)(2,1)}, u32[]{:S(2)}, u32[]{:S(2)}) collective-permute-start(bf16[512,2048]{1,0:T(8,128)(2,1)} %param.9), channel_id=1, source_target_pairs={{0,2},{2,0},{1,3},{3,1},{4,6},{6,4},{5,7},{7,5},{8,10},{10,8},{9,1... | collective-permute-start | bytes 6291464 | tf_op jit(solution)/shard_map/ppermute | solution.py:25
  9.6 47.1 %collective-permute-start.2 = (bf16[512,2048]{1,0:T(8,128)(2,1)}, bf16[512,2048]{1,0:T(8,128)(2,1)}, u32[]{:S(2)}, u32[]{:S(2)}) collective-permute-start(bf16[512,2048]{1,0:T(8,128)(2,1)} %param.9), channel_id=1, source_target_pairs={{0,16},{16,0},{1,17},{17,1},{2,18},{18,2},{3,19},{19,3},{4,20},{20... | collective-permute-start | bytes 6291464 | tf_op jit(solution)/shard_map/ppermute | solution.py:25
  72.9 8.7 %collective-permute-start.4 = (bf16[512,2048]{1,0:T(8,128)(2,1)}, bf16[512,2048]{1,0:T(8,128)(2,1)}, u32[]{:S(2)}, u32[]{:S(2)}) collective-permute-start(bf16[512,2048]{1,0:T(8,128)(2,1)} %param.9), channel_id=1, source_target_pairs={{0,1},{1,0},{2,3},{3,2},{4,5},{5,4},{6,7},{7,6},{8,9},{9,8},{10,11... | collective-permute-start | bytes 6291464 | tf_op jit(solution)/shard_map/ppermute | solution.py:25
  74.7 7.0 %collective-permute-start.10 = (bf16[512,1408]{1,0:T(8,128)(2,1)}, bf16[512,1408]{1,0:T(8,128)(2,1)S(1)}, u32[]{:S(2)}, u32[]{:S(2)}) collective-permute-start(bf16[512,1408]{1,0:T(8,128)(2,1)} %get-tuple-element.83), channel_id=1, source_target_pairs={{0,1},{1,0},{2,3},{3,2},{4,5},{5,4},{6,7},{7,6},{8,9},{9,8},{10,11... | collective-permute-start | bytes 4325384 | tf_op jit(solution)/shard_map/ppermute | solution.py:25
  75.2 64.7 %collective-permute-start.8 = (bf16[1024,1408]{1,0:T(8,128)(2,1)}, bf16[1024,1408]{1,0:T(8,128)(2,1)}, u32[]{:S(2)}, u32[]{:S(2)}) collective-permute-start(bf16[1024,1408]{1,0:T(8,128)(2,1)} %get-tuple-element.45), channel_id=1, source_target_pairs={{0,16},{16,0},{1,17},{17,1},{2,18},{18,2},{3,19},{19,3},{4,20},{20... | collective-permute-start | bytes 8650760 | tf_op jit(solution)/shard_map/ppermute | solution.py:25
  76.8 66.2 %collective-permute-start.3 = (bf16[1408,1024]{1,0:T(8,128)(2,1)}, bf16[1408,1024]{1,0:T(8,128)(2,1)}, u32[]{:S(2)}, u32[]{:S(2)}) collective-permute-start(bf16[1408,1024]{1,0:T(8,128)(2,1)} %collective-permute-done.rest_1_), channel_id=1, source_target_pairs={{0,4},{4,8},{8,12},{12,0},{1,5},{5,9},{9,13},{13,1},{2,6},{6,10},{... | collective-permute-start | bytes 8650760 | tf_op jit(solution)/shard_map/ppermute | solution.py:25
  80.2 47.6 %collective-permute-start.6 = (bf16[512,2048]{1,0:T(8,128)(2,1)}, bf16[512,2048]{1,0:T(8,128)(2,1)}, u32[]{:S(2)}, u32[]{:S(2)}) collective-permute-start(bf16[512,2048]{1,0:T(8,128)(2,1)} %collective-permute-done.2), channel_id=1, source_target_pairs={{0,2},{2,0},{1,3},{3,1},{4,6},{6,4},{5,7},{7,5},{8,10},{10,8},{9,1... | collective-permute-start | bytes 6291464 | tf_op jit(solution)/shard_map/ppermute | solution.py:25
  81.7 46.1 %collective-permute-start.7 = (bf16[512,2048]{1,0:T(8,128)(2,1)}, bf16[512,2048]{1,0:T(8,128)(2,1)}, u32[]{:S(2)}, u32[]{:S(2)}) collective-permute-start(bf16[512,2048]{1,0:T(8,128)(2,1)} %collective-permute-done.2), channel_id=1, source_target_pairs={{0,1},{1,0},{2,3},{3,2},{4,5},{5,4},{6,7},{7,6},{8,9},{9,8},{10,11... | collective-permute-start | bytes 6291464 | tf_op jit(solution)/shard_map/ppermute | solution.py:25
  81.7 22.3 %collective-permute-start.5 = (bf16[512,2048]{1,0:T(8,128)(2,1)}, bf16[512,2048]{1,0:T(8,128)(2,1)}, u32[]{:S(2)}, u32[]{:S(2)}) collective-permute-start(bf16[512,2048]{1,0:T(8,128)(2,1)} %collective-permute-done.1), channel_id=1, source_target_pairs={{0,1},{1,0},{2,3},{3,2},{4,5},{5,4},{6,7},{7,6},{8,9},{9,8},{10,11... | collective-permute-start | bytes 6291464 | tf_op jit(solution)/shard_map/ppermute | solution.py:25
  152.7 8.4 %copy-start.2 = (bf16[2048,1408]{1,0:T(8,128)(2,1)}, bf16[2048,1408]{1,0:T(8,128)(2,1)S(1)}, u32[]{:S(2)}) copy-start(bf16[2048,1408]{1,0:T(8,128)(2,1)S(1)} %get-tuple-element.82) | copy-start | bytes 17301508
  152.7 22.6 %collective-permute-start.11 = (bf16[512,1408]{1,0:T(8,128)(2,1)}, bf16[512,1408]{1,0:T(8,128)(2,1)}, u32[]{:S(2)}, u32[]{:S(2)}) collective-permute-start(bf16[512,1408]{1,0:T(8,128)(2,1)} %get-tuple-element.81), channel_id=1, source_target_pairs={{0,1},{1,0},{2,3},{3,2},{4,5},{5,4},{6,7},{7,6},{8,9},{9,8},{10,11... | collective-permute-start | bytes 4325384 | tf_op jit(solution)/shard_map/ppermute | solution.py:25
  152.7 29.3 %collective-permute-start.9 = (bf16[512,2048]{1,0:T(8,128)(2,1)}, bf16[512,2048]{1,0:T(8,128)(2,1)}, u32[]{:S(2)}, u32[]{:S(2)}) collective-permute-start(bf16[512,2048]{1,0:T(8,128)(2,1)} %collective-permute-done.6), channel_id=1, source_target_pairs={{0,1},{1,0},{2,3},{3,2},{4,5},{5,4},{6,7},{7,6},{8,9},{9,8},{10,11... | collective-permute-start | bytes 6291464 | tf_op jit(solution)/shard_map/ppermute | solution.py:25
  153.2 33.4 %collective-permute-start.12 = (bf16[512,1024]{1,0:T(8,128)(2,1)}, bf16[512,1024]{1,0:T(8,128)(2,1)S(1)}, u32[]{:S(2)}, u32[]{:S(2)}) collective-permute-start(bf16[512,1024]{1,0:T(8,128)(2,1)} %slice.53), channel_id=1, source_target_pairs={{0,4},{4,8},{8,12},{12,0},{1,5},{5,9},{9,13},{13,1},{2,6},{6,10},{... | collective-permute-start | bytes 3145736 | tf_op jit(solution)/shard_map/ppermute | solution.py:25
  153.2 52.1 %collective-permute-start.13 = (bf16[384,1024]{1,0:T(8,128)(2,1)}, bf16[384,1024]{1,0:T(8,128)(2,1)}, u32[]{:S(2)}, u32[]{:S(2)}) collective-permute-start(bf16[384,1024]{1,0:T(8,128)(2,1)} %slice.54.rest_2_), channel_id=1, source_target_pairs={{0,4},{4,8},{8,12},{12,0},{1,5},{5,9},{9,13},{13,1},{2,6},{6,10},{... | collective-permute-start | bytes 2359304 | tf_op jit(solution)/shard_map/ppermute | solution.py:25
  153.2 17.6 %collective-permute-start.18 = (s32[1,16]{1,0:T(1,128)S(1)}, s32[1,16]{1,0:T(1,128)S(1)}, u32[]{:S(2)}, u32[]{:S(2)}) collective-permute-start(s32[1,16]{1,0:T(1,128)S(1)} %copy-done.13), channel_id=1, source_target_pairs={{0,16},{16,0},{1,17},{17,1},{2,18},{18,2},{3,19},{19,3},{4,20},{20... | collective-permute-start | bytes 200 | tf_op jit(solution)/shard_map/ppermute | solution.py:25
  170.8 4.3 %collective-permute-start.16 = (f32[512,32]{0,1:T(8,128)S(1)}, f32[512,32]{0,1:T(8,128)S(1)}, u32[]{:S(2)}, u32[]{:S(2)}) collective-permute-start(f32[512,32]{0,1:T(8,128)S(1)} %fusion.27), channel_id=1, source_target_pairs={{0,2},{2,0},{1,3},{3,1},{4,6},{6,4},{5,7},{7,5},{8,10},{10,8},{9,1... | collective-permute-start | bytes 196616 | tf_op jit(solution)/shard_map/ppermute | solution.py:25
  175.1 43.8 %collective-permute-start.14 = (bf16[256,1024]{1,0:T(8,128)(2,1)}, bf16[256,1024]{1,0:T(8,128)(2,1)S(1)}, u32[]{:S(2)}, u32[]{:S(2)}) collective-permute-start(bf16[256,1024]{1,0:T(8,128)(2,1)} %get-tuple-element.69), channel_id=1, source_target_pairs={{0,4},{4,8},{8,12},{12,0},{1,5},{5,9},{9,13},{13,1},{2,6},{6,10},{... | collective-permute-start | bytes 1572872 | tf_op jit(solution)/shard_map/ppermute | solution.py:25
  175.3 53.2 %collective-permute-start.15 = (bf16[256,1024]{1,0:T(8,128)(2,1)}, bf16[256,1024]{1,0:T(8,128)(2,1)S(1)}, u32[]{:S(2)}, u32[]{:S(2)}) collective-permute-start(bf16[256,1024]{1,0:T(8,128)(2,1)} %get-tuple-element.70), channel_id=1, source_target_pairs={{0,4},{4,8},{8,12},{12,0},{1,5},{5,9},{9,13},{13,1},{2,6},{6,10},{... | collective-permute-start | bytes 1572872 | tf_op jit(solution)/shard_map/ppermute | solution.py:25
  182.0 56.2 %collective-permute-start.19 = (f32[512,32]{0,1:T(8,128)S(1)}, f32[512,32]{0,1:T(8,128)S(1)}, u32[]{:S(2)}, u32[]{:S(2)}) collective-permute-start(f32[512,32]{0,1:T(8,128)S(1)} %add.158), channel_id=1, source_target_pairs={{0,16},{1,17},{16,0},{17,1},{2,18},{3,19},{18,2},{19,3},{4,20},{5,... | collective-permute-start | bytes 196616 | tf_op jit(solution)/shard_map/ppermute | solution.py:25
  187.6 50.6 %collective-permute-start.20 = (f32[512,32]{0,1:T(8,128)S(1)}, f32[512,32]{0,1:T(8,128)}, u32[]{:S(2)}, u32[]{:S(2)}) collective-permute-start(f32[512,32]{0,1:T(8,128)S(1)} %add.158), channel_id=1, source_target_pairs={{0,17},{1,16},{16,1},{17,0},{2,19},{3,18},{18,3},{19,2},{4,21},{5,... | collective-permute-start | bytes 196616 | tf_op jit(solution)/shard_map/ppermute | solution.py:25
  191.5 14.4 %copy-start.4 = (bf16[384,1024]{1,0:T(8,128)(2,1)S(1)}, bf16[384,1024]{1,0:T(8,128)(2,1)}, u32[]{:S(2)}) copy-start(bf16[384,1024]{1,0:T(8,128)(2,1)} %slice.62.rest_1_) | copy-start | bytes 2359300
  205.3 37.5 %collective-permute-start.17 = (f32[512,32]{0,1:T(8,128)S(1)}, f32[512,32]{0,1:T(8,128)}, u32[]{:S(2)}, u32[]{:S(2)}) collective-permute-start(f32[512,32]{0,1:T(8,128)S(1)} %add.158), channel_id=1, source_target_pairs={{0,1},{1,0},{16,17},{17,16},{2,3},{3,2},{18,19},{19,18},{4,5},{5,4... | collective-permute-start | bytes 196616 | tf_op jit(solution)/shard_map/ppermute | solution.py:25
  240.8 27.9 %copy-start.1 = (bf16[512,2048]{1,0:T(8,128)(2,1)S(1)}, bf16[512,2048]{1,0:T(8,128)(2,1)}, u32[]{:S(2)}) copy-start(bf16[512,2048]{1,0:T(8,128)(2,1)} %param.8) | copy-start | bytes 6291460
  241.1 4.6 %collective-permute-start.21 = (f32[16,1024]{1,0:T(8,128)S(1)}, f32[16,1024]{1,0:T(8,128)S(1)}, u32[]{:S(2)}, u32[]{:S(2)}) collective-permute-start(f32[16,1024]{1,0:T(8,128)S(1)} %reshape.77), channel_id=1, source_target_pairs={{0,16},{16,0},{1,17},{17,1},{2,18},{18,2},{3,19},{19,3},{4,20},{20... | collective-permute-start | bytes 196616 | tf_op jit(solution)/shard_map/ppermute | solution.py:25
  245.7 4.3 %collective-permute-start.22 = (f32[16,1024]{1,0:T(8,128)S(1)}, f32[16,1024]{1,0:T(8,128)S(1)}, u32[]{:S(2)}, u32[]{:S(2)}) collective-permute-start(f32[16,1024]{1,0:T(8,128)S(1)} %add.159), channel_id=1, source_target_pairs={{0,2},{2,0},{1,3},{3,1},{4,6},{6,4},{5,7},{7,5},{8,10},{10,8},{9,1... | collective-permute-start | bytes 196616 | tf_op jit(solution)/shard_map/ppermute | solution.py:25
  250.0 1.3 collective-permute-start.23
  251.4 17.3 %copy-start.8 = (f32[16,1024]{1,0:T(8,128)}, f32[16,1024]{1,0:T(8,128)S(1)}, u32[]{:S(2)}) copy-start(f32[16,1024]{1,0:T(8,128)S(1)} %add.161.refs_0_) | copy-start | bytes 196612
  251.4 6.8 %collective-permute-start.24 = (f32[16,1024]{1,0:T(8,128)S(1)}, f32[16,1024]{1,0:T(8,128)S(1)}, u32[]{:S(2)}, u32[]{:S(2)}) collective-permute-start(f32[16,1024]{1,0:T(8,128)S(1)} %add.161.refs_0_), channel_id=1, source_target_pairs={{0,4},{4,8},{8,12},{12,0},{1,5},{5,9},{9,13},{13,1},{2,6},{6,10},{... | collective-permute-start | bytes 196616 | tf_op jit(solution)/shard_map/ppermute | solution.py:25
  251.5 8.6 %collective-permute-start.25 = (f32[16,1024]{1,0:T(8,128)S(1)}, f32[16,1024]{1,0:T(8,128)S(1)}, u32[]{:S(2)}, u32[]{:S(2)}) collective-permute-start(f32[16,1024]{1,0:T(8,128)S(1)} %add.161.refs_0_), channel_id=1, source_target_pairs={{0,8},{4,12},{8,0},{12,4},{1,9},{5,13},{9,1},{13,5},{2,10},{6,14},... | collective-permute-start | bytes 196616 | tf_op jit(solution)/shard_map/ppermute | solution.py:25
  252.0 8.1 %collective-permute-start.26 = (f32[16,1024]{1,0:T(8,128)S(1)}, f32[16,1024]{1,0:T(8,128)S(1)}, u32[]{:S(2)}, u32[]{:S(2)}) collective-permute-start(f32[16,1024]{1,0:T(8,128)S(1)} %add.161.refs_0_), channel_id=1, source_target_pairs={{0,12},{4,0},{8,4},{12,8},{1,13},{5,1},{9,5},{13,9},{2,14},{6,2},{... | collective-permute-start | bytes 196616 | tf_op jit(solution)/shard_map/ppermute | solution.py:25
  (9 other events, 19.2 us)

commit v10 on v9

--- a/solution.py
+++ b/solution.py
@@ -230,31 +230,32 @@
     for dg in range(1, n_groups):
         sheets[dg] = shifted(sheets[dg], "groups", (n_groups,), (dg,))
     turned = shifted(ring[-1], "dp", (n_dp,), (1,))
-    turned, cots = lax.optimization_barrier((turned, cots))
-    ring.append(turned)
-
-    gates, more = {}, {}
-
-    def spread(dg, sheet):
-        for ds in range(n_seq):
-            x = sheet[ds * rows:(ds + 1) * rows]
-            gates[dg, ds] = x if ds == 0 else across(x, ds)
-
-    spread(0, sheets[0])
-    for (dg, _, r), x in cots.items():
-        for ds in range(1, n_seq):
-            more[dg, ds, r] = across(x, ds)
-    for dg in range(1, n_groups):
-        for r in range(1, n_tensor):
-            more[dg, 0, r] = shifted(cots[dg, 0, 0], "tensor", (n_tensor,), (r,))
     right_part = jnp.dot(inputs, proj_in, preferred_element_type=jnp.float32)
     out_factor = lax.dynamic_slice_in_dim(proj_out, start, part, 0)
     once = start + jnp.arange(part, dtype=jnp.int32) >= mine * part
     out_factor = jnp.where(once[:, None], out_factor, 0).astype(proj_out.dtype)
     factors = [out_factor[low:high] for low, high in spans]
+    turned, cots, right_part, factors = lax.optimization_barrier((turned, cots, right_part, factors))
+    ring.append(turned)
+
+    gates, more = {}, {}
+
+    def spread(dg, sheet):
+        for ds in range(n_seq):
+            x = sheet[ds * rows:(ds + 1) * rows]
+            gates[dg, ds] = x if ds == 0 else across(x, ds)
+
+    spread(0, sheets[0])
+    for (dg, _, r), x in cots.items():
+        for ds in range(1, n_seq):
+            more[dg, ds, r] = across(x, ds)
+    for dg in range(1, n_groups):
+        for r in range(1, n_tensor):
+            more[dg, 0, r] = shifted(cots[dg, 0, 0], "tensor", (n_tensor,), (r,))
     cot = jnp.zeros((len(order) * rows, n_tensor * cotangent.shape[1]), cotangent.dtype)
-    for r in range(n_tensor):
-        cot = place(cot, 0, 0, r, cots[0, 0, r])
+    early = {**cots, **{key: block for key, block in more.items() if key[1] > 0}}
+    for key, block in early.items():
+        cot = place(cot, *key, block)
     turned = shifted(ring[-1], "dp", (n_dp,), (1,)) if n_dp > 3 else ring.pop()
     turned, cot, cots, more, sheets, right_part, doc_lens, factors = lax.optimization_barrier(
         (turned, cot, cots, more, sheets, right_part, doc_lens, factors)
@@ -281,7 +282,7 @@
 
     gate = jnp.zeros((len(order) * rows, part), gate_pre.dtype)
     for (dg, ds, r), block in sorted(cots.items(), key=lambda item: (item[0][0] * item[0][2], item[0])):
-        if (dg, ds) != (0, 0):
+        if (dg, ds, r) not in early:
             cot = place(cot, dg, ds, r, block)
     for number, block in enumerate(order):
         gate = lax.dynamic_update_slice(gate, gates[block], (number * rows, 0))

time: 270 us -> 264 us (0.978)
  local copies, waits for them, and re-layouts: 74.3 us -> 67.7 us
  waiting for transfers between devices: 100 us -> 105 us
    unnamed x29 -> x21, local copies, waits for them, and re-layouts: 9.54 us -> 1.87 us
    dynamic_update_slice x3, local copies, waits for them, and re-layouts: 3.21 us -> 9.44 us  [on_device(): gate = lax.dynamic_update_slice(gate, gates[block], (number * rows, 0))]
    ppermute x27, waiting for transfers between devices: 100 us -> 105 us  [shifted(): return lax.ppermute(x, axes, pairs)]
    slice x3, local copies, waits for them, and re-layouts: 6.6 us -> 3.01 us  [on_device(): cuts = [ring[-1][low:high] for low, high in spans]]
  transfers between devices with their start and end apart: 27 -> 27, of which waited for: 11 -> 14; matrix products, arithmetic and copies ran while one was open for 25% -> 27% of each run, Pallas kernels for 17% -> 17%
where the time goes in v10:
time: 264 us; the launch traced here: 263 us
  waiting for transfers between devices  105 us (40%)
  local copies, waits for them, and re-layouts  67.7 us (26%)
  Pallas kernels  53 us (20%)
  starting transfers between devices  24.1 us (9%)
  other arithmetic  7.34 us (3%)
  matrix products  5.11 us (2%)
    ppermute x27, waiting for transfers between devices, shifted(): return lax.ppermute(x, axes, pairs)  105 us
    pallas_call x4, Pallas kernels, add_chunk(): pl.pallas_call(functools.partial(chunk_kernel, n, skip), out_shape=jax.Sh...  46 us
    dynamic_update_slice x8, local copies, waits for them, and re-layouts, place(): return lax.dynamic_update_slice(cot, block, ((dg * n_seq + ds) * rows, at))  25.5 us
    ppermute x27, starting transfers between devices, shifted(): return lax.ppermute(x, axes, pairs)  24.1 us
    dynamic_update_slice x3, local copies, waits for them, and re-layouts, on_device(): gate = lax.dynamic_update_slice(gate, gates[block], (number * rows, 0))  9.44 us
    pallas_call x1, Pallas kernels, finish(): pl.pallas_call(functools.partial(final_kernel, n, share), out_shape=(jax....  7.02 us
    dynamic_slice x1, local copies, waits for them, and re-layouts, unit_columns(): return lax.dynamic_slice_in_dim(gate_pre, first_unit(to), part, 1)  6.07 us
    broadcast_in_dim x1, local copies, waits for them, and re-layouts, on_device(): jnp.zeros((len(order) * rows, n_tensor * cotangent.shape[1]), cotangent.d...  5.97 us
  transfers between devices with their start and end apart: 27, of which 14 were waited for; matrix products, arithmetic and copies ran while one was open for 27% of the time, Pallas kernels for 17%

profile of v10, /device:TPU:0, one launch (start us, length us, event | category | flops | bytes accessed | tf_op | source)
XLA Modules:
  0.0 263.4 jit_solution(10630426676857233496)
XLA Ops:
  0.7 4.4 %constant_dynamic-slice_fusion.6.rest_0_ = bf16[1408,1024]{1,0:T(8,128)(2,1)} fusion(bf16[5504,1024]{1,0:T(8,128)(2,1)} %param.11, s32[]{:T(128)S(6)} %select_n.89), kind=kLoop, calls=%fused_computation.38 | loop fusion | bytes 5767172 | tf_op jit(solution)/shard_map/dynamic_slice | solution.py:204
  5.1 3.0 %collective-permute-start = (bf16[1408,1024]{1,0:T(8,128)(2,1)}, bf16[1408,1024]{1,0:T(8,128)(2,1)}, u32[]{:S(2)}, u32[]{:S(2)}) collective-permute-start(bf16[1408,1024]{1,0:T(8,128)(2,1)} %constant_dynamic-slice_fusion.6.rest_0_), channel_id=1, source_target_pairs={{0,4},{4,8},{8,12},{12,0},{1,5},{5,9},{9,13},{13,1},{2,6},{6,10},{... | collective-permute-start | bytes 8650760 | tf_op jit(solution)/shard_map/ppermute | solution.py:25
  13.5 6.1 %constant_dynamic-slice_fusion.3 = (bf16[512,1408]{1,0:T(8,128)(2,1)S(1)}, bf16[512,1408]{1,0:T(8,128)(2,1)S(1)}, bf16[512,1408]{1,0:T(8,128)(2,1)S(1)}, bf16[512,1408]{1,0:T(8,128)(2,1)S(1)}) fusion(bf16[512,5504]{1,0:T(8,128)(2,1)} %param.10, s32[]{:T(128)S(6)} %select_n.96, s32[]{:T(128)S(6)} %select_n.94, s32[]{:T(128)S(6)} %select_n.92, s32[]{:T(128)S(6)} %select_n.97), kind=kLoop, calls=%fused_computation.35 | loop fusion | bytes 11534352 | tf_op jit(solution)/shard_map/dynamic_slice | solution.py:217
  19.5 5.9 %pad_maximum_fusion = (bf16[1024,1408]{1,0:T(8,128)(2,1)S(1)}, bf16[1024,1408]{1,0:T(8,128)(2,1)}) fusion(bf16[512,1408]{1,0:T(8,128)(2,1)S(1)} %get-tuple-element.72, bf16[512,1408]{1,0:T(8,128)(2,1)S(1)} %get-tuple-element.73, bf16[512,1408]{1,0:T(8,128)(2,1)S(1)} %get-tuple-element.74, bf16[512,1408]{1,0:T(8,128)(2,1)S(1)} %get-tuple-element.71), kind=kLoop, calls=%fused_computation | loop fusion | flops 11534336 | bytes 11534336 | tf_op jit(solution)/shard_map/concatenate | solution.py:225
  25.4 30.1 %collective-permute-done.1 = bf16[512,2048]{1,0:T(8,128)(2,1)} collective-permute-done((bf16[512,2048]{1,0:T(8,128)(2,1)}, bf16[512,2048]{1,0:T(8,128)(2,1)}, u32[]{:S(2)}, u32[]{:S(2)}) %collective-permute-start.1) | collective-permute-done | bytes 2097184 | tf_op jit(solution)/shard_map/ppermute | solution.py:25
  56.8 16.2 %collective-permute-done.rest_1_ = bf16[1408,1024]{1,0:T(8,128)(2,1)} collective-permute-done((bf16[1408,1024]{1,0:T(8,128)(2,1)}, bf16[1408,1024]{1,0:T(8,128)(2,1)}, u32[]{:S(2)}, u32[]{:S(2)}) %collective-permute-start) | collective-permute-done | bytes 2883616 | tf_op jit(solution)/shard_map/ppermute | solution.py:25
  76.3 3.0 %collective-permute-done.10 = bf16[512,1408]{1,0:T(8,128)(2,1)} collective-permute-done((bf16[512,1408]{1,0:T(8,128)(2,1)S(1)}, bf16[512,1408]{1,0:T(8,128)(2,1)}, u32[]{:S(2)}, u32[]{:S(2)}) %collective-permute-start.10) | collective-permute-done | bytes 1441824 | tf_op jit(solution)/shard_map/ppermute | solution.py:25
  81.0 4.3 %dynamic_update_slice.44 = bf16[2048,1408]{1,0:T(8,128)(2,1)} pad(bf16[512,1408]{1,0:T(8,128)(2,1)} %get-tuple-element.78, bf16[]{:T(256)} %constant.100.clone.1), padding=0_1536x0_0 | pad | bytes 7208962 | tf_op jit(solution)/shard_map/dynamic_update_slice | solution.py:288
  85.2 6.0 %broadcast_in_dim.18 = bf16[2048,4096]{1,0:T(8,128)(2,1)} broadcast(bf16[]{:T(256)} %constant.100.clone.1), dimensions={} | broadcast | bytes 16777218 | tf_op jit(solution)/shard_map/broadcast_in_dim | solution.py:255
  91.2 3.2 %constant_dynamic-update-slice_fusion.3 = bf16[2048,4096]{1,0:T(8,128)(2,1)} fusion(bf16[2048,4096]{1,0:T(8,128)(2,1)} %broadcast_in_dim.18, bf16[512,2048]{1,0:T(8,128)(2,1)} %param.9, s32[]{:T(128)S(6)} %select_n.100), kind=kLoop, calls=%fused_computation.32 | loop fusion | bytes 4194308 | tf_op jit(solution)/shard_map/dynamic_update_slice | solution.py:213
  94.4 3.2 %constant_dynamic-update-slice_fusion.2 = bf16[2048,4096]{1,0:T(8,128)(2,1)} fusion(bf16[2048,4096]{1,0:T(8,128)(2,1)} %constant_dynamic-update-slice_fusion.3, bf16[512,2048]{1,0:T(8,128)(2,1)} %collective-permute-done.1, s32[]{:T(128)S(6)} %select_n.102), kind=kLoop, calls=%fused_computation.31 | loop fusion | bytes 4194308 | tf_op jit(solution)/shard_map/dynamic_update_slice | solution.py:213
  97.6 3.2 %constant_dynamic-update-slice_fusion.7 = bf16[2048,4096]{1,0:T(8,128)(2,1)} fusion(bf16[2048,4096]{1,0:T(8,128)(2,1)} %constant_dynamic-update-slice_fusion.2, bf16[512,2048]{1,0:T(8,128)(2,1)} %collective-permute-done.2, s32[]{:T(128)S(6)} %select_n.100), kind=kLoop, calls=%fused_computation.44 | loop fusion | bytes 4194308 | tf_op jit(solution)/shard_map/dynamic_update_slice | solution.py:213
  103.4 3.2 %constant_dynamic-update-slice_fusion.9 = bf16[2048,4096]{1,0:T(8,128)(2,1)} fusion(bf16[2048,4096]{1,0:T(8,128)(2,1)} %constant_dynamic-update-slice_fusion.7, bf16[512,2048]{1,0:T(8,128)(2,1)} %collective-permute-done.4, s32[]{:T(128)S(6)} %select_n.100), kind=kLoop, calls=%fused_computation.46 | loop fusion | bytes 4194308 | tf_op jit(solution)/shard_map/dynamic_update_slice | solution.py:213
  106.6 3.2 %constant_dynamic-update-slice_fusion.8 = bf16[2048,4096]{1,0:T(8,128)(2,1)} fusion(bf16[2048,4096]{1,0:T(8,128)(2,1)} %constant_dynamic-update-slice_fusion.9, bf16[512,2048]{1,0:T(8,128)(2,1)} %collective-permute-done.5, s32[]{:T(128)S(6)} %select_n.102), kind=kLoop, calls=%fused_computation.45 | loop fusion | bytes 4194308 | tf_op jit(solution)/shard_map/dynamic_update_slice | solution.py:213
  109.8 3.1 %constant_dynamic-update-slice_fusion.5 = bf16[2048,4096]{1,0:T(8,128)(2,1)} fusion(bf16[2048,4096]{1,0:T(8,128)(2,1)} %constant_dynamic-update-slice_fusion.8, bf16[512,2048]{1,0:T(8,128)(2,1)} %collective-permute-done.6, s32[]{:T(128)S(6)} %select_n.100), kind=kLoop, calls=%fused_computation.42 | loop fusion | bytes 4194308 | tf_op jit(solution)/shard_map/dynamic_update_slice | solution.py:213
  112.9 14.7 %collective-permute-done.7 = bf16[512,2048]{1,0:T(8,128)(2,1)} collective-permute-done((bf16[512,2048]{1,0:T(8,128)(2,1)}, bf16[512,2048]{1,0:T(8,128)(2,1)}, u32[]{:S(2)}, u32[]{:S(2)}) %collective-permute-start.7) | collective-permute-done | bytes 2097184 | tf_op jit(solution)/shard_map/ppermute | solution.py:25
  127.7 11.8 %collective-permute-done.8 = bf16[1024,1408]{1,0:T(8,128)(2,1)} collective-permute-done((bf16[1024,1408]{1,0:T(8,128)(2,1)}, bf16[1024,1408]{1,0:T(8,128)(2,1)}, u32[]{:S(2)}, u32[]{:S(2)}) %collective-permute-start.8) | collective-permute-done | bytes 2883616 | tf_op jit(solution)/shard_map/ppermute | solution.py:25
  139.5 2.9 %collective-permute-done.3.rest_2_ = bf16[1408,1024]{1,0:T(8,128)(2,1)S(1)} collective-permute-done((bf16[1408,1024]{1,0:T(8,128)(2,1)}, bf16[1408,1024]{1,0:T(8,128)(2,1)S(1)}, u32[]{:S(2)}, u32[]{:S(2)}) %collective-permute-start.3) | collective-permute-done | bytes 2883616 | tf_op jit(solution)/shard_map/ppermute | solution.py:25
  145.5 3.7 %fusion.22 = (bf16[512,1408]{1,0:T(8,128)(2,1)}, bf16[2048,1408]{1,0:T(8,128)(2,1)}) fusion(bf16[1024,1408]{1,0:T(8,128)(2,1)} %collective-permute-done.8, bf16[2048,1408]{1,0:T(8,128)(2,1)} %constant_dynamic-update-slice_fusion.1), kind=kLoop, calls=%fused_computation.50 | loop fusion | bytes 5767168 | tf_op jit(solution)/shard_map/slice | solution.py:245
  156.1 3.2 %constant_dynamic-update-slice_fusion.6 = bf16[2048,4096]{1,0:T(8,128)(2,1)} fusion(bf16[2048,4096]{1,0:T(8,128)(2,1)} %constant_dynamic-update-slice_fusion.5, bf16[512,2048]{1,0:T(8,128)(2,1)} %collective-permute-done.7, s32[]{:T(128)S(6)} %select_n.102), kind=kLoop, calls=%fused_computation.43 | loop fusion | bytes 4194308 | tf_op jit(solution)/shard_map/dynamic_update_slice | solution.py:213
  161.8 3.9 %collective-permute-start.15 = (bf16[256,1024]{1,0:T(8,128)(2,1)}, bf16[256,1024]{1,0:T(8,128)(2,1)S(1)}, u32[]{:S(2)}, u32[]{:S(2)}) collective-permute-start(bf16[256,1024]{1,0:T(8,128)(2,1)} %get-tuple-element.64), channel_id=1, source_target_pairs={{0,4},{4,8},{8,12},{12,0},{1,5},{5,9},{9,13},{13,1},{2,6},{6,10},{... | collective-permute-start | bytes 1572872 | tf_op jit(solution)/shard_map/ppermute | solution.py:25
  169.8 3.1 %constant_dynamic-update-slice_fusion.4.cot_ref = bf16[2048,4096]{1,0:T(8,128)(2,1)} fusion(bf16[2048,4096]{1,0:T(8,128)(2,1)} %constant_dynamic-update-slice_fusion.6, bf16[512,2048]{1,0:T(8,128)(2,1)} %collective-permute-done.9, s32[]{:T(128)S(6)} %select_n.102), kind=kLoop, calls=%fused_computation.41 | loop fusion | bytes 4194308 | tf_op jit(solution)/shard_map/dynamic_update_slice | solution.py:213
  173.0 10.7 %collective-permute-done.12.rest_3_ = bf16[512,1024]{1,0:T(8,128)(2,1)} collective-permute-done((bf16[512,1024]{1,0:T(8,128)(2,1)}, bf16[512,1024]{1,0:T(8,128)(2,1)}, u32[]{:S(2)}, u32[]{:S(2)}) %collective-permute-start.12) | collective-permute-done | bytes 1048608 | tf_op jit(solution)/shard_map/ppermute | solution.py:25
  183.7 13.9 %shard_map.103.before_ref = f32[2048,32]{1,0:T(8,128)S(1)} custom-call(s32[1]{0:T(128)} %bitcast.me_ref, bf16[2048,4096]{1,0:T(8,128)(2,1)} %constant_dynamic-update-slice_fusion.4.cot_ref, bf16[2048,1408]{1,0:T(8,128)(2,1)} %constant_dynamic-update-slice_fusion.gate_ref, bf16[512,32]{1,0:T(8,128)(2,1)S(1)} %slice.65.factor_ref, ...), custom_call_target="tpu_custom_call" | custom-call | flops 8589934592 | bytes 23068672 | tf_op jit(solution)/shard_map/pallas_call | solution.py:85
  197.7 2.8 %collective-permute-done.13.rest_3_ = bf16[384,1024]{1,0:T(8,128)(2,1)} collective-permute-done((bf16[384,1024]{1,0:T(8,128)(2,1)}, bf16[384,1024]{1,0:T(8,128)(2,1)}, u32[]{:S(2)}, u32[]{:S(2)}) %collective-permute-start.13) | collective-permute-done | bytes 786464 | tf_op jit(solution)/shard_map/ppermute | solution.py:25
  200.5 13.2 %shard_map.104.before_ref = f32[2048,32]{1,0:T(8,128)S(1)} custom-call(s32[1]{0:T(128)} %bitcast.me_ref, bf16[2048,4096]{1,0:T(8,128)(2,1)} %constant_dynamic-update-slice_fusion.4.cot_ref, bf16[2048,1408]{1,0:T(8,128)(2,1)} %constant_dynamic-update-slice_fusion.gate_ref, bf16[384,32]{1,0:T(8,128)(2,1)S(1)} %slice.66.factor_ref, ...), custom_call_target="tpu_custom_call" | custom-call | flops 6442450944 | bytes 21495808 | tf_op jit(solution)/shard_map/pallas_call | solution.py:85
  213.7 9.4 %shard_map.105.before_ref = f32[2048,32]{1,0:T(8,128)S(1)} custom-call(s32[1]{0:T(128)} %bitcast.me_ref, bf16[2048,4096]{1,0:T(8,128)(2,1)} %constant_dynamic-update-slice_fusion.4.cot_ref, bf16[2048,1408]{1,0:T(8,128)(2,1)} %constant_dynamic-update-slice_fusion.gate_ref, bf16[256,32]{1,0:T(8,128)(2,1)S(1)} %get-tuple-element.58.factor_ref, ...), custom_call_target="tpu_custom_call" | custom-call | flops 4294967296 | bytes 19922944 | tf_op jit(solution)/shard_map/pallas_call | solution.py:85
  223.2 9.4 %shard_map.106 = f32[2048,32]{1,0:T(8,128)S(1)} custom-call(s32[1]{0:T(128)} %bitcast.me_ref, bf16[2048,4096]{1,0:T(8,128)(2,1)} %constant_dynamic-update-slice_fusion.4.cot_ref, bf16[2048,1408]{1,0:T(8,128)(2,1)} %constant_dynamic-update-slice_fusion.gate_ref, bf16[256,32]{1,0:T(8,128)(2,1)S(1)} %get-tuple-element.57.factor_ref, ...), custom_call_target="tpu_custom_call" | custom-call | flops 4294967296 | bytes 19922944 | tf_op jit(solution)/shard_map/pallas_call | solution.py:85
  241.0 3.7 %collective-permute-done.22 = f32[16,1024]{1,0:T(8,128)S(1)} collective-permute-done((f32[16,1024]{1,0:T(8,128)S(1)}, f32[16,1024]{1,0:T(8,128)S(1)}, u32[]{:S(2)}, u32[]{:S(2)}) %collective-permute-start.22) | collective-permute-done | bytes 65568 | tf_op jit(solution)/shard_map/ppermute | solution.py:25
  246.2 3.7 %collective-permute-start.26 = (f32[16,1024]{1,0:T(8,128)S(1)}, f32[16,1024]{1,0:T(8,128)S(1)}, u32[]{:S(2)}, u32[]{:S(2)}) collective-permute-start(f32[16,1024]{1,0:T(8,128)S(1)} %add.161.refs_0_), channel_id=1, source_target_pairs={{0,12},{4,0},{8,4},{12,8},{1,13},{5,1},{9,5},{13,9},{2,14},{6,2},{... | collective-permute-start | bytes 196616 | tf_op jit(solution)/shard_map/ppermute | solution.py:25
  250.0 2.9 %collective-permute-done.24.refs_1_ = f32[16,1024]{1,0:T(8,128)S(1)} collective-permute-done((f32[16,1024]{1,0:T(8,128)S(1)}, f32[16,1024]{1,0:T(8,128)S(1)}, u32[]{:S(2)}, u32[]{:S(2)}) %collective-permute-start.24) | collective-permute-done | bytes 65568 | tf_op jit(solution)/shard_map/ppermute | solution.py:25
  256.4 7.0 %shard_map.107 = (f32[256,1024]{1,0:T(8,128)}, f32[16,512]{1,0:T(8,128)}) custom-call(s32[2]{0:T(128)S(1)} %pad_add_fusion.1.place_ref, f32[512,1024]{1,0:T(8,128)S(1)} %copy-done.5, f32[16,1024]{1,0:T(8,128)S(1)} %add.161.refs_0_, f32[16,1024]{1,0:T(8,128)S(1)} %collective-permute-done.24.refs_1_, f32[16,1024]{1,0:T(8,128)S(1)} %collective-permute-done.25.refs_2_, ...), custom_call_target="tpu_custom_call" | custom-call | tf_op jit(solution)/shard_map/pallas_call | solution.py:168
  (103 shorter events, 43.9 us)
Async XLA Ops:
  5.1 67.8 %collective-permute-start = (bf16[1408,1024]{1,0:T(8,128)(2,1)}, bf16[1408,1024]{1,0:T(8,128)(2,1)}, u32[]{:S(2)}, u32[]{:S(2)}) collective-permute-start(bf16[1408,1024]{1,0:T(8,128)(2,1)} %constant_dynamic-slice_fusion.6.rest_0_), channel_id=1, source_target_pairs={{0,4},{4,8},{8,12},{12,0},{1,5},{5,9},{9,13},{13,1},{2,6},{6,10},{... | collective-permute-start | bytes 8650760 | tf_op jit(solution)/shard_map/ppermute | solution.py:25
  8.1 47.4 %collective-permute-start.1 = (bf16[512,2048]{1,0:T(8,128)(2,1)}, bf16[512,2048]{1,0:T(8,128)(2,1)}, u32[]{:S(2)}, u32[]{:S(2)}) collective-permute-start(bf16[512,2048]{1,0:T(8,128)(2,1)} %param.9), channel_id=1, source_target_pairs={{0,2},{2,0},{1,3},{3,1},{4,6},{6,4},{5,7},{7,5},{8,10},{10,8},{9,1... | collective-permute-start | bytes 6291464 | tf_op jit(solution)/shard_map/ppermute | solution.py:25
  9.6 47.1 %collective-permute-start.2 = (bf16[512,2048]{1,0:T(8,128)(2,1)}, bf16[512,2048]{1,0:T(8,128)(2,1)}, u32[]{:S(2)}, u32[]{:S(2)}) collective-permute-start(bf16[512,2048]{1,0:T(8,128)(2,1)} %param.9), channel_id=1, source_target_pairs={{0,16},{16,0},{1,17},{17,1},{2,18},{18,2},{3,19},{19,3},{4,20},{20... | collective-permute-start | bytes 6291464 | tf_op jit(solution)/shard_map/ppermute | solution.py:25
  73.0 6.5 %collective-permute-start.4 = (bf16[512,2048]{1,0:T(8,128)(2,1)}, bf16[512,2048]{1,0:T(8,128)(2,1)}, u32[]{:S(2)}, u32[]{:S(2)}) collective-permute-start(bf16[512,2048]{1,0:T(8,128)(2,1)} %param.9), channel_id=1, source_target_pairs={{0,1},{1,0},{2,3},{3,2},{4,5},{5,4},{6,7},{7,6},{8,9},{9,8},{10,11... | collective-permute-start | bytes 6291464 | tf_op jit(solution)/shard_map/ppermute | solution.py:25
  74.3 5.0 %collective-permute-start.10 = (bf16[512,1408]{1,0:T(8,128)(2,1)S(1)}, bf16[512,1408]{1,0:T(8,128)(2,1)}, u32[]{:S(2)}, u32[]{:S(2)}) collective-permute-start(bf16[512,1408]{1,0:T(8,128)(2,1)S(1)} %get-tuple-element.77), channel_id=1, source_target_pairs={{0,1},{1,0},{2,3},{3,2},{4,5},{5,4},{6,7},{7,6},{8,9},{9,8},{10,11... | collective-permute-start | bytes 4325384 | tf_op jit(solution)/shard_map/ppermute | solution.py:25
  74.8 64.7 %collective-permute-start.8 = (bf16[1024,1408]{1,0:T(8,128)(2,1)}, bf16[1024,1408]{1,0:T(8,128)(2,1)}, u32[]{:S(2)}, u32[]{:S(2)}) collective-permute-start(bf16[1024,1408]{1,0:T(8,128)(2,1)} %get-tuple-element.42), channel_id=1, source_target_pairs={{0,16},{16,0},{1,17},{17,1},{2,18},{18,2},{3,19},{19,3},{4,20},{20... | collective-permute-start | bytes 8650760 | tf_op jit(solution)/shard_map/ppermute | solution.py:25
  76.3 66.1 %collective-permute-start.3 = (bf16[1408,1024]{1,0:T(8,128)(2,1)}, bf16[1408,1024]{1,0:T(8,128)(2,1)S(1)}, u32[]{:S(2)}, u32[]{:S(2)}) collective-permute-start(bf16[1408,1024]{1,0:T(8,128)(2,1)} %collective-permute-done.rest_1_), channel_id=1, source_target_pairs={{0,4},{4,8},{8,12},{12,0},{1,5},{5,9},{9,13},{13,1},{2,6},{6,10},{... | collective-permute-start | bytes 8650760 | tf_op jit(solution)/shard_map/ppermute | solution.py:25
  76.3 30.3 %collective-permute-start.5 = (bf16[512,2048]{1,0:T(8,128)(2,1)}, bf16[512,2048]{1,0:T(8,128)(2,1)}, u32[]{:S(2)}, u32[]{:S(2)}) collective-permute-start(bf16[512,2048]{1,0:T(8,128)(2,1)} %collective-permute-done.1), channel_id=1, source_target_pairs={{0,1},{1,0},{2,3},{3,2},{4,5},{5,4},{6,7},{7,6},{8,9},{9,8},{10,11... | collective-permute-start | bytes 6291464 | tf_op jit(solution)/shard_map/ppermute | solution.py:25
  79.3 30.5 %collective-permute-start.6 = (bf16[512,2048]{1,0:T(8,128)(2,1)}, bf16[512,2048]{1,0:T(8,128)(2,1)}, u32[]{:S(2)}, u32[]{:S(2)}) collective-permute-start(bf16[512,2048]{1,0:T(8,128)(2,1)} %collective-permute-done.2), channel_id=1, source_target_pairs={{0,1},{1,0},{2,3},{3,2},{4,5},{5,4},{6,7},{7,6},{8,9},{9,8},{10,11... | collective-permute-start | bytes 6291464 | tf_op jit(solution)/shard_map/ppermute | solution.py:25
  79.5 48.2 %collective-permute-start.7 = (bf16[512,2048]{1,0:T(8,128)(2,1)}, bf16[512,2048]{1,0:T(8,128)(2,1)}, u32[]{:S(2)}, u32[]{:S(2)}) collective-permute-start(bf16[512,2048]{1,0:T(8,128)(2,1)} %collective-permute-done.2), channel_id=1, source_target_pairs={{0,2},{2,0},{1,3},{3,1},{4,6},{6,4},{5,7},{7,5},{8,10},{10,8},{9,1... | collective-permute-start | bytes 6291464 | tf_op jit(solution)/shard_map/ppermute | solution.py:25
  145.5 22.9 %collective-permute-start.9 = (bf16[512,2048]{1,0:T(8,128)(2,1)}, bf16[512,2048]{1,0:T(8,128)(2,1)}, u32[]{:S(2)}, u32[]{:S(2)}) collective-permute-start(bf16[512,2048]{1,0:T(8,128)(2,1)} %collective-permute-done.7), channel_id=1, source_target_pairs={{0,1},{1,0},{2,3},{3,2},{4,5},{5,4},{6,7},{7,6},{8,9},{9,8},{10,11... | collective-permute-start | bytes 6291464 | tf_op jit(solution)/shard_map/ppermute | solution.py:25
  149.2 12.6 %collective-permute-start.11 = (bf16[512,1408]{1,0:T(8,128)(2,1)}, bf16[512,1408]{1,0:T(8,128)(2,1)}, u32[]{:S(2)}, u32[]{:S(2)}) collective-permute-start(bf16[512,1408]{1,0:T(8,128)(2,1)} %get-tuple-element.75), channel_id=1, source_target_pairs={{0,1},{1,0},{2,3},{3,2},{4,5},{5,4},{6,7},{7,6},{8,9},{9,8},{10,11... | collective-permute-start | bytes 4325384 | tf_op jit(solution)/shard_map/ppermute | solution.py:25
  154.0 6.7 %collective-permute-start.16 = (f32[512,32]{0,1:T(8,128)S(1)}, f32[512,32]{0,1:T(8,128)S(1)}, u32[]{:S(2)}, u32[]{:S(2)}) collective-permute-start(f32[512,32]{0,1:T(8,128)S(1)} %fusion.27), channel_id=1, source_target_pairs={{0,2},{2,0},{1,3},{3,1},{4,6},{6,4},{5,7},{7,5},{8,10},{10,8},{9,1... | collective-permute-start | bytes 196616 | tf_op jit(solution)/shard_map/ppermute | solution.py:25
  155.5 28.2 %collective-permute-start.12 = (bf16[512,1024]{1,0:T(8,128)(2,1)}, bf16[512,1024]{1,0:T(8,128)(2,1)}, u32[]{:S(2)}, u32[]{:S(2)}) collective-permute-start(bf16[512,1024]{1,0:T(8,128)(2,1)} %slice.53), channel_id=1, source_target_pairs={{0,4},{4,8},{8,12},{12,0},{1,5},{5,9},{9,13},{13,1},{2,6},{6,10},{... | collective-permute-start | bytes 3145736 | tf_op jit(solution)/shard_map/ppermute | solution.py:25
  155.5 3.9 %collective-permute-start.18 = (s32[1,16]{1,0:T(1,128)S(1)}, s32[1,16]{1,0:T(1,128)S(1)}, u32[]{:S(2)}, u32[]{:S(2)}) collective-permute-start(s32[1,16]{1,0:T(1,128)S(1)} %copy-done.9), channel_id=1, source_target_pairs={{0,16},{16,0},{1,17},{17,1},{2,18},{18,2},{3,19},{19,3},{4,20},{20... | collective-permute-start | bytes 200 | tf_op jit(solution)/shard_map/ppermute | solution.py:25
  159.4 41.1 %collective-permute-start.13 = (bf16[384,1024]{1,0:T(8,128)(2,1)}, bf16[384,1024]{1,0:T(8,128)(2,1)}, u32[]{:S(2)}, u32[]{:S(2)}) collective-permute-start(bf16[384,1024]{1,0:T(8,128)(2,1)} %slice.54.rest_2_), channel_id=1, source_target_pairs={{0,4},{4,8},{8,12},{12,0},{1,5},{5,9},{9,13},{13,1},{2,6},{6,10},{... | collective-permute-start | bytes 2359304 | tf_op jit(solution)/shard_map/ppermute | solution.py:25
  160.6 53.1 %collective-permute-start.14 = (bf16[256,1024]{1,0:T(8,128)(2,1)}, bf16[256,1024]{1,0:T(8,128)(2,1)S(1)}, u32[]{:S(2)}, u32[]{:S(2)}) collective-permute-start(bf16[256,1024]{1,0:T(8,128)(2,1)} %get-tuple-element.63), channel_id=1, source_target_pairs={{0,4},{4,8},{8,12},{12,0},{1,5},{5,9},{9,13},{13,1},{2,6},{6,10},{... | collective-permute-start | bytes 1572872 | tf_op jit(solution)/shard_map/ppermute | solution.py:25
  161.8 61.4 %collective-permute-start.15 = (bf16[256,1024]{1,0:T(8,128)(2,1)}, bf16[256,1024]{1,0:T(8,128)(2,1)S(1)}, u32[]{:S(2)}, u32[]{:S(2)}) collective-permute-start(bf16[256,1024]{1,0:T(8,128)(2,1)} %get-tuple-element.64), channel_id=1, source_target_pairs={{0,4},{4,8},{8,12},{12,0},{1,5},{5,9},{9,13},{13,1},{2,6},{6,10},{... | collective-permute-start | bytes 1572872 | tf_op jit(solution)/shard_map/ppermute | solution.py:25
  168.3 64.6 %collective-permute-start.19 = (f32[512,32]{0,1:T(8,128)S(1)}, f32[512,32]{0,1:T(8,128)S(1)}, u32[]{:S(2)}, u32[]{:S(2)}) collective-permute-start(f32[512,32]{0,1:T(8,128)S(1)} %add.158), channel_id=1, source_target_pairs={{0,16},{1,17},{16,0},{17,1},{2,18},{3,19},{18,2},{19,3},{4,20},{5,... | collective-permute-start | bytes 196616 | tf_op jit(solution)/shard_map/ppermute | solution.py:25
  183.6 49.3 %collective-permute-start.20 = (f32[512,32]{0,1:T(8,128)S(1)}, f32[512,32]{0,1:T(8,128)}, u32[]{:S(2)}, u32[]{:S(2)}) collective-permute-start(f32[512,32]{0,1:T(8,128)S(1)} %add.158), channel_id=1, source_target_pairs={{0,17},{1,16},{16,1},{17,0},{2,19},{3,18},{18,3},{19,2},{4,21},{5,... | collective-permute-start | bytes 196616 | tf_op jit(solution)/shard_map/ppermute | solution.py:25
  183.7 16.8 %copy-start.2 = (bf16[384,1024]{1,0:T(8,128)(2,1)S(1)}, bf16[384,1024]{1,0:T(8,128)(2,1)}, u32[]{:S(2)}) copy-start(bf16[384,1024]{1,0:T(8,128)(2,1)} %slice.54.rest_2_) | copy-start | bytes 2359300
  183.7 16.8 %copy-start.3 = (bf16[384,1024]{1,0:T(8,128)(2,1)S(1)}, bf16[384,1024]{1,0:T(8,128)(2,1)}, u32[]{:S(2)}) copy-start(bf16[384,1024]{1,0:T(8,128)(2,1)} %constant_dynamic-slice_fusion.rest_0_) | copy-start | bytes 2359300
  183.7 16.8 %copy-start.4 = (bf16[384,1024]{1,0:T(8,128)(2,1)S(1)}, bf16[384,1024]{1,0:T(8,128)(2,1)}, u32[]{:S(2)}) copy-start(bf16[384,1024]{1,0:T(8,128)(2,1)} %slice.62.rest_1_) | copy-start | bytes 2359300
  200.5 36.1 %collective-permute-start.17 = (f32[512,32]{0,1:T(8,128)S(1)}, f32[512,32]{0,1:T(8,128)S(1)}, u32[]{:S(2)}, u32[]{:S(2)}) collective-permute-start(f32[512,32]{0,1:T(8,128)S(1)} %add.158), channel_id=1, source_target_pairs={{0,1},{1,0},{16,17},{17,16},{2,3},{3,2},{18,19},{19,18},{4,5},{5,4... | collective-permute-start | bytes 196616 | tf_op jit(solution)/shard_map/ppermute | solution.py:25
  235.6 27.8 %copy-start.1 = (bf16[512,2048]{1,0:T(8,128)(2,1)S(1)}, bf16[512,2048]{1,0:T(8,128)(2,1)}, u32[]{:S(2)}) copy-start(bf16[512,2048]{1,0:T(8,128)(2,1)} %param.8) | copy-start | bytes 6291460
  235.8 4.6 %collective-permute-start.21 = (f32[16,1024]{1,0:T(8,128)S(1)}, f32[16,1024]{1,0:T(8,128)S(1)}, u32[]{:S(2)}, u32[]{:S(2)}) collective-permute-start(f32[16,1024]{1,0:T(8,128)S(1)} %reshape.77), channel_id=1, source_target_pairs={{0,16},{16,0},{1,17},{17,1},{2,18},{18,2},{3,19},{19,3},{4,20},{20... | collective-permute-start | bytes 196616 | tf_op jit(solution)/shard_map/ppermute | solution.py:25
  240.4 4.3 %collective-permute-start.22 = (f32[16,1024]{1,0:T(8,128)S(1)}, f32[16,1024]{1,0:T(8,128)S(1)}, u32[]{:S(2)}, u32[]{:S(2)}) collective-permute-start(f32[16,1024]{1,0:T(8,128)S(1)} %add.159), channel_id=1, source_target_pairs={{0,2},{2,0},{1,3},{3,1},{4,6},{6,4},{5,7},{7,5},{8,10},{10,8},{9,1... | collective-permute-start | bytes 196616 | tf_op jit(solution)/shard_map/ppermute | solution.py:25
  244.7 1.3 collective-permute-start.23
  246.1 17.3 %copy-start.6 = (f32[16,1024]{1,0:T(8,128)}, f32[16,1024]{1,0:T(8,128)S(1)}, u32[]{:S(2)}) copy-start(f32[16,1024]{1,0:T(8,128)S(1)} %add.161.refs_0_) | copy-start | bytes 196612
  246.1 6.8 %collective-permute-start.24 = (f32[16,1024]{1,0:T(8,128)S(1)}, f32[16,1024]{1,0:T(8,128)S(1)}, u32[]{:S(2)}, u32[]{:S(2)}) collective-permute-start(f32[16,1024]{1,0:T(8,128)S(1)} %add.161.refs_0_), channel_id=1, source_target_pairs={{0,4},{4,8},{8,12},{12,0},{1,5},{5,9},{9,13},{13,1},{2,6},{6,10},{... | collective-permute-start | bytes 196616 | tf_op jit(solution)/shard_map/ppermute | solution.py:25
  246.1 8.6 %collective-permute-start.25 = (f32[16,1024]{1,0:T(8,128)S(1)}, f32[16,1024]{1,0:T(8,128)S(1)}, u32[]{:S(2)}, u32[]{:S(2)}) collective-permute-start(f32[16,1024]{1,0:T(8,128)S(1)} %add.161.refs_0_), channel_id=1, source_target_pairs={{0,8},{4,12},{8,0},{12,4},{1,9},{5,13},{9,1},{13,5},{2,10},{6,14},... | collective-permute-start | bytes 196616 | tf_op jit(solution)/shard_map/ppermute | solution.py:25
  246.2 8.5 %collective-permute-start.26 = (f32[16,1024]{1,0:T(8,128)S(1)}, f32[16,1024]{1,0:T(8,128)S(1)}, u32[]{:S(2)}, u32[]{:S(2)}) collective-permute-start(f32[16,1024]{1,0:T(8,128)S(1)} %add.161.refs_0_), channel_id=1, source_target_pairs={{0,12},{4,0},{8,4},{12,8},{1,13},{5,1},{9,5},{13,9},{2,14},{6,2},{... | collective-permute-start | bytes 196616 | tf_op jit(solution)/shard_map/ppermute | solution.py:25
  (5 other events, 41.8 us)

commit v11 on v10

--- a/solution.py
+++ b/solution.py
@@ -257,8 +257,10 @@
     for key, block in early.items():
         cot = place(cot, *key, block)
     turned = shifted(ring[-1], "dp", (n_dp,), (1,)) if n_dp > 3 else ring.pop()
-    turned, cot, cots, more, sheets, right_part, doc_lens, factors = lax.optimization_barrier(
-        (turned, cot, cots, more, sheets, right_part, doc_lens, factors)
+    uneven = [c for c, (low, high) in enumerate(spans) if low % (high - low)]
+    kept = {c: [slot[slice(*spans[c])] for slot in ring[:2]] for c in uneven}
+    turned, cot, cots, more, sheets, right_part, doc_lens, factors, kept = lax.optimization_barrier(
+        (turned, cot, cots, more, sheets, right_part, doc_lens, factors, kept)
     )
     ring.append(turned)
     cots.update(more)
@@ -275,7 +277,12 @@
             for ds in range(1, n_seq):
                 cots[dg, ds, r] = across(cots[dg, 0, r], ds)
         spread(dg, sheets[dg])
-    chunks = [ring + [block] for block in turned]
+    chunks = [
+        (kept[c] + [slot[slice(*spans[c])] for slot in ring[2:-1]] + [cuts[c]] if c in kept else ring) + [block]
+        for c, block in enumerate(turned)
+    ]
+    beside = (n_groups - 1, n_seq - 1)
+    right_part, doc_lens, gates[beside] = lax.optimization_barrier((right_part, doc_lens, gates[beside]))
     right = sum_over(right_part, "tensor")
     rights = [right if dg == ds == 0 else shifted(right, pair, sizes, (dg, ds)) for dg, ds in order]
     lens = [doc_lens if dg == 0 else shifted(doc_lens, "groups", (n_groups,), (dg,)) for dg in range(n_groups)]

time: 264 us -> 259 us (0.981)
  waiting for transfers between devices: 105 us -> 90.5 us
  other arithmetic: 7.34 us -> 11.2 us
  local copies, waits for them, and re-layouts: 67.7 us -> 71.1 us
    ppermute x27, waiting for transfers between devices: 105 us -> 90.5 us  [shifted(): return lax.ppermute(x, axes, pairs)]
    slice x2 -> x1, local copies, waits for them, and re-layouts: 5.03 us -> 1.33 us  [spread(): x = sheet[ds * rows:(ds + 1) * rows]]
    dynamic_update_slice x3 -> x4, local copies, waits for them, and re-layouts: 9.44 us -> 13 us  [on_device(): gate = lax.dynamic_update_slice(gate, gates[block], (number * rows, 0))]
  transfers between devices with their start and end apart: 27 -> 27, of which waited for: 14 -> 15; matrix products, arithmetic and copies ran while one was open for 27% -> 30% of each run, Pallas kernels for 17% -> 18%
where the time goes in v11:
time: 259 us; the launch traced here: 258 us
  waiting for transfers between devices  90.5 us (35%)
  local copies, waits for them, and re-layouts  71.1 us (27%)
  Pallas kernels  53 us (20%)
  starting transfers between devices  24.7 us (10%)
  other arithmetic  11.2 us (4%)
  matrix products  6.61 us (3%)
    ppermute x27, waiting for transfers between devices, shifted(): return lax.ppermute(x, axes, pairs)  90.5 us
    pallas_call x4, Pallas kernels, add_chunk(): pl.pallas_call(functools.partial(chunk_kernel, n, skip), out_shape=jax.Sh...  46 us
    dynamic_update_slice x8, local copies, waits for them, and re-layouts, place(): return lax.dynamic_update_slice(cot, block, ((dg * n_seq + ds) * rows, at))  26.2 us
    ppermute x27, starting transfers between devices, shifted(): return lax.ppermute(x, axes, pairs)  24.7 us
    dynamic_update_slice x4, local copies, waits for them, and re-layouts, on_device(): gate = lax.dynamic_update_slice(gate, gates[block], (number * rows, 0))  13 us
    pallas_call x1, Pallas kernels, finish(): pl.pallas_call(functools.partial(final_kernel, n, share), out_shape=(jax....  7.02 us
    dynamic_slice x1, local copies, waits for them, and re-layouts, unit_columns(): return lax.dynamic_slice_in_dim(gate_pre, first_unit(to), part, 1)  6.05 us
    broadcast_in_dim x1, local copies, waits for them, and re-layouts, on_device(): jnp.zeros((len(order) * rows, n_tensor * cotangent.shape[1]), cotangent.d...  5.98 us
  transfers between devices with their start and end apart: 27, of which 15 were waited for; matrix products, arithmetic and copies ran while one was open for 30% of the time, Pallas kernels for 18%

profile of v11, /device:TPU:0, one launch (start us, length us, event | category | flops | bytes accessed | tf_op | source)
XLA Modules:
  0.0 258.1 jit_solution(10856729591240039275)
XLA Ops:
  0.7 4.5 %constant_dynamic-slice_fusion.6.rest_0_ = bf16[1408,1024]{1,0:T(8,128)(2,1)} fusion(bf16[5504,1024]{1,0:T(8,128)(2,1)} %param.11, s32[]{:T(128)S(6)} %select_n.89), kind=kLoop, calls=%fused_computation.38 | loop fusion | bytes 5767172 | tf_op jit(solution)/shard_map/dynamic_slice | solution.py:204
  5.1 3.0 %collective-permute-start = (bf16[1408,1024]{1,0:T(8,128)(2,1)}, bf16[1408,1024]{1,0:T(8,128)(2,1)}, u32[]{:S(2)}, u32[]{:S(2)}) collective-permute-start(bf16[1408,1024]{1,0:T(8,128)(2,1)} %constant_dynamic-slice_fusion.6.rest_0_), channel_id=1, source_target_pairs={{0,4},{4,8},{8,12},{12,0},{1,5},{5,9},{9,13},{13,1},{2,6},{6,10},{... | collective-permute-start | bytes 8650760 | tf_op jit(solution)/shard_map/ppermute | solution.py:25
  15.3 6.0 %constant_dynamic-slice_fusion.3 = (bf16[512,1408]{1,0:T(8,128)(2,1)S(1)}, bf16[512,1408]{1,0:T(8,128)(2,1)S(1)}, bf16[512,1408]{1,0:T(8,128)(2,1)S(1)}, bf16[512,1408]{1,0:T(8,128)(2,1)S(1)}) fusion(bf16[512,5504]{1,0:T(8,128)(2,1)} %param.10, s32[]{:T(128)S(6)} %select_n.96, s32[]{:T(128)S(6)} %select_n.94, s32[]{:T(128)S(6)} %select_n.92, s32[]{:T(128)S(6)} %select_n.97), kind=kLoop, calls=%fused_computation.35 | loop fusion | bytes 11534352 | tf_op jit(solution)/shard_map/dynamic_slice | solution.py:217
  21.4 5.9 %pad_maximum_fusion = (bf16[1024,1408]{1,0:T(8,128)(2,1)S(1)}, bf16[1024,1408]{1,0:T(8,128)(2,1)}) fusion(bf16[512,1408]{1,0:T(8,128)(2,1)S(1)} %get-tuple-element.82, bf16[512,1408]{1,0:T(8,128)(2,1)S(1)} %get-tuple-element.83, bf16[512,1408]{1,0:T(8,128)(2,1)S(1)} %get-tuple-element.84, bf16[512,1408]{1,0:T(8,128)(2,1)S(1)} %get-tuple-element.81), kind=kLoop, calls=%fused_computation | loop fusion | flops 11534336 | bytes 11534336 | tf_op jit(solution)/shard_map/concatenate | solution.py:225
  27.3 28.3 %collective-permute-done.1 = bf16[512,2048]{1,0:T(8,128)(2,1)} collective-permute-done((bf16[512,2048]{1,0:T(8,128)(2,1)}, bf16[512,2048]{1,0:T(8,128)(2,1)}, u32[]{:S(2)}, u32[]{:S(2)}) %collective-permute-start.1) | collective-permute-done | bytes 2097184 | tf_op jit(solution)/shard_map/ppermute | solution.py:25
  56.8 16.2 %collective-permute-done.rest_1_ = bf16[1408,1024]{1,0:T(8,128)(2,1)} collective-permute-done((bf16[1408,1024]{1,0:T(8,128)(2,1)}, bf16[1408,1024]{1,0:T(8,128)(2,1)}, u32[]{:S(2)}, u32[]{:S(2)}) %collective-permute-start) | collective-permute-done | bytes 2883616 | tf_op jit(solution)/shard_map/ppermute | solution.py:25
  76.3 3.0 %collective-permute-done.10 = bf16[512,1408]{1,0:T(8,128)(2,1)} collective-permute-done((bf16[512,1408]{1,0:T(8,128)(2,1)S(1)}, bf16[512,1408]{1,0:T(8,128)(2,1)}, u32[]{:S(2)}, u32[]{:S(2)}) %collective-permute-start.10) | collective-permute-done | bytes 1441824 | tf_op jit(solution)/shard_map/ppermute | solution.py:25
  83.2 4.3 %dynamic_update_slice.44 = bf16[2048,1408]{1,0:T(8,128)(2,1)} pad(bf16[512,1408]{1,0:T(8,128)(2,1)} %get-tuple-element.88, bf16[]{:T(256)} %constant.100.clone.1), padding=0_1536x0_0 | pad | bytes 7208962 | tf_op jit(solution)/shard_map/dynamic_update_slice | solution.py:295
  89.6 6.0 %broadcast_in_dim.18 = bf16[2048,4096]{1,0:T(8,128)(2,1)} broadcast(bf16[]{:T(256)} %constant.100.clone.1), dimensions={} | broadcast | bytes 16777218 | tf_op jit(solution)/shard_map/broadcast_in_dim | solution.py:255
  95.6 3.3 %constant_dynamic-update-slice_fusion.3 = bf16[2048,4096]{1,0:T(8,128)(2,1)} fusion(bf16[2048,4096]{1,0:T(8,128)(2,1)} %broadcast_in_dim.18, bf16[512,2048]{1,0:T(8,128)(2,1)} %param.9, s32[]{:T(128)S(6)} %select_n.100), kind=kLoop, calls=%fused_computation.32 | loop fusion | bytes 4194308 | tf_op jit(solution)/shard_map/dynamic_update_slice | solution.py:213
  98.8 3.3 %constant_dynamic-update-slice_fusion.2 = bf16[2048,4096]{1,0:T(8,128)(2,1)} fusion(bf16[2048,4096]{1,0:T(8,128)(2,1)} %constant_dynamic-update-slice_fusion.3, bf16[512,2048]{1,0:T(8,128)(2,1)} %collective-permute-done.1, s32[]{:T(128)S(6)} %select_n.102), kind=kLoop, calls=%fused_computation.31 | loop fusion | bytes 4194308 | tf_op jit(solution)/shard_map/dynamic_update_slice | solution.py:213
  102.1 3.3 %constant_dynamic-update-slice_fusion.7 = bf16[2048,4096]{1,0:T(8,128)(2,1)} fusion(bf16[2048,4096]{1,0:T(8,128)(2,1)} %constant_dynamic-update-slice_fusion.2, bf16[512,2048]{1,0:T(8,128)(2,1)} %collective-permute-done.2, s32[]{:T(128)S(6)} %select_n.100), kind=kLoop, calls=%fused_computation.44 | loop fusion | bytes 4194308 | tf_op jit(solution)/shard_map/dynamic_update_slice | solution.py:213
  107.9 3.3 %constant_dynamic-update-slice_fusion.9 = bf16[2048,4096]{1,0:T(8,128)(2,1)} fusion(bf16[2048,4096]{1,0:T(8,128)(2,1)} %constant_dynamic-update-slice_fusion.7, bf16[512,2048]{1,0:T(8,128)(2,1)} %collective-permute-done.4, s32[]{:T(128)S(6)} %select_n.100), kind=kLoop, calls=%fused_computation.46 | loop fusion | bytes 4194308 | tf_op jit(solution)/shard_map/dynamic_update_slice | solution.py:213
  111.3 3.3 %constant_dynamic-update-slice_fusion.8 = bf16[2048,4096]{1,0:T(8,128)(2,1)} fusion(bf16[2048,4096]{1,0:T(8,128)(2,1)} %constant_dynamic-update-slice_fusion.9, bf16[512,2048]{1,0:T(8,128)(2,1)} %collective-permute-done.5, s32[]{:T(128)S(6)} %select_n.102), kind=kLoop, calls=%fused_computation.45 | loop fusion | bytes 4194308 | tf_op jit(solution)/shard_map/dynamic_update_slice | solution.py:213
  114.6 3.3 %constant_dynamic-update-slice_fusion.5 = bf16[2048,4096]{1,0:T(8,128)(2,1)} fusion(bf16[2048,4096]{1,0:T(8,128)(2,1)} %constant_dynamic-update-slice_fusion.8, bf16[512,2048]{1,0:T(8,128)(2,1)} %collective-permute-done.6, s32[]{:T(128)S(6)} %select_n.100), kind=kLoop, calls=%fused_computation.42 | loop fusion | bytes 4194308 | tf_op jit(solution)/shard_map/dynamic_update_slice | solution.py:213
  117.8 9.9 %collective-permute-done.7 = bf16[512,2048]{1,0:T(8,128)(2,1)} collective-permute-done((bf16[512,2048]{1,0:T(8,128)(2,1)}, bf16[512,2048]{1,0:T(8,128)(2,1)}, u32[]{:S(2)}, u32[]{:S(2)}) %collective-permute-start.7) | collective-permute-done | bytes 2097184 | tf_op jit(solution)/shard_map/ppermute | solution.py:25
  127.7 11.8 %collective-permute-done.8 = bf16[1024,1408]{1,0:T(8,128)(2,1)} collective-permute-done((bf16[1024,1408]{1,0:T(8,128)(2,1)}, bf16[1024,1408]{1,0:T(8,128)(2,1)}, u32[]{:S(2)}, u32[]{:S(2)}) %collective-permute-start.8) | collective-permute-done | bytes 2883616 | tf_op jit(solution)/shard_map/ppermute | solution.py:25
  139.5 2.9 %collective-permute-done.3.rest_2_ = bf16[1408,1024]{1,0:T(8,128)(2,1)S(1)} collective-permute-done((bf16[1408,1024]{1,0:T(8,128)(2,1)}, bf16[1408,1024]{1,0:T(8,128)(2,1)S(1)}, u32[]{:S(2)}, u32[]{:S(2)}) %collective-permute-start.3) | collective-permute-done | bytes 2883616 | tf_op jit(solution)/shard_map/ppermute | solution.py:25
  145.5 3.6 %slice_dynamic-update-slice_fusion = (bf16[2048,1408]{1,0:T(8,128)(2,1)}, bf16[512,1408]{1,0:T(8,128)(2,1)}) fusion(bf16[2048,1408]{1,0:T(8,128)(2,1)} %constant_dynamic-update-slice_fusion.1, bf16[1024,1408]{1,0:T(8,128)(2,1)} %collective-permute-done.8), kind=kLoop, calls=%fused_computation.6 | loop fusion | bytes 5767168 | tf_op jit(solution)/shard_map/dynamic_update_slice | solution.py:295
  151.3 3.3 %constant_dynamic-update-slice_fusion.6 = bf16[2048,4096]{1,0:T(8,128)(2,1)} fusion(bf16[2048,4096]{1,0:T(8,128)(2,1)} %constant_dynamic-update-slice_fusion.5, bf16[512,2048]{1,0:T(8,128)(2,1)} %collective-permute-done.7, s32[]{:T(128)S(6)} %select_n.102), kind=kLoop, calls=%fused_computation.43 | loop fusion | bytes 4194308 | tf_op jit(solution)/shard_map/dynamic_update_slice | solution.py:213
  163.7 3.9 %collective-permute-start.15 = (bf16[256,1024]{1,0:T(8,128)(2,1)}, bf16[256,1024]{1,0:T(8,128)(2,1)S(1)}, u32[]{:S(2)}, u32[]{:S(2)}) collective-permute-start(bf16[256,1024]{1,0:T(8,128)(2,1)} %get-tuple-element.74), channel_id=1, source_target_pairs={{0,4},{4,8},{8,12},{12,0},{1,5},{5,9},{9,13},{13,1},{2,6},{6,10},{... | collective-permute-start | bytes 1572872 | tf_op jit(solution)/shard_map/ppermute | solution.py:25
  170.6 3.3 %constant_dynamic-update-slice_fusion.4.cot_ref = bf16[2048,4096]{1,0:T(8,128)(2,1)} fusion(bf16[2048,4096]{1,0:T(8,128)(2,1)} %constant_dynamic-update-slice_fusion.6, bf16[512,2048]{1,0:T(8,128)(2,1)} %collective-permute-done.9, s32[]{:T(128)S(6)} %select_n.102), kind=kLoop, calls=%fused_computation.41 | loop fusion | bytes 4194308 | tf_op jit(solution)/shard_map/dynamic_update_slice | solution.py:213
  173.8 4.5 %collective-permute-done.12.rest_3_ = bf16[512,1024]{1,0:T(8,128)(2,1)} collective-permute-done((bf16[512,1024]{1,0:T(8,128)(2,1)}, bf16[512,1024]{1,0:T(8,128)(2,1)}, u32[]{:S(2)}, u32[]{:S(2)}) %collective-permute-start.12) | collective-permute-done | bytes 1048608 | tf_op jit(solution)/shard_map/ppermute | solution.py:25
  178.4 13.9 %shard_map.103.before_ref = f32[2048,32]{1,0:T(8,128)S(1)} custom-call(s32[1]{0:T(128)} %bitcast.me_ref, bf16[2048,4096]{1,0:T(8,128)(2,1)} %constant_dynamic-update-slice_fusion.4.cot_ref, bf16[2048,1408]{1,0:T(8,128)(2,1)} %constant_dynamic-update-slice_fusion.gate_ref, bf16[512,32]{1,0:T(8,128)(2,1)S(1)} %slice.64.factor_ref, ...), custom_call_target="tpu_custom_call" | custom-call | flops 8589934592 | bytes 23068672 | tf_op jit(solution)/shard_map/pallas_call | solution.py:85
  192.4 2.8 %collective-permute-done.13.rest_3_ = bf16[384,1024]{1,0:T(8,128)(2,1)} collective-permute-done((bf16[384,1024]{1,0:T(8,128)(2,1)}, bf16[384,1024]{1,0:T(8,128)(2,1)}, u32[]{:S(2)}, u32[]{:S(2)}) %collective-permute-start.13) | collective-permute-done | bytes 786464 | tf_op jit(solution)/shard_map/ppermute | solution.py:25
  195.2 13.2 %shard_map.104.before_ref = f32[2048,32]{1,0:T(8,128)S(1)} custom-call(s32[1]{0:T(128)} %bitcast.me_ref, bf16[2048,4096]{1,0:T(8,128)(2,1)} %constant_dynamic-update-slice_fusion.4.cot_ref, bf16[2048,1408]{1,0:T(8,128)(2,1)} %constant_dynamic-update-slice_fusion.gate_ref, bf16[384,32]{1,0:T(8,128)(2,1)S(1)} %copy-done.6, ...), custom_call_target="tpu_custom_call" | custom-call | flops 6442450944 | bytes 21495808 | tf_op jit(solution)/shard_map/pallas_call | solution.py:85
  208.4 9.4 %shard_map.105.before_ref = f32[2048,32]{1,0:T(8,128)S(1)} custom-call(s32[1]{0:T(128)} %bitcast.me_ref, bf16[2048,4096]{1,0:T(8,128)(2,1)} %constant_dynamic-update-slice_fusion.4.cot_ref, bf16[2048,1408]{1,0:T(8,128)(2,1)} %constant_dynamic-update-slice_fusion.gate_ref, bf16[256,32]{1,0:T(8,128)(2,1)S(1)} %copy-done.8, ...), custom_call_target="tpu_custom_call" | custom-call | flops 4294967296 | bytes 19922944 | tf_op jit(solution)/shard_map/pallas_call | solution.py:85
  217.9 9.4 %shard_map.106 = f32[2048,32]{1,0:T(8,128)S(1)} custom-call(s32[1]{0:T(128)} %bitcast.me_ref, bf16[2048,4096]{1,0:T(8,128)(2,1)} %constant_dynamic-update-slice_fusion.4.cot_ref, bf16[2048,1408]{1,0:T(8,128)(2,1)} %constant_dynamic-update-slice_fusion.gate_ref, bf16[256,32]{1,0:T(8,128)(2,1)S(1)} %copy-done.7, f32[2048,32]{1,0:T(8,128)S(1)} %shard_map.105.before_ref, ...), custom_call_target="tpu_custom_call" | custom-call | flops 4294967296 | bytes 19922944 | tf_op jit(solution)/shard_map/pallas_call | solution.py:85
  236.7 2.8 %collective-permute-done.22 = f32[16,1024]{1,0:T(8,128)S(1)} collective-permute-done((f32[16,1024]{1,0:T(8,128)S(1)}, f32[16,1024]{1,0:T(8,128)S(1)}, u32[]{:S(2)}, u32[]{:S(2)}) %collective-permute-start.22) | collective-permute-done | bytes 65568 | tf_op jit(solution)/shard_map/ppermute | solution.py:25
  241.0 3.7 %collective-permute-start.26 = (f32[16,1024]{1,0:T(8,128)S(1)}, f32[16,1024]{1,0:T(8,128)S(1)}, u32[]{:S(2)}, u32[]{:S(2)}) collective-permute-start(f32[16,1024]{1,0:T(8,128)S(1)} %add.161.refs_0_), channel_id=1, source_target_pairs={{0,12},{4,0},{8,4},{12,8},{1,13},{5,1},{9,5},{13,9},{2,14},{6,2},{... | collective-permute-start | bytes 196616 | tf_op jit(solution)/shard_map/ppermute | solution.py:25
  244.8 2.9 %collective-permute-done.24.refs_1_ = f32[16,1024]{1,0:T(8,128)S(1)} collective-permute-done((f32[16,1024]{1,0:T(8,128)S(1)}, f32[16,1024]{1,0:T(8,128)S(1)}, u32[]{:S(2)}, u32[]{:S(2)}) %collective-permute-start.24) | collective-permute-done | bytes 65568 | tf_op jit(solution)/shard_map/ppermute | solution.py:25
  251.1 7.0 %shard_map.107 = (f32[256,1024]{1,0:T(8,128)}, f32[16,512]{1,0:T(8,128)}) custom-call(s32[2]{0:T(128)S(1)} %pad_add_fusion.1.place_ref, f32[512,1024]{1,0:T(8,128)S(1)} %copy-done.5, f32[16,1024]{1,0:T(8,128)S(1)} %add.161.refs_0_, f32[16,1024]{1,0:T(8,128)S(1)} %collective-permute-done.24.refs_1_, f32[16,1024]{1,0:T(8,128)S(1)} %collective-permute-done.25.refs_2_, ...), custom_call_target="tpu_custom_call" | custom-call | tf_op jit(solution)/shard_map/pallas_call | solution.py:168
  (109 shorter events, 52.0 us)
Async XLA Ops:
  5.1 67.8 %collective-permute-start = (bf16[1408,1024]{1,0:T(8,128)(2,1)}, bf16[1408,1024]{1,0:T(8,128)(2,1)}, u32[]{:S(2)}, u32[]{:S(2)}) collective-permute-start(bf16[1408,1024]{1,0:T(8,128)(2,1)} %constant_dynamic-slice_fusion.6.rest_0_), channel_id=1, source_target_pairs={{0,4},{4,8},{8,12},{12,0},{1,5},{5,9},{9,13},{13,1},{2,6},{6,10},{... | collective-permute-start | bytes 8650760 | tf_op jit(solution)/shard_map/ppermute | solution.py:25
  8.1 47.4 %collective-permute-start.1 = (bf16[512,2048]{1,0:T(8,128)(2,1)}, bf16[512,2048]{1,0:T(8,128)(2,1)}, u32[]{:S(2)}, u32[]{:S(2)}) collective-permute-start(bf16[512,2048]{1,0:T(8,128)(2,1)} %param.9), channel_id=1, source_target_pairs={{0,2},{2,0},{1,3},{3,1},{4,6},{6,4},{5,7},{7,5},{8,10},{10,8},{9,1... | collective-permute-start | bytes 6291464 | tf_op jit(solution)/shard_map/ppermute | solution.py:25
  9.6 47.1 %collective-permute-start.2 = (bf16[512,2048]{1,0:T(8,128)(2,1)}, bf16[512,2048]{1,0:T(8,128)(2,1)}, u32[]{:S(2)}, u32[]{:S(2)}) collective-permute-start(bf16[512,2048]{1,0:T(8,128)(2,1)} %param.9), channel_id=1, source_target_pairs={{0,16},{16,0},{1,17},{17,1},{2,18},{18,2},{3,19},{19,3},{4,20},{20... | collective-permute-start | bytes 6291464 | tf_op jit(solution)/shard_map/ppermute | solution.py:25
  73.0 6.5 %collective-permute-start.4 = (bf16[512,2048]{1,0:T(8,128)(2,1)}, bf16[512,2048]{1,0:T(8,128)(2,1)}, u32[]{:S(2)}, u32[]{:S(2)}) collective-permute-start(bf16[512,2048]{1,0:T(8,128)(2,1)} %param.9), channel_id=1, source_target_pairs={{0,1},{1,0},{2,3},{3,2},{4,5},{5,4},{6,7},{7,6},{8,9},{9,8},{10,11... | collective-permute-start | bytes 6291464 | tf_op jit(solution)/shard_map/ppermute | solution.py:25
  74.3 5.0 %collective-permute-start.10 = (bf16[512,1408]{1,0:T(8,128)(2,1)S(1)}, bf16[512,1408]{1,0:T(8,128)(2,1)}, u32[]{:S(2)}, u32[]{:S(2)}) collective-permute-start(bf16[512,1408]{1,0:T(8,128)(2,1)S(1)} %get-tuple-element.87), channel_id=1, source_target_pairs={{0,1},{1,0},{2,3},{3,2},{4,5},{5,4},{6,7},{7,6},{8,9},{9,8},{10,11... | collective-permute-start | bytes 4325384 | tf_op jit(solution)/shard_map/ppermute | solution.py:25
  74.8 64.7 %collective-permute-start.8 = (bf16[1024,1408]{1,0:T(8,128)(2,1)}, bf16[1024,1408]{1,0:T(8,128)(2,1)}, u32[]{:S(2)}, u32[]{:S(2)}) collective-permute-start(bf16[1024,1408]{1,0:T(8,128)(2,1)} %get-tuple-element.47), channel_id=1, source_target_pairs={{0,16},{16,0},{1,17},{17,1},{2,18},{18,2},{3,19},{19,3},{4,20},{20... | collective-permute-start | bytes 8650760 | tf_op jit(solution)/shard_map/ppermute | solution.py:25
  76.3 66.1 %collective-permute-start.3 = (bf16[1408,1024]{1,0:T(8,128)(2,1)}, bf16[1408,1024]{1,0:T(8,128)(2,1)S(1)}, u32[]{:S(2)}, u32[]{:S(2)}) collective-permute-start(bf16[1408,1024]{1,0:T(8,128)(2,1)} %collective-permute-done.rest_1_), channel_id=1, source_target_pairs={{0,4},{4,8},{8,12},{12,0},{1,5},{5,9},{9,13},{13,1},{2,6},{6,10},{... | collective-permute-start | bytes 8650760 | tf_op jit(solution)/shard_map/ppermute | solution.py:25
  76.3 34.9 %collective-permute-start.5 = (bf16[512,2048]{1,0:T(8,128)(2,1)}, bf16[512,2048]{1,0:T(8,128)(2,1)}, u32[]{:S(2)}, u32[]{:S(2)}) collective-permute-start(bf16[512,2048]{1,0:T(8,128)(2,1)} %collective-permute-done.1), channel_id=1, source_target_pairs={{0,1},{1,0},{2,3},{3,2},{4,5},{5,4},{6,7},{7,6},{8,9},{9,8},{10,11... | collective-permute-start | bytes 6291464 | tf_op jit(solution)/shard_map/ppermute | solution.py:25
  79.3 35.2 %collective-permute-start.6 = (bf16[512,2048]{1,0:T(8,128)(2,1)}, bf16[512,2048]{1,0:T(8,128)(2,1)}, u32[]{:S(2)}, u32[]{:S(2)}) collective-permute-start(bf16[512,2048]{1,0:T(8,128)(2,1)} %collective-permute-done.2), channel_id=1, source_target_pairs={{0,1},{1,0},{2,3},{3,2},{4,5},{5,4},{6,7},{7,6},{8,9},{9,8},{10,11... | collective-permute-start | bytes 6291464 | tf_op jit(solution)/shard_map/ppermute | solution.py:25
  79.5 48.2 %collective-permute-start.7 = (bf16[512,2048]{1,0:T(8,128)(2,1)}, bf16[512,2048]{1,0:T(8,128)(2,1)}, u32[]{:S(2)}, u32[]{:S(2)}) collective-permute-start(bf16[512,2048]{1,0:T(8,128)(2,1)} %collective-permute-done.2), channel_id=1, source_target_pairs={{0,2},{2,0},{1,3},{3,1},{4,6},{6,4},{5,7},{7,5},{8,10},{10,8},{9,1... | collective-permute-start | bytes 6291464 | tf_op jit(solution)/shard_map/ppermute | solution.py:25
  149.1 5.5 %collective-permute-start.11 = (bf16[512,1408]{1,0:T(8,128)(2,1)}, bf16[512,1408]{1,0:T(8,128)(2,1)}, u32[]{:S(2)}, u32[]{:S(2)}) collective-permute-start(bf16[512,1408]{1,0:T(8,128)(2,1)} %get-tuple-element.86), channel_id=1, source_target_pairs={{0,1},{1,0},{2,3},{3,2},{4,5},{5,4},{6,7},{7,6},{8,9},{9,8},{10,11... | collective-permute-start | bytes 4325384 | tf_op jit(solution)/shard_map/ppermute | solution.py:25
  149.1 20.0 %collective-permute-start.9 = (bf16[512,2048]{1,0:T(8,128)(2,1)}, bf16[512,2048]{1,0:T(8,128)(2,1)}, u32[]{:S(2)}, u32[]{:S(2)}) collective-permute-start(bf16[512,2048]{1,0:T(8,128)(2,1)} %collective-permute-done.7), channel_id=1, source_target_pairs={{0,1},{1,0},{2,3},{3,2},{4,5},{5,4},{6,7},{7,6},{8,9},{9,8},{10,11... | collective-permute-start | bytes 6291464 | tf_op jit(solution)/shard_map/ppermute | solution.py:25
  150.2 28.1 %collective-permute-start.12 = (bf16[512,1024]{1,0:T(8,128)(2,1)}, bf16[512,1024]{1,0:T(8,128)(2,1)}, u32[]{:S(2)}, u32[]{:S(2)}) collective-permute-start(bf16[512,1024]{1,0:T(8,128)(2,1)} %slice.54), channel_id=1, source_target_pairs={{0,4},{4,8},{8,12},{12,0},{1,5},{5,9},{9,13},{13,1},{2,6},{6,10},{... | collective-permute-start | bytes 3145736 | tf_op jit(solution)/shard_map/ppermute | solution.py:25
  150.2 45.0 %collective-permute-start.13 = (bf16[384,1024]{1,0:T(8,128)(2,1)}, bf16[384,1024]{1,0:T(8,128)(2,1)}, u32[]{:S(2)}, u32[]{:S(2)}) collective-permute-start(bf16[384,1024]{1,0:T(8,128)(2,1)} %slice.55.rest_2_), channel_id=1, source_target_pairs={{0,4},{4,8},{8,12},{12,0},{1,5},{5,9},{9,13},{13,1},{2,6},{6,10},{... | collective-permute-start | bytes 2359304 | tf_op jit(solution)/shard_map/ppermute | solution.py:25
  150.2 58.2 %collective-permute-start.14 = (bf16[256,1024]{1,0:T(8,128)(2,1)}, bf16[256,1024]{1,0:T(8,128)(2,1)S(1)}, u32[]{:S(2)}, u32[]{:S(2)}) collective-permute-start(bf16[256,1024]{1,0:T(8,128)(2,1)} %get-tuple-element.73), channel_id=1, source_target_pairs={{0,4},{4,8},{8,12},{12,0},{1,5},{5,9},{9,13},{13,1},{2,6},{6,10},{... | collective-permute-start | bytes 1572872 | tf_op jit(solution)/shard_map/ppermute | solution.py:25
  154.5 4.5 %collective-permute-start.18 = (s32[1,16]{1,0:T(1,128)}, s32[1,16]{1,0:T(1,128)}, u32[]{:S(2)}, u32[]{:S(2)}) collective-permute-start(s32[1,16]{1,0:T(1,128)} %param.14), channel_id=1, source_target_pairs={{0,16},{16,0},{1,17},{17,1},{2,18},{18,2},{3,19},{19,3},{4,20},{20... | collective-permute-start | bytes 200 | tf_op jit(solution)/shard_map/ppermute | solution.py:25
  159.1 4.6 %collective-permute-start.16 = (f32[512,32]{0,1:T(8,128)}, f32[512,32]{0,1:T(8,128)}, u32[]{:S(2)}, u32[]{:S(2)}) collective-permute-start(f32[512,32]{0,1:T(8,128)} %fusion.26), channel_id=1, source_target_pairs={{0,2},{2,0},{1,3},{3,1},{4,6},{6,4},{5,7},{7,5},{8,10},{10,8},{9,1... | collective-permute-start | bytes 196616 | tf_op jit(solution)/shard_map/ppermute | solution.py:25
  163.7 54.2 %collective-permute-start.15 = (bf16[256,1024]{1,0:T(8,128)(2,1)}, bf16[256,1024]{1,0:T(8,128)(2,1)S(1)}, u32[]{:S(2)}, u32[]{:S(2)}) collective-permute-start(bf16[256,1024]{1,0:T(8,128)(2,1)} %get-tuple-element.74), channel_id=1, source_target_pairs={{0,4},{4,8},{8,12},{12,0},{1,5},{5,9},{9,13},{13,1},{2,6},{6,10},{... | collective-permute-start | bytes 1572872 | tf_op jit(solution)/shard_map/ppermute | solution.py:25
  169.0 58.6 %collective-permute-start.19 = (f32[512,32]{0,1:T(8,128)}, f32[512,32]{0,1:T(8,128)}, u32[]{:S(2)}, u32[]{:S(2)}) collective-permute-start(f32[512,32]{0,1:T(8,128)} %add.158), channel_id=1, source_target_pairs={{0,16},{1,17},{16,0},{17,1},{2,18},{3,19},{18,2},{19,3},{4,20},{5,... | collective-permute-start | bytes 196616 | tf_op jit(solution)/shard_map/ppermute | solution.py:25
  178.3 49.3 %collective-permute-start.20 = (f32[512,32]{0,1:T(8,128)}, f32[512,32]{0,1:T(8,128)}, u32[]{:S(2)}, u32[]{:S(2)}) collective-permute-start(f32[512,32]{0,1:T(8,128)} %add.158), channel_id=1, source_target_pairs={{0,17},{1,16},{16,1},{17,0},{2,19},{3,18},{18,3},{19,2},{4,21},{5,... | collective-permute-start | bytes 196616 | tf_op jit(solution)/shard_map/ppermute | solution.py:25
  178.4 16.8 %copy-start.2 = (bf16[384,1024]{1,0:T(8,128)(2,1)S(1)}, bf16[384,1024]{1,0:T(8,128)(2,1)}, u32[]{:S(2)}) copy-start(bf16[384,1024]{1,0:T(8,128)(2,1)} %constant_dynamic-slice_fusion.rest_0_) | copy-start | bytes 2359300
  178.4 16.8 %copy-start.3 = (bf16[384,1024]{1,0:T(8,128)(2,1)S(1)}, bf16[384,1024]{1,0:T(8,128)(2,1)}, u32[]{:S(2)}) copy-start(bf16[384,1024]{1,0:T(8,128)(2,1)} %slice.53.rest_1_) | copy-start | bytes 2359300
  178.4 16.8 %copy-start.4 = (bf16[384,1024]{1,0:T(8,128)(2,1)S(1)}, bf16[384,1024]{1,0:T(8,128)(2,1)}, u32[]{:S(2)}) copy-start(bf16[384,1024]{1,0:T(8,128)(2,1)} %slice.55.rest_2_) | copy-start | bytes 2359300
  195.2 36.1 %collective-permute-start.17 = (f32[512,32]{0,1:T(8,128)}, f32[512,32]{0,1:T(8,128)S(1)}, u32[]{:S(2)}, u32[]{:S(2)}) collective-permute-start(f32[512,32]{0,1:T(8,128)} %add.158), channel_id=1, source_target_pairs={{0,1},{1,0},{16,17},{17,16},{2,3},{3,2},{18,19},{19,18},{4,5},{5,4... | collective-permute-start | bytes 196616 | tf_op jit(solution)/shard_map/ppermute | solution.py:25
  230.3 27.8 %copy-start.1 = (bf16[512,2048]{1,0:T(8,128)(2,1)S(1)}, bf16[512,2048]{1,0:T(8,128)(2,1)}, u32[]{:S(2)}) copy-start(bf16[512,2048]{1,0:T(8,128)(2,1)} %param.8) | copy-start | bytes 6291460
  230.6 4.6 %collective-permute-start.21 = (f32[16,1024]{1,0:T(8,128)S(1)}, f32[16,1024]{1,0:T(8,128)S(1)}, u32[]{:S(2)}, u32[]{:S(2)}) collective-permute-start(f32[16,1024]{1,0:T(8,128)S(1)} %reshape.77), channel_id=1, source_target_pairs={{0,16},{16,0},{1,17},{17,1},{2,18},{18,2},{3,19},{19,3},{4,20},{20... | collective-permute-start | bytes 196616 | tf_op jit(solution)/shard_map/ppermute | solution.py:25
  235.1 4.3 %collective-permute-start.22 = (f32[16,1024]{1,0:T(8,128)S(1)}, f32[16,1024]{1,0:T(8,128)S(1)}, u32[]{:S(2)}, u32[]{:S(2)}) collective-permute-start(f32[16,1024]{1,0:T(8,128)S(1)} %add.159), channel_id=1, source_target_pairs={{0,2},{2,0},{1,3},{3,1},{4,6},{6,4},{5,7},{7,5},{8,10},{10,8},{9,1... | collective-permute-start | bytes 196616 | tf_op jit(solution)/shard_map/ppermute | solution.py:25
  239.5 1.3 collective-permute-start.23
  240.8 17.3 %copy-start.9 = (f32[16,1024]{1,0:T(8,128)}, f32[16,1024]{1,0:T(8,128)S(1)}, u32[]{:S(2)}) copy-start(f32[16,1024]{1,0:T(8,128)S(1)} %add.161.refs_0_) | copy-start | bytes 196612
  240.8 6.8 %collective-permute-start.24 = (f32[16,1024]{1,0:T(8,128)S(1)}, f32[16,1024]{1,0:T(8,128)S(1)}, u32[]{:S(2)}, u32[]{:S(2)}) collective-permute-start(f32[16,1024]{1,0:T(8,128)S(1)} %add.161.refs_0_), channel_id=1, source_target_pairs={{0,4},{4,8},{8,12},{12,0},{1,5},{5,9},{9,13},{13,1},{2,6},{6,10},{... | collective-permute-start | bytes 196616 | tf_op jit(solution)/shard_map/ppermute | solution.py:25
  240.9 8.6 %collective-permute-start.25 = (f32[16,1024]{1,0:T(8,128)S(1)}, f32[16,1024]{1,0:T(8,128)S(1)}, u32[]{:S(2)}, u32[]{:S(2)}) collective-permute-start(f32[16,1024]{1,0:T(8,128)S(1)} %add.161.refs_0_), channel_id=1, source_target_pairs={{0,8},{4,12},{8,0},{12,4},{1,9},{5,13},{9,1},{13,5},{2,10},{6,14},... | collective-permute-start | bytes 196616 | tf_op jit(solution)/shard_map/ppermute | solution.py:25
  241.0 8.5 %collective-permute-start.26 = (f32[16,1024]{1,0:T(8,128)S(1)}, f32[16,1024]{1,0:T(8,128)S(1)}, u32[]{:S(2)}, u32[]{:S(2)}) collective-permute-start(f32[16,1024]{1,0:T(8,128)S(1)} %add.161.refs_0_), channel_id=1, source_target_pairs={{0,12},{4,0},{8,4},{12,8},{1,13},{5,1},{9,5},{13,9},{2,14},{6,2},{... | collective-permute-start | bytes 196616 | tf_op jit(solution)/shard_map/ppermute | solution.py:25
  (8 other events, 84.3 us)

commit v12 on v11

--- a/solution.py
+++ b/solution.py
@@ -116,7 +116,9 @@
 
 
 def final_kernel(n, share, place_ref, queries_ref, *refs):
-    pieces, (fisher_ref, scores_ref, every_ref) = refs[:n], refs[n:]
+    pieces, (fisher_ref, scores_ref, every_ref, held_ref, sem) = refs[:n], refs[n:]
+    copy = pltpu.make_async_copy(queries_ref, held_ref, sem)
+    copy.start()
     docs, width = pieces[0].shape
     total = n * docs
     stage, which = place_ref[0], place_ref[1]
@@ -135,7 +137,6 @@
     lane = lax.broadcasted_iota(jnp.int32, (total, lanes), 1)
     own = (lane >= total) & (lane - total == row - stage * docs) & (lane < total + docs)
     table = dot3(every, tall, ((1,), (1,))) * scale + jnp.where((lane == row) | own, 1.0, 0.0)
-    products = dot3(every, queries_ref[...], ((1,), (1,)))
 
     def pick(condition, x, axis):
         return jnp.sum(jnp.where(condition, x, 0.0), axis=axis, keepdims=True)
@@ -158,6 +159,8 @@
         return jnp.where(row == k, new0, jnp.where(row == k + 1, new1, table))
 
     table = lax.fori_loop(0, total // 2, step, table)
+    copy.wait()
+    products = dot3(every, held_ref[...], ((1,), (1,)))
     scores_ref[...] = dot3(table, products, ((0,), (0,)))[total:total + docs]
 
 
@@ -171,10 +174,14 @@
             jax.ShapeDtypeStruct((share, width), jnp.float32),
             jax.ShapeDtypeStruct((docs, queries.shape[0]), jnp.float32),
         ),
-        in_specs=[pl.BlockSpec(memory_space=pltpu.SMEM)] + [in_vmem] * (n + 1),
+        in_specs=[pl.BlockSpec(memory_space=pltpu.SMEM), pl.BlockSpec(memory_space=pl.ANY)] + [in_vmem] * n,
         out_specs=(in_vmem, in_vmem),
-        scratch_shapes=[pltpu.VMEM((n * docs, width), jnp.float32)],
-        compiler_params=pltpu.CompilerParams(vmem_limit_bytes=32 * 1024 * 1024),
+        scratch_shapes=[
+            pltpu.VMEM((n * docs, width), jnp.float32),
+            pltpu.VMEM(queries.shape, jnp.float32),
+            pltpu.SemaphoreType.DMA,
+        ],
+        compiler_params=pltpu.CompilerParams(vmem_limit_bytes=56 * 1024 * 1024),
     )(jnp.stack([stage, which]).astype(jnp.int32), queries, *pieces)
 
 

time: 259 us -> 260 us (level)
  no operation moved by 1% of the time
where the time goes in v12:
time: 260 us; the launch traced here: 259 us
  waiting for transfers between devices  89.9 us (35%)
  local copies, waits for them, and re-layouts  70.7 us (27%)
  Pallas kernels  54.5 us (21%)
  starting transfers between devices  24.8 us (10%)
  other arithmetic  11.7 us (4%)
  matrix products  6.61 us (3%)
    ppermute x27, waiting for transfers between devices, shifted(): return lax.ppermute(x, axes, pairs)  89.9 us
    pallas_call x4, Pallas kernels, add_chunk(): pl.pallas_call(functools.partial(chunk_kernel, n, skip), out_shape=jax.Sh...  46 us
    dynamic_update_slice x8, local copies, waits for them, and re-layouts, place(): return lax.dynamic_update_slice(cot, block, ((dg * n_seq + ds) * rows, at))  26.2 us
    ppermute x27, starting transfers between devices, shifted(): return lax.ppermute(x, axes, pairs)  24.8 us
    dynamic_update_slice x4, local copies, waits for them, and re-layouts, on_device(): gate = lax.dynamic_update_slice(gate, gates[block], (number * rows, 0))  13 us
    pallas_call x1, Pallas kernels, finish(): pl.pallas_call(functools.partial(final_kernel, n, share), out_shape=(jax....  8.46 us
    dynamic_slice x1, local copies, waits for them, and re-layouts, unit_columns(): return lax.dynamic_slice_in_dim(gate_pre, first_unit(to), part, 1)  6.05 us
    broadcast_in_dim x1, local copies, waits for them, and re-layouts, on_device(): jnp.zeros((len(order) * rows, n_tensor * cotangent.shape[1]), cotangent.d...  5.99 us
  transfers between devices with their start and end apart: 27, of which 15 were waited for; matrix products, arithmetic and copies ran while one was open for 30% of the time, Pallas kernels for 18%

profile of v12, /device:TPU:0, one launch (start us, length us, event | category | flops | bytes accessed | tf_op | source)
XLA Modules:
  0.0 259.5 jit_solution(10486540661767648059)
XLA Ops:
  0.7 4.4 %constant_dynamic-slice_fusion.6.rest_0_ = bf16[1408,1024]{1,0:T(8,128)(2,1)} fusion(bf16[5504,1024]{1,0:T(8,128)(2,1)} %param.11, s32[]{:T(128)S(6)} %select_n.89), kind=kLoop, calls=%fused_computation.38 | loop fusion | bytes 5767172 | tf_op jit(solution)/shard_map/dynamic_slice | solution.py:211
  5.1 3.0 %collective-permute-start = (bf16[1408,1024]{1,0:T(8,128)(2,1)}, bf16[1408,1024]{1,0:T(8,128)(2,1)}, u32[]{:S(2)}, u32[]{:S(2)}) collective-permute-start(bf16[1408,1024]{1,0:T(8,128)(2,1)} %constant_dynamic-slice_fusion.6.rest_0_), channel_id=1, source_target_pairs={{0,4},{4,8},{8,12},{12,0},{1,5},{5,9},{9,13},{13,1},{2,6},{6,10},{... | collective-permute-start | bytes 8650760 | tf_op jit(solution)/shard_map/ppermute | solution.py:25
  15.3 6.0 %constant_dynamic-slice_fusion.3 = (bf16[512,1408]{1,0:T(8,128)(2,1)S(1)}, bf16[512,1408]{1,0:T(8,128)(2,1)S(1)}, bf16[512,1408]{1,0:T(8,128)(2,1)S(1)}, bf16[512,1408]{1,0:T(8,128)(2,1)S(1)}) fusion(bf16[512,5504]{1,0:T(8,128)(2,1)} %param.10, s32[]{:T(128)S(6)} %select_n.96, s32[]{:T(128)S(6)} %select_n.94, s32[]{:T(128)S(6)} %select_n.92, s32[]{:T(128)S(6)} %select_n.97), kind=kLoop, calls=%fused_computation.35 | loop fusion | bytes 11534352 | tf_op jit(solution)/shard_map/dynamic_slice | solution.py:224
  21.4 5.9 %pad_maximum_fusion = (bf16[1024,1408]{1,0:T(8,128)(2,1)S(1)}, bf16[1024,1408]{1,0:T(8,128)(2,1)}) fusion(bf16[512,1408]{1,0:T(8,128)(2,1)S(1)} %get-tuple-element.82, bf16[512,1408]{1,0:T(8,128)(2,1)S(1)} %get-tuple-element.83, bf16[512,1408]{1,0:T(8,128)(2,1)S(1)} %get-tuple-element.84, bf16[512,1408]{1,0:T(8,128)(2,1)S(1)} %get-tuple-element.81), kind=kLoop, calls=%fused_computation | loop fusion | flops 11534336 | bytes 11534336 | tf_op jit(solution)/shard_map/concatenate | solution.py:232
  27.3 28.2 %collective-permute-done.1 = bf16[512,2048]{1,0:T(8,128)(2,1)} collective-permute-done((bf16[512,2048]{1,0:T(8,128)(2,1)}, bf16[512,2048]{1,0:T(8,128)(2,1)}, u32[]{:S(2)}, u32[]{:S(2)}) %collective-permute-start.1) | collective-permute-done | bytes 2097184 | tf_op jit(solution)/shard_map/ppermute | solution.py:25
  56.8 16.2 %collective-permute-done.rest_1_ = bf16[1408,1024]{1,0:T(8,128)(2,1)} collective-permute-done((bf16[1408,1024]{1,0:T(8,128)(2,1)}, bf16[1408,1024]{1,0:T(8,128)(2,1)}, u32[]{:S(2)}, u32[]{:S(2)}) %collective-permute-start) | collective-permute-done | bytes 2883616 | tf_op jit(solution)/shard_map/ppermute | solution.py:25
  76.3 3.0 %collective-permute-done.10 = bf16[512,1408]{1,0:T(8,128)(2,1)} collective-permute-done((bf16[512,1408]{1,0:T(8,128)(2,1)S(1)}, bf16[512,1408]{1,0:T(8,128)(2,1)}, u32[]{:S(2)}, u32[]{:S(2)}) %collective-permute-start.10) | collective-permute-done | bytes 1441824 | tf_op jit(solution)/shard_map/ppermute | solution.py:25
  83.2 4.3 %dynamic_update_slice.44 = bf16[2048,1408]{1,0:T(8,128)(2,1)} pad(bf16[512,1408]{1,0:T(8,128)(2,1)} %get-tuple-element.88, bf16[]{:T(256)} %constant.100.clone.1), padding=0_1536x0_0 | pad | bytes 7208962 | tf_op jit(solution)/shard_map/dynamic_update_slice | solution.py:302
  89.6 6.0 %broadcast_in_dim.18 = bf16[2048,4096]{1,0:T(8,128)(2,1)} broadcast(bf16[]{:T(256)} %constant.100.clone.1), dimensions={} | broadcast | bytes 16777218 | tf_op jit(solution)/shard_map/broadcast_in_dim | solution.py:262
  95.6 3.3 %constant_dynamic-update-slice_fusion.3 = bf16[2048,4096]{1,0:T(8,128)(2,1)} fusion(bf16[2048,4096]{1,0:T(8,128)(2,1)} %broadcast_in_dim.18, bf16[512,2048]{1,0:T(8,128)(2,1)} %param.9, s32[]{:T(128)S(6)} %select_n.100), kind=kLoop, calls=%fused_computation.32 | loop fusion | bytes 4194308 | tf_op jit(solution)/shard_map/dynamic_update_slice | solution.py:220
  98.8 3.3 %constant_dynamic-update-slice_fusion.2 = bf16[2048,4096]{1,0:T(8,128)(2,1)} fusion(bf16[2048,4096]{1,0:T(8,128)(2,1)} %constant_dynamic-update-slice_fusion.3, bf16[512,2048]{1,0:T(8,128)(2,1)} %collective-permute-done.1, s32[]{:T(128)S(6)} %select_n.102), kind=kLoop, calls=%fused_computation.31 | loop fusion | bytes 4194308 | tf_op jit(solution)/shard_map/dynamic_update_slice | solution.py:220
  102.1 3.3 %constant_dynamic-update-slice_fusion.7 = bf16[2048,4096]{1,0:T(8,128)(2,1)} fusion(bf16[2048,4096]{1,0:T(8,128)(2,1)} %constant_dynamic-update-slice_fusion.2, bf16[512,2048]{1,0:T(8,128)(2,1)} %collective-permute-done.2, s32[]{:T(128)S(6)} %select_n.100), kind=kLoop, calls=%fused_computation.44 | loop fusion | bytes 4194308 | tf_op jit(solution)/shard_map/dynamic_update_slice | solution.py:220
  108.0 3.3 %constant_dynamic-update-slice_fusion.9 = bf16[2048,4096]{1,0:T(8,128)(2,1)} fusion(bf16[2048,4096]{1,0:T(8,128)(2,1)} %constant_dynamic-update-slice_fusion.7, bf16[512,2048]{1,0:T(8,128)(2,1)} %collective-permute-done.4, s32[]{:T(128)S(6)} %select_n.100), kind=kLoop, calls=%fused_computation.46 | loop fusion | bytes 4194308 | tf_op jit(solution)/shard_map/dynamic_update_slice | solution.py:220
  111.3 3.3 %constant_dynamic-update-slice_fusion.8 = bf16[2048,4096]{1,0:T(8,128)(2,1)} fusion(bf16[2048,4096]{1,0:T(8,128)(2,1)} %constant_dynamic-update-slice_fusion.9, bf16[512,2048]{1,0:T(8,128)(2,1)} %collective-permute-done.5, s32[]{:T(128)S(6)} %select_n.102), kind=kLoop, calls=%fused_computation.45 | loop fusion | bytes 4194308 | tf_op jit(solution)/shard_map/dynamic_update_slice | solution.py:220
  114.6 3.3 %constant_dynamic-update-slice_fusion.5 = bf16[2048,4096]{1,0:T(8,128)(2,1)} fusion(bf16[2048,4096]{1,0:T(8,128)(2,1)} %constant_dynamic-update-slice_fusion.8, bf16[512,2048]{1,0:T(8,128)(2,1)} %collective-permute-done.6, s32[]{:T(128)S(6)} %select_n.100), kind=kLoop, calls=%fused_computation.42 | loop fusion | bytes 4194308 | tf_op jit(solution)/shard_map/dynamic_update_slice | solution.py:220
  117.8 9.8 %collective-permute-done.7 = bf16[512,2048]{1,0:T(8,128)(2,1)} collective-permute-done((bf16[512,2048]{1,0:T(8,128)(2,1)}, bf16[512,2048]{1,0:T(8,128)(2,1)}, u32[]{:S(2)}, u32[]{:S(2)}) %collective-permute-start.7) | collective-permute-done | bytes 2097184 | tf_op jit(solution)/shard_map/ppermute | solution.py:25
  127.7 11.9 %collective-permute-done.8 = bf16[1024,1408]{1,0:T(8,128)(2,1)} collective-permute-done((bf16[1024,1408]{1,0:T(8,128)(2,1)}, bf16[1024,1408]{1,0:T(8,128)(2,1)}, u32[]{:S(2)}, u32[]{:S(2)}) %collective-permute-start.8) | collective-permute-done | bytes 2883616 | tf_op jit(solution)/shard_map/ppermute | solution.py:25
  139.5 2.9 %collective-permute-done.3.rest_2_ = bf16[1408,1024]{1,0:T(8,128)(2,1)S(1)} collective-permute-done((bf16[1408,1024]{1,0:T(8,128)(2,1)}, bf16[1408,1024]{1,0:T(8,128)(2,1)S(1)}, u32[]{:S(2)}, u32[]{:S(2)}) %collective-permute-start.3) | collective-permute-done | bytes 2883616 | tf_op jit(solution)/shard_map/ppermute | solution.py:25
  145.5 3.6 %slice_dynamic-update-slice_fusion = (bf16[2048,1408]{1,0:T(8,128)(2,1)}, bf16[512,1408]{1,0:T(8,128)(2,1)}) fusion(bf16[2048,1408]{1,0:T(8,128)(2,1)} %constant_dynamic-update-slice_fusion.1, bf16[1024,1408]{1,0:T(8,128)(2,1)} %collective-permute-done.8), kind=kLoop, calls=%fused_computation.6 | loop fusion | bytes 5767168 | tf_op jit(solution)/shard_map/dynamic_update_slice | solution.py:302
  151.3 3.3 %constant_dynamic-update-slice_fusion.6 = bf16[2048,4096]{1,0:T(8,128)(2,1)} fusion(bf16[2048,4096]{1,0:T(8,128)(2,1)} %constant_dynamic-update-slice_fusion.5, bf16[512,2048]{1,0:T(8,128)(2,1)} %collective-permute-done.7, s32[]{:T(128)S(6)} %select_n.102), kind=kLoop, calls=%fused_computation.43 | loop fusion | bytes 4194308 | tf_op jit(solution)/shard_map/dynamic_update_slice | solution.py:220
  163.7 3.9 %collective-permute-start.15 = (bf16[256,1024]{1,0:T(8,128)(2,1)}, bf16[256,1024]{1,0:T(8,128)(2,1)S(1)}, u32[]{:S(2)}, u32[]{:S(2)}) collective-permute-start(bf16[256,1024]{1,0:T(8,128)(2,1)} %get-tuple-element.74), channel_id=1, source_target_pairs={{0,4},{4,8},{8,12},{12,0},{1,5},{5,9},{9,13},{13,1},{2,6},{6,10},{... | collective-permute-start | bytes 1572872 | tf_op jit(solution)/shard_map/ppermute | solution.py:25
  170.6 3.2 %constant_dynamic-update-slice_fusion.4.cot_ref = bf16[2048,4096]{1,0:T(8,128)(2,1)} fusion(bf16[2048,4096]{1,0:T(8,128)(2,1)} %constant_dynamic-update-slice_fusion.6, bf16[512,2048]{1,0:T(8,128)(2,1)} %collective-permute-done.9, s32[]{:T(128)S(6)} %select_n.102), kind=kLoop, calls=%fused_computation.41 | loop fusion | bytes 4194308 | tf_op jit(solution)/shard_map/dynamic_update_slice | solution.py:220
  173.8 4.5 %collective-permute-done.12.rest_3_ = bf16[512,1024]{1,0:T(8,128)(2,1)} collective-permute-done((bf16[512,1024]{1,0:T(8,128)(2,1)}, bf16[512,1024]{1,0:T(8,128)(2,1)}, u32[]{:S(2)}, u32[]{:S(2)}) %collective-permute-start.12) | collective-permute-done | bytes 1048608 | tf_op jit(solution)/shard_map/ppermute | solution.py:25
  178.5 13.9 %shard_map.103.before_ref = f32[2048,32]{1,0:T(8,128)S(1)} custom-call(s32[1]{0:T(128)} %bitcast.me_ref, bf16[2048,4096]{1,0:T(8,128)(2,1)} %constant_dynamic-update-slice_fusion.4.cot_ref, bf16[2048,1408]{1,0:T(8,128)(2,1)} %constant_dynamic-update-slice_fusion.gate_ref, bf16[512,32]{1,0:T(8,128)(2,1)S(1)} %slice.64.factor_ref, ...), custom_call_target="tpu_custom_call" | custom-call | flops 8589934592 | bytes 23068672 | tf_op jit(solution)/shard_map/pallas_call | solution.py:85
  192.4 2.8 %collective-permute-done.13.rest_3_ = bf16[384,1024]{1,0:T(8,128)(2,1)} collective-permute-done((bf16[384,1024]{1,0:T(8,128)(2,1)}, bf16[384,1024]{1,0:T(8,128)(2,1)}, u32[]{:S(2)}, u32[]{:S(2)}) %collective-permute-start.13) | collective-permute-done | bytes 786464 | tf_op jit(solution)/shard_map/ppermute | solution.py:25
  195.2 13.2 %shard_map.104.before_ref = f32[2048,32]{1,0:T(8,128)S(1)} custom-call(s32[1]{0:T(128)} %bitcast.me_ref, bf16[2048,4096]{1,0:T(8,128)(2,1)} %constant_dynamic-update-slice_fusion.4.cot_ref, bf16[2048,1408]{1,0:T(8,128)(2,1)} %constant_dynamic-update-slice_fusion.gate_ref, bf16[384,32]{1,0:T(8,128)(2,1)S(1)} %copy-done.5, ...), custom_call_target="tpu_custom_call" | custom-call | flops 6442450944 | bytes 21495808 | tf_op jit(solution)/shard_map/pallas_call | solution.py:85
  208.5 9.4 %shard_map.105.before_ref = f32[2048,32]{1,0:T(8,128)S(1)} custom-call(s32[1]{0:T(128)} %bitcast.me_ref, bf16[2048,4096]{1,0:T(8,128)(2,1)} %constant_dynamic-update-slice_fusion.4.cot_ref, bf16[2048,1408]{1,0:T(8,128)(2,1)} %constant_dynamic-update-slice_fusion.gate_ref, bf16[256,32]{1,0:T(8,128)(2,1)S(1)} %copy-done.7, ...), custom_call_target="tpu_custom_call" | custom-call | flops 4294967296 | bytes 19922944 | tf_op jit(solution)/shard_map/pallas_call | solution.py:85
  218.0 9.4 %shard_map.106 = f32[2048,32]{1,0:T(8,128)S(1)} custom-call(s32[1]{0:T(128)} %bitcast.me_ref, bf16[2048,4096]{1,0:T(8,128)(2,1)} %constant_dynamic-update-slice_fusion.4.cot_ref, bf16[2048,1408]{1,0:T(8,128)(2,1)} %constant_dynamic-update-slice_fusion.gate_ref, bf16[256,32]{1,0:T(8,128)(2,1)S(1)} %copy-done.6, f32[2048,32]{1,0:T(8,128)S(1)} %shard_map.105.before_ref, ...), custom_call_target="tpu_custom_call" | custom-call | flops 4294967296 | bytes 19922944 | tf_op jit(solution)/shard_map/pallas_call | solution.py:85
  227.7 2.6 %fusion.7 = f32[16,32,32]{2,0,1:T(8,128)S(1)} fusion(f32[1024,16]{0,1:T(8,128)S(1)} %copy-done.14, f32[1024,32]{0,1:T(8,128)S(1)} %copy.29, f32[512,32]{0,1:T(8,128)} %collective-permute-done.20, f32[512,32]{0,1:T(8,128)} %collective-permute-done.19), kind=kOutput, calls=%fused_computation.8 | convolution fusion | flops 201883648 | bytes 393216 | tf_op jit(solution)/shard_map/tc,ti,tj->cij/dot_general | solution.py:319
  236.7 2.8 %collective-permute-done.22 = f32[16,1024]{1,0:T(8,128)S(1)} collective-permute-done((f32[16,1024]{1,0:T(8,128)S(1)}, f32[16,1024]{1,0:T(8,128)S(1)}, u32[]{:S(2)}, u32[]{:S(2)}) %collective-permute-start.22) | collective-permute-done | bytes 65568 | tf_op jit(solution)/shard_map/ppermute | solution.py:25
  241.0 3.7 %collective-permute-start.26 = (f32[16,1024]{1,0:T(8,128)S(1)}, f32[16,1024]{1,0:T(8,128)S(1)}, u32[]{:S(2)}, u32[]{:S(2)}) collective-permute-start(f32[16,1024]{1,0:T(8,128)S(1)} %add.161.refs_0_), channel_id=1, source_target_pairs={{0,12},{4,0},{8,4},{12,8},{1,13},{5,1},{9,5},{13,9},{2,14},{6,2},{... | collective-permute-start | bytes 196616 | tf_op jit(solution)/shard_map/ppermute | solution.py:25
  250.8 8.5 %shard_map.107 = (f32[256,1024]{1,0:T(8,128)}, f32[16,512]{1,0:T(8,128)}) custom-call(s32[2]{0:T(128)} %pad_add_fusion.1.place_ref, f32[512,1024]{1,0:T(8,128)} %queries_ref.1, f32[16,1024]{1,0:T(8,128)} %copy-done.8, f32[16,1024]{1,0:T(8,128)} %copy-done.10, f32[16,1024]{1,0:T(8,128)} %copy-done.11, f32[16,1024]{1,0:T(8,128)} %copy-done.12), custom_call_target="tpu_custom_call" | custom-call | tf_op jit(solution)/shard_map/pallas_call | solution.py:171
  (113 shorter events, 51.9 us)
Async XLA Ops:
  5.1 67.8 %collective-permute-start = (bf16[1408,1024]{1,0:T(8,128)(2,1)}, bf16[1408,1024]{1,0:T(8,128)(2,1)}, u32[]{:S(2)}, u32[]{:S(2)}) collective-permute-start(bf16[1408,1024]{1,0:T(8,128)(2,1)} %constant_dynamic-slice_fusion.6.rest_0_), channel_id=1, source_target_pairs={{0,4},{4,8},{8,12},{12,0},{1,5},{5,9},{9,13},{13,1},{2,6},{6,10},{... | collective-permute-start | bytes 8650760 | tf_op jit(solution)/shard_map/ppermute | solution.py:25
  8.1 47.4 %collective-permute-start.1 = (bf16[512,2048]{1,0:T(8,128)(2,1)}, bf16[512,2048]{1,0:T(8,128)(2,1)}, u32[]{:S(2)}, u32[]{:S(2)}) collective-permute-start(bf16[512,2048]{1,0:T(8,128)(2,1)} %param.9), channel_id=1, source_target_pairs={{0,2},{2,0},{1,3},{3,1},{4,6},{6,4},{5,7},{7,5},{8,10},{10,8},{9,1... | collective-permute-start | bytes 6291464 | tf_op jit(solution)/shard_map/ppermute | solution.py:25
  9.6 47.1 %collective-permute-start.2 = (bf16[512,2048]{1,0:T(8,128)(2,1)}, bf16[512,2048]{1,0:T(8,128)(2,1)}, u32[]{:S(2)}, u32[]{:S(2)}) collective-permute-start(bf16[512,2048]{1,0:T(8,128)(2,1)} %param.9), channel_id=1, source_target_pairs={{0,16},{16,0},{1,17},{17,1},{2,18},{18,2},{3,19},{19,3},{4,20},{20... | collective-permute-start | bytes 6291464 | tf_op jit(solution)/shard_map/ppermute | solution.py:25
  73.0 6.5 %collective-permute-start.4 = (bf16[512,2048]{1,0:T(8,128)(2,1)}, bf16[512,2048]{1,0:T(8,128)(2,1)}, u32[]{:S(2)}, u32[]{:S(2)}) collective-permute-start(bf16[512,2048]{1,0:T(8,128)(2,1)} %param.9), channel_id=1, source_target_pairs={{0,1},{1,0},{2,3},{3,2},{4,5},{5,4},{6,7},{7,6},{8,9},{9,8},{10,11... | collective-permute-start | bytes 6291464 | tf_op jit(solution)/shard_map/ppermute | solution.py:25
  74.3 5.0 %collective-permute-start.10 = (bf16[512,1408]{1,0:T(8,128)(2,1)S(1)}, bf16[512,1408]{1,0:T(8,128)(2,1)}, u32[]{:S(2)}, u32[]{:S(2)}) collective-permute-start(bf16[512,1408]{1,0:T(8,128)(2,1)S(1)} %get-tuple-element.87), channel_id=1, source_target_pairs={{0,1},{1,0},{2,3},{3,2},{4,5},{5,4},{6,7},{7,6},{8,9},{9,8},{10,11... | collective-permute-start | bytes 4325384 | tf_op jit(solution)/shard_map/ppermute | solution.py:25
  74.8 64.7 %collective-permute-start.8 = (bf16[1024,1408]{1,0:T(8,128)(2,1)}, bf16[1024,1408]{1,0:T(8,128)(2,1)}, u32[]{:S(2)}, u32[]{:S(2)}) collective-permute-start(bf16[1024,1408]{1,0:T(8,128)(2,1)} %get-tuple-element.47), channel_id=1, source_target_pairs={{0,16},{16,0},{1,17},{17,1},{2,18},{18,2},{3,19},{19,3},{4,20},{20... | collective-permute-start | bytes 8650760 | tf_op jit(solution)/shard_map/ppermute | solution.py:25
  76.3 66.1 %collective-permute-start.3 = (bf16[1408,1024]{1,0:T(8,128)(2,1)}, bf16[1408,1024]{1,0:T(8,128)(2,1)S(1)}, u32[]{:S(2)}, u32[]{:S(2)}) collective-permute-start(bf16[1408,1024]{1,0:T(8,128)(2,1)} %collective-permute-done.rest_1_), channel_id=1, source_target_pairs={{0,4},{4,8},{8,12},{12,0},{1,5},{5,9},{9,13},{13,1},{2,6},{6,10},{... | collective-permute-start | bytes 8650760 | tf_op jit(solution)/shard_map/ppermute | solution.py:25
  76.3 34.9 %collective-permute-start.5 = (bf16[512,2048]{1,0:T(8,128)(2,1)}, bf16[512,2048]{1,0:T(8,128)(2,1)}, u32[]{:S(2)}, u32[]{:S(2)}) collective-permute-start(bf16[512,2048]{1,0:T(8,128)(2,1)} %collective-permute-done.1), channel_id=1, source_target_pairs={{0,1},{1,0},{2,3},{3,2},{4,5},{5,4},{6,7},{7,6},{8,9},{9,8},{10,11... | collective-permute-start | bytes 6291464 | tf_op jit(solution)/shard_map/ppermute | solution.py:25
  79.3 35.3 %collective-permute-start.6 = (bf16[512,2048]{1,0:T(8,128)(2,1)}, bf16[512,2048]{1,0:T(8,128)(2,1)}, u32[]{:S(2)}, u32[]{:S(2)}) collective-permute-start(bf16[512,2048]{1,0:T(8,128)(2,1)} %collective-permute-done.2), channel_id=1, source_target_pairs={{0,1},{1,0},{2,3},{3,2},{4,5},{5,4},{6,7},{7,6},{8,9},{9,8},{10,11... | collective-permute-start | bytes 6291464 | tf_op jit(solution)/shard_map/ppermute | solution.py:25
  79.5 48.2 %collective-permute-start.7 = (bf16[512,2048]{1,0:T(8,128)(2,1)}, bf16[512,2048]{1,0:T(8,128)(2,1)}, u32[]{:S(2)}, u32[]{:S(2)}) collective-permute-start(bf16[512,2048]{1,0:T(8,128)(2,1)} %collective-permute-done.2), channel_id=1, source_target_pairs={{0,2},{2,0},{1,3},{3,1},{4,6},{6,4},{5,7},{7,5},{8,10},{10,8},{9,1... | collective-permute-start | bytes 6291464 | tf_op jit(solution)/shard_map/ppermute | solution.py:25
  149.1 5.5 %collective-permute-start.11 = (bf16[512,1408]{1,0:T(8,128)(2,1)}, bf16[512,1408]{1,0:T(8,128)(2,1)}, u32[]{:S(2)}, u32[]{:S(2)}) collective-permute-start(bf16[512,1408]{1,0:T(8,128)(2,1)} %get-tuple-element.86), channel_id=1, source_target_pairs={{0,1},{1,0},{2,3},{3,2},{4,5},{5,4},{6,7},{7,6},{8,9},{9,8},{10,11... | collective-permute-start | bytes 4325384 | tf_op jit(solution)/shard_map/ppermute | solution.py:25
  149.1 19.9 %collective-permute-start.9 = (bf16[512,2048]{1,0:T(8,128)(2,1)}, bf16[512,2048]{1,0:T(8,128)(2,1)}, u32[]{:S(2)}, u32[]{:S(2)}) collective-permute-start(bf16[512,2048]{1,0:T(8,128)(2,1)} %collective-permute-done.7), channel_id=1, source_target_pairs={{0,1},{1,0},{2,3},{3,2},{4,5},{5,4},{6,7},{7,6},{8,9},{9,8},{10,11... | collective-permute-start | bytes 6291464 | tf_op jit(solution)/shard_map/ppermute | solution.py:25
  150.2 28.1 %collective-permute-start.12 = (bf16[512,1024]{1,0:T(8,128)(2,1)}, bf16[512,1024]{1,0:T(8,128)(2,1)}, u32[]{:S(2)}, u32[]{:S(2)}) collective-permute-start(bf16[512,1024]{1,0:T(8,128)(2,1)} %slice.54), channel_id=1, source_target_pairs={{0,4},{4,8},{8,12},{12,0},{1,5},{5,9},{9,13},{13,1},{2,6},{6,10},{... | collective-permute-start | bytes 3145736 | tf_op jit(solution)/shard_map/ppermute | solution.py:25
  150.2 45.0 %collective-permute-start.13 = (bf16[384,1024]{1,0:T(8,128)(2,1)}, bf16[384,1024]{1,0:T(8,128)(2,1)}, u32[]{:S(2)}, u32[]{:S(2)}) collective-permute-start(bf16[384,1024]{1,0:T(8,128)(2,1)} %slice.55.rest_2_), channel_id=1, source_target_pairs={{0,4},{4,8},{8,12},{12,0},{1,5},{5,9},{9,13},{13,1},{2,6},{6,10},{... | collective-permute-start | bytes 2359304 | tf_op jit(solution)/shard_map/ppermute | solution.py:25
  150.2 58.3 %collective-permute-start.14 = (bf16[256,1024]{1,0:T(8,128)(2,1)}, bf16[256,1024]{1,0:T(8,128)(2,1)S(1)}, u32[]{:S(2)}, u32[]{:S(2)}) collective-permute-start(bf16[256,1024]{1,0:T(8,128)(2,1)} %get-tuple-element.73), channel_id=1, source_target_pairs={{0,4},{4,8},{8,12},{12,0},{1,5},{5,9},{9,13},{13,1},{2,6},{6,10},{... | collective-permute-start | bytes 1572872 | tf_op jit(solution)/shard_map/ppermute | solution.py:25
  154.6 4.5 %collective-permute-start.18 = (s32[1,16]{1,0:T(1,128)}, s32[1,16]{1,0:T(1,128)}, u32[]{:S(2)}, u32[]{:S(2)}) collective-permute-start(s32[1,16]{1,0:T(1,128)} %param.14), channel_id=1, source_target_pairs={{0,16},{16,0},{1,17},{17,1},{2,18},{18,2},{3,19},{19,3},{4,20},{20... | collective-permute-start | bytes 200 | tf_op jit(solution)/shard_map/ppermute | solution.py:25
  159.1 4.6 %collective-permute-start.16 = (f32[512,32]{0,1:T(8,128)}, f32[512,32]{0,1:T(8,128)}, u32[]{:S(2)}, u32[]{:S(2)}) collective-permute-start(f32[512,32]{0,1:T(8,128)} %fusion.26), channel_id=1, source_target_pairs={{0,2},{2,0},{1,3},{3,1},{4,6},{6,4},{5,7},{7,5},{8,10},{10,8},{9,1... | collective-permute-start | bytes 196616 | tf_op jit(solution)/shard_map/ppermute | solution.py:25
  163.7 54.3 %collective-permute-start.15 = (bf16[256,1024]{1,0:T(8,128)(2,1)}, bf16[256,1024]{1,0:T(8,128)(2,1)S(1)}, u32[]{:S(2)}, u32[]{:S(2)}) collective-permute-start(bf16[256,1024]{1,0:T(8,128)(2,1)} %get-tuple-element.74), channel_id=1, source_target_pairs={{0,4},{4,8},{8,12},{12,0},{1,5},{5,9},{9,13},{13,1},{2,6},{6,10},{... | collective-permute-start | bytes 1572872 | tf_op jit(solution)/shard_map/ppermute | solution.py:25
  169.1 58.6 %collective-permute-start.19 = (f32[512,32]{0,1:T(8,128)}, f32[512,32]{0,1:T(8,128)}, u32[]{:S(2)}, u32[]{:S(2)}) collective-permute-start(f32[512,32]{0,1:T(8,128)} %add.158), channel_id=1, source_target_pairs={{0,16},{1,17},{16,0},{17,1},{2,18},{3,19},{18,2},{19,3},{4,20},{5,... | collective-permute-start | bytes 196616 | tf_op jit(solution)/shard_map/ppermute | solution.py:25
  178.4 49.3 %collective-permute-start.20 = (f32[512,32]{0,1:T(8,128)}, f32[512,32]{0,1:T(8,128)}, u32[]{:S(2)}, u32[]{:S(2)}) collective-permute-start(f32[512,32]{0,1:T(8,128)} %add.158), channel_id=1, source_target_pairs={{0,17},{1,16},{16,1},{17,0},{2,19},{3,18},{18,3},{19,2},{4,21},{5,... | collective-permute-start | bytes 196616 | tf_op jit(solution)/shard_map/ppermute | solution.py:25
  178.4 16.8 %copy-start.2 = (bf16[384,1024]{1,0:T(8,128)(2,1)S(1)}, bf16[384,1024]{1,0:T(8,128)(2,1)}, u32[]{:S(2)}) copy-start(bf16[384,1024]{1,0:T(8,128)(2,1)} %constant_dynamic-slice_fusion.rest_0_) | copy-start | bytes 2359300
  178.5 16.8 %copy-start.3 = (bf16[384,1024]{1,0:T(8,128)(2,1)S(1)}, bf16[384,1024]{1,0:T(8,128)(2,1)}, u32[]{:S(2)}) copy-start(bf16[384,1024]{1,0:T(8,128)(2,1)} %slice.53.rest_1_) | copy-start | bytes 2359300
  178.5 16.8 %copy-start.4 = (bf16[384,1024]{1,0:T(8,128)(2,1)S(1)}, bf16[384,1024]{1,0:T(8,128)(2,1)}, u32[]{:S(2)}) copy-start(bf16[384,1024]{1,0:T(8,128)(2,1)} %slice.55.rest_2_) | copy-start | bytes 2359300
  178.5 16.8 %copy-start.5 = (bf16[384,32]{1,0:T(8,128)(2,1)S(1)}, bf16[384,32]{1,0:T(8,128)(2,1)}, u32[]{:S(2)}) copy-start(bf16[384,32]{1,0:T(8,128)(2,1)} %slice.65.factor_ref) | copy-start | bytes 73732
  195.2 36.1 %collective-permute-start.17 = (f32[512,32]{0,1:T(8,128)}, f32[512,32]{0,1:T(8,128)S(1)}, u32[]{:S(2)}, u32[]{:S(2)}) collective-permute-start(f32[512,32]{0,1:T(8,128)} %add.158), channel_id=1, source_target_pairs={{0,1},{1,0},{16,17},{17,16},{2,3},{3,2},{18,19},{19,18},{4,5},{5,4... | collective-permute-start | bytes 196616 | tf_op jit(solution)/shard_map/ppermute | solution.py:25
  230.4 28.9 %copy-start.1 = (bf16[512,2048]{1,0:T(8,128)(2,1)S(1)}, bf16[512,2048]{1,0:T(8,128)(2,1)}, u32[]{:S(2)}) copy-start(bf16[512,2048]{1,0:T(8,128)(2,1)} %param.8) | copy-start | bytes 6291460
  230.6 4.6 %collective-permute-start.21 = (f32[16,1024]{1,0:T(8,128)S(1)}, f32[16,1024]{1,0:T(8,128)S(1)}, u32[]{:S(2)}, u32[]{:S(2)}) collective-permute-start(f32[16,1024]{1,0:T(8,128)S(1)} %reshape.77), channel_id=1, source_target_pairs={{0,16},{16,0},{1,17},{17,1},{2,18},{18,2},{3,19},{19,3},{4,20},{20... | collective-permute-start | bytes 196616 | tf_op jit(solution)/shard_map/ppermute | solution.py:25
  235.2 4.3 %collective-permute-start.22 = (f32[16,1024]{1,0:T(8,128)S(1)}, f32[16,1024]{1,0:T(8,128)S(1)}, u32[]{:S(2)}, u32[]{:S(2)}) collective-permute-start(f32[16,1024]{1,0:T(8,128)S(1)} %add.159), channel_id=1, source_target_pairs={{0,2},{2,0},{1,3},{3,1},{4,6},{6,4},{5,7},{7,5},{8,10},{10,8},{9,1... | collective-permute-start | bytes 196616 | tf_op jit(solution)/shard_map/ppermute | solution.py:25
  239.5 1.3 collective-permute-start.23
  240.9 6.8 %collective-permute-start.24 = (f32[16,1024]{1,0:T(8,128)S(1)}, f32[16,1024]{1,0:T(8,128)S(1)}, u32[]{:S(2)}, u32[]{:S(2)}) collective-permute-start(f32[16,1024]{1,0:T(8,128)S(1)} %add.161.refs_0_), channel_id=1, source_target_pairs={{0,4},{4,8},{8,12},{12,0},{1,5},{5,9},{9,13},{13,1},{2,6},{6,10},{... | collective-permute-start | bytes 196616 | tf_op jit(solution)/shard_map/ppermute | solution.py:25
  240.9 8.6 %collective-permute-start.25 = (f32[16,1024]{1,0:T(8,128)S(1)}, f32[16,1024]{1,0:T(8,128)S(1)}, u32[]{:S(2)}, u32[]{:S(2)}) collective-permute-start(f32[16,1024]{1,0:T(8,128)S(1)} %add.161.refs_0_), channel_id=1, source_target_pairs={{0,8},{4,12},{8,0},{12,4},{1,9},{5,13},{9,1},{13,5},{2,10},{6,14},... | collective-permute-start | bytes 196616 | tf_op jit(solution)/shard_map/ppermute | solution.py:25
  241.0 8.5 %collective-permute-start.26 = (f32[16,1024]{1,0:T(8,128)S(1)}, f32[16,1024]{1,0:T(8,128)S(1)}, u32[]{:S(2)}, u32[]{:S(2)}) collective-permute-start(f32[16,1024]{1,0:T(8,128)S(1)} %add.161.refs_0_), channel_id=1, source_target_pairs={{0,12},{4,0},{8,4},{12,8},{1,13},{5,1},{9,5},{13,9},{2,14},{6,2},{... | collective-permute-start | bytes 196616 | tf_op jit(solution)/shard_map/ppermute | solution.py:25
  (10 other events, 77.8 us)
